TPU v7x, 32 devices: a whole 2x2x4 slice. The times are simulated.
32 devices in a mesh: dp: 8 (over z, x), tensor: 4 (over y, core).
Axes of the slice: x: 2, y: 2, z: 4, core: 2. Of those that a mesh axis runs over, the one named last changes fastest.
Arguments:
- inputs: bfloat16 [8192, 2048], P(('dp', 'tensor')), may hold values from -6 to 6
- segment_ids: int32 [8192], P('dp'), may hold values from 0 to 127, never falling along the last dimension, each value on 1 to 1024 neighbouring positions
- gain_mixer: bfloat16 [2048], P('dp'), may hold values from 0.5 to 1.5
- branch_weight: bfloat16 [2048, 2560], P('dp', 'tensor'), may hold values from -0.125 to 0.125
- input_weight: bfloat16 [2048, 2560], P('dp', 'tensor'), may hold values from -0.125 to 0.125
- conv_weight: bfloat16 [4, 16, 160], P(None, 'tensor', 'dp'), may hold values from -3 to 3
- conv_bias: bfloat16 [16, 160], P('tensor', 'dp'), may hold values from -1.5 to 1.5
- rate_weight: bfloat16 [16, 160, 160], P('tensor', 'dp'), may hold values from -0.5 to 0.5
- rate_bias: bfloat16 [16, 160], P('tensor', 'dp'), may hold values from -3 to 3
- entry_weight: bfloat16 [16, 160, 160], P('tensor', 'dp'), may hold values from -0.5 to 0.5
- entry_bias: bfloat16 [16, 160], P('tensor', 'dp'), may hold values from -3 to 3
- decay_param: bfloat16 [16, 160], P('tensor', 'dp'), may hold values from 2 to 6
- output_weight: bfloat16 [2560, 2048], P('tensor', 'dp'), may hold values from -0.5 to 0.5
- gain_mlp: bfloat16 [2048], P('dp'), may hold values from 0.5 to 1.5
- gate_weight: bfloat16 [2048, 6144], P('dp', 'tensor'), may hold values from -0.125 to 0.125
- up_weight: bfloat16 [2048, 6144], P('dp', 'tensor'), may hold values from -0.125 to 0.125
- down_weight: bfloat16 [6144, 2048], P('tensor', 'dp'), may hold values from -0.15625 to 0.15625
- cotangent: bfloat16 [8192, 2048], P(('dp', 'tensor')), may hold values from -6 to 6
Outputs:
- layer_out: bfloat16 [8192, 2048], P(('dp', 'tensor'))
- inputs_grad: bfloat16 [8192, 2048], P(('dp', 'tensor'))
- gain_mixer_grad: float32 [2048], P('dp')
- branch_weight_grad: float32 [2048, 2560], P('dp', 'tensor')
- input_weight_grad: float32 [2048, 2560], P('dp', 'tensor')
- conv_weight_grad: float32 [4, 16, 160], P(None, 'tensor', 'dp')
- conv_bias_grad: float32 [16, 160], P('tensor', 'dp')
- rate_weight_grad: float32 [16, 160, 160], P('tensor', 'dp')
- rate_bias_grad: float32 [16, 160], P('tensor', 'dp')
- entry_weight_grad: float32 [16, 160, 160], P('tensor', 'dp')
- entry_bias_grad: float32 [16, 160], P('tensor', 'dp')
- decay_param_grad: float32 [16, 160], P('tensor', 'dp')
- output_weight_grad: float32 [2560, 2048], P('tensor', 'dp')
- gain_mlp_grad: float32 [2048], P('dp')
- gate_weight_grad: float32 [2048, 6144], P('dp', 'tensor')
- up_weight_grad: float32 [2048, 6144], P('dp', 'tensor')
- down_weight_grad: float32 [6144, 2048], P('tensor', 'dp')
Inputs may be any that keep to these rules, and one draw needn't show every extreme that they name: `segment_ids`: ids never fall along the tokens; each document holds 1 to 1024 tokens, and a document that crosses a sequence's end restarts there.
All inputs are finite; a program needn't handle non-finite values.
Results may differ from a plain program's by a relative error of at most 0.023.
Values may be sent and summed in bfloat16 or wider, within the bound.
No kernel may reach another device: no remote copies, remote signals or barrier semaphores. Data moves between devices by JAX's collectives and lax.ppermute only.
A program may use at most 256 MiB of HBM per device.

v0:
```python
import jax
import jax.numpy as jnp
from jax import lax
from jax.sharding import PartitionSpec as P

epsilon = 1e-06
lru_scale = 8.0


def rms_norm(values, gain):
    scale = lax.rsqrt(jnp.mean(values * values, axis=-1, keepdims=True) + epsilon)
    return values * scale * gain


def shifted(values, offset, fill):
    head = jnp.full((offset,) + values.shape[1:], fill, values.dtype)
    return jnp.concatenate([head, values[: values.shape[0] - offset]], axis=0)


def combine(first, second):
    return (first[0] * second[0], second[0] * first[1] + second[1])


def recurrent_core(
    branch_pre,
    entry_pre,
    conv_weight,
    conv_bias,
    rate_weight,
    rate_bias,
    entry_weight,
    entry_bias,
    decay_param,
    segment_ids,
):
    length, width = entry_pre.shape
    blocks = rate_weight.shape[0]
    block_width = rate_weight.shape[1]
    taps = conv_weight.shape[0]
    kernel = conv_weight.reshape(taps, width)
    mixed = entry_pre * kernel[0] + conv_bias.reshape(width)
    for offset in range(1, taps):
        earlier = shifted(segment_ids, offset, -1)
        same = (earlier == segment_ids).astype(entry_pre.dtype)[:, None]
        mixed = mixed + shifted(entry_pre, offset, 0.0) * same * kernel[offset]
    grouped = mixed.reshape(length, blocks, block_width)
    highest = lax.Precision.HIGHEST
    rate_pre = jnp.einsum("lhi,hij->lhj", grouped, rate_weight, precision=highest) + rate_bias
    entry_gate_pre = (
        jnp.einsum("lhi,hij->lhj", grouped, entry_weight, precision=highest) + entry_bias
    )
    rate = jax.nn.sigmoid(rate_pre).reshape(length, width)
    entry = jax.nn.sigmoid(entry_gate_pre).reshape(length, width)
    log_decay = -lru_scale * rate * jax.nn.softplus(-decay_param.reshape(width))
    start = (shifted(segment_ids, 1, -1) != segment_ids)[:, None]
    decay = jnp.where(start, 0.0, jnp.exp(log_decay))
    factor = jnp.where(start, 1.0, jnp.sqrt(-jnp.expm1(2.0 * log_decay)))
    drive = factor * entry * mixed
    carried, state = lax.associative_scan(combine, (decay, drive), axis=0)
    return jax.nn.gelu(branch_pre) * state


def gated_unit(gate_value, up_value):
    return jax.nn.gelu(gate_value) * up_value


def dot_rows(left, right):
    return lax.dot_general(
        left, right, (((0,), (0,)), ((), ())), preferred_element_type=jnp.float32
    )


def dot_back(left, right):
    return lax.dot_general(
        left, right, (((1,), (1,)), ((), ())), preferred_element_type=jnp.float32
    )


def body(
    inputs,
    segment_ids,
    gain_mixer,
    branch_weight,
    input_weight,
    conv_weight,
    conv_bias,
    rate_weight,
    rate_bias,
    entry_weight,
    entry_bias,
    decay_param,
    output_weight,
    gain_mlp,
    gate_weight,
    up_weight,
    down_weight,
    cotangent,
):
    (
        gain_one,
        branch_full,
        input_full,
        conv_full,
        conv_bias_full,
        rate_full,
        rate_bias_full,
        entry_full,
        entry_bias_full,
        decay_full,
        output_full,
    ) = (
        lax.all_gather(gain_mixer, "dp", axis=0, tiled=True),
        lax.all_gather(branch_weight, "dp", axis=0, tiled=True),
        lax.all_gather(input_weight, "dp", axis=0, tiled=True),
        lax.all_gather(conv_weight, "dp", axis=2, tiled=True),
        lax.all_gather(conv_bias, "dp", axis=1, tiled=True),
        lax.all_gather(rate_weight, "dp", axis=1, tiled=True),
        lax.all_gather(rate_bias, "dp", axis=1, tiled=True),
        lax.all_gather(entry_weight, "dp", axis=1, tiled=True),
        lax.all_gather(entry_bias, "dp", axis=1, tiled=True),
        lax.all_gather(decay_param, "dp", axis=1, tiled=True),
        lax.all_gather(output_weight, "dp", axis=1, tiled=True),
    )
    tokens = inputs.astype(jnp.float32)
    mixer_in, norm_one_back = jax.vjp(rms_norm, tokens, gain_one.astype(jnp.float32))
    mixer_rows = lax.all_gather(mixer_in.astype(jnp.bfloat16), "tensor", axis=0, tiled=True)
    branch_pre = jnp.dot(mixer_rows, branch_full, preferred_element_type=jnp.float32)
    entry_pre = jnp.dot(mixer_rows, input_full, preferred_element_type=jnp.float32)

    def core(
        branch_value,
        entry_value,
        conv_value,
        conv_shift,
        rate_value,
        rate_shift,
        entry_gate,
        entry_shift,
        decay_value,
    ):
        return recurrent_core(
            branch_value,
            entry_value,
            conv_value,
            conv_shift,
            rate_value,
            rate_shift,
            entry_gate,
            entry_shift,
            decay_value,
            segment_ids,
        )

    mixer_value, core_back = jax.vjp(
        core,
        branch_pre,
        entry_pre,
        conv_full.astype(jnp.float32),
        conv_bias_full.astype(jnp.float32),
        rate_full.astype(jnp.float32),
        rate_bias_full.astype(jnp.float32),
        entry_full.astype(jnp.float32),
        entry_bias_full.astype(jnp.float32),
        decay_full.astype(jnp.float32),
    )
    mixer_low = mixer_value.astype(jnp.bfloat16)
    part = mixer_low
    mixer_sum = lax.psum_scatter(
        jnp.dot(part, output_full, preferred_element_type=jnp.float32).astype(jnp.bfloat16),
        "tensor",
        scatter_dimension=0,
        tiled=True,
    ).astype(jnp.float32)
    middle = tokens + mixer_sum
    gain_two, gate_full, up_full, down_full = (
        lax.all_gather(gain_mlp, "dp", axis=0, tiled=True),
        lax.all_gather(gate_weight, "dp", axis=0, tiled=True),
        lax.all_gather(up_weight, "dp", axis=0, tiled=True),
        lax.all_gather(down_weight, "dp", axis=1, tiled=True),
    )
    mlp_in, norm_two_back = jax.vjp(rms_norm, middle, gain_two.astype(jnp.float32))
    mlp_rows = lax.all_gather(mlp_in.astype(jnp.bfloat16), "tensor", axis=0, tiled=True)
    gate_pre = jnp.dot(mlp_rows, gate_full, preferred_element_type=jnp.float32)
    up_pre = jnp.dot(mlp_rows, up_full, preferred_element_type=jnp.float32)
    hidden, gated_back = jax.vjp(gated_unit, gate_pre, up_pre)
    hidden_low = hidden.astype(jnp.bfloat16)
    part = hidden_low
    mlp_sum = lax.psum_scatter(
        jnp.dot(part, down_full, preferred_element_type=jnp.float32).astype(jnp.bfloat16),
        "tensor",
        scatter_dimension=0,
        tiled=True,
    ).astype(jnp.float32)
    layer_out = (middle + mlp_sum).astype(jnp.bfloat16)
    cotangent_rows = lax.all_gather(cotangent, "tensor", axis=0, tiled=True)
    down_grad = dot_rows(hidden_low, cotangent_rows)
    hidden_grad = dot_back(cotangent_rows, down_full)
    gate_grad, up_grad = gated_back(hidden_grad)
    gate_low = gate_grad.astype(jnp.bfloat16)
    up_low = up_grad.astype(jnp.bfloat16)
    gate_wgrad = dot_rows(mlp_rows, gate_low)
    up_wgrad = dot_rows(mlp_rows, up_low)
    mlp_in_grad = lax.psum_scatter(
        (dot_back(gate_low, gate_full) + dot_back(up_low, up_full)).astype(jnp.bfloat16),
        "tensor",
        scatter_dimension=0,
        tiled=True,
    ).astype(jnp.float32)
    middle_norm_grad, gain_two_part = norm_two_back(mlp_in_grad)
    middle_grad = cotangent.astype(jnp.float32) + middle_norm_grad
    residual_rows = lax.all_gather(middle_grad.astype(jnp.bfloat16), "tensor", axis=0, tiled=True)
    output_wgrad = dot_rows(mixer_low, residual_rows)
    mixer_grad = dot_back(residual_rows, output_full)
    (
        branch_grad,
        entry_grad,
        conv_grad,
        conv_bias_grad,
        rate_grad,
        rate_bias_grad,
        entry_wgrad,
        entry_bias_grad,
        decay_grad,
    ) = core_back(mixer_grad)
    branch_low = branch_grad.astype(jnp.bfloat16)
    entry_low = entry_grad.astype(jnp.bfloat16)
    branch_wgrad = dot_rows(mixer_rows, branch_low)
    input_wgrad = dot_rows(mixer_rows, entry_low)
    mixer_in_grad = lax.psum_scatter(
        (dot_back(branch_low, branch_full) + dot_back(entry_low, input_full)).astype(jnp.bfloat16),
        "tensor",
        scatter_dimension=0,
        tiled=True,
    ).astype(jnp.float32)
    tokens_norm_grad, gain_one_part = norm_one_back(mixer_in_grad)
    inputs_grad = (middle_grad + tokens_norm_grad).astype(jnp.bfloat16)
    gain_one_sum, gain_two_sum = lax.psum((gain_one_part, gain_two_part), "tensor")
    shards = (
        lax.psum_scatter(
            gain_one_sum.astype(jnp.bfloat16), "dp", scatter_dimension=0, tiled=True
        ).astype(jnp.float32),
        lax.psum_scatter(
            branch_wgrad.astype(jnp.bfloat16), "dp", scatter_dimension=0, tiled=True
        ).astype(jnp.float32),
        lax.psum_scatter(
            input_wgrad.astype(jnp.bfloat16), "dp", scatter_dimension=0, tiled=True
        ).astype(jnp.float32),
        lax.psum_scatter(
            conv_grad.astype(jnp.bfloat16), "dp", scatter_dimension=2, tiled=True
        ).astype(jnp.float32),
        lax.psum_scatter(
            conv_bias_grad.astype(jnp.bfloat16), "dp", scatter_dimension=1, tiled=True
        ).astype(jnp.float32),
        lax.psum_scatter(
            rate_grad.astype(jnp.bfloat16), "dp", scatter_dimension=1, tiled=True
        ).astype(jnp.float32),
        lax.psum_scatter(
            rate_bias_grad.astype(jnp.bfloat16), "dp", scatter_dimension=1, tiled=True
        ).astype(jnp.float32),
        lax.psum_scatter(
            entry_wgrad.astype(jnp.bfloat16), "dp", scatter_dimension=1, tiled=True
        ).astype(jnp.float32),
        lax.psum_scatter(
            entry_bias_grad.astype(jnp.bfloat16), "dp", scatter_dimension=1, tiled=True
        ).astype(jnp.float32),
        lax.psum_scatter(
            decay_grad.astype(jnp.bfloat16), "dp", scatter_dimension=1, tiled=True
        ).astype(jnp.float32),
        lax.psum_scatter(
            output_wgrad.astype(jnp.bfloat16), "dp", scatter_dimension=1, tiled=True
        ).astype(jnp.float32),
        lax.psum_scatter(
            gain_two_sum.astype(jnp.bfloat16), "dp", scatter_dimension=0, tiled=True
        ).astype(jnp.float32),
        lax.psum_scatter(
            gate_wgrad.astype(jnp.bfloat16), "dp", scatter_dimension=0, tiled=True
        ).astype(jnp.float32),
        lax.psum_scatter(
            up_wgrad.astype(jnp.bfloat16), "dp", scatter_dimension=0, tiled=True
        ).astype(jnp.float32),
        lax.psum_scatter(
            down_grad.astype(jnp.bfloat16), "dp", scatter_dimension=1, tiled=True
        ).astype(jnp.float32),
    )
    return (layer_out, inputs_grad) + tuple(shards)


def solution(mesh):
    return jax.shard_map(
        body,
        mesh=mesh,
        in_specs=(
            P(("dp", "tensor"), None),
            P("dp"),
            P("dp"),
            P("dp", "tensor"),
            P("dp", "tensor"),
            P(None, "tensor", "dp"),
            P("tensor", "dp"),
            P("tensor", "dp", None),
            P("tensor", "dp"),
            P("tensor", "dp", None),
            P("tensor", "dp"),
            P("tensor", "dp"),
            P("tensor", "dp"),
            P("dp"),
            P("dp", "tensor"),
            P("dp", "tensor"),
            P("tensor", "dp"),
            P(("dp", "tensor"), None),
        ),
        out_specs=(
            P(("dp", "tensor"), None),
            P(("dp", "tensor"), None),
            P("dp"),
            P("dp", "tensor"),
            P("dp", "tensor"),
            P(None, "tensor", "dp"),
            P("tensor", "dp"),
            P("tensor", "dp", None),
            P("tensor", "dp"),
            P("tensor", "dp", None),
            P("tensor", "dp"),
            P("tensor", "dp"),
            P("tensor", "dp"),
            P("dp"),
            P("dp", "tensor"),
            P("dp", "tensor"),
            P("tensor", "dp"),
        ),
        check_vma=False,
    )
```

profile of v0, /device:TPU:0, one launch (start us, length us, event | category | flops | bytes accessed | tf_op | source)
XLA Modules:
  0.0 1723.5 jit_solution(14707639825385378687)
XLA Ops:
  8.6 22.3 %all-gather = bf16[8,1,256]{2,1,0:T(2,128)(2,1)S(1)} all-gather(bf16[1,1,256]{2,1,0:T(2,128)(2,1)S(1)} %reshape.174), channel_id=1, replica_groups=mesh['dp'=8,'tensor'=4] {'dp'}, dimensions={0}, use_global_device_ids=true | all-gather | bytes 4608 | tf_op jit(solution)/shard_map/all_gather | solution.py:112
  37.7 31.2 %all_gather.61 = bf16[4,4,160]{1,0,2:T(4,128)(2,1)S(1)} all-gather(bf16[4,4,20]{1,0,2:T(4,128)(2,1)S(1)} %copy.106), channel_id=1, replica_groups=mesh['dp'=8,'tensor'=4] {'dp'}, dimensions={2}, use_global_device_ids=true | all-gather | bytes 5760 | tf_op jit(solution)/shard_map/all_gather | solution.py:115
  69.7 16.4 all-gather.1
  86.4 18.2 %all-gather.2 = bf16[8,20,4]{1,2,0:T(4,128)(2,1)S(1)} all-gather(bf16[1,20,4]{1,2,0:T(4,128)(2,1)S(1)} %bitcast.164), channel_id=1, replica_groups=mesh['dp'=8,'tensor'=4] {'dp'}, dimensions={0}, use_global_device_ids=true | all-gather | bytes 1440 | tf_op jit(solution)/shard_map/all_gather | solution.py:118
  104.7 31.4 %all_gather.63 = bf16[4,160,160]{2,0,1:T(4,128)(2,1)S(1)} all-gather(bf16[4,20,160]{2,0,1:T(4,128)(2,1)S(1)} %copy-done.148), channel_id=1, replica_groups=mesh['dp'=8,'tensor'=4] {'dp'}, dimensions={1}, use_global_device_ids=true | all-gather | bytes 230400 | tf_op jit(solution)/shard_map/all_gather | solution.py:117
  136.1 16.6 all-gather.3
  153.5 18.0 %all-gather.4 = bf16[8,20,4]{1,2,0:T(4,128)(2,1)S(1)} all-gather(bf16[1,20,4]{1,2,0:T(4,128)(2,1)S(1)} %bitcast.166), channel_id=1, replica_groups=mesh['dp'=8,'tensor'=4] {'dp'}, dimensions={0}, use_global_device_ids=true | all-gather | bytes 1440 | tf_op jit(solution)/shard_map/all_gather | solution.py:120
  171.6 31.5 %all_gather.66 = bf16[4,160,160]{2,0,1:T(4,128)(2,1)S(1)} all-gather(bf16[4,20,160]{2,0,1:T(4,128)(2,1)S(1)} %copy-done.149), channel_id=1, replica_groups=mesh['dp'=8,'tensor'=4] {'dp'}, dimensions={1}, use_global_device_ids=true | all-gather | bytes 230400 | tf_op jit(solution)/shard_map/all_gather | solution.py:119
  232.2 7.1 exponential_select_fusion
  251.9 7.3 slice.355
  259.1 7.0 slice.354
  326.5 7.0 slice.352
  380.1 9.1 pad.414
  394.5 10.6 multiply_convert_fusion.2
  406.1 6.7 convolution_convert_fusion.4
  413.5 16.5 all-gather.5
  430.0 24.7 %reduce-scatter.16.cloned.1.call-done = bf16[256,2048]{1,0:T(8,128)(2,1)} async-done(((bf16[1024,2048]{1,0:T(8,128)(2,1)}), bf16[256,2048]{1,0:T(8,128)(2,1)}) %reduce-scatter.16.cloned.1.call-update) | async-done | bytes 1048592 | tf_op jit(solution)/shard_map/reduce_scatter | solution.py:168
  460.1 95.9 %all-gather.27.cloned.1.call-done = bf16[2048,1536]{1,0:T(8,128)(2,1)} async-done(((bf16[256,1536]{1,0:T(8,128)(2,1)}), bf16[2048,1536]{1,0:T(8,128)(2,1)}) %all-gather.27.cloned.1.call-update) | async-done | bytes 6291472 | tf_op jit(solution)/shard_map/all_gather | solution.py:177
  556.0 34.9 %all-gather.25.cloned.1.call-done = bf16[1024,2048]{1,0:T(8,128)(2,1)} async-done(((bf16[256,2048]{1,0:T(8,128)(2,1)}), bf16[1024,2048]{1,0:T(8,128)(2,1)}) %all-gather.25.cloned.1.call-update) | async-done | bytes 4194320 | tf_op jit(solution)/shard_map/all_gather | solution.py:182
  590.9 12.1 fusion.144
  603.1 89.3 %all-gather.29.cloned.1.call-done = bf16[2048,1536]{1,0:T(8,128)(2,1)} async-done(((bf16[256,1536]{1,0:T(8,128)(2,1)}), bf16[2048,1536]{1,0:T(8,128)(2,1)}) %all-gather.29.cloned.1.call-update) | async-done | bytes 6291472 | tf_op jit(solution)/shard_map/all_gather | solution.py:178
  692.4 11.7 fusion.145
  704.1 22.6 %all-gather.33.cloned.1.call-done = bf16[1024,2048]{1,0:T(8,128)(2,1)} async-done(((bf16[256,2048]{1,0:T(8,128)(2,1)}), bf16[1024,2048]{1,0:T(8,128)(2,1)}) %all-gather.33.cloned.1.call-update) | async-done | bytes 4194320 | tf_op jit(solution)/shard_map/all_gather | solution.py:195
  726.8 102.1 %all-gather.31.cloned.1.call-done = bf16[1536,2048]{1,0:T(8,128)(2,1)} async-done(((bf16[1536,256]{1,0:T(8,128)(2,1)}), bf16[1536,2048]{1,0:T(8,128)(2,1)}) %all-gather.31.cloned.1.call-update) | async-done | bytes 6291472 | tf_op jit(solution)/shard_map/all_gather | solution.py:179
  828.8 18.6 %multiply_convert_fusion = (bf16[1024,1536]{1,0:T(8,128)(2,1)}, bf16[1024,1536]{1,0:T(8,128)(2,1)S(1)}, bf16[1024,1536]{1,0:T(8,128)(2,1)}) fusion(f32[1024,1536]{1,0:T(8,128)} %fusion.144, f32[1024,1536]{1,0:T(8,128)} %fusion.145, bf16[1024,2048]{1,0:T(8,128)(2,1)} %all-gather.33.cloned.1.call-done, bf16[1536,2048]{1,0:T(8,128)(2,1)} %all-gather.31.cloned.1.call-done), kind=kOutput, calls=%fused_computation.14 | convolution fusion | flops 6483345408 | bytes 32505856 | tf_op jit(solution)/shard_map/dot_general | solution.py:74
  847.4 10.0 fusion.146
  857.4 10.4 add_convert_fusion.1
  867.9 42.8 %reduce-scatter.20.cloned.1.call-done = bf16[256,2048]{1,0:T(8,128)(2,1)} async-done(((bf16[1024,2048]{1,0:T(8,128)(2,1)}), bf16[256,2048]{1,0:T(8,128)(2,1)}) %reduce-scatter.20.cloned.1.call-update) | async-done | bytes 1048592 | tf_op jit(solution)/shard_map/reduce_scatter | solution.py:203
  916.3 11.5 convolution_convert_fusion.2
  927.9 11.6 convolution_convert_fusion.1
  939.5 11.5 convolution_convert_fusion
  951.1 10.4 fusion.52
  964.1 7.4 slice.427
  971.5 7.0 slice.426
  1077.2 9.2 pad.510
  1102.6 9.4 pad.418
  1112.0 9.4 multiply_reduce_fusion
  1143.4 7.8 convolution_convert_fusion.7
  1162.4 7.4 fusion.101
  1198.8 11.1 convolution_convert_fusion.3
  1217.5 96.5 %reduce-scatter.34.cloned.1.call-done = bf16[1536,256]{1,0:T(8,128)(2,1)} async-done(((bf16[1536,2048]{1,0:T(8,128)(2,1)}), bf16[1536,256]{1,0:T(8,128)(2,1)}) %reduce-scatter.34.cloned.1.call-update) | async-done | bytes 786448 | tf_op jit(solution)/shard_map/reduce_scatter | solution.py:281
  1320.5 70.8 %all-reduce.121.cloned.1.call-done = (bf16[4,160,160]{2,0,1:T(4,128)(2,1)}, bf16[4,160,160]{2,0,1:T(4,128)(2,1)}) async-done(((bf16[4,160,160]{2,0,1:T(4,128)(2,1)}, bf16[4,160,160]{2,0,1:T(4,128)(2,1)}), (bf16[4,160,160]{2,0,1:T(4,128)(2,1)}, bf16[4,160,160]{2,0,1:T(4,128)(2,1)})) %all-reduce.121.cloned.1.call-update) | async-done | bytes 409616
  1394.3 70.3 %reduce-scatter.24.cloned.1.call-done = bf16[256,640]{1,0:T(8,128)(2,1)} async-done(((bf16[2048,640]{1,0:T(8,128)(2,1)}), bf16[256,640]{1,0:T(8,128)(2,1)}) %reduce-scatter.24.cloned.1.call-update) | async-done | bytes 327696 | tf_op jit(solution)/shard_map/reduce_scatter | solution.py:242
  1466.5 71.1 %reduce-scatter.26.cloned.1.call-done = bf16[256,640]{1,0:T(8,128)(2,1)} async-done(((bf16[2048,640]{1,0:T(8,128)(2,1)}), bf16[256,640]{1,0:T(8,128)(2,1)}) %reduce-scatter.26.cloned.1.call-update) | async-done | bytes 327696 | tf_op jit(solution)/shard_map/reduce_scatter | solution.py:245
  1539.5 71.9 %reduce-scatter.28.cloned.1.call-done = bf16[640,256]{1,0:T(8,128)(2,1)} async-done(((bf16[640,2048]{1,0:T(8,128)(2,1)}), bf16[640,256]{1,0:T(8,128)(2,1)}) %reduce-scatter.28.cloned.1.call-update) | async-done | bytes 327696 | tf_op jit(solution)/shard_map/reduce_scatter | solution.py:269
  1613.2 44.2 %reduce-scatter.22.cloned.1.call-done = bf16[256,2048]{1,0:T(8,128)(2,1)} async-done(((bf16[1024,2048]{1,0:T(8,128)(2,1)}), bf16[256,2048]{1,0:T(8,128)(2,1)}) %reduce-scatter.22.cloned.1.call-update) | async-done | bytes 1048592 | tf_op jit(solution)/shard_map/reduce_scatter | solution.py:229
  1659.6 10.2 all-reduce.116
  1669.8 37.2 %all-reduce.117 = (bf16[2048]{0:T(1024)(128)(2,1)S(1)}, bf16[4,4,160]{2,1,0:T(4,128)(2,1)S(1)}, bf16[4,160]{1,0:T(4,128)(2,1)S(1)}, bf16[4,160]{1,0:T(4,128)(2,1...) all-reduce(bf16[2048]{0:T(1024)(128)(2,1)S(1)} %get-tuple-element.6, ...), channel_id=6, replica_groups=mesh['dp'=8,'tensor'=4] {'dp'}, use_global_device_ids=true, to_apply=%region_10.11.clone | all-reduce | flops 9216 | bytes 36864
  (774 shorter events, 387.2 us)
Async XLA Ops:
  7.2 196.1 %all-gather.21.cloned.1.call-start = ((), (), s32[]{:S(2)}) async-start(), calls=%async_computation.12 | async-start | bytes 2949120 | tf_op jit(solution)/shard_map/all_gather | solution.py:114
  7.9 195.4 %all-gather.17.cloned.1.call-start = ((), (), s32[]{:S(2)}) async-start(), calls=%async_computation.10 | async-start | bytes 5242880 | tf_op jit(solution)/shard_map/all_gather | solution.py:126
  32.4 53.9 %copy-start.185 = (bf16[4,20]{1,0:T(4,128)(2,1)S(1)}, bf16[4,20]{1,0:T(4,128)(2,1)}, u32[]{:S(2)}) copy-start(bf16[4,20]{1,0:T(4,128)(2,1)} %param.26) | copy-start | bytes 484
  32.5 72.2 %copy-start.148 = (bf16[4,20,160]{2,0,1:T(4,128)(2,1)S(1)}, bf16[4,20,160]{2,0,1:T(4,128)(2,1)}, u32[]{:S(2)}) copy-start(bf16[4,20,160]{2,0,1:T(4,128)(2,1)} %param.25) | copy-start | bytes 76804
  33.6 102.5 %copy-start.186 = (bf16[4,20]{1,0:T(4,128)(2,1)S(1)}, bf16[4,20]{1,0:T(4,128)(2,1)}, u32[]{:S(2)}) copy-start(bf16[4,20]{1,0:T(4,128)(2,1)} %param.29) | copy-start | bytes 484
  33.6 119.9 %copy-start.187 = (bf16[4,20]{1,0:T(4,128)(2,1)S(1)}, bf16[4,20]{1,0:T(4,128)(2,1)}, u32[]{:S(2)}) copy-start(bf16[4,20]{1,0:T(4,128)(2,1)} %param.28) | copy-start | bytes 484
  33.6 138.1 %copy-start.149 = (bf16[4,20,160]{2,0,1:T(4,128)(2,1)S(1)}, bf16[4,20,160]{2,0,1:T(4,128)(2,1)}, u32[]{:S(2)}) copy-start(bf16[4,20,160]{2,0,1:T(4,128)(2,1)} %param.27) | copy-start | bytes 76804
  33.6 169.6 %copy-start.139 = (s32[1024]{0:T(1024)S(1)}, s32[1024]{0:T(1024)}, u32[]{:S(2)}) copy-start(s32[1024]{0:T(1024)} %param.19) | copy-start | bytes 12292
  36.2 358.3 %all-gather.19.cloned.1.call-start = ((), (), s32[]{:S(2)}) async-start(), calls=%async_computation.11 | async-start | bytes 2949120 | tf_op jit(solution)/shard_map/all_gather | solution.py:113
  36.9 368.1 %all-gather.23.cloned.1.call-start = ((), (), s32[]{:S(2)}) async-start(), calls=%async_computation.13 | async-start | bytes 2949120 | tf_op jit(solution)/shard_map/all_gather | solution.py:122
  37.5 417.2 %reduce-scatter.16.cloned.1.call-start = ((), (), s32[]{:S(2)}) async-start(), calls=%async_computation.14 | async-start | bytes 5242880 | tf_op jit(solution)/shard_map/reduce_scatter | solution.py:168
  69.3 140.1 %copy-start.150 = (f32[640]{0:T(1024)}, f32[640]{0:T(1024)S(1)}, u32[]{:S(2)}) copy-start(f32[640]{0:T(1024)S(1)} %mul.685) | copy-start | bytes 7684
  69.5 140.0 %copy-start.152 = (f32[640]{0:T(1024)}, f32[640]{0:T(1024)S(1)}, u32[]{:S(2)}) copy-start(f32[640]{0:T(1024)S(1)} %mul.680) | copy-start | bytes 7684
  69.6 139.8 %copy-start.154 = (f32[640]{0:T(1024)}, f32[640]{0:T(1024)S(1)}, u32[]{:S(2)}) copy-start(f32[640]{0:T(1024)S(1)} %mul.675) | copy-start | bytes 7684
  86.4 123.1 %copy-start.156 = (f32[640]{0:T(1024)}, f32[640]{0:T(1024)S(1)}, u32[]{:S(2)}) copy-start(f32[640]{0:T(1024)S(1)} %mul.670) | copy-start | bytes 7684
  136.1 79.3 %copy-start.79 = (bf16[4,160,160]{2,0,1:T(4,128)(2,1)}, bf16[4,160,160]{2,0,1:T(4,128)(2,1)S(1)}, u32[]{:S(2)}) copy-start(bf16[4,160,160]{2,0,1:T(4,128)(2,1)S(1)} %all_gather.63) | copy-start | bytes 614404
  152.8 56.6 %copy-start.158 = (f32[160,4]{0,1:T(4,128)}, f32[160,4]{0,1:T(4,128)S(1)}, u32[]{:S(2)}) copy-start(f32[160,4]{0,1:T(4,128)S(1)} %reshape.192) | copy-start | bytes 7684
  153.5 78.7 %copy-start.126 = (f32[640]{0:T(1024)}, f32[640]{0:T(1024)S(1)}, u32[]{:S(2)}) copy-start(f32[640]{0:T(1024)S(1)} %get-tuple-element.197) | copy-start | bytes 7684
  412.8 143.2 %all-gather.27.cloned.1.call-start = ((), (), s32[]{:S(2)}) async-start(), calls=%async_computation.16 | async-start | bytes 7077888 | tf_op jit(solution)/shard_map/all_gather | solution.py:177
  413.4 177.5 %all-gather.25.cloned.1.call-start = ((), (), s32[]{:S(2)}) async-start(), calls=%async_computation.15 | async-start | bytes 5242880 | tf_op jit(solution)/shard_map/all_gather | solution.py:182
  430.0 483.6 %copy-start.112 = (f32[8,1,256]{2,1,0:T(1,128)}, f32[8,1,256]{2,1,0:T(1,128)S(1)}, u32[]{:S(2)}) copy-start(f32[8,1,256]{2,1,0:T(1,128)S(1)} %convert_element_type.255) | copy-start | bytes 24580
  456.5 457.2 %copy-start.165 = (f32[256]{0:T(256)}, f32[256]{0:T(256)S(1)}, u32[]{:S(2)}) copy-start(f32[256]{0:T(256)S(1)} %fusion.83) | copy-start | bytes 3076
  458.0 234.4 %all-gather.29.cloned.1.call-start = ((), (), s32[]{:S(2)}) async-start(), calls=%async_computation.17 | async-start | bytes 7077888 | tf_op jit(solution)/shard_map/all_gather | solution.py:178
  458.7 268.0 %all-gather.33.cloned.1.call-start = ((), (), s32[]{:S(2)}) async-start(), calls=%async_computation.20 | async-start | bytes 5242880 | tf_op jit(solution)/shard_map/all_gather | solution.py:195
  459.5 369.4 %all-gather.31.cloned.1.call-start = ((), (), s32[]{:S(2)}) async-start(), calls=%async_computation.18 | async-start | bytes 7077888 | tf_op jit(solution)/shard_map/all_gather | solution.py:179
  460.1 450.7 %reduce-scatter.20.cloned.1.call-start = ((), (), s32[]{:S(2)}) async-start(), calls=%async_computation.21 | async-start | bytes 5242880 | tf_op jit(solution)/shard_map/reduce_scatter | solution.py:203
  867.9 83.2 %all-gather.35.cloned.1.call-start = ((), (), s32[]{:S(2)}) async-start(), calls=%async_computation.22 | async-start | bytes 5242880 | tf_op jit(solution)/shard_map/all_gather | solution.py:211
  916.2 296.2 %reduce-scatter.30.cloned.1.call-start = ((), (), s32[]{:S(2)}) async-start(), calls=%async_computation.27 | async-start | bytes 7077888 | tf_op jit(solution)/shard_map/reduce_scatter | solution.py:275
  927.8 287.1 %reduce-scatter.32.cloned.1.call-start = ((), (), s32[]{:S(2)}) async-start(), calls=%async_computation.28 | async-start | bytes 7077888 | tf_op jit(solution)/shard_map/reduce_scatter | solution.py:278
  939.4 374.6 %reduce-scatter.34.cloned.1.call-start = ((), (), s32[]{:S(2)}) async-start(), calls=%async_computation.29 | async-start | bytes 7077888 | tf_op jit(solution)/shard_map/reduce_scatter | solution.py:281
  951.0 440.3 %all-reduce.121.cloned.1.call-start = ((), (), s32[]{:S(2)}) async-start(), calls=%async_computation.30 | async-start | bytes 1310720
  1143.0 321.7 %reduce-scatter.24.cloned.1.call-start = ((), (), s32[]{:S(2)}) async-start(), calls=%async_computation.24 | async-start | bytes 2949120 | tf_op jit(solution)/shard_map/reduce_scatter | solution.py:242
  1151.2 386.4 %reduce-scatter.26.cloned.1.call-start = ((), (), s32[]{:S(2)}) async-start(), calls=%async_computation.25 | async-start | bytes 2949120 | tf_op jit(solution)/shard_map/reduce_scatter | solution.py:245
  1179.0 432.3 %reduce-scatter.28.cloned.1.call-start = ((), (), s32[]{:S(2)}) async-start(), calls=%async_computation.26 | async-start | bytes 2949120 | tf_op jit(solution)/shard_map/reduce_scatter | solution.py:269
  1186.9 470.4 %reduce-scatter.22.cloned.1.call-start = ((), (), s32[]{:S(2)}) async-start(), calls=%async_computation.23 | async-start | bytes 5242880 | tf_op jit(solution)/shard_map/reduce_scatter | solution.py:229
  1198.7 512.8 %reduce-scatter.18.cloned.1.call-start = ((), (), s32[]{:S(2)}) async-start(), calls=%async_computation.19 | async-start | bytes 5242880 | tf_op jit(solution)/shard_map/reduce_scatter | solution.py:188
  1214.9 101.9 %copy-start.159 = (f32[160,4]{0,1:T(4,128)S(1)}, f32[160,4]{0,1:T(4,128)}, u32[]{:S(2)}) copy-start(f32[160,4]{0,1:T(4,128)} %copy-done.158) | copy-start | bytes 7684
  1214.9 101.9 %copy-start.9 = (f32[4,1024,160]{1,2,0:T(8,128)S(1)}, f32[4,1024,160]{1,2,0:T(8,128)}, u32[]{:S(2)}) copy-start(f32[4,1024,160]{1,2,0:T(8,128)} %add_divide_fusion.1) | copy-start | bytes 7864324
  1320.5 336.8 %copy-start.3 = (bf16[256,2048]{1,0:T(8,128)(2,1)S(1)}, bf16[256,2048]{1,0:T(8,128)(2,1)}, u32[]{:S(2)}) copy-start(bf16[256,2048]{1,0:T(8,128)(2,1)} %param.18) | copy-start | bytes 3145732
  1320.5 336.8 %copy-start.125 = (f32[8,1,256]{2,1,0:T(1,128)S(1)}, f32[8,1,256]{2,1,0:T(1,128)}, u32[]{:S(2)}) copy-start(f32[8,1,256]{2,1,0:T(1,128)} %copy-done.124) | copy-start | bytes 24580
  1320.5 336.8 %copy-start.170 = (f32[256]{0:T(256)S(1)}, f32[256]{0:T(256)}, u32[]{:S(2)}) copy-start(f32[256]{0:T(256)} %copy-done.169) | copy-start | bytes 3076
  1392.7 266.9 %copy-start.160 = (f32[2048]{0:T(1024)S(1)}, f32[2048]{0:T(1024)}, u32[]{:S(2)}) copy-start(f32[2048]{0:T(1024)} %get-tuple-element.51) | copy-start | bytes 24580
  1392.7 318.8 %copy-start.180 = (f32[256]{0:T(256)S(1)}, f32[256]{0:T(256)}, u32[]{:S(2)}) copy-start(f32[256]{0:T(256)} %copy-done.179) | copy-start | bytes 3076
  1392.7 318.8 %copy-start.17 = (bf16[256,2048]{1,0:T(8,128)(2,1)S(1)}, bf16[256,2048]{1,0:T(8,128)(2,1)}, u32[]{:S(2)}) copy-start(bf16[256,2048]{1,0:T(8,128)(2,1)} %reduce-scatter.16.cloned.1.call-done) | copy-start | bytes 3145732
  1392.7 318.8 %copy-start.34 = (bf16[256,2048]{1,0:T(8,128)(2,1)S(1)}, bf16[256,2048]{1,0:T(8,128)(2,1)}, u32[]{:S(2)}) copy-start(bf16[256,2048]{1,0:T(8,128)(2,1)} %param.35) | copy-start | bytes 3145732
  1392.7 318.9 %copy-start.113 = (f32[8,1,256]{2,1,0:T(1,128)S(1)}, f32[8,1,256]{2,1,0:T(1,128)}, u32[]{:S(2)}) copy-start(f32[8,1,256]{2,1,0:T(1,128)} %copy-done.112) | copy-start | bytes 24580
  1392.7 318.9 %copy-start.166 = (f32[256]{0:T(256)S(1)}, f32[256]{0:T(256)}, u32[]{:S(2)}) copy-start(f32[256]{0:T(256)} %copy-done.165) | copy-start | bytes 3076
  1392.8 318.9 %copy-start.182 = (f32[256]{0:T(256)S(1)}, f32[256]{0:T(256)}, u32[]{:S(2)}) copy-start(f32[256]{0:T(256)} %copy-done.181) | copy-start | bytes 3076
  (175 other events, 1310.2 us)
Sparse Core Ops, SparseCore 0:
  10.2 58.9 all-gather.20
  71.3 33.6 all-gather.16
  107.2 57.3 all-gather.18
  166.4 57.1 all-gather.22
  413.0 41.6 reduce-scatter.15
  457.0 99.0 all-gather.26
  558.2 32.6 all-gather.24
  593.4 99.0 all-gather.28
  694.1 32.6 all-gather.32
  728.9 99.9 all-gather.30
  868.0 42.6 reduce-scatter.19
  916.3 34.4 all-gather.34
  954.4 117.9 reduce-scatter.29
  1075.8 117.1 reduce-scatter.31
  1196.4 117.5 reduce-scatter.33
  1318.5 72.7 all-reduce.120
  1395.1 69.5 reduce-scatter.23
  1468.4 69.1 reduce-scatter.25
  1541.6 69.7 reduce-scatter.27
  1613.9 43.4 reduce-scatter.21
  1659.9 44.4 reduce-scatter.17
where the time goes:
time: 1730 us; the launch traced here: 1720 us
  waiting for transfers between devices  842 us (49%)
  local copies, waits for them, and re-layouts  283 us (16%)
  blocking collectives  250 us (14%)
  matrix products  198 us (11%)
  other arithmetic  131 us (8%)
  between operations  18.5 us (1%)
    slice x78, local copies, waits for them, and re-layouts, recurrent_core(): carried, state = lax.associative_scan(combine, (decay, drive), axis=0)  132 us
    pad x79, local copies, waits for them, and re-layouts, recurrent_core(): carried, state = lax.associative_scan(combine, (decay, drive), axis=0)  108 us
    all_gather x1, waiting for transfers between devices, body(): lax.all_gather(down_weight, 'dp', axis=1, tiled=True)  102 us
    reduce_scatter x1, waiting for transfers between devices, body(): lax.psum_scatter(down_grad.astype(jnp.bfloat16), 'dp', scatter_dimension=...  96.5 us
    all_gather x1, waiting for transfers between devices, body(): lax.all_gather(gate_weight, 'dp', axis=0, tiled=True)  95.9 us
    all_gather x1, waiting for transfers between devices, body(): lax.all_gather(up_weight, 'dp', axis=0, tiled=True)  89.3 us
    unnamed x22, waiting for transfers between devices  75.3 us
    reduce_scatter x1, waiting for transfers between devices, body(): lax.psum_scatter(output_wgrad.astype(jnp.bfloat16), 'dp', scatter_dimensi...  71.9 us
  transfers between devices with their start and end apart: 21, of which 13 were waited for; matrix products, arithmetic and copies ran while one was open for 31% of the time, Pallas kernels for 0%

commit v1 on v0

v1 whole, which is shorter than its diff:
```python
import functools

import jax
import jax.numpy as jnp
from jax import lax
from jax.experimental import pallas as pl
from jax.experimental.pallas import tpu as pltpu
from jax.sharding import PartitionSpec as P

epsilon = 1e-06
lru_scale = 8.0
root = 0.7978845608028654
cubic = 0.044715
f32 = jnp.float32
bf16 = jnp.bfloat16
vmem_bytes = 60 * 1024 * 1024


def gelu_both(value):
    square = value * value
    th = jnp.tanh(root * value * (1.0 + cubic * square))
    half = 0.5 * (1.0 + th)
    slope = half + 0.5 * value * (1.0 - th * th) * (root * (1.0 + 3.0 * cubic * square))
    return value * half, slope


def gelu(value):
    return value * (0.5 * (1.0 + jnp.tanh(root * value * (1.0 + cubic * value * value))))


def one_minus_exp(x, exp_x):
    series = 1.0 + x * (1.0 / 7.0)
    for order in (6.0, 5.0, 4.0, 3.0, 2.0):
        series = 1.0 + x * (1.0 / order) * series
    return jnp.where(x > -0.5, -x * series, 1.0 - exp_x)


def decay_terms(rate, slope, keep):
    log_decay = slope * rate
    expo = jnp.exp(log_decay)
    square = expo * expo
    factor = jnp.where(keep > 0.0, jnp.sqrt(one_minus_exp(2.0 * log_decay, square)), 1.0)
    return expo * keep, square, factor


def row_index(width):
    return lax.broadcasted_iota(jnp.int32, (8, width), 0)


def down_by(current, before, offset, rows):
    if offset == 0:
        return current
    return jnp.where(
        rows < offset, pltpu.roll(before, offset, 0), pltpu.roll(current, offset, 0)
    )


def up_by(current, after, offset, rows):
    if offset == 0:
        return current
    return jnp.where(
        rows < 8 - offset,
        pltpu.roll(current, 8 - offset, 0),
        pltpu.roll(after, 8 - offset, 0),
    )


def core_forward_kernel(
    place, branch, entry_pre, masks, gates, small, out, mixed_out, rate_out, entry_out, state_out,
    mixed_low, pre, last_entry, last_state,
):
    length, width = entry_pre.shape
    rows = row_index(width)

    @pl.when(pl.program_id(0) == 0)
    def _():
        last_entry[...] = jnp.zeros_like(last_entry)
        last_state[...] = jnp.zeros_like(last_state)

    taps = [small[k : k + 1, :] for k in range(4)]
    conv_bias = small[4:5, :]

    def convolve(step, before):
        parts = []
        for half in range(2):
            at = pl.ds(pl.multiple_of(step * 16 + half * 8, 8), 8)
            here = entry_pre[at, :]
            mask = masks[at, :]
            mixed = here * taps[0] + conv_bias
            for k in range(1, 4):
                mixed += down_by(here, before, k, rows) * mask[:, k : k + 1] * taps[k]
            mixed_out[at, :] = mixed
            parts.append(mixed)
            before = here
        mixed_low[pl.ds(pl.multiple_of(step * 16, 16), 16), :] = jnp.concatenate(
            parts, axis=0
        ).astype(bf16)
        return before

    last_entry[...] = lax.fori_loop(0, length // 16, convolve, last_entry[...])
    pre[...] = jnp.dot(mixed_low[...], gates[...], preferred_element_type=f32)
    rate_bias = small[5:6, :]
    entry_bias = small[6:7, :]
    slope = small[7:8, :]

    def scan(step, carry):
        parts = []
        for half in range(2):
            at = pl.ds(pl.multiple_of(step * 16 + half * 8, 8), 8)
            keep = masks[at, :][:, 0:1]
            rate = jax.nn.sigmoid(pre[at, :width] + rate_bias)
            entry = jax.nn.sigmoid(pre[at, width:] + entry_bias)
            decay, _, factor = decay_terms(rate, slope, keep)
            drive = factor * entry * mixed_out[at, :]
            for shift in (1, 2, 4):
                inside = rows >= shift
                drive += decay * jnp.where(inside, pltpu.roll(drive, shift, 0), 0.0)
                decay = decay * jnp.where(inside, pltpu.roll(decay, shift, 0), 1.0)
            state = drive + decay * carry
            carry = jnp.broadcast_to(state[7:8, :], state.shape)
            rate_out[at, :] = rate
            entry_out[at, :] = entry
            state_out[at, :] = state
            parts.append(gelu(branch[at, :]) * state)
        out[pl.ds(pl.multiple_of(step * 16, 16), 16), :] = jnp.concatenate(parts, axis=0).astype(
            bf16
        )
        return carry

    last_state[...] = lax.fori_loop(0, length // 16, scan, last_state[...])


def core_backward_kernel(
    place, grad, branch, entry_pre, mixed_in, rate_in, entry_in, state_in, state_tail, entry_tail,
    masks, gates, small, low, gate_grads, small_grads,
    state_long, entry_long, gate_low, mixed_grad, sums, next_decay, next_carried, next_mixed,
):
    length, width = entry_pre.shape
    rows = row_index(width)

    @pl.when(pl.program_id(0) == 0)
    def _():
        next_decay[...] = jnp.zeros_like(next_decay)
        next_carried[...] = jnp.zeros_like(next_carried)
        next_mixed[...] = jnp.zeros_like(next_mixed)
        sums[...] = jnp.zeros_like(sums)
        gate_grads[...] = jnp.zeros_like(gate_grads)

    state_long[0:8, :] = state_tail[...]
    state_long[8:, :] = state_in[...]
    entry_long[0:8, :] = entry_tail[...]
    entry_long[8:, :] = entry_pre[...]
    slope = small[7:8, :]

    def reverse(step, carry):
        after_decay, carried_after = carry
        step = length // 16 - 1 - step
        branch_parts, rate_parts, entry_parts = [], [], []
        for half in (1, 0):
            start = pl.multiple_of(step * 16 + half * 8, 8)
            at = pl.ds(start, 8)
            keep = masks[at, :][:, 0:1]
            rate = rate_in[at, :]
            entry = entry_in[at, :]
            mixed = mixed_in[at, :]
            decay, square, factor = decay_terms(rate, slope, keep)
            up = grad[at, :]
            act, act_slope = gelu_both(branch[at, :])
            state = state_in[at, :]
            branch_parts.append(up * state * act_slope)
            value = up * act
            ahead = up_by(decay, after_decay, 1, rows)
            after_decay = decay
            for shift in (1, 2, 4):
                inside = rows < 8 - shift
                value += ahead * jnp.where(inside, pltpu.roll(value, 8 - shift, 0), 0.0)
                ahead = ahead * jnp.where(inside, pltpu.roll(ahead, 8 - shift, 0), 1.0)
            carried = value + ahead * carried_after
            carried_after = jnp.broadcast_to(carried[0:1, :], carried.shape)
            earlier = down_by(state, state_long[at, :], 1, rows)
            driven = carried * entry
            log_grad = keep * (carried * earlier * decay - driven * mixed * square / factor)
            scaled = log_grad * rate
            rate_pre_grad = slope * scaled * (1.0 - rate)
            entry_pre_grad = driven * factor * mixed * (1.0 - entry)
            mixed_grad[at, :] = driven * factor
            sums[40:48, :] += rate_pre_grad
            sums[48:56, :] += entry_pre_grad
            sums[56:64, :] += scaled
            rate_parts.append(rate_pre_grad)
            entry_parts.append(entry_pre_grad)
        both = pl.ds(pl.multiple_of(step * 16, 16), 16)
        low[both, :width] = jnp.concatenate(branch_parts[::-1], axis=0).astype(bf16)
        gate_low[both, :width] = jnp.concatenate(rate_parts[::-1], axis=0).astype(bf16)
        gate_low[both, width:] = jnp.concatenate(entry_parts[::-1], axis=0).astype(bf16)
        return after_decay, carried_after

    after_decay, carried_after = lax.fori_loop(
        0, length // 16, reverse, (next_decay[...], next_carried[...])
    )
    next_decay[...] = after_decay
    next_carried[...] = carried_after
    mixed_grad[...] += lax.dot_general(
        gate_low[...], gates[...], (((1,), (1,)), ((), ())), preferred_element_type=f32
    )
    gate_grads[...] += lax.dot_general(
        mixed_in[...].astype(bf16),
        gate_low[...],
        (((0,), (0,)), ((), ())),
        preferred_element_type=f32,
    )
    taps = [small[k : k + 1, :] for k in range(4)]

    def convolve(step, after):
        step = length // 16 - 1 - step
        parts = []
        for half in (1, 0):
            start = pl.multiple_of(step * 16 + half * 8, 8)
            at = pl.ds(start, 8)
            mask = masks[at, :]
            here = mixed_grad[at, :]
            value = entry_pre[at, :]
            before = entry_long[at, :]
            sums[32:40, :] += here
            sums[0:8, :] += here * value
            total = here * taps[0]
            masked = [here * mask[:, k : k + 1] for k in range(1, 4)]
            for k in range(1, 4):
                sums[8 * k : 8 * k + 8, :] += masked[k - 1] * down_by(value, before, k, rows)
                total += up_by(masked[k - 1], after[k - 1], k, rows) * taps[k]
            after = masked
            parts.append(total)
        low[pl.ds(pl.multiple_of(step * 16, 16), 16), width:] = jnp.concatenate(
            parts[::-1], axis=0
        ).astype(bf16)
        return after

    after = lax.fori_loop(
        0,
        length // 16,
        convolve,
        [next_mixed[8 * k : 8 * k + 8, :] for k in range(3)],
    )
    for k in range(3):
        next_mixed[8 * k : 8 * k + 8, :] = after[k]

    @pl.when(pl.program_id(0) == pl.num_programs(0) - 1)
    def _():
        for k in range(8):
            small_grads[k : k + 1, :] = jnp.sum(sums[8 * k : 8 * k + 8, :], axis=0, keepdims=True)


def core_forward(place, pre, masks, gates, small, blocks):
    total, width = pre.shape[0], pre.shape[1] // 2
    length = total // blocks
    wide = lambda column: pl.BlockSpec((length, width), lambda b, t: (b ^ t[0], column))
    whole = lambda shape: pl.BlockSpec(shape, lambda b, t: (0, 0))
    kept = jax.ShapeDtypeStruct((total, width), f32)
    return pl.pallas_call(
        core_forward_kernel,
        grid_spec=pltpu.PrefetchScalarGridSpec(
            num_scalar_prefetch=1,
            grid=(blocks,),
            in_specs=[
                wide(0),
                wide(1),
                pl.BlockSpec((length, 128), lambda b, t: (b, 0)),
                whole(gates.shape),
                whole(small.shape),
            ],
            out_specs=[wide(0)] * 5,
            scratch_shapes=[
                pltpu.VMEM((length, width), bf16),
                pltpu.VMEM((length, 2 * width), f32),
                pltpu.VMEM((8, width), f32),
                pltpu.VMEM((8, width), f32),
            ],
        ),
        out_shape=[jax.ShapeDtypeStruct((total, width), bf16)] + [kept] * 4,
        compiler_params=pltpu.CompilerParams(vmem_limit_bytes=vmem_bytes),
        cost_estimate=pl.CostEstimate(
            flops=4 * total * width * width, bytes_accessed=32 * total * width, transcendentals=0
        ),
        name="core_forward",
    )(place, pre, pre, masks, gates, small)


def core_backward(place, grad, pre, mixed, rate, entry, state, masks, gates, small, blocks):
    total, width = grad.shape
    length = total // blocks
    back = lambda g: blocks - 1 - g
    wide = lambda column: pl.BlockSpec((length, width), lambda g, t: (back(g) ^ t[0], column))
    whole = lambda shape: pl.BlockSpec(shape, lambda g, t: (0, 0))

    def tail(column):
        def at(g, t):
            block = jnp.maximum(back(g) - 1, 0) ^ t[0]
            return (block * (length // 8) + length // 8 - 1, column)

        return pl.BlockSpec((8, width), at)

    return pl.pallas_call(
        core_backward_kernel,
        grid_spec=pltpu.PrefetchScalarGridSpec(
            num_scalar_prefetch=1,
            grid=(blocks,),
            in_specs=[
                wide(0),
                wide(0),
                wide(1),
                wide(0),
                wide(0),
                wide(0),
                wide(0),
                tail(0),
                tail(1),
                pl.BlockSpec((length, 128), lambda g, t: (back(g), 0)),
                whole(gates.shape),
                whole(small.shape),
            ],
            out_specs=[
                pl.BlockSpec((length, 2 * width), lambda g, t: (back(g) ^ t[0], 0)),
                whole(gates.shape),
                whole((8, width)),
            ],
            scratch_shapes=[
                pltpu.VMEM((length + 8, width), f32),
                pltpu.VMEM((length + 8, width), f32),
                pltpu.VMEM((length, 2 * width), bf16),
                pltpu.VMEM((length, width), f32),
                pltpu.VMEM((64, width), f32),
                pltpu.VMEM((8, width), f32),
                pltpu.VMEM((8, width), f32),
                pltpu.VMEM((24, width), f32),
            ],
        ),
        out_shape=[
            jax.ShapeDtypeStruct((total, 2 * width), bf16),
            jax.ShapeDtypeStruct(gates.shape, f32),
            jax.ShapeDtypeStruct((8, width), f32),
        ],
        compiler_params=pltpu.CompilerParams(vmem_limit_bytes=vmem_bytes),
        cost_estimate=pl.CostEstimate(
            flops=8 * total * width * width, bytes_accessed=40 * total * width, transcendentals=0
        ),
        name="core_backward",
    )(place, grad, pre, pre, mixed, rate, entry, state, state, pre, masks, gates, small)


def dot(left, right):
    return jnp.dot(left, right, preferred_element_type=f32)


def dot_rows(left, right):
    return lax.dot_general(left, right, (((0,), (0,)), ((), ())), preferred_element_type=f32)


def dot_back(left, right):
    return lax.dot_general(left, right, (((1,), (1,)), ((), ())), preferred_element_type=f32)


class Ring:
    def __init__(self, count):
        self.count = count
        order = list(range(0, count, 2)) + list(range(1, count, 2))[::-1]
        self.order = order
        self.place_of = [order.index(index) for index in range(count)]
        self.ahead = [(order[(i + 1) % count], order[i]) for i in range(count)]
        self.behind = [(order[i], order[(i + 1) % count]) for i in range(count)]
        self.place = jnp.asarray(self.place_of, jnp.int32)[lax.axis_index("dp")]

    def reach(self, far):
        return self.count // 2 if far else (self.count - 1) // 2

    def gather(self, own, far):
        count = self.count
        blocks = [own] + [None] * (count - 1)
        reach = self.reach(far)
        for r in range(1, count):
            if r <= reach:
                blocks[r] = lax.ppermute(blocks[r - 1], "dp", self.ahead)
            if r <= count - 1 - reach:
                blocks[count - r] = lax.ppermute(blocks[(count - r + 1) % count], "dp", self.behind)
        return blocks

    def scatter(self, part, far):
        count = self.count
        reach = self.reach(far)
        steps = max(reach, count - 1 - reach)
        right = left = None
        right_sum = left_sum = None
        for r in range(steps, 0, -1):
            if r <= reach:
                value = part(r)
                if right is not None:
                    value = value + right.astype(f32)
                right = lax.ppermute(value.astype(bf16), "dp", self.behind)
            if r <= count - 1 - reach:
                value = part(count - r)
                if left is not None:
                    value = value + left.astype(f32)
                left = lax.ppermute(value.astype(bf16), "dp", self.ahead)
        return part(0) + right.astype(f32) + left.astype(f32)

    def scatter_direct(self, blocks):
        total = blocks[0]
        for r in range(1, self.count):
            pairs = [
                (self.order[i], self.order[(i + r) % self.count]) for i in range(self.count)
            ]
            total = total + lax.ppermute(blocks[r], "dp", pairs)
        return total

    def from_whole(self, whole, axis, size):
        ordered = [lax.slice_in_dim(whole, i * size, (i + 1) * size, axis=axis) for i in self.order]
        return lax.dynamic_slice_in_dim(
            jnp.concatenate(ordered + ordered, axis=axis),
            self.place * size,
            self.count * size,
            axis=axis,
        )

    def to_whole(self, ringed, axis, size):
        start = lax.rem(self.count - self.place, self.count) * size
        ordered = lax.dynamic_slice_in_dim(
            jnp.concatenate([ringed, ringed], axis=axis), start, self.count * size, axis=axis
        )
        return jnp.concatenate(
            [
                lax.slice_in_dim(ordered, i * size, (i + 1) * size, axis=axis)
                for i in self.place_of
            ],
            axis=axis,
        )


core_pairs = [(0, 1), (1, 0), (2, 3), (3, 2)]
chip_pairs = [(0, 2), (1, 3), (2, 0), (3, 1)]


def tensor_gather(own):
    sibling = lax.ppermute(own, "tensor", core_pairs)
    across = lax.ppermute(own, "tensor", chip_pairs)
    far = lax.ppermute(across, "tensor", core_pairs)
    return jnp.concatenate([own, sibling, across, far], axis=0)


def tensor_scatter(part):
    far = lax.ppermute(part(3).astype(bf16), "tensor", core_pairs)
    across = lax.ppermute((part(2) + far.astype(f32)).astype(bf16), "tensor", chip_pairs)
    sibling = lax.ppermute(part(1).astype(bf16), "tensor", core_pairs)
    return part(0) + sibling.astype(f32) + across.astype(f32)


def tensor_sum(value):
    value = value + lax.ppermute(value, "tensor", core_pairs)
    return value + lax.ppermute(value, "tensor", chip_pairs)


def norm_forward(values, gain):
    scale = lax.rsqrt(jnp.mean(values * values, axis=-1, keepdims=True) + epsilon)
    return scale, values * scale * gain


def norm_backward(values, scale, gain, grad):
    weighted = grad * gain
    inner = jnp.mean(weighted * values, axis=-1, keepdims=True)
    row_grad = scale * weighted - values * (scale * scale * scale * inner)
    return row_grad, jnp.sum(grad * values * scale, axis=0)


def body(
    inputs,
    segment_ids,
    gain_mixer,
    branch_weight,
    input_weight,
    conv_weight,
    conv_bias,
    rate_weight,
    rate_bias,
    entry_weight,
    entry_bias,
    decay_param,
    output_weight,
    gain_mlp,
    gate_weight,
    up_weight,
    down_weight,
    cotangent,
    *,
    dp,
    tensor,
):
    ring = Ring(dp)
    shard, width = branch_weight.shape
    features = inputs.shape[1]
    rows = inputs.shape[0]
    length = segment_ids.shape[0]
    gate_blocks, piece, block_width = rate_weight.shape
    taps = conv_weight.shape[0]
    place = lax.axis_index("tensor").astype(jnp.int32).reshape(1)

    columns = jnp.stack(
        [conv_weight[k] for k in range(taps)] + [conv_bias, rate_bias, entry_bias, decay_param],
        axis=-1,
    )
    table = jnp.concatenate([rate_weight, entry_weight, columns], axis=-1)
    table = table.reshape(gate_blocks * piece, table.shape[-1])
    table_rows, table_columns = table.shape
    wide = -(-table_columns // 128) * 128
    high = -(-(table_rows + 2) // 16) * 16
    gains = jnp.pad(jnp.stack([gain_mixer, gain_mlp]), ((0, 0), (0, wide - shard)))
    table = jnp.concatenate(
        [jnp.pad(table, ((0, 0), (0, wide - table_columns))), gains], axis=0
    )
    table = jnp.pad(table, ((0, high - table_rows - 2), (0, 0)))

    tables = jnp.stack(ring.gather(table, True))
    gain_one = tables[:, table_rows, :shard].reshape(features).astype(f32)
    gain_two = tables[:, table_rows + 1, :shard].reshape(features).astype(f32)
    whole_table = ring.to_whole(tables[:, :table_rows], 0, 1)
    whole_table = (
        whole_table.reshape(dp, gate_blocks, piece, wide)
        .transpose(1, 0, 2, 3)
        .reshape(width, wide)
    )
    channel_block = jnp.arange(width) // block_width
    same_block = channel_block[:, None] == channel_block[None, :]

    def spread(weights):
        return jnp.where(same_block, jnp.tile(weights, (1, gate_blocks)), jnp.zeros((), bf16))

    gates = jnp.concatenate(
        [
            spread(whole_table[:, :block_width]),
            spread(whole_table[:, block_width : 2 * block_width]),
        ],
        axis=1,
    )
    small = whole_table[:, 2 * block_width : 2 * block_width + 8].astype(f32).T
    decay_full = small[7]
    small = jnp.concatenate(
        [small[:7], -lru_scale * jax.nn.softplus(-decay_full)[None]], axis=0
    )

    masks = []
    for offset in range(1, taps):
        earlier = jnp.concatenate(
            [jnp.full((offset,), -1, segment_ids.dtype), segment_ids[: length - offset]]
        )
        masks.append((earlier == segment_ids).astype(f32))
    masks = jnp.stack([masks[0]] + masks, axis=1)
    masks = jnp.pad(masks, ((0, 0), (0, 128 - taps)))

    tokens = ring.from_whole(inputs, 1, shard).astype(f32)
    cotangent_own = ring.from_whole(cotangent, 1, shard)
    scale_one, mixer_in = norm_forward(tokens, gain_one)
    mixer_rows = tensor_gather(mixer_in.astype(bf16))
    pair_weight = jnp.concatenate(
        [
            jnp.concatenate(ring.gather(branch_weight, True), axis=0),
            jnp.concatenate(ring.gather(input_weight, False), axis=0),
        ],
        axis=1,
    )
    pre = dot(mixer_rows, pair_weight)
    mixer_low, mixed, rate, entry, state = core_forward(
        place, pre, masks, gates, small, tensor
    )
    output_full = jnp.concatenate(ring.gather(output_weight, True), axis=1)

    def block(array, j):
        return lax.slice_in_dim(array, j * rows, (j + 1) * rows, axis=0)

    middle = tokens + tensor_scatter(lambda j: dot(block(mixer_low, j), output_full))
    scale_two, mlp_in = norm_forward(middle, gain_two)
    mlp_rows = tensor_gather(mlp_in.astype(bf16))
    cotangent_rows = tensor_gather(cotangent_own)

    gate_full = jnp.concatenate(ring.gather(gate_weight, True), axis=0)
    up_full = jnp.concatenate(ring.gather(up_weight, False), axis=0)
    down_full = jnp.concatenate(ring.gather(down_weight, False), axis=1)
    gate_pre = dot(mlp_rows, gate_full)
    up_pre = dot(mlp_rows, up_full)
    act, act_slope = gelu_both(gate_pre)
    hidden_low = (act * up_pre).astype(bf16)

    def columns_of(array, r):
        return lax.slice_in_dim(array, r * shard, (r + 1) * shard, axis=1)

    down_grad = ring.scatter(lambda r: dot_rows(hidden_low, columns_of(cotangent_rows, r)), False)
    hidden_grad = dot_back(cotangent_rows, down_full)
    gate_low = (hidden_grad * up_pre * act_slope).astype(bf16)
    up_low = (hidden_grad * act).astype(bf16)
    mlp_in_grad = tensor_scatter(
        lambda j: dot_back(block(gate_low, j), gate_full) + dot_back(block(up_low, j), up_full)
    )
    gate_wgrad = ring.scatter(lambda r: dot_rows(columns_of(mlp_rows, r), gate_low), True)
    up_wgrad = ring.scatter(lambda r: dot_rows(columns_of(mlp_rows, r), up_low), False)
    middle_norm_grad, gain_two_part = norm_backward(middle, scale_two, gain_two, mlp_in_grad)
    middle_grad = cotangent_own.astype(f32) + middle_norm_grad
    residual_rows = tensor_gather(middle_grad.astype(bf16))

    mixer_grad = dot_back(residual_rows, output_full)
    pair_low, gate_grads, small_grads = core_backward(
        place, mixer_grad, pre, mixed, rate, entry, state, masks, gates, small, tensor
    )
    mixer_in_grad = tensor_scatter(lambda j: dot_back(block(pair_low, j), pair_weight))
    output_wgrad = ring.scatter(lambda r: dot_rows(mixer_low, columns_of(residual_rows, r)), True)
    branch_low = pair_low[:, :width]
    entry_low = pair_low[:, width:]
    branch_wgrad = ring.scatter(lambda r: dot_rows(columns_of(mixer_rows, r), branch_low), True)
    input_wgrad = ring.scatter(lambda r: dot_rows(columns_of(mixer_rows, r), entry_low), False)

    def folded(grads):
        kept = jnp.where(same_block, grads, 0.0).reshape(width, gate_blocks, block_width)
        return jnp.sum(kept, axis=1)

    decay_grad = lru_scale * small_grads[7:8] * jax.nn.sigmoid(-decay_full)[None]
    small_columns = jnp.concatenate([small_grads[:7], decay_grad], axis=0).T
    grad_table = jnp.concatenate(
        [folded(gate_grads[:, :width]), folded(gate_grads[:, width:]), small_columns], axis=1
    ).astype(bf16)
    grad_table = jnp.pad(grad_table, ((0, 0), (0, wide - table_columns)))
    grad_table = (
        grad_table.reshape(gate_blocks, dp, piece, wide)
        .transpose(1, 0, 2, 3)
        .reshape(dp, table_rows, wide)
    )
    grad_tables = ring.from_whole(grad_table, 0, 1)
    table_grad = ring.scatter(lambda r: grad_tables[r].astype(f32), True)
    table_grad = table_grad.reshape(gate_blocks, piece, wide)
    rate_wgrad = table_grad[:, :, :block_width]
    entry_wgrad = table_grad[:, :, block_width : 2 * block_width]
    singles = [table_grad[:, :, 2 * block_width + k] for k in range(taps + 4)]

    mlp_sum = tensor_scatter(lambda j: dot(block(hidden_low, j), down_full))
    layer_out = ring.to_whole((middle + mlp_sum).astype(bf16), 1, shard)
    tokens_norm_grad, gain_one_part = norm_backward(tokens, scale_one, gain_one, mixer_in_grad)
    inputs_grad = ring.to_whole((middle_grad + tokens_norm_grad).astype(bf16), 1, shard)
    gain_parts = tensor_sum(jnp.stack([gain_one_part, gain_two_part]))
    gain_sums = ring.scatter_direct([columns_of(gain_parts, r) for r in range(dp)])
    return (
        layer_out,
        inputs_grad,
        gain_sums[0],
        branch_wgrad,
        input_wgrad,
        jnp.stack(singles[:taps]),
        singles[taps],
        rate_wgrad,
        singles[taps + 1],
        entry_wgrad,
        singles[taps + 2],
        singles[taps + 3],
        output_wgrad,
        gain_sums[1],
        gate_wgrad,
        up_wgrad,
        down_grad,
    )


def solution(mesh):
    return jax.shard_map(
        functools.partial(body, dp=mesh.shape["dp"], tensor=mesh.shape["tensor"]),
        mesh=mesh,
        in_specs=(
            P(("dp", "tensor"), None),
            P("dp"),
            P("dp"),
            P("dp", "tensor"),
            P("dp", "tensor"),
            P(None, "tensor", "dp"),
            P("tensor", "dp"),
            P("tensor", "dp", None),
            P("tensor", "dp"),
            P("tensor", "dp", None),
            P("tensor", "dp"),
            P("tensor", "dp"),
            P("tensor", "dp"),
            P("dp"),
            P("dp", "tensor"),
            P("dp", "tensor"),
            P("tensor", "dp"),
            P(("dp", "tensor"), None),
        ),
        out_specs=(
            P(("dp", "tensor"), None),
            P(("dp", "tensor"), None),
            P("dp"),
            P("dp", "tensor"),
            P("dp", "tensor"),
            P(None, "tensor", "dp"),
            P("tensor", "dp"),
            P("tensor", "dp", None),
            P("tensor", "dp"),
            P("tensor", "dp", None),
            P("tensor", "dp"),
            P("tensor", "dp"),
            P("tensor", "dp"),
            P("dp"),
            P("dp", "tensor"),
            P("dp", "tensor"),
            P("tensor", "dp"),
        ),
        check_vma=False,
    )
```

time: 1730 us -> 929 us (0.54)
  waiting for transfers between devices: 842 us -> 357 us
  blocking collectives: 250 us -> 0 us
  local copies, waits for them, and re-layouts: 283 us -> 135 us
  starting transfers between devices: 1.42 us -> 134 us
  other arithmetic: 131 us -> 27 us
  Pallas kernels: 0 us -> 49.5 us
    reduce_scatter x10 -> x0, waiting for transfers between devices: 422 us -> none  [the longest x1 96.5 us: body(): lax.psum_scatter(down_grad.astype(jnp.bfloat16), 'dp', scatter_dimension=...]
    ppermute x0 -> x131, waiting for transfers between devices: none -> 357 us  [the longest x24 124 us: gather(): lax.ppermute(blocks[(count - r + 1) % count], 'dp', self.behind)]
    all_gather x10 -> x0, waiting for transfers between devices: 345 us -> none  [the longest x1 102 us: body(): lax.all_gather(down_weight, 'dp', axis=1, tiled=True)]
    all_gather x9 -> x0, blocking collectives: 202 us -> none  [the longest x1 31.5 us: body(): lax.all_gather(entry_weight, 'dp', axis=1, tiled=True)]
    ppermute x0 -> x131, starting transfers between devices: none -> 134 us  [the longest x25 39.2 us: gather(): blocks[r] = lax.ppermute(blocks[r - 1], 'dp', self.ahead)]
    slice x83 -> x20, local copies, waits for them, and re-layouts: 133 us -> 18 us  [the longest x9 11.2 us: from_whole(): lax.slice_in_dim(whole, i * size, (i + 1) * size, axis=axis)]
    pad x79 -> x2, local copies, waits for them, and re-layouts: 108 us -> 0.07 us  [the longest x1 0.06 us: body(): grad_table = jnp.pad(grad_table, ((0, 0), (0, wide - table_columns)))]
    unnamed x22 -> x0, waiting for transfers between devices: 75.3 us -> none
  transfers between devices with their start and end apart: 21 -> 131, of which waited for: 13 -> 54; matrix products, arithmetic and copies ran while one was open for 31% -> 25% of each run, Pallas kernels for 0% -> 2%
where the time goes in v1:
time: 929 us; the launch traced here: 917 us
  waiting for transfers between devices  357 us (38%)
  matrix products  209 us (22%)
  local copies, waits for them, and re-layouts  135 us (15%)
  starting transfers between devices  134 us (14%)
  Pallas kernels  49.5 us (5%)
  other arithmetic  27 us (3%)
    ppermute x24, waiting for transfers between devices, gather(): lax.ppermute(blocks[(count - r + 1) % count], 'dp', self.behind)  124 us
    ppermute x25, waiting for transfers between devices, gather(): blocks[r] = lax.ppermute(blocks[r - 1], 'dp', self.ahead)  88.8 us
    unnamed x308, local copies, waits for them, and re-layouts  84.9 us
    dot_general x48, matrix products, dot_rows(): lax.dot_general(left, right, (((0,), (0,)), ((), ())), preferred_element_...  76.5 us
    dot_general x14, matrix products, dot_back(): lax.dot_general(left, right, (((1,), (1,)), ((), ())), preferred_element_...  67.7 us
    dot_general x11, matrix products, dot(): return jnp.dot(left, right, preferred_element_type=f32)  65.2 us
    ppermute x25, waiting for transfers between devices, scatter(): right = lax.ppermute(value.astype(bf16), 'dp', self.behind)  58.4 us
    ppermute x24, waiting for transfers between devices, scatter(): left = lax.ppermute(value.astype(bf16), 'dp', self.ahead)  54.5 us
  transfers between devices with their start and end apart: 131, of which 54 were waited for; matrix products, arithmetic and copies ran while one was open for 25% of the time, Pallas kernels for 2%

profile of v1, /device:TPU:0, one launch (start us, length us, event | category | flops | bytes accessed | tf_op | source)
XLA Modules:
  0.0 917.3 jit_solution(16364674187249770876)
XLA Ops:
  60.5 5.0 collective-permute-done.6
  95.9 17.9 %collective-permute-done.11 = bf16[256,640]{1,0:T(8,128)(2,1)S(1)} collective-permute-done((bf16[256,640]{1,0:T(8,128)(2,1)}, bf16[256,640]{1,0:T(8,128)(2,1)S(1)}, u32[]{:S(2)}, u32[]{:S(2)}) %collective-permute-start.11) | collective-permute-done | bytes 327712 | tf_op jit(solution)/shard_map/ppermute | solution.py:381
  115.4 5.4 collective-permute-done.18
  121.4 23.3 %collective-permute-done.25 = bf16[640,256]{1,0:T(8,128)(2,1)S(1)} collective-permute-done((bf16[640,256]{1,0:T(8,128)(2,1)}, bf16[640,256]{1,0:T(8,128)(2,1)S(1)}, u32[]{:S(2)}, u32[]{:S(2)}) %collective-permute-start.25) | collective-permute-done | bytes 327712 | tf_op jit(solution)/shard_map/ppermute | solution.py:381
  149.8 22.4 %collective-permute-done.21 = bf16[256,640]{1,0:T(8,128)(2,1)S(1)} collective-permute-done((bf16[256,640]{1,0:T(8,128)(2,1)}, bf16[256,640]{1,0:T(8,128)(2,1)S(1)}, u32[]{:S(2)}, u32[]{:S(2)}) %collective-permute-start.21) | collective-permute-done | bytes 327712 | tf_op jit(solution)/shard_map/ppermute | solution.py:383
  172.6 6.6 collective-permute-done.29
  190.3 10.0 %collective-permute-done.16 = bf16[256,640]{1,0:T(8,128)(2,1)S(1)} collective-permute-done((bf16[256,640]{1,0:T(8,128)(2,1)S(1)}, bf16[256,640]{1,0:T(8,128)(2,1)S(1)}, u32[]{:S(2)}, u32[]{:S(2)}) %collective-permute-start.16) | collective-permute-done | bytes 327712 | tf_op jit(solution)/shard_map/ppermute | solution.py:383
  202.4 16.9 %collective-permute-done.22 = bf16[256,640]{1,0:T(8,128)(2,1)S(1)} collective-permute-done((bf16[256,640]{1,0:T(8,128)(2,1)S(1)}, bf16[256,640]{1,0:T(8,128)(2,1)S(1)}, u32[]{:S(2)}, u32[]{:S(2)}) %collective-permute-start.22) | collective-permute-done | bytes 327712 | tf_op jit(solution)/shard_map/ppermute | solution.py:383
  221.1 5.2 collective-permute-done.23
  231.5 5.5 collective-permute-done.27
  240.4 10.6 %collective-permute-done.45 = bf16[256,1536]{1,0:T(8,128)(2,1)} collective-permute-done((bf16[256,1536]{1,0:T(8,128)(2,1)S(1)}, bf16[256,1536]{1,0:T(8,128)(2,1)}, u32[]{:S(2)}, u32[]{:S(2)}) %collective-permute-start.45) | collective-permute-done | bytes 786464 | tf_op jit(solution)/shard_map/ppermute | solution.py:381
  250.9 8.4 collective-permute-done.52
  261.4 6.2 collective-permute-done.38
  275.9 12.4 %collective-permute-done.55 = bf16[1536,256]{1,0:T(8,128)(2,1)} collective-permute-done((bf16[1536,256]{1,0:T(8,128)(2,1)S(1)}, bf16[1536,256]{1,0:T(8,128)(2,1)}, u32[]{:S(2)}, u32[]{:S(2)}) %collective-permute-start.55) | collective-permute-done | bytes 786464 | tf_op jit(solution)/shard_map/ppermute | solution.py:383
  290.5 7.9 fusion.177.branch.entry_pre.entry_tail
  298.4 20.9 %core_forward.1 = (bf16[1024,640]{1,0:T(8,128)(2,1)}, f32[1024,640]{1,0:T(8,128)}, f32[1024,640]{1,0:T(8,128)}, f32[1024,640]{1,0:T(8,128)}, f32[1024,640]{1,0:T(8,128)}) custom-call(s32[1]{0:T(128)} %bitcast.1.place, f32[1024,1280]{1,0:T(8,128)} %fusion.177.branch.entry_pre.entry_tail, f32[1024,1280]{1,0:T(8,128)} %fusion.177.branch.entry_pre.entry_tail, ...), custom_call_target="tpu_custom_call" | custom-call | flops 1677721600 | bytes 20971520 | tf_op jit(solution)/shard_map/core_forward/pallas_call | solution.py:259
  326.0 9.7 %collective-permute-done.56 = bf16[1536,256]{1,0:T(8,128)(2,1)} collective-permute-done((bf16[1536,256]{1,0:T(8,128)(2,1)}, bf16[1536,256]{1,0:T(8,128)(2,1)}, u32[]{:S(2)}, u32[]{:S(2)}) %collective-permute-start.56) | collective-permute-done | bytes 786464 | tf_op jit(solution)/shard_map/ppermute | solution.py:383
  345.3 7.1 collective-permute-done.49
  354.3 28.6 %collective-permute-done.57 = bf16[1536,256]{1,0:T(8,128)(2,1)S(1)} collective-permute-done((bf16[1536,256]{1,0:T(8,128)(2,1)}, bf16[1536,256]{1,0:T(8,128)(2,1)S(1)}, u32[]{:S(2)}, u32[]{:S(2)}) %collective-permute-start.57) | collective-permute-done | bytes 786464 | tf_op jit(solution)/shard_map/ppermute | solution.py:383
  393.6 14.2 %fusion.178 = f32[1024,1536]{1,0:T(8,128)} fusion(bf16[1536,2048]{1,0:T(8,128)(2,1)} %constant_dynamic-update-slice_fusion.69, bf16[256,2048]{1,0:T(8,128)(2,1)S(1)} %copy-done.34, bf16[256,2048]{1,0:T(8,128)(2,1)S(1)} %copy-done.28, bf16[256,2048]{1,0:T(8,128)(2,1)S(1)} %copy-done.32, bf16[256,2048]{1,0:T(8,128)(2,1)S(1)} %copy-done.19), kind=kOutput, calls=%fused_computation.445 | convolution fusion | flops 6459228160 | bytes 16777216 | tf_op jit(solution)/shard_map/dot_general | solution.py:359
  422.0 14.0 %fusion.179 = f32[1024,1536]{1,0:T(8,128)} fusion(bf16[2048,1536]{1,0:T(8,128)(2,1)} %constant_dynamic-update-slice_fusion.61, bf16[256,2048]{1,0:T(8,128)(2,1)S(1)} %collective-permute-done.36, bf16[256,2048]{1,0:T(8,128)(2,1)S(1)} %collective-permute-done.35, bf16[256,2048]{1,0:T(8,128)(2,1)S(1)} %collective-permute-done.34, ...), kind=kOutput, calls=%fused_computation.446 | convolution fusion | flops 6459228160 | bytes 16777216 | tf_op jit(solution)/shard_map/dot_general | solution.py:351
  435.9 19.0 %multiply_convert_fusion.1 = (bf16[1024,1536]{1,0:T(8,128)(2,1)S(1)}, bf16[1024,1536]{1,0:T(8,128)(2,1)}, bf16[1024,1536]{1,0:T(8,128)(2,1)}) fusion(f32[1024,1536]{1,0:T(8,128)} %fusion.178, f32[1024,1536]{1,0:T(8,128)} %fusion.179, bf16[2048,1536]{1,0:T(8,128)(2,1)} %constant_dynamic-update-slice_fusion.53, bf16[256,2048]{1,0:T(8,128)(2,1)} %copy-done.41, ...), kind=kOutput, calls=%fused_computation.1 | convolution fusion | flops 6496976896 | bytes 32505856 | tf_op jit(solution)/shard_map/dot_general | solution.py:351
  473.2 5.0 convolution_convert_fusion.7
  487.8 5.2 fusion.28
  493.0 5.2 fusion.30
  499.2 5.9 fusion.65
  505.2 13.2 %collective-permute-done.117 = bf16[256,1536]{1,0:T(8,128)(2,1)S(1)} collective-permute-done((bf16[256,1536]{1,0:T(8,128)(2,1)S(1)}, bf16[256,1536]{1,0:T(8,128)(2,1)S(1)}, u32[]{:S(2)}, u32[]{:S(2)}) %collective-permute-start.117) | collective-permute-done | bytes 786464 | tf_op jit(solution)/shard_map/ppermute | solution.py:397
  524.5 10.4 %collective-permute-done.110 = bf16[256,1536]{1,0:T(8,128)(2,1)} collective-permute-done((bf16[256,1536]{1,0:T(8,128)(2,1)}, bf16[256,1536]{1,0:T(8,128)(2,1)}, u32[]{:S(2)}, u32[]{:S(2)}) %collective-permute-start.110) | collective-permute-done | bytes 786464 | tf_op jit(solution)/shard_map/ppermute | solution.py:397
  545.4 5.3 fusion.29
  551.3 5.8 fusion.27
  557.1 4.9 collective-permute-done.118
  571.0 6.9 collective-permute-done.111
  585.9 10.9 %collective-permute-done.128 = bf16[1536,256]{1,0:T(8,128)(2,1)S(1)} collective-permute-done((bf16[1536,256]{1,0:T(8,128)(2,1)S(1)}, bf16[1536,256]{1,0:T(8,128)(2,1)S(1)}, u32[]{:S(2)}, u32[]{:S(2)}) %collective-permute-start.128) | collective-permute-done | bytes 786464 | tf_op jit(solution)/shard_map/ppermute | solution.py:402
  604.4 4.2 collective-permute-done.66
  610.2 5.7 multiply_reduce_fusion
  616.4 10.1 %collective-permute-done.60 = bf16[256,2048]{1,0:T(8,128)(2,1)} collective-permute-done((bf16[256,2048]{1,0:T(8,128)(2,1)}, bf16[256,2048]{1,0:T(8,128)(2,1)}, u32[]{:S(2)}, u32[]{:S(2)}) %collective-permute-start.60) | collective-permute-done | bytes 1048608 | tf_op jit(solution)/shard_map/ppermute | solution.py:450
  628.2 5.3 fusion.32
  647.0 7.8 collective-permute-done.116
  658.5 13.1 %collective-permute-done.123 = bf16[256,1536]{1,0:T(8,128)(2,1)S(1)} collective-permute-done((bf16[256,1536]{1,0:T(8,128)(2,1)S(1)}, bf16[256,1536]{1,0:T(8,128)(2,1)S(1)}, u32[]{:S(2)}, u32[]{:S(2)}) %collective-permute-start.123) | collective-permute-done | bytes 786464 | tf_op jit(solution)/shard_map/ppermute | solution.py:402
  675.9 8.9 collective-permute-done.130
  691.7 5.0 fusion.187.grad
  696.7 28.6 %core_backward.1 = (bf16[1024,1280]{1,0:T(8,128)(2,1)}, f32[640,1280]{1,0:T(8,128)}, f32[8,640]{1,0:T(8,128)}) custom-call(s32[1]{0:T(128)} %bitcast.1.place, f32[1024,640]{1,0:T(8,128)} %fusion.187.grad, f32[1024,1280]{1,0:T(8,128)} %fusion.177.branch.entry_pre.entry_tail, f32[1024,1280]{1,0:T(8,128)} %fusion.177.branch.entry_pre.entry_tail, ...), custom_call_target="tpu_custom_call" | custom-call | flops 3355443200 | bytes 26214400 | tf_op jit(solution)/shard_map/core_backward/pallas_call | solution.py:302
  726.8 5.5 convolution_convert_fusion.11
  732.3 3.8 convolution_convert_fusion.10
  827.7 4.5 collective-permute-done.104
  853.6 8.0 collective-permute-done.94
  867.3 5.1 collective-permute-done.84
  885.8 6.9 collective-permute-done.72
  (709 shorter events, 432.8 us)
Async XLA Ops:
  8.2 38.3 %collective-permute-start = (bf16[96,384]{1,0:T(8,128)(2,1)S(1)}, bf16[96,384]{1,0:T(8,128)(2,1)S(1)}, u32[]{:S(2)}, u32[]{:S(2)}) collective-permute-start(bf16[96,384]{1,0:T(8,128)(2,1)S(1)} %pad.26), channel_id=1, source_target_pairs={{8,0},{16,8},{24,16},{28,24},{20,28},{12,20},{4,12},{0,4},{9,1},{1... | collective-permute-start | bytes 221192 | tf_op jit(solution)/shard_map/ppermute | solution.py:381
  11.2 37.0 %collective-permute-start.4 = (bf16[96,384]{1,0:T(8,128)(2,1)S(1)}, bf16[96,384]{1,0:T(8,128)(2,1)S(1)}, u32[]{:S(2)}, u32[]{:S(2)}) collective-permute-start(bf16[96,384]{1,0:T(8,128)(2,1)S(1)} %pad.26), channel_id=1, source_target_pairs={{0,8},{8,16},{16,24},{24,28},{28,20},{20,12},{12,4},{4,0},{1,9},{9... | collective-permute-start | bytes 221192 | tf_op jit(solution)/shard_map/ppermute | solution.py:383
  11.3 74.4 %collective-permute-start.10 = (bf16[256,640]{1,0:T(8,128)(2,1)}, bf16[256,640]{1,0:T(8,128)(2,1)}, u32[]{:S(2)}, u32[]{:S(2)}) collective-permute-start(bf16[256,640]{1,0:T(8,128)(2,1)} %param.22), channel_id=1, source_target_pairs={{8,0},{16,8},{24,16},{28,24},{20,28},{12,20},{4,12},{0,4},{9,1},{1... | collective-permute-start | bytes 983048 | tf_op jit(solution)/shard_map/ppermute | solution.py:381
  13.2 73.1 %collective-permute-start.14 = (bf16[256,640]{1,0:T(8,128)(2,1)}, bf16[256,640]{1,0:T(8,128)(2,1)}, u32[]{:S(2)}, u32[]{:S(2)}) collective-permute-start(bf16[256,640]{1,0:T(8,128)(2,1)} %param.22), channel_id=1, source_target_pairs={{0,8},{8,16},{16,24},{24,28},{28,20},{20,12},{12,4},{4,0},{1,9},{9... | collective-permute-start | bytes 983048 | tf_op jit(solution)/shard_map/ppermute | solution.py:383
  13.4 75.1 %collective-permute-start.17 = (bf16[256,640]{1,0:T(8,128)(2,1)}, bf16[256,640]{1,0:T(8,128)(2,1)}, u32[]{:S(2)}, u32[]{:S(2)}) collective-permute-start(bf16[256,640]{1,0:T(8,128)(2,1)} %param.23), channel_id=1, source_target_pairs={{8,0},{16,8},{24,16},{28,24},{20,28},{12,20},{4,12},{0,4},{9,1},{1... | collective-permute-start | bytes 983048 | tf_op jit(solution)/shard_map/ppermute | solution.py:381
  57.3 32.9 %collective-permute-start.20 = (bf16[256,640]{1,0:T(8,128)(2,1)}, bf16[256,640]{1,0:T(8,128)(2,1)}, u32[]{:S(2)}, u32[]{:S(2)}) collective-permute-start(bf16[256,640]{1,0:T(8,128)(2,1)} %param.23), channel_id=1, source_target_pairs={{0,8},{8,16},{16,24},{24,28},{28,20},{20,12},{12,4},{4,0},{1,9},{9... | collective-permute-start | bytes 983048 | tf_op jit(solution)/shard_map/ppermute | solution.py:383
  86.3 59.6 %collective-permute-start.44 = (bf16[256,1536]{1,0:T(8,128)(2,1)S(1)}, bf16[256,1536]{1,0:T(8,128)(2,1)S(1)}, u32[]{:S(2)}, u32[]{:S(2)}) collective-permute-start(bf16[256,1536]{1,0:T(8,128)(2,1)S(1)} %copy-done.43), channel_id=1, source_target_pairs={{8,0},{16,8},{24,16},{28,24},{20,28},{12,20},{4,12},{0,4},{9,1},{1... | collective-permute-start | bytes 2359304 | tf_op jit(solution)/shard_map/ppermute | solution.py:381
  90.2 30.6 %collective-permute-start.18 = (bf16[256,640]{1,0:T(8,128)(2,1)}, bf16[256,640]{1,0:T(8,128)(2,1)S(1)}, u32[]{:S(2)}, u32[]{:S(2)}) collective-permute-start(bf16[256,640]{1,0:T(8,128)(2,1)} %collective-permute-done.17), channel_id=1, source_target_pairs={{8,0},{16,8},{24,16},{28,24},{20,28},{12,20},{4,12},{0,4},{9,1},{1... | collective-permute-start | bytes 983048 | tf_op jit(solution)/shard_map/ppermute | solution.py:381
  91.8 56.6 %collective-permute-start.51 = (bf16[1536,256]{1,0:T(8,128)(2,1)S(1)}, bf16[1536,256]{1,0:T(8,128)(2,1)S(1)}, u32[]{:S(2)}, u32[]{:S(2)}) collective-permute-start(bf16[1536,256]{1,0:T(8,128)(2,1)S(1)} %copy-done.45), channel_id=1, source_target_pairs={{8,0},{16,8},{24,16},{28,24},{20,28},{12,20},{4,12},{0,4},{9,1},{1... | collective-permute-start | bytes 2359304 | tf_op jit(solution)/shard_map/ppermute | solution.py:381
  93.4 51.3 %collective-permute-start.25 = (bf16[640,256]{1,0:T(8,128)(2,1)}, bf16[640,256]{1,0:T(8,128)(2,1)S(1)}, u32[]{:S(2)}, u32[]{:S(2)}) collective-permute-start(bf16[640,256]{1,0:T(8,128)(2,1)} %collective-permute-done.24), channel_id=1, source_target_pairs={{8,0},{16,8},{24,16},{28,24},{20,28},{12,20},{4,12},{0,4},{9,1},{1... | collective-permute-start | bytes 983048 | tf_op jit(solution)/shard_map/ppermute | solution.py:381
  113.8 67.0 %collective-permute-start.37 = (bf16[256,1536]{1,0:T(8,128)(2,1)S(1)}, bf16[256,1536]{1,0:T(8,128)(2,1)S(1)}, u32[]{:S(2)}, u32[]{:S(2)}) collective-permute-start(bf16[256,1536]{1,0:T(8,128)(2,1)S(1)} %copy-done.47), channel_id=1, source_target_pairs={{8,0},{16,8},{24,16},{28,24},{20,28},{12,20},{4,12},{0,4},{9,1},{1... | collective-permute-start | bytes 2359304 | tf_op jit(solution)/shard_map/ppermute | solution.py:381
  144.7 38.8 %collective-permute-start.47 = (bf16[256,1536]{1,0:T(8,128)(2,1)S(1)}, bf16[256,1536]{1,0:T(8,128)(2,1)S(1)}, u32[]{:S(2)}, u32[]{:S(2)}) collective-permute-start(bf16[256,1536]{1,0:T(8,128)(2,1)S(1)} %copy-done.43), channel_id=1, source_target_pairs={{0,8},{8,16},{16,24},{24,28},{28,20},{20,12},{12,4},{4,0},{1,9},{9... | collective-permute-start | bytes 2359304 | tf_op jit(solution)/shard_map/ppermute | solution.py:383
  145.9 33.3 %collective-permute-start.29 = (bf16[640,256]{1,0:T(8,128)(2,1)S(1)}, bf16[640,256]{1,0:T(8,128)(2,1)S(1)}, u32[]{:S(2)}, u32[]{:S(2)}) collective-permute-start(bf16[640,256]{1,0:T(8,128)(2,1)S(1)} %collective-permute-done.28), channel_id=1, source_target_pairs={{0,8},{8,16},{16,24},{24,28},{28,20},{20,12},{12,4},{4,0},{1,9},{9... | collective-permute-start | bytes 983048 | tf_op jit(solution)/shard_map/ppermute | solution.py:383
  148.4 35.3 %collective-permute-start.12 = (bf16[256,640]{1,0:T(8,128)(2,1)S(1)}, bf16[256,640]{1,0:T(8,128)(2,1)S(1)}, u32[]{:S(2)}, u32[]{:S(2)}) collective-permute-start(bf16[256,640]{1,0:T(8,128)(2,1)S(1)} %collective-permute-done.11), channel_id=1, source_target_pairs={{8,0},{16,8},{24,16},{28,24},{20,28},{12,20},{4,12},{0,4},{9,1},{1... | collective-permute-start | bytes 983048 | tf_op jit(solution)/shard_map/ppermute | solution.py:381
  172.2 47.5 %collective-permute-start.54 = (bf16[1536,256]{1,0:T(8,128)(2,1)S(1)}, bf16[1536,256]{1,0:T(8,128)(2,1)S(1)}, u32[]{:S(2)}, u32[]{:S(2)}) collective-permute-start(bf16[1536,256]{1,0:T(8,128)(2,1)S(1)} %copy-done.45), channel_id=1, source_target_pairs={{0,8},{8,16},{16,24},{24,28},{28,20},{20,12},{12,4},{4,0},{1,9},{9... | collective-permute-start | bytes 2359304 | tf_op jit(solution)/shard_map/ppermute | solution.py:383
  186.3 41.7 %collective-permute-start.41 = (bf16[256,1536]{1,0:T(8,128)(2,1)S(1)}, bf16[256,1536]{1,0:T(8,128)(2,1)}, u32[]{:S(2)}, u32[]{:S(2)}) collective-permute-start(bf16[256,1536]{1,0:T(8,128)(2,1)S(1)} %copy-done.47), channel_id=1, source_target_pairs={{0,8},{8,16},{16,24},{24,28},{28,20},{20,12},{12,4},{4,0},{1,9},{9... | collective-permute-start | bytes 2359304 | tf_op jit(solution)/shard_map/ppermute | solution.py:383
  200.3 39.3 %collective-permute-start.62 = (bf16[256,2048]{1,0:T(8,128)(2,1)S(1)}, bf16[256,2048]{1,0:T(8,128)(2,1)S(1)}, u32[]{:S(2)}, u32[]{:S(2)}) collective-permute-start(bf16[256,2048]{1,0:T(8,128)(2,1)S(1)} %copy-done.18), channel_id=1, source_target_pairs={{0,2},{1,3},{2,0},{3,1},{4,6},{5,7},{6,4},{7,5},{8,10},{9,11},{10,... | collective-permute-start | bytes 3145736 | tf_op jit(solution)/shard_map/ppermute | solution.py:443
  201.8 37.9 %collective-permute-start.8 = (bf16[256,2048]{1,0:T(8,128)(2,1)S(1)}, bf16[256,2048]{1,0:T(8,128)(2,1)S(1)}, u32[]{:S(2)}, u32[]{:S(2)}) collective-permute-start(bf16[256,2048]{1,0:T(8,128)(2,1)S(1)} %fusion.35), channel_id=1, source_target_pairs={{0,2},{1,3},{2,0},{3,1},{4,6},{5,7},{6,4},{7,5},{8,10},{9,11},{10,... | collective-permute-start | bytes 3145736 | tf_op jit(solution)/shard_map/ppermute | solution.py:443
  237.0 30.7 %collective-permute-start.38 = (bf16[256,1536]{1,0:T(8,128)(2,1)S(1)}, bf16[256,1536]{1,0:T(8,128)(2,1)S(1)}, u32[]{:S(2)}, u32[]{:S(2)}) collective-permute-start(bf16[256,1536]{1,0:T(8,128)(2,1)S(1)} %collective-permute-done.37), channel_id=1, source_target_pairs={{8,0},{16,8},{24,16},{28,24},{20,28},{12,20},{4,12},{0,4},{9,1},{1... | collective-permute-start | bytes 2359304 | tf_op jit(solution)/shard_map/ppermute | solution.py:381
  239.7 31.4 %collective-permute-start.61 = (bf16[256,2048]{1,0:T(8,128)(2,1)S(1)}, bf16[256,2048]{1,0:T(8,128)(2,1)S(1)}, u32[]{:S(2)}, u32[]{:S(2)}) collective-permute-start(bf16[256,2048]{1,0:T(8,128)(2,1)S(1)} %copy-done.18), channel_id=1, source_target_pairs={{0,1},{1,0},{2,3},{3,2},{4,5},{5,4},{6,7},{7,6},{8,9},{9,8},{10,11... | collective-permute-start | bytes 3145736 | tf_op jit(solution)/shard_map/ppermute | solution.py:442
  239.8 31.6 %collective-permute-start.63 = (bf16[256,2048]{1,0:T(8,128)(2,1)S(1)}, bf16[256,2048]{1,0:T(8,128)(2,1)S(1)}, u32[]{:S(2)}, u32[]{:S(2)}) collective-permute-start(bf16[256,2048]{1,0:T(8,128)(2,1)S(1)} %collective-permute-done.62), channel_id=1, source_target_pairs={{0,1},{1,0},{2,3},{3,2},{4,5},{5,4},{6,7},{7,6},{8,9},{9,8},{10,11... | collective-permute-start | bytes 3145736 | tf_op jit(solution)/shard_map/ppermute | solution.py:444
  259.4 30.5 %collective-permute-start.9 = (bf16[256,2048]{1,0:T(8,128)(2,1)S(1)}, bf16[256,2048]{1,0:T(8,128)(2,1)S(1)}, u32[]{:S(2)}, u32[]{:S(2)}) collective-permute-start(bf16[256,2048]{1,0:T(8,128)(2,1)S(1)} %collective-permute-done.8), channel_id=1, source_target_pairs={{0,1},{1,0},{2,3},{3,2},{4,5},{5,4},{6,7},{7,6},{8,9},{9,8},{10,11... | collective-permute-start | bytes 3145736 | tf_op jit(solution)/shard_map/ppermute | solution.py:444
  271.1 48.2 %collective-permute-start.48 = (bf16[256,1536]{1,0:T(8,128)(2,1)S(1)}, bf16[256,1536]{1,0:T(8,128)(2,1)}, u32[]{:S(2)}, u32[]{:S(2)}) collective-permute-start(bf16[256,1536]{1,0:T(8,128)(2,1)S(1)} %collective-permute-done.47), channel_id=1, source_target_pairs={{0,8},{8,16},{16,24},{24,28},{28,20},{20,12},{12,4},{4,0},{1,9},{9... | collective-permute-start | bytes 2359304 | tf_op jit(solution)/shard_map/ppermute | solution.py:383
  271.4 53.8 %collective-permute-start.42 = (bf16[256,1536]{1,0:T(8,128)(2,1)}, bf16[256,1536]{1,0:T(8,128)(2,1)}, u32[]{:S(2)}, u32[]{:S(2)}) collective-permute-start(bf16[256,1536]{1,0:T(8,128)(2,1)} %collective-permute-done.41), channel_id=1, source_target_pairs={{0,8},{8,16},{16,24},{24,28},{28,20},{20,12},{12,4},{4,0},{1,9},{9... | collective-permute-start | bytes 2359304 | tf_op jit(solution)/shard_map/ppermute | solution.py:383
  274.1 48.8 %collective-permute-start.46 = (bf16[256,1536]{1,0:T(8,128)(2,1)}, bf16[256,1536]{1,0:T(8,128)(2,1)}, u32[]{:S(2)}, u32[]{:S(2)}) collective-permute-start(bf16[256,1536]{1,0:T(8,128)(2,1)} %collective-permute-done.45), channel_id=1, source_target_pairs={{8,0},{16,8},{24,16},{28,24},{20,28},{12,20},{4,12},{0,4},{9,1},{1... | collective-permute-start | bytes 2359304 | tf_op jit(solution)/shard_map/ppermute | solution.py:381
  288.3 37.3 %collective-permute-start.53 = (bf16[1536,256]{1,0:T(8,128)(2,1)}, bf16[1536,256]{1,0:T(8,128)(2,1)}, u32[]{:S(2)}, u32[]{:S(2)}) collective-permute-start(bf16[1536,256]{1,0:T(8,128)(2,1)} %collective-permute-done.52), channel_id=1, source_target_pairs={{8,0},{16,8},{24,16},{28,24},{20,28},{12,20},{4,12},{0,4},{9,1},{1... | collective-permute-start | bytes 2359304 | tf_op jit(solution)/shard_map/ppermute | solution.py:381
  289.9 45.8 %collective-permute-start.56 = (bf16[1536,256]{1,0:T(8,128)(2,1)}, bf16[1536,256]{1,0:T(8,128)(2,1)}, u32[]{:S(2)}, u32[]{:S(2)}) collective-permute-start(bf16[1536,256]{1,0:T(8,128)(2,1)} %collective-permute-done.55), channel_id=1, source_target_pairs={{0,8},{8,16},{16,24},{24,28},{28,20},{20,12},{12,4},{4,0},{1,9},{9... | collective-permute-start | bytes 2359304 | tf_op jit(solution)/shard_map/ppermute | solution.py:383
  325.6 89.3 %collective-permute-start.43 = (bf16[256,1536]{1,0:T(8,128)(2,1)}, bf16[256,1536]{1,0:T(8,128)(2,1)S(1)}, u32[]{:S(2)}, u32[]{:S(2)}) collective-permute-start(bf16[256,1536]{1,0:T(8,128)(2,1)} %collective-permute-done.42), channel_id=1, source_target_pairs={{0,8},{8,16},{16,24},{24,28},{28,20},{20,12},{12,4},{4,0},{1,9},{9... | collective-permute-start | bytes 2359304 | tf_op jit(solution)/shard_map/ppermute | solution.py:383
  335.7 47.3 %collective-permute-start.57 = (bf16[1536,256]{1,0:T(8,128)(2,1)}, bf16[1536,256]{1,0:T(8,128)(2,1)S(1)}, u32[]{:S(2)}, u32[]{:S(2)}) collective-permute-start(bf16[1536,256]{1,0:T(8,128)(2,1)} %collective-permute-done.56), channel_id=1, source_target_pairs={{0,8},{8,16},{16,24},{24,28},{28,20},{20,12},{12,4},{4,0},{1,9},{9... | collective-permute-start | bytes 2359304 | tf_op jit(solution)/shard_map/ppermute | solution.py:383
  340.0 49.9 %collective-permute-start.31 = (bf16[256,2048]{1,0:T(8,128)(2,1)S(1)}, bf16[256,2048]{1,0:T(8,128)(2,1)S(1)}, u32[]{:S(2)}, u32[]{:S(2)}) collective-permute-start(bf16[256,2048]{1,0:T(8,128)(2,1)S(1)} %convolution_convert_fusion.9), channel_id=1, source_target_pairs={{0,1},{1,0},{2,3},{3,2},{4,5},{5,4},{6,7},{7,6},{8,9},{9,8},{10,11... | collective-permute-start | bytes 3145736 | tf_op jit(solution)/shard_map/ppermute | solution.py:451
  341.1 48.8 %collective-permute-start.33 = (bf16[256,2048]{1,0:T(8,128)(2,1)S(1)}, bf16[256,2048]{1,0:T(8,128)(2,1)S(1)}, u32[]{:S(2)}, u32[]{:S(2)}) collective-permute-start(bf16[256,2048]{1,0:T(8,128)(2,1)S(1)} %fusion.31), channel_id=1, source_target_pairs={{0,2},{1,3},{2,0},{3,1},{4,6},{5,7},{6,4},{7,5},{8,10},{9,11},{10,... | collective-permute-start | bytes 3145736 | tf_op jit(solution)/shard_map/ppermute | solution.py:450
  352.4 61.5 %collective-permute-start.40 = (bf16[256,1536]{1,0:T(8,128)(2,1)S(1)}, bf16[256,1536]{1,0:T(8,128)(2,1)S(1)}, u32[]{:S(2)}, u32[]{:S(2)}) collective-permute-start(bf16[256,1536]{1,0:T(8,128)(2,1)S(1)} %collective-permute-done.39), channel_id=1, source_target_pairs={{8,0},{16,8},{24,16},{28,24},{20,28},{12,20},{4,12},{0,4},{9,1},{1... | collective-permute-start | bytes 2359304 | tf_op jit(solution)/shard_map/ppermute | solution.py:381
  481.1 41.8 %collective-permute-start.124 = (bf16[1536,256]{1,0:T(8,128)(2,1)S(1)}, bf16[1536,256]{1,0:T(8,128)(2,1)S(1)}, u32[]{:S(2)}, u32[]{:S(2)}) collective-permute-start(bf16[1536,256]{1,0:T(8,128)(2,1)S(1)} %convolution_convert_fusion.1), channel_id=1, source_target_pairs={{0,8},{8,16},{16,24},{24,28},{28,20},{20,12},{12,4},{4,0},{1,9},{9... | collective-permute-start | bytes 2359304 | tf_op jit(solution)/shard_map/ppermute | solution.py:397
  481.4 56.5 %collective-permute-start.127 = (bf16[1536,256]{1,0:T(8,128)(2,1)}, bf16[1536,256]{1,0:T(8,128)(2,1)}, u32[]{:S(2)}, u32[]{:S(2)}) collective-permute-start(bf16[1536,256]{1,0:T(8,128)(2,1)} %convolution_convert_fusion), channel_id=1, source_target_pairs={{8,0},{16,8},{24,16},{28,24},{20,28},{12,20},{4,12},{0,4},{9,1},{1... | collective-permute-start | bytes 2359304 | tf_op jit(solution)/shard_map/ppermute | solution.py:402
  483.2 35.2 %collective-permute-start.117 = (bf16[256,1536]{1,0:T(8,128)(2,1)S(1)}, bf16[256,1536]{1,0:T(8,128)(2,1)S(1)}, u32[]{:S(2)}, u32[]{:S(2)}) collective-permute-start(bf16[256,1536]{1,0:T(8,128)(2,1)S(1)} %convolution_convert_fusion.3), channel_id=1, source_target_pairs={{0,8},{8,16},{16,24},{24,28},{28,20},{20,12},{12,4},{4,0},{1,9},{9... | collective-permute-start | bytes 2359304 | tf_op jit(solution)/shard_map/ppermute | solution.py:397
  483.5 37.5 %collective-permute-start.120 = (bf16[256,1536]{1,0:T(8,128)(2,1)S(1)}, bf16[256,1536]{1,0:T(8,128)(2,1)S(1)}, u32[]{:S(2)}, u32[]{:S(2)}) collective-permute-start(bf16[256,1536]{1,0:T(8,128)(2,1)S(1)} %convolution_convert_fusion.2), channel_id=1, source_target_pairs={{8,0},{16,8},{24,16},{28,24},{20,28},{12,20},{4,12},{0,4},{9,1},{1... | collective-permute-start | bytes 2359304 | tf_op jit(solution)/shard_map/ppermute | solution.py:402
  487.1 47.8 %collective-permute-start.110 = (bf16[256,1536]{1,0:T(8,128)(2,1)}, bf16[256,1536]{1,0:T(8,128)(2,1)}, u32[]{:S(2)}, u32[]{:S(2)}) collective-permute-start(bf16[256,1536]{1,0:T(8,128)(2,1)} %convolution_convert_fusion.5), channel_id=1, source_target_pairs={{0,8},{8,16},{16,24},{24,28},{28,20},{20,12},{12,4},{4,0},{1,9},{9... | collective-permute-start | bytes 2359304 | tf_op jit(solution)/shard_map/ppermute | solution.py:397
  520.9 83.0 %collective-permute-start.64 = (bf16[256,2048]{1,0:T(8,128)(2,1)S(1)}, bf16[256,2048]{1,0:T(8,128)(2,1)S(1)}, u32[]{:S(2)}, u32[]{:S(2)}) collective-permute-start(bf16[256,2048]{1,0:T(8,128)(2,1)S(1)} %fusion.28), channel_id=1, source_target_pairs={{0,1},{1,0},{2,3},{3,2},{4,5},{5,4},{6,7},{7,6},{8,9},{9,8},{10,11... | collective-permute-start | bytes 3145736 | tf_op jit(solution)/shard_map/ppermute | solution.py:451
  534.9 81.0 %collective-permute-start.58 = (bf16[256,2048]{1,0:T(8,128)(2,1)S(1)}, bf16[256,2048]{1,0:T(8,128)(2,1)S(1)}, u32[]{:S(2)}, u32[]{:S(2)}) collective-permute-start(bf16[256,2048]{1,0:T(8,128)(2,1)S(1)} %convolution_convert_fusion.7), channel_id=1, source_target_pairs={{0,1},{1,0},{2,3},{3,2},{4,5},{5,4},{6,7},{7,6},{8,9},{9,8},{10,11... | collective-permute-start | bytes 3145736 | tf_op jit(solution)/shard_map/ppermute | solution.py:451
  566.7 30.1 %collective-permute-start.128 = (bf16[1536,256]{1,0:T(8,128)(2,1)S(1)}, bf16[1536,256]{1,0:T(8,128)(2,1)S(1)}, u32[]{:S(2)}, u32[]{:S(2)}) collective-permute-start(bf16[1536,256]{1,0:T(8,128)(2,1)S(1)} %copy-done.87), channel_id=1, source_target_pairs={{8,0},{16,8},{24,16},{28,24},{20,28},{12,20},{4,12},{0,4},{9,1},{1... | collective-permute-start | bytes 2359304 | tf_op jit(solution)/shard_map/ppermute | solution.py:402
  600.4 43.0 %collective-permute-start.129 = (bf16[1536,256]{1,0:T(8,128)(2,1)}, bf16[1536,256]{1,0:T(8,128)(2,1)}, u32[]{:S(2)}, u32[]{:S(2)}) collective-permute-start(bf16[1536,256]{1,0:T(8,128)(2,1)} %fusion.25), channel_id=1, source_target_pairs={{8,0},{16,8},{24,16},{28,24},{20,28},{12,20},{4,12},{0,4},{9,1},{1... | collective-permute-start | bytes 2359304 | tf_op jit(solution)/shard_map/ppermute | solution.py:402
  603.9 42.0 %collective-permute-start.119 = (bf16[256,1536]{1,0:T(8,128)(2,1)}, bf16[256,1536]{1,0:T(8,128)(2,1)S(1)}, u32[]{:S(2)}, u32[]{:S(2)}) collective-permute-start(bf16[256,1536]{1,0:T(8,128)(2,1)} %fusion.17), channel_id=1, source_target_pairs={{0,8},{8,16},{16,24},{24,28},{28,20},{20,12},{12,4},{4,0},{1,9},{9... | collective-permute-start | bytes 2359304 | tf_op jit(solution)/shard_map/ppermute | solution.py:397
  640.6 31.0 %collective-permute-start.123 = (bf16[256,1536]{1,0:T(8,128)(2,1)S(1)}, bf16[256,1536]{1,0:T(8,128)(2,1)S(1)}, u32[]{:S(2)}, u32[]{:S(2)}) collective-permute-start(bf16[256,1536]{1,0:T(8,128)(2,1)S(1)} %fusion.19), channel_id=1, source_target_pairs={{8,0},{16,8},{24,16},{28,24},{20,28},{12,20},{4,12},{0,4},{9,1},{1... | collective-permute-start | bytes 2359304 | tf_op jit(solution)/shard_map/ppermute | solution.py:402
  643.4 30.4 %collective-permute-start.113 = (bf16[256,1536]{1,0:T(8,128)(2,1)S(1)}, bf16[256,1536]{1,0:T(8,128)(2,1)S(1)}, u32[]{:S(2)}, u32[]{:S(2)}) collective-permute-start(bf16[256,1536]{1,0:T(8,128)(2,1)S(1)} %fusion.12), channel_id=1, source_target_pairs={{0,8},{8,16},{16,24},{24,28},{28,20},{20,12},{12,4},{4,0},{1,9},{9... | collective-permute-start | bytes 2359304 | tf_op jit(solution)/shard_map/ppermute | solution.py:397
  646.0 29.9 %collective-permute-start.126 = (bf16[1536,256]{1,0:T(8,128)(2,1)S(1)}, bf16[1536,256]{1,0:T(8,128)(2,1)S(1)}, u32[]{:S(2)}, u32[]{:S(2)}) collective-permute-start(bf16[1536,256]{1,0:T(8,128)(2,1)S(1)} %copy-done.86), channel_id=1, source_target_pairs={{0,8},{8,16},{16,24},{24,28},{28,20},{20,12},{12,4},{4,0},{1,9},{9... | collective-permute-start | bytes 2359304 | tf_op jit(solution)/shard_map/ppermute | solution.py:397
  654.8 32.3 %collective-permute-start.67 = (bf16[256,2048]{1,0:T(8,128)(2,1)S(1)}, bf16[256,2048]{1,0:T(8,128)(2,1)S(1)}, u32[]{:S(2)}, u32[]{:S(2)}) collective-permute-start(bf16[256,2048]{1,0:T(8,128)(2,1)S(1)} %fusion.176), channel_id=1, source_target_pairs={{0,1},{1,0},{2,3},{3,2},{4,5},{5,4},{6,7},{7,6},{8,9},{9,8},{10,11... | collective-permute-start | bytes 3145736 | tf_op jit(solution)/shard_map/ppermute | solution.py:442
  817.7 68.1 %collective-permute-start.70 = (bf16[256,2048]{1,0:T(8,128)(2,1)S(1)}, bf16[256,2048]{1,0:T(8,128)(2,1)S(1)}, u32[]{:S(2)}, u32[]{:S(2)}) collective-permute-start(bf16[256,2048]{1,0:T(8,128)(2,1)S(1)} %copy-done.85), channel_id=1, source_target_pairs={{0,1},{1,0},{2,3},{3,2},{4,5},{5,4},{6,7},{7,6},{8,9},{9,8},{10,11... | collective-permute-start | bytes 3145736 | tf_op jit(solution)/shard_map/ppermute | solution.py:451
  819.6 43.8 %collective-permute-start.71 = (bf16[256,2048]{1,0:T(8,128)(2,1)}, bf16[256,2048]{1,0:T(8,128)(2,1)S(1)}, u32[]{:S(2)}, u32[]{:S(2)}) collective-permute-start(bf16[256,2048]{1,0:T(8,128)(2,1)} %convolution_convert_fusion.10), channel_id=1, source_target_pairs={{0,1},{1,0},{2,3},{3,2},{4,5},{5,4},{6,7},{7,6},{8,9},{9,8},{10,11... | collective-permute-start | bytes 3145736 | tf_op jit(solution)/shard_map/ppermute | solution.py:449
  (180 other events, 3514.4 us)

commit v2 on v1

--- a/solution.py
+++ b/solution.py
@@ -13,7 +13,8 @@
 cubic = 0.044715
 f32 = jnp.float32
 bf16 = jnp.bfloat16
-vmem_bytes = 60 * 1024 * 1024
+vmem_bytes = 56 * 1024 * 1024
+light = pl.CostEstimate(flops=1000, bytes_accessed=1000, transcendentals=0)
 
 
 def gelu_both(value):
@@ -278,9 +279,7 @@
         ),
         out_shape=[jax.ShapeDtypeStruct((total, width), bf16)] + [kept] * 4,
         compiler_params=pltpu.CompilerParams(vmem_limit_bytes=vmem_bytes),
-        cost_estimate=pl.CostEstimate(
-            flops=4 * total * width * width, bytes_accessed=32 * total * width, transcendentals=0
-        ),
+        cost_estimate=light,
         name="core_forward",
     )(place, pre, pre, masks, gates, small)
 
@@ -340,9 +339,7 @@
             jax.ShapeDtypeStruct((8, width), f32),
         ],
         compiler_params=pltpu.CompilerParams(vmem_limit_bytes=vmem_bytes),
-        cost_estimate=pl.CostEstimate(
-            flops=8 * total * width * width, bytes_accessed=40 * total * width, transcendentals=0
-        ),
+        cost_estimate=light,
         name="core_backward",
     )(place, grad, pre, pre, mixed, rate, entry, state, state, pre, masks, gates, small)
 
@@ -357,6 +354,219 @@
 
 def dot_back(left, right):
     return lax.dot_general(left, right, (((1,), (1,)), ((), ())), preferred_element_type=f32)
+
+
+def fixed(shape):
+    zeros = (0,) * len(shape)
+    return pl.BlockSpec(shape, lambda *_: zeros)
+
+
+def call(kernel, name, grid, in_specs, out_specs, out_shape, scratch=()):
+    return pl.pallas_call(
+        kernel,
+        grid=grid,
+        in_specs=in_specs,
+        out_specs=out_specs,
+        out_shape=out_shape,
+        scratch_shapes=list(scratch),
+        compiler_params=pltpu.CompilerParams(vmem_limit_bytes=vmem_bytes),
+        cost_estimate=light,
+        name=name,
+    )
+
+
+def spread(lefts, weights, first, count, transposed, name):
+    rows = lefts[0][0].shape[0] // 4
+    pieces = len(weights[0])
+    product = dot_back if transposed else dot
+    sizes = [w.shape[0 if transposed else 1] for w in weights[0]]
+    widths = [w[0].shape[1 if transposed else 0] for w in weights]
+    features = sum(sizes)
+    terms = len(lefts)
+
+    def kernel(*refs):
+        left = [ref[...] for ref in refs[:terms]]
+        flat = refs[terms : terms + terms * pieces]
+        outs = refs[terms + terms * pieces : -1]
+        total = refs[-1]
+        at = 0
+        for r in range(pieces):
+            value = product(left[0], flat[r][...])
+            for i in range(1, terms):
+                value += product(left[i], flat[i * pieces + r][...])
+            total[:, at : at + sizes[r]] = value.astype(bf16)
+            at += sizes[r]
+        for g in range(count):
+
+            @pl.when(pl.program_id(0) == g)
+            def _():
+                outs[g][...] = total[...]
+
+    def left_spec(width, column):
+        return pl.BlockSpec((rows, width), lambda g: (first - g, column))
+
+    return call(
+        kernel,
+        name,
+        (count,),
+        [left_spec(width, column) for width, (_, column) in zip(widths, lefts)]
+        + [fixed(w.shape) for group in weights for w in group],
+        [fixed((rows, features))] * count,
+        [jax.ShapeDtypeStruct((rows, features), bf16)] * count,
+        [pltpu.VMEM((rows, features), bf16)],
+    )(*[left for left, _ in lefts], *[w for group in weights for w in group])
+
+
+def collect(left, weights, transposed, name):
+    total, features = left.shape
+    rows = total // 4
+    pieces = len(weights[0])
+    product = dot_back if transposed else dot
+    sizes = [w.shape[1 if transposed else 0] for w in weights[0]]
+    widths = [w[0].shape[0 if transposed else 1] for w in weights]
+
+    def kernel(*refs):
+        out = refs[-1]
+        column = 0
+        for i, width in enumerate(widths):
+            at = 0
+            value = None
+            for r in range(pieces):
+                term = product(refs[0][:, at : at + sizes[r]], refs[1 + i * pieces + r][...])
+                value = term if value is None else value + term
+                at += sizes[r]
+            out[:, column : column + width] = value
+            column += width
+
+    width = sum(widths)
+    return call(
+        kernel,
+        name,
+        (4,),
+        [pl.BlockSpec((rows, features), lambda g: (g, 0))]
+        + [fixed(w.shape) for group in weights for w in group],
+        pl.BlockSpec((rows, width), lambda g: (g, 0)),
+        jax.ShapeDtypeStruct((total, width), f32),
+    )(left, *[w for group in weights for w in group])
+
+
+def gated_forward(left, weights):
+    total, features = left.shape
+    rows = total // 4
+    pieces = len(weights)
+    size = features // pieces
+    units = weights[0].shape[1] // 2
+    step = units // 3
+
+    def kernel(*refs):
+        left_ref = refs[0]
+        hidden, act_out, slope_out = refs[1 + pieces :]
+        for c in range(3):
+            at = slice(c * step, (c + 1) * step)
+            after = slice(units + c * step, units + (c + 1) * step)
+            gate = up = None
+            for r in range(pieces):
+                part = left_ref[:, r * size : (r + 1) * size]
+                one = dot(part, refs[1 + r][:, at])
+                two = dot(part, refs[1 + r][:, after])
+                gate = one if gate is None else gate + one
+                up = two if up is None else up + two
+            act, slope = gelu_both(gate)
+            hidden[:, at] = (act * up).astype(bf16)
+            act_out[:, at] = act.astype(bf16)
+            slope_out[:, at] = (up * slope).astype(bf16)
+
+    block = pl.BlockSpec((rows, units), lambda g: (g, 0))
+    return call(
+        kernel,
+        "gated_forward",
+        (4,),
+        [pl.BlockSpec((rows, features), lambda g: (g, 0))] + [fixed(w.shape) for w in weights],
+        [block] * 3,
+        [jax.ShapeDtypeStruct((total, units), bf16)] * 3,
+    )(left, *weights)
+
+
+def gated_backward(left, down_pieces, act, slope):
+    total, features = left.shape
+    rows = total // 4
+    pieces = len(down_pieces)
+    size = features // pieces
+    units = down_pieces[0].shape[0]
+
+    def kernel(*refs):
+        left_ref = refs[0]
+        act_ref, slope_ref, out = refs[1 + pieces :]
+        grad = None
+        for r in range(pieces):
+            term = dot_back(left_ref[:, r * size : (r + 1) * size], refs[1 + r][...])
+            grad = term if grad is None else grad + term
+        out[:, :units] = (grad * slope_ref[...].astype(f32)).astype(bf16)
+        out[:, units:] = (grad * act_ref[...].astype(f32)).astype(bf16)
+
+    block = pl.BlockSpec((rows, units), lambda g: (g, 0))
+    return call(
+        kernel,
+        "gated_backward",
+        (4,),
+        [pl.BlockSpec((rows, features), lambda g: (g, 0))]
+        + [fixed(w.shape) for w in down_pieces]
+        + [block] * 2,
+        pl.BlockSpec((rows, 2 * units), lambda g: (g, 0)),
+        jax.ShapeDtypeStruct((total, 2 * units), bf16),
+    )(left, *down_pieces, act, slope)
+
+
+def normalize(values, gain):
+    total, features = values.shape
+
+    def kernel(value_ref, gain_ref, out_ref):
+        def step(c, carry):
+            at = pl.ds(pl.multiple_of(c * 16, 16), 16)
+            value = value_ref[at, :].astype(f32)
+            scale = lax.rsqrt(jnp.mean(value * value, axis=1, keepdims=True) + epsilon)
+            out_ref[at, :] = (value * scale * gain_ref[...]).astype(bf16)
+            return carry
+
+        lax.fori_loop(0, value_ref.shape[0] // 16, step, 0)
+
+    block = pl.BlockSpec((total // 4, features), lambda g: (g, 0))
+    return call(
+        kernel,
+        "normalize",
+        (4,),
+        [block, fixed((1, features))],
+        block,
+        jax.ShapeDtypeStruct((total, features), bf16),
+    )(values, gain.reshape(1, features))
+
+
+def move_columns(blocks, order, size):
+    rows, features = blocks[0].shape
+    groups = features // size
+
+    def kernel(order_ref, *refs):
+        out = refs[-1]
+        for r in range(groups):
+            start = pl.multiple_of(order_ref[r] * size, size)
+            for j, ref in enumerate(refs[:-1]):
+                out[j * rows : (j + 1) * rows, r * size : (r + 1) * size] = ref[
+                    :, pl.ds(start, size)
+                ]
+
+    return pl.pallas_call(
+        kernel,
+        grid_spec=pltpu.PrefetchScalarGridSpec(
+            num_scalar_prefetch=1,
+            grid=(1,),
+            in_specs=[fixed((rows, features))] * len(blocks),
+            out_specs=fixed((rows * len(blocks), features)),
+        ),
+        out_shape=jax.ShapeDtypeStruct((rows * len(blocks), features), blocks[0].dtype),
+        compiler_params=pltpu.CompilerParams(vmem_limit_bytes=vmem_bytes),
+        cost_estimate=light,
+        name="move_columns",
+    )(order, *blocks)
 
 
 class Ring:
@@ -365,44 +575,23 @@
         order = list(range(0, count, 2)) + list(range(1, count, 2))[::-1]
         self.order = order
         self.place_of = [order.index(index) for index in range(count)]
-        self.ahead = [(order[(i + 1) % count], order[i]) for i in range(count)]
-        self.behind = [(order[i], order[(i + 1) % count]) for i in range(count)]
-        self.place = jnp.asarray(self.place_of, jnp.int32)[lax.axis_index("dp")]
-
-    def reach(self, far):
-        return self.count // 2 if far else (self.count - 1) // 2
-
-    def gather(self, own, far):
-        count = self.count
-        blocks = [own] + [None] * (count - 1)
-        reach = self.reach(far)
-        for r in range(1, count):
-            if r <= reach:
-                blocks[r] = lax.ppermute(blocks[r - 1], "dp", self.ahead)
-            if r <= count - 1 - reach:
-                blocks[count - r] = lax.ppermute(blocks[(count - r + 1) % count], "dp", self.behind)
-        return blocks
-
-    def scatter(self, part, far):
-        count = self.count
-        reach = self.reach(far)
-        steps = max(reach, count - 1 - reach)
-        right = left = None
-        right_sum = left_sum = None
-        for r in range(steps, 0, -1):
-            if r <= reach:
-                value = part(r)
-                if right is not None:
-                    value = value + right.astype(f32)
-                right = lax.ppermute(value.astype(bf16), "dp", self.behind)
-            if r <= count - 1 - reach:
-                value = part(count - r)
-                if left is not None:
-                    value = value + left.astype(f32)
-                left = lax.ppermute(value.astype(bf16), "dp", self.ahead)
-        return part(0) + right.astype(f32) + left.astype(f32)
-
-    def scatter_direct(self, blocks):
+        ahead = [(order[(i + 1) % count], order[i]) for i in range(count)]
+        behind = [(order[i], order[(i + 1) % count]) for i in range(count)]
+        self.pairs = (ahead, behind)
+        index = lax.axis_index("dp")
+        half = (count + 1) // 2
+        self.place = jnp.where(
+            lax.rem(index, 2) == 0, lax.div(index, 2), count - 1 - lax.div(index, 2)
+        ).astype(jnp.int32)
+        spots = lax.rem(jnp.arange(count, dtype=jnp.int32) + self.place, count)
+        self.block_of = jnp.where(spots < half, 2 * spots, 2 * (count - 1 - spots) + 1)
+        self.step_of = self.steps_to(jnp.arange(count, dtype=jnp.int32))
+
+    def steps_to(self, index):
+        places = jnp.where(index % 2 == 0, index // 2, self.count - 1 - index // 2)
+        return (places - self.place + self.count) % self.count
+
+    def direct(self, blocks):
         total = blocks[0]
         for r in range(1, self.count):
             pairs = [
@@ -411,27 +600,152 @@
             total = total + lax.ppermute(blocks[r], "dp", pairs)
         return total
 
-    def from_whole(self, whole, axis, size):
-        ordered = [lax.slice_in_dim(whole, i * size, (i + 1) * size, axis=axis) for i in self.order]
+    def columns_in(self, blocks, size):
+        if size % 128 == 0:
+            return move_columns(blocks, self.block_of, size)
+        whole = jnp.concatenate(blocks, axis=0)
+        ordered = [whole[:, i * size : (i + 1) * size] for i in self.order]
         return lax.dynamic_slice_in_dim(
-            jnp.concatenate(ordered + ordered, axis=axis),
+            jnp.concatenate(ordered + ordered, axis=1),
             self.place * size,
             self.count * size,
-            axis=axis,
+            axis=1,
         )
 
-    def to_whole(self, ringed, axis, size):
+    def columns_out(self, whole, size):
+        if size % 128 == 0:
+            return move_columns([whole], self.step_of, size)
         start = lax.rem(self.count - self.place, self.count) * size
         ordered = lax.dynamic_slice_in_dim(
-            jnp.concatenate([ringed, ringed], axis=axis), start, self.count * size, axis=axis
+            jnp.concatenate([whole, whole], axis=1), start, self.count * size, axis=1
         )
         return jnp.concatenate(
-            [
-                lax.slice_in_dim(ordered, i * size, (i + 1) * size, axis=axis)
-                for i in self.place_of
-            ],
-            axis=axis,
+            [ordered[:, i * size : (i + 1) * size] for i in self.place_of], axis=1
         )
+
+
+class Gather:
+    work = 0.0
+
+    def __init__(self, ring, own, far, axis):
+        count = ring.count
+        reach = count // 2 if far else (count - 1) // 2
+        self.total = count
+        self.hops = (reach, count - 1 - reach)
+        self.left = count - 1
+        self.blocks = [own] + [None] * (count - 1)
+        self.axis = axis
+
+    def receive(self, way, hop, value):
+        self.blocks[hop + 1 if way == 0 else self.total - 1 - hop] = value
+        self.left -= 1
+
+    def operand(self, way, hop, gate):
+        return self.blocks[hop if way == 0 else (self.total - hop) % self.total]
+
+    def pieces(self):
+        if self.blocks[0].shape[self.axis] % 128 == 0:
+            return self.blocks
+        return [jnp.concatenate(self.blocks, axis=self.axis)]
+
+
+class Scatter:
+    work = 2.0
+
+    def __init__(self, ring, part, far):
+        count = ring.count
+        reach = count // 2 if far else (count - 1) // 2
+        self.total = count
+        self.hops = (count - 1 - reach, reach)
+        self.left = count - 1
+        self.part = part
+        self.got = [None, None]
+
+    def receive(self, way, hop, value):
+        self.got[way] = value
+        self.left -= 1
+
+    def operand(self, way, hop, gate):
+        distance = self.hops[way] - hop
+        value = self.part(distance if way == 1 else self.total - distance)
+        if hop:
+            (got,) = gate(self.got[way])
+            value = value + got.astype(f32)
+        return value.astype(bf16)
+
+    def result(self, gate):
+        got = gate(*self.got)
+        return self.part(0) + got[0].astype(f32) + got[1].astype(f32)
+
+
+class Lanes:
+    def __init__(self, ring, depth):
+        self.ring = ring
+        self.depth = depth
+        self.queue = ([], [])
+        self.flying = ([], [])
+        self.link = [0.0, 0.0]
+        self.now = 0.0
+        self.marks = []
+
+    def gate(self, *values):
+        if not self.marks:
+            return values
+        return lax.optimization_barrier(tuple(values) + tuple(self.marks))[: len(values)]
+
+    def mark(self, *values):
+        self.marks = list(values)
+
+    def add(self, *chains):
+        for chain in chains:
+            for way in range(2):
+                if chain.hops[way]:
+                    self.queue[way].append(chain)
+        self.fill()
+
+    def start(self, way, chain, hop):
+        (operand,) = self.gate(chain.operand(way, hop, self.gate))
+        self.mark(operand)
+        self.now += chain.work + 1.5
+        value = lax.ppermute(operand, "dp", self.ring.pairs[way])
+        begin = max(self.now, self.link[way])
+        self.link[way] = begin + operand.size / 22000.0
+        self.flying[way].append((self.link[way] + 3.0, chain, hop, value))
+
+    def fill(self):
+        for way in range(2):
+            while self.queue[way] and len(self.flying[way]) < self.depth:
+                self.start(way, self.queue[way].pop(0), 0)
+
+    def step(self, limit):
+        heads = [(self.flying[way][0][0], way) for way in range(2) if self.flying[way]]
+        if not heads or min(heads)[0] > limit:
+            return False
+        finish, way = min(heads)
+        _, chain, hop, value = self.flying[way].pop(0)
+        self.now = max(self.now, finish)
+        chain.receive(way, hop, value)
+        if hop + 1 < chain.hops[way]:
+            self.start(way, chain, hop + 1)
+        else:
+            self.mark(value, *self.marks)
+        self.fill()
+        return True
+
+    def catch_up(self, time=None):
+        time = self.now if time is None else time
+        while self.step(time):
+            time = max(time, self.now)
+        self.now = max(self.now, time)
+
+    def until(self, *chains):
+        while any(chain.left for chain in chains):
+            assert self.step(float("inf"))
+
+    def did(self, time, *values):
+        self.mark(*values)
+        self.now += time
+        self.catch_up()
 
 
 core_pairs = [(0, 1), (1, 0), (2, 3), (3, 2)]
@@ -439,17 +753,23 @@
 
 
 def tensor_gather(own):
+    across = lax.ppermute(own, "tensor", chip_pairs)
     sibling = lax.ppermute(own, "tensor", core_pairs)
-    across = lax.ppermute(own, "tensor", chip_pairs)
     far = lax.ppermute(across, "tensor", core_pairs)
-    return jnp.concatenate([own, sibling, across, far], axis=0)
-
-
-def tensor_scatter(part):
-    far = lax.ppermute(part(3).astype(bf16), "tensor", core_pairs)
-    across = lax.ppermute((part(2) + far.astype(f32)).astype(bf16), "tensor", chip_pairs)
-    sibling = lax.ppermute(part(1).astype(bf16), "tensor", core_pairs)
-    return part(0) + sibling.astype(f32) + across.astype(f32)
+    return [own, sibling, across, far]
+
+
+def tensor_scatter(blocks):
+    own, sibling, across, far = blocks
+    far = lax.ppermute(far, "tensor", core_pairs)
+    sibling = lax.ppermute(sibling, "tensor", core_pairs)
+    across = (across.astype(f32) + far.astype(f32)).astype(bf16)
+    return own, sibling, across, lax.ppermute(across, "tensor", chip_pairs)
+
+
+def summed(parts):
+    own, sibling, _, across = parts
+    return own.astype(f32) + sibling.astype(f32) + across.astype(f32)
 
 
 def tensor_sum(value):
@@ -457,9 +777,8 @@
     return value + lax.ppermute(value, "tensor", chip_pairs)
 
 
-def norm_forward(values, gain):
-    scale = lax.rsqrt(jnp.mean(values * values, axis=-1, keepdims=True) + epsilon)
-    return scale, values * scale * gain
+def row_scale(values):
+    return lax.rsqrt(jnp.mean(values * values, axis=-1, keepdims=True) + epsilon)
 
 
 def norm_backward(values, scale, gain, grad):
@@ -493,12 +812,13 @@
     tensor,
 ):
     ring = Ring(dp)
+    lanes = Lanes(ring, 2)
     shard, width = branch_weight.shape
     features = inputs.shape[1]
-    rows = inputs.shape[0]
     length = segment_ids.shape[0]
     gate_blocks, piece, block_width = rate_weight.shape
     taps = conv_weight.shape[0]
+    units = gate_weight.shape[1]
     place = lax.axis_index("tensor").astype(jnp.int32).reshape(1)
 
     columns = jnp.stack(
@@ -516,34 +836,6 @@
     )
     table = jnp.pad(table, ((0, high - table_rows - 2), (0, 0)))
 
-    tables = jnp.stack(ring.gather(table, True))
-    gain_one = tables[:, table_rows, :shard].reshape(features).astype(f32)
-    gain_two = tables[:, table_rows + 1, :shard].reshape(features).astype(f32)
-    whole_table = ring.to_whole(tables[:, :table_rows], 0, 1)
-    whole_table = (
-        whole_table.reshape(dp, gate_blocks, piece, wide)
-        .transpose(1, 0, 2, 3)
-        .reshape(width, wide)
-    )
-    channel_block = jnp.arange(width) // block_width
-    same_block = channel_block[:, None] == channel_block[None, :]
-
-    def spread(weights):
-        return jnp.where(same_block, jnp.tile(weights, (1, gate_blocks)), jnp.zeros((), bf16))
-
-    gates = jnp.concatenate(
-        [
-            spread(whole_table[:, :block_width]),
-            spread(whole_table[:, block_width : 2 * block_width]),
-        ],
-        axis=1,
-    )
-    small = whole_table[:, 2 * block_width : 2 * block_width + 8].astype(f32).T
-    decay_full = small[7]
-    small = jnp.concatenate(
-        [small[:7], -lru_scale * jax.nn.softplus(-decay_full)[None]], axis=0
-    )
-
     masks = []
     for offset in range(1, taps):
         earlier = jnp.concatenate(
@@ -553,100 +845,214 @@
     masks = jnp.stack([masks[0]] + masks, axis=1)
     masks = jnp.pad(masks, ((0, 0), (0, 128 - taps)))
 
-    tokens = ring.from_whole(inputs, 1, shard).astype(f32)
-    cotangent_own = ring.from_whole(cotangent, 1, shard)
-    scale_one, mixer_in = norm_forward(tokens, gain_one)
-    mixer_rows = tensor_gather(mixer_in.astype(bf16))
-    pair_weight = jnp.concatenate(
-        [
-            jnp.concatenate(ring.gather(branch_weight, True), axis=0),
-            jnp.concatenate(ring.gather(input_weight, False), axis=0),
-        ],
-        axis=1,
-    )
-    pre = dot(mixer_rows, pair_weight)
-    mixer_low, mixed, rate, entry, state = core_forward(
-        place, pre, masks, gates, small, tensor
-    )
-    output_full = jnp.concatenate(ring.gather(output_weight, True), axis=1)
-
-    def block(array, j):
-        return lax.slice_in_dim(array, j * rows, (j + 1) * rows, axis=0)
-
-    middle = tokens + tensor_scatter(lambda j: dot(block(mixer_low, j), output_full))
-    scale_two, mlp_in = norm_forward(middle, gain_two)
-    mlp_rows = tensor_gather(mlp_in.astype(bf16))
-    cotangent_rows = tensor_gather(cotangent_own)
-
-    gate_full = jnp.concatenate(ring.gather(gate_weight, True), axis=0)
-    up_full = jnp.concatenate(ring.gather(up_weight, False), axis=0)
-    down_full = jnp.concatenate(ring.gather(down_weight, False), axis=1)
-    gate_pre = dot(mlp_rows, gate_full)
-    up_pre = dot(mlp_rows, up_full)
-    act, act_slope = gelu_both(gate_pre)
-    hidden_low = (act * up_pre).astype(bf16)
+    half = units // 2
+    halves = (slice(0, half), slice(half, units))
+    small_chain = Gather(ring, table, True, 0)
+    pair_chain = Gather(ring, jnp.concatenate([branch_weight, input_weight], axis=1), False, 0)
+    output_chain = Gather(ring, output_weight, True, 1)
+    gated_chains = [
+        Gather(
+            ring,
+            jnp.concatenate([gate_weight[:, at], up_weight[:, at]], axis=1),
+            at.start == 0,
+            0,
+        )
+        for at in halves
+    ]
+    down_chains = [Gather(ring, down_weight[at], at.start == 0, 1) for at in halves]
+    input_blocks = tensor_gather(inputs)
+    lanes.add(pair_chain, small_chain, output_chain, *gated_chains, *down_chains)
+    lanes.catch_up(12.0)
+    cotangent_blocks = tensor_gather(cotangent)
+
+    lanes.until(small_chain)
+    tables = jnp.concatenate(small_chain.blocks, axis=0)
+    (tables,) = lanes.gate(tables)
+    by_block = tables.reshape(dp, high, wide)
+    gain_one = by_block[:, table_rows, :shard].reshape(features).astype(f32)
+    gain_two = by_block[:, table_rows + 1, :shard].reshape(features).astype(f32)
+    channel = jnp.arange(width)
+    owner = (channel % block_width) // piece
+    source = ring.steps_to(owner) * high + (channel // block_width) * piece + channel % piece
+    mover = (source[:, None] == jnp.arange(dp * high)[None, :]).astype(bf16)
+    whole_table = dot(mover, tables).astype(bf16)
+    gate_column = jnp.arange(2 * width)
+    picked = (gate_column // width) * block_width + gate_column % block_width
+    spreader = (jnp.arange(wide)[:, None] == picked[None, :]).astype(bf16)
+    same_block = (channel // block_width)[:, None] == (
+        (gate_column % width) // block_width
+    )[None, :]
+    gates = jnp.where(same_block, dot(whole_table, spreader), 0.0).astype(bf16)
+    picker = (jnp.arange(wide)[None, :] == (2 * block_width + jnp.arange(8))[:, None]).astype(bf16)
+    small = dot_back(picker, whole_table)
+    decay_full = small[7:8]
+    small = jnp.concatenate([small[:7], -lru_scale * jax.nn.softplus(-decay_full)], axis=0)
+
+    token_rows = ring.columns_in(input_blocks, shard)
+    mixer_rows = normalize(token_rows, gain_one)
+    rows = inputs.shape[0]
+    lanes.did(25.0, mixer_rows, gates, small)
+    lanes.until(pair_chain)
+    (mixer_rows,) = lanes.gate(mixer_rows)
+    pre = collect(mixer_rows, [pair_chain.pieces()], False, "mixer_in")
+    lanes.did(11.0, pre)
+    (pre,) = lanes.gate(pre)
+    mixer_low, mixed, rate, entry, state = core_forward(place, pre, masks, gates, small, tensor)
+    lanes.did(21.0, mixer_low)
+    lanes.until(output_chain)
+    output_pieces = output_chain.pieces()
+    (mixer_low,) = lanes.gate(mixer_low)
+    blocks = spread([(mixer_low, 0)], [output_pieces], 3, 4, False, "mixer_out")[::-1]
+    parts = tensor_scatter(blocks)
+    lanes.did(11.0, parts[2])
+    arrival = lanes.now + 26.0
+    (moved,) = lanes.gate(cotangent_blocks[0])
+    cotangent_rows = ring.columns_in([moved] + cotangent_blocks[1:], shard)
+    lanes.did(5.0, cotangent_rows)
+    lanes.catch_up(arrival)
+    parts = lanes.gate(*parts)
+    tokens = token_rows[:rows].astype(f32)
+    middle = tokens + summed(parts)
+    scale_two = row_scale(middle)
+    mlp_blocks = tensor_gather((middle * scale_two * gain_two).astype(bf16))
+    lanes.did(5.0, mlp_blocks[0])
+    lanes.catch_up(lanes.now + 28.0)
+    mlp_blocks = lanes.gate(*mlp_blocks)
+    mlp_rows = jnp.concatenate(mlp_blocks, axis=0)
+    lanes.did(5.0, mlp_rows)
 
     def columns_of(array, r):
         return lax.slice_in_dim(array, r * shard, (r + 1) * shard, axis=1)
 
-    down_grad = ring.scatter(lambda r: dot_rows(hidden_low, columns_of(cotangent_rows, r)), False)
-    hidden_grad = dot_back(cotangent_rows, down_full)
-    gate_low = (hidden_grad * up_pre * act_slope).astype(bf16)
-    up_low = (hidden_grad * act).astype(bf16)
-    mlp_in_grad = tensor_scatter(
-        lambda j: dot_back(block(gate_low, j), gate_full) + dot_back(block(up_low, j), up_full)
-    )
-    gate_wgrad = ring.scatter(lambda r: dot_rows(columns_of(mlp_rows, r), gate_low), True)
-    up_wgrad = ring.scatter(lambda r: dot_rows(columns_of(mlp_rows, r), up_low), False)
-    middle_norm_grad, gain_two_part = norm_backward(middle, scale_two, gain_two, mlp_in_grad)
-    middle_grad = cotangent_own.astype(f32) + middle_norm_grad
-    residual_rows = tensor_gather(middle_grad.astype(bf16))
-
-    mixer_grad = dot_back(residual_rows, output_full)
+    hidden, acts, slopes, down_scatters = [], [], [], []
+    for h in range(2):
+        lanes.until(gated_chains[h])
+        (gated,) = lanes.gate(mlp_rows)
+        one, two, three = gated_forward(gated, gated_chains[h].pieces())
+        hidden.append(one)
+        acts.append(two)
+        slopes.append(three)
+        down_scatters.append(
+            Scatter(
+                ring,
+                lambda r, one=one: dot_rows(one, columns_of(cotangent_rows, r)),
+                h == 1,
+            )
+        )
+        lanes.did(12.0, one)
+    lanes.add(*down_scatters)
+    gated_lows, gated_scatters = [], []
+    for h in range(2):
+        lanes.until(down_chains[h])
+        (gated,) = lanes.gate(cotangent_rows)
+        low = gated_backward(gated, down_chains[h].pieces(), acts[h], slopes[h])
+        gated_lows.append(low)
+        gated_scatters.append(
+            Scatter(
+                ring,
+                lambda r, low=low: dot_rows(columns_of(mlp_rows, r), low),
+                h == 0,
+            )
+        )
+        lanes.did(8.5, low)
+    lanes.add(*gated_scatters)
+    weights = [chain.pieces() for chain in gated_chains]
+
+    def lefts():
+        return [(low, 0) for low in lanes.gate(*gated_lows)]
+
+    far, across = spread(lefts(), weights, 3, 2, True, "mlp_in_grad")
+    lanes.did(14.0, far)
+    sibling, own = spread(lefts(), weights, 1, 2, True, "mlp_in_grad")
+    parts = tensor_scatter([own, sibling, across, far])
+    lanes.did(14.0, own)
+    lanes.catch_up(lanes.now + 28.0)
+    parts = lanes.gate(*parts)
+    middle_norm_grad, gain_two_part = norm_backward(middle, scale_two, gain_two, summed(parts))
+    middle_grad = (
+        lax.slice_in_dim(cotangent_rows, 0, rows, axis=0).astype(f32) + middle_norm_grad
+    )
+    residual_blocks = tensor_gather(middle_grad.astype(bf16))
+    lanes.did(5.0, residual_blocks[0])
+    lanes.catch_up(lanes.now + 26.0)
+    residual_blocks = lanes.gate(*residual_blocks)
+    residual_rows = jnp.concatenate(residual_blocks, axis=0)
+    lanes.did(5.0, residual_rows)
+
+    (residual_rows,) = lanes.gate(residual_rows)
+    mixer_grad = collect(residual_rows, [output_pieces], True, "mixer_grad")
+    lanes.did(8.0, mixer_grad)
+    (mixer_grad,) = lanes.gate(mixer_grad)
     pair_low, gate_grads, small_grads = core_backward(
         place, mixer_grad, pre, mixed, rate, entry, state, masks, gates, small, tensor
     )
-    mixer_in_grad = tensor_scatter(lambda j: dot_back(block(pair_low, j), pair_weight))
-    output_wgrad = ring.scatter(lambda r: dot_rows(mixer_low, columns_of(residual_rows, r)), True)
-    branch_low = pair_low[:, :width]
-    entry_low = pair_low[:, width:]
-    branch_wgrad = ring.scatter(lambda r: dot_rows(columns_of(mixer_rows, r), branch_low), True)
-    input_wgrad = ring.scatter(lambda r: dot_rows(columns_of(mixer_rows, r), entry_low), False)
-
-    def folded(grads):
-        kept = jnp.where(same_block, grads, 0.0).reshape(width, gate_blocks, block_width)
-        return jnp.sum(kept, axis=1)
-
-    decay_grad = lru_scale * small_grads[7:8] * jax.nn.sigmoid(-decay_full)[None]
-    small_columns = jnp.concatenate([small_grads[:7], decay_grad], axis=0).T
-    grad_table = jnp.concatenate(
-        [folded(gate_grads[:, :width]), folded(gate_grads[:, width:]), small_columns], axis=1
-    ).astype(bf16)
-    grad_table = jnp.pad(grad_table, ((0, 0), (0, wide - table_columns)))
-    grad_table = (
-        grad_table.reshape(gate_blocks, dp, piece, wide)
-        .transpose(1, 0, 2, 3)
-        .reshape(dp, table_rows, wide)
-    )
-    grad_tables = ring.from_whole(grad_table, 0, 1)
-    table_grad = ring.scatter(lambda r: grad_tables[r].astype(f32), True)
-    table_grad = table_grad.reshape(gate_blocks, piece, wide)
+    lanes.did(28.0, pair_low)
+    output_scatter = Scatter(
+        ring, lambda r: dot_rows(mixer_low, columns_of(residual_rows, r)), True
+    )
+    whole_low = pair_low
+    pair_scatter = Scatter(ring, lambda r: dot_rows(columns_of(mixer_rows, r), whole_low), False)
+    lanes.add(output_scatter, pair_scatter)
+    (pair_low,) = lanes.gate(pair_low)
+    blocks = spread([(pair_low, 0)], [pair_chain.pieces()], 3, 4, True, "mixer_in_grad")[::-1]
+    parts = tensor_scatter(blocks)
+    lanes.did(14.0, parts[2])
+    arrival = lanes.now + 26.0
+
+    (gate_grads,) = lanes.gate(gate_grads)
+    decay_grad = lru_scale * small_grads[7:8] * jax.nn.sigmoid(-decay_full)
+    small_grads = jnp.concatenate([small_grads[:7], decay_grad], axis=0).astype(bf16)
+    grad_table = dot_back(
+        jnp.where(same_block, gate_grads, 0.0).astype(bf16), spreader
+    ) + dot_rows(small_grads, picker)
+    grad_tables = dot_rows(mover, grad_table.astype(bf16)).astype(bf16)
+    table_scatter = Scatter(
+        ring,
+        lambda r: lax.slice_in_dim(grad_tables, r * high, (r + 1) * high, axis=0).astype(f32),
+        True,
+    )
+    lanes.did(12.0, grad_tables)
+    lanes.add(table_scatter)
+    lanes.catch_up(arrival)
+    parts = lanes.gate(*parts)
+    tokens_norm_grad, gain_one_part = norm_backward(tokens, row_scale(tokens), gain_one, summed(parts))
+    inputs_grad = ring.columns_out((middle_grad + tokens_norm_grad).astype(bf16), shard)
+    gain_parts = tensor_sum(jnp.stack([gain_one_part, gain_two_part]))
+    gain_sums = ring.direct([columns_of(gain_parts, r) for r in range(dp)])
+    lanes.did(8.0, inputs_grad)
+
+    late = lanes.gate(*hidden)
+    blocks = spread(
+        [(low, 0) for low in late],
+        [chain.pieces() for chain in down_chains],
+        3,
+        4,
+        False,
+        "mlp_out",
+    )[::-1]
+    parts = tensor_scatter(blocks)
+    lanes.did(14.0, parts[2])
+    lanes.catch_up(lanes.now + 26.0)
+    parts = lanes.gate(*parts)
+    layer_out = ring.columns_out((middle + summed(parts)).astype(bf16), shard)
+    lanes.did(5.0, layer_out)
+    lanes.until(
+        *down_scatters, *gated_scatters, output_scatter, pair_scatter, table_scatter
+    )
+
+    free = lambda *values: values
+    table_grad = table_scatter.result(free)[:table_rows].reshape(gate_blocks, piece, wide)
     rate_wgrad = table_grad[:, :, :block_width]
     entry_wgrad = table_grad[:, :, block_width : 2 * block_width]
     singles = [table_grad[:, :, 2 * block_width + k] for k in range(taps + 4)]
-
-    mlp_sum = tensor_scatter(lambda j: dot(block(hidden_low, j), down_full))
-    layer_out = ring.to_whole((middle + mlp_sum).astype(bf16), 1, shard)
-    tokens_norm_grad, gain_one_part = norm_backward(tokens, scale_one, gain_one, mixer_in_grad)
-    inputs_grad = ring.to_whole((middle_grad + tokens_norm_grad).astype(bf16), 1, shard)
-    gain_parts = tensor_sum(jnp.stack([gain_one_part, gain_two_part]))
-    gain_sums = ring.scatter_direct([columns_of(gain_parts, r) for r in range(dp)])
+    pair_wgrad = pair_scatter.result(free)
+    gated_wgrads = [scatter.result(free) for scatter in gated_scatters]
     return (
         layer_out,
         inputs_grad,
         gain_sums[0],
-        branch_wgrad,
-        input_wgrad,
+        pair_wgrad[:, :width],
+        pair_wgrad[:, width:],
         jnp.stack(singles[:taps]),
         singles[taps],
         rate_wgrad,
@@ -654,11 +1060,11 @@
         entry_wgrad,
         singles[taps + 2],
         singles[taps + 3],
-        output_wgrad,
+        output_scatter.result(free),
         gain_sums[1],
-        gate_wgrad,
-        up_wgrad,
-        down_grad,
+        jnp.concatenate([wgrad[:, :half] for wgrad in gated_wgrads], axis=1),
+        jnp.concatenate([wgrad[:, half:] for wgrad in gated_wgrads], axis=1),
+        jnp.concatenate([scatter.result(free) for scatter in down_scatters], axis=0),
     )
 
 

time: 929 us -> 787 us (0.85)
  Pallas kernels: 49.5 us -> 196 us
  local copies, waits for them, and re-layouts: 135 us -> 27.2 us
  matrix products: 209 us -> 105 us
  waiting for transfers between devices: 357 us -> 277 us
  other arithmetic: 27 us -> 38.9 us
    pallas_call x0 -> x16, Pallas kernels: none -> 146 us  [the longest x5 59.2 us: spread(): call(kernel, name, (count,), [left_spec(width, column) for width, (_, col...]
    ppermute x117, waiting for transfers between devices: 351 us -> 255 us  [the longest x98 236 us: start(): value = lax.ppermute(operand, 'dp', self.ring.pairs[way])]
    unnamed x308 -> x221, local copies, waits for them, and re-layouts: 84.9 us -> 10.4 us
    dot_general x14 -> x2, matrix products: 67.7 us -> 2.27 us  [dot_back(): lax.dot_general(left, right, (((1,), (1,)), ((), ())), preferred_element_...]
    dot_general x11 -> x2, matrix products: 65.2 us -> 2.95 us  [dot(): return jnp.dot(left, right, preferred_element_type=f32)]
    dot_general x48 -> x49, matrix products: 76.5 us -> 99.9 us  [dot_rows(): lax.dot_general(left, right, (((0,), (0,)), ((), ())), preferred_element_...]
    ppermute x4, waiting for transfers between devices: 2.65 us -> 21.4 us  [tensor_gather(): across = lax.ppermute(own, 'tensor', chip_pairs)]
    convert_element_type x8 -> x18, other arithmetic: 5.58 us -> 18.2 us  [the longest x4 6.93 us: tensor_scatter(): across = (across.astype(f32) + far.astype(f32)).astype(bf16)]
  transfers between devices with their start and end apart: 131 -> 131, of which waited for: 54 -> 49; matrix products, arithmetic and copies ran while one was open for 25% -> 20% of each run, Pallas kernels for 2% -> 23%
where the time goes in v2:
time: 787 us; the launch traced here: 777 us
  waiting for transfers between devices  277 us (35%)
  Pallas kernels  196 us (25%)
  starting transfers between devices  130 us (17%)
  matrix products  105 us (13%)
  other arithmetic  38.9 us (5%)
  local copies, waits for them, and re-layouts  27.2 us (3%)
    ppermute x98, waiting for transfers between devices, start(): value = lax.ppermute(operand, 'dp', self.ring.pairs[way])  236 us
    ppermute x98, starting transfers between devices, start(): value = lax.ppermute(operand, 'dp', self.ring.pairs[way])  107 us
    dot_general x49, matrix products, dot_rows(): lax.dot_general(left, right, (((0,), (0,)), ((), ())), preferred_element_...  99.9 us
    pallas_call x5, Pallas kernels, spread(): call(kernel, name, (count,), [left_spec(width, column) for width, (_, col...  59.2 us
    pallas_call x1, Pallas kernels, core_backward(): pl.pallas_call(core_backward_kernel, grid_spec=pltpu.PrefetchScalarGridSp...  28.5 us
    pallas_call x2, Pallas kernels, gated_forward(): call(kernel, 'gated_forward', (4,), [pl.BlockSpec((rows, features), lambd...  25.8 us
    ppermute x4, waiting for transfers between devices, tensor_gather(): across = lax.ppermute(own, 'tensor', chip_pairs)  21.4 us
    pallas_call x1, Pallas kernels, core_forward(): pl.pallas_call(core_forward_kernel, grid_spec=pltpu.PrefetchScalarGridSpe...  20.9 us
  transfers between devices with their start and end apart: 131, of which 49 were waited for; matrix products, arithmetic and copies ran while one was open for 20% of the time, Pallas kernels for 23%

profile of v2, /device:TPU:0, one launch (start us, length us, event | category | flops | bytes accessed | tf_op | source)
XLA Modules:
  0.0 776.8 jit_solution(18379726358235086899)
XLA Ops:
  17.3 4.0 collective-permute-done.4.refs_2_
  23.3 7.4 collective-permute-done.8.refs_8_
  39.3 6.3 collective-permute-done.12.refs_7_
  48.5 12.9 %collective-permute-done.11 = bf16[96,384]{1,0:T(8,128)(2,1)S(1)} collective-permute-done((bf16[96,384]{1,0:T(8,128)(2,1)S(1)}, bf16[96,384]{1,0:T(8,128)(2,1)S(1)}, u32[]{:S(2)}, u32[]{:S(2)}) %collective-permute-start.11) | collective-permute-done | bytes 73760 | tf_op jit(solution)/shard_map/ppermute | solution.py:710
  72.6 5.6 move_columns.4.value_ref
  83.4 9.6 %normalize.1.refs_0_ = bf16[1024,2048]{1,0:T(8,128)(2,1)} custom-call(bf16[1024,2048]{1,0:T(8,128)(2,1)} %move_columns.4.value_ref, f32[1,2048]{1,0:T(1,128)} %bitcast.68), custom_call_target="tpu_custom_call" | custom-call | flops 1000 | bytes 1000 | tf_op jit(solution)/shard_map/normalize/pallas_call | solution.py:534
  95.5 7.5 collective-permute-done.17.refs_2_.refs_3_
  108.7 10.3 %mixer_in.1.branch.entry_pre.entry_tail = f32[1024,1280]{1,0:T(8,128)} custom-call(bf16[1024,2048]{1,0:T(8,128)(2,1)} %normalize.1.refs_0_, bf16[256,1280]{1,0:T(8,128)(2,1)} %copy-done.34, bf16[256,1280]{1,0:T(8,128)(2,1)} %copy-done.38, bf16[256,1280]{1,0:T(8,128)(2,1)} %copy-done.40, bf16[256,1280]{1,0:T(8,128)(2,1)} %copy-done.41, ...), custom_call_target="tpu_custom_call" | custom-call | flops 1000 | bytes 1000 | tf_op jit(solution)/shard_map/mixer_in/pallas_call | solution.py:442
  119.0 3.8 collective-permute-done.21.refs_4_
  123.5 20.9 %core_forward.1 = (bf16[1024,640]{1,0:T(8,128)(2,1)}, f32[1024,640]{1,0:T(8,128)}, f32[1024,640]{1,0:T(8,128)}, f32[1024,640]{1,0:T(8,128)}, f32[1024,640]{1,0:T(8,128)}) custom-call(s32[1]{0:T(128)} %bitcast.place, f32[1024,1280]{1,0:T(8,128)} %mixer_in.1.branch.entry_pre.entry_tail, f32[1024,1280]{1,0:T(8,128)} %mixer_in.1.branch.entry_pre.entry_tail, ...), custom_call_target="tpu_custom_call" | custom-call | flops 1000 | bytes 1000 | tf_op jit(solution)/shard_map/core_forward/pallas_call | solution.py:260
  150.2 13.9 %collective-permute-done.28.refs_5_ = bf16[640,256]{1,0:T(8,128)(2,1)S(1)} collective-permute-done((bf16[640,256]{1,0:T(8,128)(2,1)S(1)}, bf16[640,256]{1,0:T(8,128)(2,1)S(1)}, u32[]{:S(2)}, u32[]{:S(2)}) %collective-permute-start.28) | collective-permute-done | bytes 327712 | tf_op jit(solution)/shard_map/ppermute | solution.py:710
  165.6 8.1 %mixer_out.1 = (bf16[256,2048]{1,0:T(8,128)(2,1)}, bf16[256,2048]{1,0:T(8,128)(2,1)}, bf16[256,2048]{1,0:T(8,128)(2,1)}, bf16[256,2048]{1,0:T(8,128)(2,1)}) custom-call(bf16[1024,640]{1,0:T(8,128)(2,1)} %get-tuple-element.250.refs_0_, bf16[640,256]{1,0:T(8,128)(2,1)} %refs_1_.3, bf16[640,256]{1,0:T(8,128)(2,1)} %copy-done.59, bf16[640,256]{1,0:T(8,128)(2,1)} %copy-done.60, ...), custom_call_target="tpu_custom_call" | custom-call | flops 1000 | bytes 1000 | tf_op jit(solution)/shard_map/mixer_out/pallas_call | solution.py:408
  184.1 10.6 %collective-permute-done.35.refs_2_.refs_11_ = bf16[256,1536]{1,0:T(8,128)(2,1)S(1)} collective-permute-done((bf16[256,1536]{1,0:T(8,128)(2,1)S(1)}, bf16[256,1536]{1,0:T(8,128)(2,1)S(1)}, u32[]{:S(2)}, u32[]{:S(2)}) %collective-permute-start.35) | collective-permute-done | bytes 786464 | tf_op jit(solution)/shard_map/ppermute | solution.py:710
  195.6 5.5 move_columns.5.refs_0_
  202.4 8.7 %collective-permute-done.33.refs_5_.refs_6_ = bf16[256,1536]{1,0:T(8,128)(2,1)S(1)} collective-permute-done((bf16[256,1536]{1,0:T(8,128)(2,1)S(1)}, bf16[256,1536]{1,0:T(8,128)(2,1)S(1)}, u32[]{:S(2)}, u32[]{:S(2)}) %collective-permute-start.33) | collective-permute-done | bytes 786464 | tf_op jit(solution)/shard_map/ppermute | solution.py:710
  211.1 7.3 collective-permute-done.32.refs_8_.refs_17_
  225.1 21.4 %collective-permute-done.40 = bf16[256,2048]{1,0:T(8,128)(2,1)S(1)} collective-permute-done((bf16[256,2048]{1,0:T(8,128)(2,1)S(1)}, bf16[256,2048]{1,0:T(8,128)(2,1)S(1)}, u32[]{:S(2)}, u32[]{:S(2)}) %collective-permute-start.40) | collective-permute-done | bytes 1048608 | tf_op jit(solution)/shard_map/ppermute | solution.py:756
  248.1 10.8 %collective-permute-done.42.refs_8_.refs_9_ = bf16[768,256]{1,0:T(8,128)(2,1)S(1)} collective-permute-done((bf16[768,256]{1,0:T(8,128)(2,1)S(1)}, bf16[768,256]{1,0:T(8,128)(2,1)S(1)}, u32[]{:S(2)}, u32[]{:S(2)}) %collective-permute-start.42) | collective-permute-done | bytes 393248 | tf_op jit(solution)/shard_map/ppermute | solution.py:710
  260.9 8.8 %collective-permute-done.45.refs_2_.refs_3_ = bf16[768,256]{1,0:T(8,128)(2,1)} collective-permute-done((bf16[768,256]{1,0:T(8,128)(2,1)S(1)}, bf16[768,256]{1,0:T(8,128)(2,1)}, u32[]{:S(2)}, u32[]{:S(2)}) %collective-permute-start.45) | collective-permute-done | bytes 393248 | tf_op jit(solution)/shard_map/ppermute | solution.py:710
  271.3 4.4 collective-permute-done.44.refs_7_.refs_16_
  277.7 6.4 collective-permute-done.43.refs_7_.refs_8_
  285.3 4.9 collective-permute-done.47.refs_4_.refs_13_
  292.7 12.9 %gated_forward.2 = (bf16[1024,768]{1,0:T(8,128)(2,1)}, bf16[1024,768]{1,0:T(8,128)(2,1)}, bf16[1024,768]{1,0:T(8,128)(2,1)}) custom-call(bf16[1024,2048]{1,0:T(8,128)(2,1)} %copy-done.14, bf16[256,1536]{1,0:T(8,128)(2,1)} %copy-done.16, bf16[256,1536]{1,0:T(8,128)(2,1)} %copy-done.19, bf16[256,1536]{1,0:T(8,128)(2,1)} %collective-permute-done.25.refs_3_.refs_4_, ...), custom_call_target="tpu_custom_call" | custom-call | flops 1000 | bytes 1000 | tf_op jit(solution)/shard_map/gated_forward/pallas_call | solution.py:480
  309.7 3.4 collective-permute-done.54.refs_6_.refs_7_
  313.1 4.9 collective-permute-done.53.refs_4_.refs_5_
  330.7 12.9 %gated_forward.3 = (bf16[1024,768]{1,0:T(8,128)(2,1)}, bf16[1024,768]{1,0:T(8,128)(2,1)}, bf16[1024,768]{1,0:T(8,128)(2,1)}) custom-call(bf16[1024,2048]{1,0:T(8,128)(2,1)} %copy-done.14, bf16[256,1536]{1,0:T(8,128)(2,1)} %copy-done.17, bf16[256,1536]{1,0:T(8,128)(2,1)} %copy-done.23, bf16[256,1536]{1,0:T(8,128)(2,1)} %copy-done.27, ...), custom_call_target="tpu_custom_call" | custom-call | flops 1000 | bytes 1000 | tf_op jit(solution)/shard_map/gated_forward/pallas_call | solution.py:480
  345.8 8.5 %gated_backward.2.refs_0_ = bf16[1024,1536]{1,0:T(8,128)(2,1)} custom-call(bf16[1024,2048]{1,0:T(8,128)(2,1)} %move_columns.5.refs_0_, bf16[768,256]{1,0:T(8,128)(2,1)} %copy-done.36, bf16[768,256]{1,0:T(8,128)(2,1)} %collective-permute-done.45.refs_2_.refs_3_, bf16[768,256]{1,0:T(8,128)(2,1)} %collective-permute-done.49.refs_3_.refs_4_, ...), custom_call_target="tpu_custom_call" | custom-call | flops 1000 | bytes 1000 | tf_op jit(solution)/shard_map/gated_backward/pallas_call | solution.py:508
  354.2 4.1 convolution_convert_fusion.4
  367.8 6.4 collective-permute-done.60
  376.9 5.7 collective-permute-done.66
  387.4 3.6 collective-permute-done.64
  396.5 8.7 %gated_backward.3.refs_1_ = bf16[1024,1536]{1,0:T(8,128)(2,1)} custom-call(bf16[1024,2048]{1,0:T(8,128)(2,1)} %move_columns.5.refs_0_, bf16[768,256]{1,0:T(8,128)(2,1)} %copy-done.35, bf16[768,256]{1,0:T(8,128)(2,1)} %collective-permute-done.51.refs_2_.refs_11_, bf16[768,256]{1,0:T(8,128)(2,1)} %copy-done.50, bf16[768,256]{1,0:T(8,128)(2,1)} %copy-done.53, ...), custom_call_target="tpu_custom_call" | custom-call | flops 1000 | bytes 1000 | tf_op jit(solution)/shard_map/gated_backward/pallas_call | solution.py:508
  414.5 13.4 %mlp_in_grad.2 = (bf16[256,2048]{1,0:T(8,128)(2,1)}, bf16[256,2048]{1,0:T(8,128)(2,1)}) custom-call(bf16[1024,1536]{1,0:T(8,128)(2,1)} %gated_backward.2.refs_0_, bf16[1024,1536]{1,0:T(8,128)(2,1)} %gated_backward.3.refs_1_, bf16[256,1536]{1,0:T(8,128)(2,1)} %copy-done.16, bf16[256,1536]{1,0:T(8,128)(2,1)} %copy-done.19, ...), custom_call_target="tpu_custom_call" | custom-call | flops 1000 | bytes 1000 | tf_op jit(solution)/shard_map/mlp_in_grad/pallas_call | solution.py:408
  441.9 13.4 %mlp_in_grad.3 = (bf16[256,2048]{1,0:T(8,128)(2,1)}, bf16[256,2048]{1,0:T(8,128)(2,1)}) custom-call(bf16[1024,1536]{1,0:T(8,128)(2,1)} %gated_backward.2.refs_0_, bf16[1024,1536]{1,0:T(8,128)(2,1)} %gated_backward.3.refs_1_, bf16[256,1536]{1,0:T(8,128)(2,1)} %copy-done.16, bf16[256,1536]{1,0:T(8,128)(2,1)} %copy-done.19, ...), custom_call_target="tpu_custom_call" | custom-call | flops 1000 | bytes 1000 | tf_op jit(solution)/shard_map/mlp_in_grad/pallas_call | solution.py:408
  472.4 12.6 %collective-permute-done.81 = bf16[256,1536]{1,0:T(8,128)(2,1)S(1)} collective-permute-done((bf16[256,1536]{1,0:T(8,128)(2,1)S(1)}, bf16[256,1536]{1,0:T(8,128)(2,1)S(1)}, u32[]{:S(2)}, u32[]{:S(2)}) %collective-permute-start.81) | collective-permute-done | bytes 786464 | tf_op jit(solution)/shard_map/ppermute | solution.py:710
  487.1 5.1 collective-permute-done.76
  506.4 12.2 %collective-permute-done.89 = bf16[256,1536]{1,0:T(8,128)(2,1)S(1)} collective-permute-done((bf16[256,1536]{1,0:T(8,128)(2,1)S(1)}, bf16[256,1536]{1,0:T(8,128)(2,1)S(1)}, u32[]{:S(2)}, u32[]{:S(2)}) %collective-permute-start.89) | collective-permute-done | bytes 786464 | tf_op jit(solution)/shard_map/ppermute | solution.py:710
  519.5 12.9 %collective-permute-done.87 = bf16[256,1536]{1,0:T(8,128)(2,1)S(1)} collective-permute-done((bf16[256,1536]{1,0:T(8,128)(2,1)S(1)}, bf16[256,1536]{1,0:T(8,128)(2,1)S(1)}, u32[]{:S(2)}, u32[]{:S(2)}) %collective-permute-start.87) | collective-permute-done | bytes 786464 | tf_op jit(solution)/shard_map/ppermute | solution.py:710
  546.1 7.4 mixer_grad.1.grad
  553.5 28.5 %core_backward.1 = (bf16[1024,1280]{1,0:T(8,128)(2,1)}, f32[640,1280]{1,0:T(8,128)}, f32[8,640]{1,0:T(8,128)}) custom-call(s32[1]{0:T(128)} %bitcast.place, f32[1024,640]{1,0:T(8,128)} %mixer_grad.1.grad, f32[1024,1280]{1,0:T(8,128)} %mixer_in.1.branch.entry_pre.entry_tail, f32[1024,1280]{1,0:T(8,128)} %mixer_in.1.branch.entry_pre.entry_tail, ...), custom_call_target="tpu_custom_call" | custom-call | flops 1000 | bytes 1000 | tf_op jit(solution)/shard_map/core_backward/pallas_call | solution.py:301
  589.9 3.3 fusion.14
  597.0 11.4 %mixer_in_grad.1 = (bf16[256,2048]{1,0:T(8,128)(2,1)}, bf16[256,2048]{1,0:T(8,128)(2,1)}, bf16[256,2048]{1,0:T(8,128)(2,1)}, bf16[256,2048]{1,0:T(8,128)(2,1)}) custom-call(bf16[1024,1280]{1,0:T(8,128)(2,1)} %get-tuple-element.364.refs_0_, bf16[256,1280]{1,0:T(8,128)(2,1)} %copy-done.34, bf16[256,1280]{1,0:T(8,128)(2,1)} %copy-done.38, ...), custom_call_target="tpu_custom_call" | custom-call | flops 1000 | bytes 1000 | tf_op jit(solution)/shard_map/mixer_in_grad/pallas_call | solution.py:408
  624.8 11.1 %collective-permute-done.99 = bf16[256,1280]{1,0:T(8,128)(2,1)S(1)} collective-permute-done((bf16[256,1280]{1,0:T(8,128)(2,1)S(1)}, bf16[256,1280]{1,0:T(8,128)(2,1)S(1)}, u32[]{:S(2)}, u32[]{:S(2)}) %collective-permute-start.99) | collective-permute-done | bytes 655392 | tf_op jit(solution)/shard_map/ppermute | solution.py:710
  655.1 5.3 collective-permute-done.100
  673.6 3.6 fusion.24.refs_0_
  688.6 12.7 %mlp_out.1 = (bf16[256,2048]{1,0:T(8,128)(2,1)}, bf16[256,2048]{1,0:T(8,128)(2,1)}, bf16[256,2048]{1,0:T(8,128)(2,1)}, bf16[256,2048]{1,0:T(8,128)(2,1)}) custom-call(bf16[1024,768]{1,0:T(8,128)(2,1)} %get-tuple-element.399.refs_0_, bf16[1024,768]{1,0:T(8,128)(2,1)} %get-tuple-element.400.refs_1_, bf16[768,256]{1,0:T(8,128)(2,1)} %copy-done.36, ...), custom_call_target="tpu_custom_call" | custom-call | flops 1000 | bytes 1000 | tf_op jit(solution)/shard_map/mlp_out/pallas_call | solution.py:408
  725.2 11.7 %collective-permute-done.113 = bf16[256,1280]{1,0:T(8,128)(2,1)S(1)} collective-permute-done((bf16[256,1280]{1,0:T(8,128)(2,1)S(1)}, bf16[256,1280]{1,0:T(8,128)(2,1)S(1)}, u32[]{:S(2)}, u32[]{:S(2)}) %collective-permute-start.113) | collective-permute-done | bytes 655392 | tf_op jit(solution)/shard_map/ppermute | solution.py:710
  758.4 11.1 %collective-permute-done.112 = bf16[256,2048]{1,0:T(8,128)(2,1)} collective-permute-done((bf16[256,2048]{1,0:T(8,128)(2,1)}, bf16[256,2048]{1,0:T(8,128)(2,1)}, u32[]{:S(2)}, u32[]{:S(2)}) %collective-permute-start.112) | collective-permute-done | bytes 1048608 | tf_op jit(solution)/shard_map/ppermute | solution.py:767
  (592 shorter events, 328.2 us)
Async XLA Ops:
  14.0 32.8 %collective-permute-start.1 = (bf16[256,2048]{1,0:T(8,128)(2,1)}, bf16[256,2048]{1,0:T(8,128)(2,1)}, u32[]{:S(2)}, u32[]{:S(2)}) collective-permute-start(bf16[256,2048]{1,0:T(8,128)(2,1)} %refs_0_.1), channel_id=1, source_target_pairs={{0,2},{1,3},{2,0},{3,1},{4,6},{5,7},{6,4},{7,5},{8,10},{9,11},{10,... | collective-permute-start | bytes 3145736 | tf_op jit(solution)/shard_map/ppermute | solution.py:756
  23.3 48.3 %collective-permute-start = (bf16[256,2048]{1,0:T(8,128)(2,1)}, bf16[256,2048]{1,0:T(8,128)(2,1)}, u32[]{:S(2)}, u32[]{:S(2)}) collective-permute-start(bf16[256,2048]{1,0:T(8,128)(2,1)} %refs_0_.1), channel_id=1, source_target_pairs={{0,1},{1,0},{2,3},{3,2},{4,5},{5,4},{6,7},{7,6},{8,9},{9,8},{10,11... | collective-permute-start | bytes 3145736 | tf_op jit(solution)/shard_map/ppermute | solution.py:757
  37.7 25.3 %collective-permute-start.10 = (bf16[256,1280]{1,0:T(8,128)(2,1)S(1)}, bf16[256,1280]{1,0:T(8,128)(2,1)S(1)}, u32[]{:S(2)}, u32[]{:S(2)}) collective-permute-start(bf16[256,1280]{1,0:T(8,128)(2,1)S(1)} %collective-permute-done.6.refs_3_), channel_id=1, source_target_pairs={{8,0},{16,8},{24,16},{28,24},{20,28},{12,20},{4,12},{0,4},{9,1},{1... | collective-permute-start | bytes 1966088 | tf_op jit(solution)/shard_map/ppermute | solution.py:710
  46.8 24.8 %collective-permute-start.2 = (bf16[256,2048]{1,0:T(8,128)(2,1)}, bf16[256,2048]{1,0:T(8,128)(2,1)S(1)}, u32[]{:S(2)}, u32[]{:S(2)}) collective-permute-start(bf16[256,2048]{1,0:T(8,128)(2,1)} %collective-permute-done.1.refs_2_), channel_id=1, source_target_pairs={{0,1},{1,0},{2,3},{3,2},{4,5},{5,4},{6,7},{7,6},{8,9},{9,8},{10,11... | collective-permute-start | bytes 3145736 | tf_op jit(solution)/shard_map/ppermute | solution.py:758
  69.6 25.6 %collective-permute-start.20 = (bf16[256,1280]{1,0:T(8,128)(2,1)S(1)}, bf16[256,1280]{1,0:T(8,128)(2,1)S(1)}, u32[]{:S(2)}, u32[]{:S(2)}) collective-permute-start(bf16[256,1280]{1,0:T(8,128)(2,1)S(1)} %collective-permute-done.16.refs_6_), channel_id=1, source_target_pairs={{0,8},{8,16},{16,24},{24,28},{28,20},{20,12},{12,4},{4,0},{1,9},{9... | collective-permute-start | bytes 1966088 | tf_op jit(solution)/shard_map/ppermute | solution.py:710
  70.6 24.9 %collective-permute-start.18 = (bf16[640,256]{1,0:T(8,128)(2,1)S(1)}, bf16[640,256]{1,0:T(8,128)(2,1)}, u32[]{:S(2)}, u32[]{:S(2)}) collective-permute-start(bf16[640,256]{1,0:T(8,128)(2,1)S(1)} %copy-done.58), channel_id=1, source_target_pairs={{0,8},{8,16},{16,24},{24,28},{28,20},{20,12},{12,4},{4,0},{1,9},{9... | collective-permute-start | bytes 983048 | tf_op jit(solution)/shard_map/ppermute | solution.py:710
  79.3 23.7 %collective-permute-start.17 = (bf16[256,1536]{1,0:T(8,128)(2,1)S(1)}, bf16[256,1536]{1,0:T(8,128)(2,1)S(1)}, u32[]{:S(2)}, u32[]{:S(2)}) collective-permute-start(bf16[256,1536]{1,0:T(8,128)(2,1)S(1)} %pad_maximum_fusion.3.refs_1_.refs_2_), channel_id=1, source_target_pairs={{8,0},{16,8},{24,16},{28,24},{20,28},{12,20},{4,12},{0,4},{9,1},{1... | collective-permute-start | bytes 2359304 | tf_op jit(solution)/shard_map/ppermute | solution.py:710
  95.2 49.1 %collective-permute-start.23 = (bf16[256,1536]{1,0:T(8,128)(2,1)S(1)}, bf16[256,1536]{1,0:T(8,128)(2,1)S(1)}, u32[]{:S(2)}, u32[]{:S(2)}) collective-permute-start(bf16[256,1536]{1,0:T(8,128)(2,1)S(1)} %pad_maximum_fusion.3.refs_1_.refs_2_), channel_id=1, source_target_pairs={{0,8},{8,16},{16,24},{24,28},{28,20},{20,12},{12,4},{4,0},{1,9},{9... | collective-permute-start | bytes 2359304 | tf_op jit(solution)/shard_map/ppermute | solution.py:710
  103.0 41.9 %collective-permute-start.25 = (bf16[256,1536]{1,0:T(8,128)(2,1)S(1)}, bf16[256,1536]{1,0:T(8,128)(2,1)}, u32[]{:S(2)}, u32[]{:S(2)}) collective-permute-start(bf16[256,1536]{1,0:T(8,128)(2,1)S(1)} %collective-permute-done.17.refs_2_.refs_3_), channel_id=1, source_target_pairs={{8,0},{16,8},{24,16},{28,24},{20,28},{12,20},{4,12},{0,4},{9,1},{1... | collective-permute-start | bytes 2359304 | tf_op jit(solution)/shard_map/ppermute | solution.py:710
  105.9 39.0 %collective-permute-start.22 = (bf16[640,256]{1,0:T(8,128)(2,1)}, bf16[640,256]{1,0:T(8,128)(2,1)}, u32[]{:S(2)}, u32[]{:S(2)}) collective-permute-start(bf16[640,256]{1,0:T(8,128)(2,1)} %collective-permute-done.18.refs_8_), channel_id=1, source_target_pairs={{0,8},{8,16},{16,24},{24,28},{28,20},{20,12},{12,4},{4,0},{1,9},{9... | collective-permute-start | bytes 983048 | tf_op jit(solution)/shard_map/ppermute | solution.py:710
  148.6 25.7 %collective-permute-start.37 = (bf16[256,2048]{1,0:T(8,128)(2,1)S(1)}, bf16[256,2048]{1,0:T(8,128)(2,1)}, u32[]{:S(2)}, u32[]{:S(2)}) collective-permute-start(bf16[256,2048]{1,0:T(8,128)(2,1)S(1)} %copy-done.68), channel_id=1, source_target_pairs={{0,2},{1,3},{2,0},{3,1},{4,6},{5,7},{6,4},{7,5},{8,10},{9,11},{10,... | collective-permute-start | bytes 3145736 | tf_op jit(solution)/shard_map/ppermute | solution.py:756
  176.9 41.6 %collective-permute-start.29 = (bf16[256,2048]{1,0:T(8,128)(2,1)}, bf16[256,2048]{1,0:T(8,128)(2,1)}, u32[]{:S(2)}, u32[]{:S(2)}) collective-permute-start(bf16[256,2048]{1,0:T(8,128)(2,1)} %get-tuple-element.252), channel_id=1, source_target_pairs={{0,1},{1,0},{2,3},{3,2},{4,5},{5,4},{6,7},{7,6},{8,9},{9,8},{10,11... | collective-permute-start | bytes 3145736 | tf_op jit(solution)/shard_map/ppermute | solution.py:765
  180.0 38.5 %collective-permute-start.31 = (bf16[256,2048]{1,0:T(8,128)(2,1)}, bf16[256,2048]{1,0:T(8,128)(2,1)}, u32[]{:S(2)}, u32[]{:S(2)}) collective-permute-start(bf16[256,2048]{1,0:T(8,128)(2,1)} %add_convert_fusion.4), channel_id=1, source_target_pairs={{0,2},{1,3},{2,0},{3,1},{4,6},{5,7},{6,4},{7,5},{8,10},{9,11},{10,... | collective-permute-start | bytes 3145736 | tf_op jit(solution)/shard_map/ppermute | solution.py:767
  181.6 29.5 %collective-permute-start.33 = (bf16[256,1536]{1,0:T(8,128)(2,1)S(1)}, bf16[256,1536]{1,0:T(8,128)(2,1)S(1)}, u32[]{:S(2)}, u32[]{:S(2)}) collective-permute-start(bf16[256,1536]{1,0:T(8,128)(2,1)S(1)} %collective-permute-done.26.refs_4_.refs_5_), channel_id=1, source_target_pairs={{8,0},{16,8},{24,16},{28,24},{20,28},{12,20},{4,12},{0,4},{9,1},{1... | collective-permute-start | bytes 2359304 | tf_op jit(solution)/shard_map/ppermute | solution.py:710
  194.7 23.7 %collective-permute-start.32 = (bf16[256,1536]{1,0:T(8,128)(2,1)S(1)}, bf16[256,1536]{1,0:T(8,128)(2,1)S(1)}, u32[]{:S(2)}, u32[]{:S(2)}) collective-permute-start(bf16[256,1536]{1,0:T(8,128)(2,1)S(1)} %pad_maximum_fusion.4.refs_1_.refs_10_), channel_id=1, source_target_pairs={{0,8},{8,16},{16,24},{24,28},{28,20},{20,12},{12,4},{4,0},{1,9},{9... | collective-permute-start | bytes 2359304 | tf_op jit(solution)/shard_map/ppermute | solution.py:710
  222.0 24.4 %collective-permute-start.40 = (bf16[256,2048]{1,0:T(8,128)(2,1)S(1)}, bf16[256,2048]{1,0:T(8,128)(2,1)S(1)}, u32[]{:S(2)}, u32[]{:S(2)}) collective-permute-start(bf16[256,2048]{1,0:T(8,128)(2,1)S(1)} %multiply_convert_fusion), channel_id=1, source_target_pairs={{0,2},{1,3},{2,0},{3,1},{4,6},{5,7},{6,4},{7,5},{8,10},{9,11},{10,... | collective-permute-start | bytes 3145736 | tf_op jit(solution)/shard_map/ppermute | solution.py:756
  222.6 38.3 %collective-permute-start.46 = (bf16[256,1536]{1,0:T(8,128)(2,1)S(1)}, bf16[256,1536]{1,0:T(8,128)(2,1)S(1)}, u32[]{:S(2)}, u32[]{:S(2)}) collective-permute-start(bf16[256,1536]{1,0:T(8,128)(2,1)S(1)} %collective-permute-done.35.refs_2_.refs_11_), channel_id=1, source_target_pairs={{8,0},{16,8},{24,16},{28,24},{20,28},{12,20},{4,12},{0,4},{9,1},{1... | collective-permute-start | bytes 2359304 | tf_op jit(solution)/shard_map/ppermute | solution.py:710
  225.1 59.0 %collective-permute-start.39 = (bf16[256,2048]{1,0:T(8,128)(2,1)S(1)}, bf16[256,2048]{1,0:T(8,128)(2,1)S(1)}, u32[]{:S(2)}, u32[]{:S(2)}) collective-permute-start(bf16[256,2048]{1,0:T(8,128)(2,1)S(1)} %multiply_convert_fusion), channel_id=1, source_target_pairs={{0,1},{1,0},{2,3},{3,2},{4,5},{5,4},{6,7},{7,6},{8,9},{9,8},{10,11... | collective-permute-start | bytes 3145736 | tf_op jit(solution)/shard_map/ppermute | solution.py:757
  246.4 38.6 %collective-permute-start.41 = (bf16[256,2048]{1,0:T(8,128)(2,1)S(1)}, bf16[256,2048]{1,0:T(8,128)(2,1)S(1)}, u32[]{:S(2)}, u32[]{:S(2)}) collective-permute-start(bf16[256,2048]{1,0:T(8,128)(2,1)S(1)} %collective-permute-done.40), channel_id=1, source_target_pairs={{0,1},{1,0},{2,3},{3,2},{4,5},{5,4},{6,7},{7,6},{8,9},{9,8},{10,11... | collective-permute-start | bytes 3145736 | tf_op jit(solution)/shard_map/ppermute | solution.py:758
  246.5 29.3 %collective-permute-start.44 = (bf16[256,1536]{1,0:T(8,128)(2,1)S(1)}, bf16[256,1536]{1,0:T(8,128)(2,1)S(1)}, u32[]{:S(2)}, u32[]{:S(2)}) collective-permute-start(bf16[256,1536]{1,0:T(8,128)(2,1)S(1)} %collective-permute-done.32.refs_8_.refs_17_), channel_id=1, source_target_pairs={{0,8},{8,16},{16,24},{24,28},{28,20},{20,12},{12,4},{4,0},{1,9},{9... | collective-permute-start | bytes 2359304 | tf_op jit(solution)/shard_map/ppermute | solution.py:710
  260.9 23.2 %collective-permute-start.43 = (bf16[768,256]{1,0:T(8,128)(2,1)S(1)}, bf16[768,256]{1,0:T(8,128)(2,1)}, u32[]{:S(2)}, u32[]{:S(2)}) collective-permute-start(bf16[768,256]{1,0:T(8,128)(2,1)S(1)} %collective-permute-done.42.refs_8_.refs_9_), channel_id=1, source_target_pairs={{0,8},{8,16},{16,24},{24,28},{28,20},{20,12},{12,4},{4,0},{1,9},{9... | collective-permute-start | bytes 1179656 | tf_op jit(solution)/shard_map/ppermute | solution.py:710
  275.7 29.9 %collective-permute-start.49 = (bf16[768,256]{1,0:T(8,128)(2,1)}, bf16[768,256]{1,0:T(8,128)(2,1)}, u32[]{:S(2)}, u32[]{:S(2)}) collective-permute-start(bf16[768,256]{1,0:T(8,128)(2,1)} %collective-permute-done.45.refs_2_.refs_3_), channel_id=1, source_target_pairs={{8,0},{16,8},{24,16},{28,24},{20,28},{12,20},{4,12},{0,4},{9,1},{1... | collective-permute-start | bytes 1179656 | tf_op jit(solution)/shard_map/ppermute | solution.py:710
  284.1 28.9 %collective-permute-start.54 = (bf16[768,256]{1,0:T(8,128)(2,1)}, bf16[768,256]{1,0:T(8,128)(2,1)}, u32[]{:S(2)}, u32[]{:S(2)}) collective-permute-start(bf16[768,256]{1,0:T(8,128)(2,1)} %collective-permute-done.43.refs_7_.refs_8_), channel_id=1, source_target_pairs={{0,8},{8,16},{16,24},{24,28},{28,20},{20,12},{12,4},{4,0},{1,9},{9... | collective-permute-start | bytes 1179656 | tf_op jit(solution)/shard_map/ppermute | solution.py:710
  313.1 30.5 %collective-permute-start.55 = (bf16[768,256]{1,0:T(8,128)(2,1)S(1)}, bf16[768,256]{1,0:T(8,128)(2,1)S(1)}, u32[]{:S(2)}, u32[]{:S(2)}) collective-permute-start(bf16[768,256]{1,0:T(8,128)(2,1)S(1)} %get-tuple-element.278.refs_1_.refs_10_), channel_id=1, source_target_pairs={{0,8},{8,16},{16,24},{24,28},{28,20},{20,12},{12,4},{4,0},{1,9},{9... | collective-permute-start | bytes 1179656 | tf_op jit(solution)/shard_map/ppermute | solution.py:710
  318.0 25.6 %collective-permute-start.56 = (bf16[768,256]{1,0:T(8,128)(2,1)S(1)}, bf16[768,256]{1,0:T(8,128)(2,1)S(1)}, u32[]{:S(2)}, u32[]{:S(2)}) collective-permute-start(bf16[768,256]{1,0:T(8,128)(2,1)S(1)} %collective-permute-done.53.refs_4_.refs_5_), channel_id=1, source_target_pairs={{8,0},{16,8},{24,16},{28,24},{20,28},{12,20},{4,12},{0,4},{9,1},{1... | collective-permute-start | bytes 1179656 | tf_op jit(solution)/shard_map/ppermute | solution.py:710
  326.4 35.6 %collective-permute-start.58 = (bf16[768,256]{1,0:T(8,128)(2,1)S(1)}, bf16[768,256]{1,0:T(8,128)(2,1)S(1)}, u32[]{:S(2)}, u32[]{:S(2)}) collective-permute-start(bf16[768,256]{1,0:T(8,128)(2,1)S(1)} %collective-permute-done.52.refs_3_.refs_12_), channel_id=1, source_target_pairs={{8,0},{16,8},{24,16},{28,24},{20,28},{12,20},{4,12},{0,4},{9,1},{1... | collective-permute-start | bytes 1179656 | tf_op jit(solution)/shard_map/ppermute | solution.py:710
  395.7 32.3 %collective-permute-start.73 = (bf16[768,256]{1,0:T(8,128)(2,1)}, bf16[768,256]{1,0:T(8,128)(2,1)}, u32[]{:S(2)}, u32[]{:S(2)}) collective-permute-start(bf16[768,256]{1,0:T(8,128)(2,1)} %convolution_convert_fusion.7), channel_id=1, source_target_pairs={{0,8},{8,16},{16,24},{24,28},{28,20},{20,12},{12,4},{4,0},{1,9},{9... | collective-permute-start | bytes 1179656 | tf_op jit(solution)/shard_map/ppermute | solution.py:710
  407.7 25.3 %collective-permute-start.71 = (bf16[256,1536]{1,0:T(8,128)(2,1)}, bf16[256,1536]{1,0:T(8,128)(2,1)}, u32[]{:S(2)}, u32[]{:S(2)}) collective-permute-start(bf16[256,1536]{1,0:T(8,128)(2,1)} %convolution_convert_fusion.4), channel_id=1, source_target_pairs={{0,8},{8,16},{16,24},{24,28},{28,20},{20,12},{12,4},{4,0},{1,9},{9... | collective-permute-start | bytes 2359304 | tf_op jit(solution)/shard_map/ppermute | solution.py:710
  409.7 27.2 %collective-permute-start.70 = (bf16[256,1536]{1,0:T(8,128)(2,1)}, bf16[256,1536]{1,0:T(8,128)(2,1)}, u32[]{:S(2)}, u32[]{:S(2)}) collective-permute-start(bf16[256,1536]{1,0:T(8,128)(2,1)} %convolution_convert_fusion.5), channel_id=1, source_target_pairs={{8,0},{16,8},{24,16},{28,24},{20,28},{12,20},{4,12},{0,4},{9,1},{1... | collective-permute-start | bytes 2359304 | tf_op jit(solution)/shard_map/ppermute | solution.py:710
  427.9 36.6 %collective-permute-start.75 = (bf16[256,2048]{1,0:T(8,128)(2,1)}, bf16[256,2048]{1,0:T(8,128)(2,1)}, u32[]{:S(2)}, u32[]{:S(2)}) collective-permute-start(bf16[256,2048]{1,0:T(8,128)(2,1)} %get-tuple-element.314), channel_id=1, source_target_pairs={{0,1},{1,0},{2,3},{3,2},{4,5},{5,4},{6,7},{7,6},{8,9},{9,8},{10,11... | collective-permute-start | bytes 3145736 | tf_op jit(solution)/shard_map/ppermute | solution.py:764
  431.0 24.3 %collective-permute-start.78 = (bf16[768,256]{1,0:T(8,128)(2,1)}, bf16[768,256]{1,0:T(8,128)(2,1)}, u32[]{:S(2)}, u32[]{:S(2)}) collective-permute-start(bf16[768,256]{1,0:T(8,128)(2,1)} %fusion.46), channel_id=1, source_target_pairs={{0,8},{8,16},{16,24},{24,28},{28,20},{20,12},{12,4},{4,0},{1,9},{9... | collective-permute-start | bytes 1179656 | tf_op jit(solution)/shard_map/ppermute | solution.py:710
  431.2 26.7 %collective-permute-start.77 = (bf16[256,1536]{1,0:T(8,128)(2,1)}, bf16[256,1536]{1,0:T(8,128)(2,1)}, u32[]{:S(2)}, u32[]{:S(2)}) collective-permute-start(bf16[256,1536]{1,0:T(8,128)(2,1)} %convolution_convert_fusion.3), channel_id=1, source_target_pairs={{8,0},{16,8},{24,16},{28,24},{20,28},{12,20},{4,12},{0,4},{9,1},{1... | collective-permute-start | bytes 2359304 | tf_op jit(solution)/shard_map/ppermute | solution.py:710
  436.3 25.9 %collective-permute-start.80 = (bf16[256,1536]{1,0:T(8,128)(2,1)}, bf16[256,1536]{1,0:T(8,128)(2,1)}, u32[]{:S(2)}, u32[]{:S(2)}) collective-permute-start(bf16[256,1536]{1,0:T(8,128)(2,1)} %fusion.6), channel_id=1, source_target_pairs={{0,8},{8,16},{16,24},{24,28},{28,20},{20,12},{12,4},{4,0},{1,9},{9... | collective-permute-start | bytes 2359304 | tf_op jit(solution)/shard_map/ppermute | solution.py:710
  440.1 29.8 %collective-permute-start.82 = (bf16[256,1536]{1,0:T(8,128)(2,1)}, bf16[256,1536]{1,0:T(8,128)(2,1)}, u32[]{:S(2)}, u32[]{:S(2)}) collective-permute-start(bf16[256,1536]{1,0:T(8,128)(2,1)} %fusion.5), channel_id=1, source_target_pairs={{8,0},{16,8},{24,16},{28,24},{20,28},{12,20},{4,12},{0,4},{9,1},{1... | collective-permute-start | bytes 2359304 | tf_op jit(solution)/shard_map/ppermute | solution.py:710
  460.7 25.4 %collective-permute-start.79 = (bf16[256,1536]{1,0:T(8,128)(2,1)S(1)}, bf16[256,1536]{1,0:T(8,128)(2,1)S(1)}, u32[]{:S(2)}, u32[]{:S(2)}) collective-permute-start(bf16[256,1536]{1,0:T(8,128)(2,1)S(1)} %fusion.8), channel_id=1, source_target_pairs={{8,0},{16,8},{24,16},{28,24},{20,28},{12,20},{4,12},{0,4},{9,1},{1... | collective-permute-start | bytes 2359304 | tf_op jit(solution)/shard_map/ppermute | solution.py:710
  462.2 24.8 %collective-permute-start.74 = (bf16[256,2048]{1,0:T(8,128)(2,1)S(1)}, bf16[256,2048]{1,0:T(8,128)(2,1)S(1)}, u32[]{:S(2)}, u32[]{:S(2)}) collective-permute-start(bf16[256,2048]{1,0:T(8,128)(2,1)S(1)} %copy-done.94), channel_id=1, source_target_pairs={{0,1},{1,0},{2,3},{3,2},{4,5},{5,4},{6,7},{7,6},{8,9},{9,8},{10,11... | collective-permute-start | bytes 3145736 | tf_op jit(solution)/shard_map/ppermute | solution.py:765
  468.1 24.0 %collective-permute-start.76 = (bf16[256,2048]{1,0:T(8,128)(2,1)S(1)}, bf16[256,2048]{1,0:T(8,128)(2,1)S(1)}, u32[]{:S(2)}, u32[]{:S(2)}) collective-permute-start(bf16[256,2048]{1,0:T(8,128)(2,1)S(1)} %add_convert_fusion.3), channel_id=1, source_target_pairs={{0,2},{1,3},{2,0},{3,1},{4,6},{5,7},{6,4},{7,5},{8,10},{9,11},{10,... | collective-permute-start | bytes 3145736 | tf_op jit(solution)/shard_map/ppermute | solution.py:767
  469.9 33.7 %collective-permute-start.90 = (bf16[768,256]{1,0:T(8,128)(2,1)S(1)}, bf16[768,256]{1,0:T(8,128)(2,1)S(1)}, u32[]{:S(2)}, u32[]{:S(2)}) collective-permute-start(bf16[768,256]{1,0:T(8,128)(2,1)S(1)} %fusion.48), channel_id=1, source_target_pairs={{0,8},{8,16},{16,24},{24,28},{28,20},{20,12},{12,4},{4,0},{1,9},{9... | collective-permute-start | bytes 1179656 | tf_op jit(solution)/shard_map/ppermute | solution.py:710
  495.7 36.6 %collective-permute-start.85 = (bf16[256,2048]{1,0:T(8,128)(2,1)S(1)}, bf16[256,2048]{1,0:T(8,128)(2,1)S(1)}, u32[]{:S(2)}, u32[]{:S(2)}) collective-permute-start(bf16[256,2048]{1,0:T(8,128)(2,1)S(1)} %get-tuple-element.347), channel_id=1, source_target_pairs={{0,2},{1,3},{2,0},{3,1},{4,6},{5,7},{6,4},{7,5},{8,10},{9,11},{10,... | collective-permute-start | bytes 3145736 | tf_op jit(solution)/shard_map/ppermute | solution.py:756
  500.2 32.1 %collective-permute-start.87 = (bf16[256,1536]{1,0:T(8,128)(2,1)S(1)}, bf16[256,1536]{1,0:T(8,128)(2,1)S(1)}, u32[]{:S(2)}, u32[]{:S(2)}) collective-permute-start(bf16[256,1536]{1,0:T(8,128)(2,1)S(1)} %fusion.7), channel_id=1, source_target_pairs={{8,0},{16,8},{24,16},{28,24},{20,28},{12,20},{4,12},{0,4},{9,1},{1... | collective-permute-start | bytes 2359304 | tf_op jit(solution)/shard_map/ppermute | solution.py:710
  506.4 31.6 %collective-permute-start.84 = (bf16[256,2048]{1,0:T(8,128)(2,1)S(1)}, bf16[256,2048]{1,0:T(8,128)(2,1)S(1)}, u32[]{:S(2)}, u32[]{:S(2)}) collective-permute-start(bf16[256,2048]{1,0:T(8,128)(2,1)S(1)} %get-tuple-element.347), channel_id=1, source_target_pairs={{0,1},{1,0},{2,3},{3,2},{4,5},{5,4},{6,7},{7,6},{8,9},{9,8},{10,11... | collective-permute-start | bytes 3145736 | tf_op jit(solution)/shard_map/ppermute | solution.py:757
  534.2 55.7 %collective-permute-start.93 = (bf16[256,1536]{1,0:T(8,128)(2,1)}, bf16[256,1536]{1,0:T(8,128)(2,1)}, u32[]{:S(2)}, u32[]{:S(2)}) collective-permute-start(bf16[256,1536]{1,0:T(8,128)(2,1)} %fusion.12), channel_id=1, source_target_pairs={{8,0},{16,8},{24,16},{28,24},{20,28},{12,20},{4,12},{0,4},{9,1},{1... | collective-permute-start | bytes 2359304 | tf_op jit(solution)/shard_map/ppermute | solution.py:710
  540.3 49.6 %collective-permute-start.92 = (bf16[256,1536]{1,0:T(8,128)(2,1)}, bf16[256,1536]{1,0:T(8,128)(2,1)}, u32[]{:S(2)}, u32[]{:S(2)}) collective-permute-start(bf16[256,1536]{1,0:T(8,128)(2,1)} %fusion.13), channel_id=1, source_target_pairs={{0,8},{8,16},{16,24},{24,28},{28,20},{20,12},{12,4},{4,0},{1,9},{9... | collective-permute-start | bytes 2359304 | tf_op jit(solution)/shard_map/ppermute | solution.py:710
  614.2 54.2 %collective-permute-start.108 = (bf16[256,2048]{1,0:T(8,128)(2,1)}, bf16[256,2048]{1,0:T(8,128)(2,1)}, u32[]{:S(2)}, u32[]{:S(2)}) collective-permute-start(bf16[256,2048]{1,0:T(8,128)(2,1)} %get-tuple-element.387), channel_id=1, source_target_pairs={{0,1},{1,0},{2,3},{3,2},{4,5},{5,4},{6,7},{7,6},{8,9},{9,8},{10,11... | collective-permute-start | bytes 3145736 | tf_op jit(solution)/shard_map/ppermute | solution.py:765
  619.7 48.7 %collective-permute-start.109 = (bf16[256,2048]{1,0:T(8,128)(2,1)}, bf16[256,2048]{1,0:T(8,128)(2,1)}, u32[]{:S(2)}, u32[]{:S(2)}) collective-permute-start(bf16[256,2048]{1,0:T(8,128)(2,1)} %add_convert_fusion.2), channel_id=1, source_target_pairs={{0,2},{1,3},{2,0},{3,1},{4,6},{5,7},{6,4},{7,5},{8,10},{9,11},{10,... | collective-permute-start | bytes 3145736 | tf_op jit(solution)/shard_map/ppermute | solution.py:767
  622.8 27.6 %collective-permute-start.101 = (bf16[256,1280]{1,0:T(8,128)(2,1)}, bf16[256,1280]{1,0:T(8,128)(2,1)}, u32[]{:S(2)}, u32[]{:S(2)}) collective-permute-start(bf16[256,1280]{1,0:T(8,128)(2,1)} %convolution_convert_fusion), channel_id=1, source_target_pairs={{0,8},{8,16},{16,24},{24,28},{28,20},{20,12},{12,4},{4,0},{1,9},{9... | collective-permute-start | bytes 1966088 | tf_op jit(solution)/shard_map/ppermute | solution.py:710
  635.9 29.0 %collective-permute-start.98 = (bf16[640,256]{1,0:T(8,128)(2,1)}, bf16[640,256]{1,0:T(8,128)(2,1)}, u32[]{:S(2)}, u32[]{:S(2)}) collective-permute-start(bf16[640,256]{1,0:T(8,128)(2,1)} %add_convert_fusion.8), channel_id=1, source_target_pairs={{0,8},{8,16},{16,24},{24,28},{28,20},{20,12},{12,4},{4,0},{1,9},{9... | collective-permute-start | bytes 983048 | tf_op jit(solution)/shard_map/ppermute | solution.py:710
  723.9 34.5 %collective-permute-start.110 = (bf16[256,2048]{1,0:T(8,128)(2,1)}, bf16[256,2048]{1,0:T(8,128)(2,1)}, u32[]{:S(2)}, u32[]{:S(2)}) collective-permute-start(bf16[256,2048]{1,0:T(8,128)(2,1)} %get-tuple-element.402), channel_id=1, source_target_pairs={{0,1},{1,0},{2,3},{3,2},{4,5},{5,4},{6,7},{7,6},{8,9},{9,8},{10,11... | collective-permute-start | bytes 3145736 | tf_op jit(solution)/shard_map/ppermute | solution.py:765
  (185 other events, 2967.8 us)

commit v3 on v2

--- a/solution.py
+++ b/solution.py
@@ -14,7 +14,7 @@
 f32 = jnp.float32
 bf16 = jnp.bfloat16
 vmem_bytes = 56 * 1024 * 1024
-light = pl.CostEstimate(flops=1000, bytes_accessed=1000, transcendentals=0)
+light = pl.CostEstimate(flops=6_000_000_000, bytes_accessed=30_000_000, transcendentals=0)
 
 
 def gelu_both(value):
@@ -375,78 +375,102 @@
     )
 
 
-def spread(lefts, weights, first, count, transposed, name):
-    rows = lefts[0][0].shape[0] // 4
+def spread(lefts, weights, place, blocks, transposed, name):
+    total = lefts[0][0].shape[0]
+    rows = total // 4
     pieces = len(weights[0])
     product = dot_back if transposed else dot
     sizes = [w.shape[0 if transposed else 1] for w in weights[0]]
-    widths = [w[0].shape[1 if transposed else 0] for w in weights]
+    widths = [width for _, _, width in lefts]
     features = sum(sizes)
     terms = len(lefts)
-
-    def kernel(*refs):
+    count = len(blocks) if blocks else 4
+
+    def kernel(place_ref, *refs):
         left = [ref[...] for ref in refs[:terms]]
         flat = refs[terms : terms + terms * pieces]
-        outs = refs[terms + terms * pieces : -1]
-        total = refs[-1]
+        outs = refs[terms + terms * pieces :]
+        result = outs[-1]
         at = 0
         for r in range(pieces):
-            value = product(left[0], flat[r][...])
-            for i in range(1, terms):
-                value += product(left[i], flat[i * pieces + r][...])
-            total[:, at : at + sizes[r]] = value.astype(bf16)
+            value = None
+            for i in range(terms):
+                weight = flat[i * pieces + r]
+                if transposed:
+                    weight = weight[:, : widths[i]]
+                else:
+                    weight = weight[...]
+                term = product(left[i], weight)
+                value = term if value is None else value + term
+            result[:, at : at + sizes[r]] = value.astype(bf16)
             at += sizes[r]
-        for g in range(count):
-
-            @pl.when(pl.program_id(0) == g)
-            def _():
-                outs[g][...] = total[...]
-
-    def left_spec(width, column):
-        return pl.BlockSpec((rows, width), lambda g: (first - g, column))
-
-    return call(
+        if blocks:
+            for g in range(count):
+
+                @pl.when(pl.program_id(0) == g)
+                def _():
+                    outs[g][...] = result[...]
+
+    def left_spec(column, width):
+        if blocks:
+            first = blocks[0]
+            return pl.BlockSpec((rows, width), lambda g, t: ((first - g) ^ t[0], column))
+        return pl.BlockSpec((rows, width), lambda g, t: (g, column))
+
+    if blocks:
+        out_specs = [fixed((rows, features))] * count
+        out_shape = [jax.ShapeDtypeStruct((rows, features), bf16)] * count
+        scratch = [pltpu.VMEM((rows, features), bf16)]
+    else:
+        out_specs = pl.BlockSpec((rows, features), lambda g, t: (g, 0))
+        out_shape = jax.ShapeDtypeStruct((total, features), bf16)
+        scratch = []
+    return pl.pallas_call(
         kernel,
-        name,
-        (count,),
-        [left_spec(width, column) for width, (_, column) in zip(widths, lefts)]
-        + [fixed(w.shape) for group in weights for w in group],
-        [fixed((rows, features))] * count,
-        [jax.ShapeDtypeStruct((rows, features), bf16)] * count,
-        [pltpu.VMEM((rows, features), bf16)],
-    )(*[left for left, _ in lefts], *[w for group in weights for w in group])
-
-
-def collect(left, weights, transposed, name):
+        grid_spec=pltpu.PrefetchScalarGridSpec(
+            num_scalar_prefetch=1,
+            grid=(count,),
+            in_specs=[left_spec(column, width) for _, column, width in lefts]
+            + [fixed(w.shape) for group in weights for w in group],
+            out_specs=out_specs,
+            scratch_shapes=scratch,
+        ),
+        out_shape=out_shape,
+        compiler_params=pltpu.CompilerParams(vmem_limit_bytes=vmem_bytes),
+        cost_estimate=light,
+        name=name,
+    )(place, *[left for left, _, _ in lefts], *[w for group in weights for w in group])
+
+
+def collect(left, weights, width, transposed, name):
     total, features = left.shape
     rows = total // 4
+    count = len(weights)
     pieces = len(weights[0])
     product = dot_back if transposed else dot
     sizes = [w.shape[1 if transposed else 0] for w in weights[0]]
-    widths = [w[0].shape[0 if transposed else 1] for w in weights]
 
     def kernel(*refs):
         out = refs[-1]
-        column = 0
-        for i, width in enumerate(widths):
+        for i in range(count):
             at = 0
             value = None
             for r in range(pieces):
-                term = product(refs[0][:, at : at + sizes[r]], refs[1 + i * pieces + r][...])
+                ref = refs[1 + i * pieces + r]
+                weight = ref[...] if transposed else ref[:, :width]
+                term = product(refs[0][:, at : at + sizes[r]], weight)
                 value = term if value is None else value + term
                 at += sizes[r]
-            out[:, column : column + width] = value
-            column += width
-
-    width = sum(widths)
+            out[:, i * width : (i + 1) * width] = value
+
     return call(
         kernel,
         name,
         (4,),
         [pl.BlockSpec((rows, features), lambda g: (g, 0))]
         + [fixed(w.shape) for group in weights for w in group],
-        pl.BlockSpec((rows, width), lambda g: (g, 0)),
-        jax.ShapeDtypeStruct((total, width), f32),
+        pl.BlockSpec((rows, count * width), lambda g: (g, 0)),
+        jax.ShapeDtypeStruct((total, count * width), f32),
     )(left, *[w for group in weights for w in group])
 
 
@@ -517,28 +541,233 @@
     )(left, *down_pieces, act, slope)
 
 
-def normalize(values, gain):
-    total, features = values.shape
-
-    def kernel(value_ref, gain_ref, out_ref):
+def weight_grads(lefts, right, pieces, by_left, name, extras=()):
+    total = right.shape[0]
+    terms = len(lefts)
+    operands = list(lefts) + [right]
+    if (lefts[0] if by_left else right).shape[1] // pieces % 128:
+        return weight_grads_plain(lefts, right, pieces, by_left, extras)
+    if by_left:
+        (left,) = lefts
+        size = left.shape[1] // pieces
+        parts = len(extras) or 1
+        width = right.shape[1] // parts
+        more = extras[0].shape[1] if extras else 0
+        shapes = [(size, width + more)] * parts
+        in_specs = [pl.BlockSpec((total, size), lambda g: (0, g)), fixed(right.shape)]
+        operands += extras
+        in_specs += [pl.BlockSpec((size, more), lambda g: (g, 0)) for _ in extras]
+    else:
+        size = right.shape[1] // pieces
+        parts = terms
+        shapes = [(left.shape[1], size) for left in lefts]
+        in_specs = [fixed(left.shape) for left in lefts] + [
+            pl.BlockSpec((total, size), lambda g: (0, g))
+        ]
+
+    def kernel(*refs):
+        outs = refs[len(operands) : len(operands) + parts * pieces]
+        results = refs[len(operands) + parts * pieces :]
+        for i in range(parts):
+            if by_left:
+                value = dot_rows(refs[0][...], refs[1][:, i * width : (i + 1) * width])
+                results[i][:, :width] = value.astype(bf16)
+                if extras:
+                    results[i][:, width:] = refs[2 + i][...]
+            else:
+                results[i][...] = dot_rows(refs[i][...], refs[terms][...]).astype(bf16)
+        for r in range(pieces):
+
+            @pl.when(pl.program_id(0) == r)
+            def _():
+                for i in range(parts):
+                    outs[i * pieces + r][...] = results[i][...]
+
+    out = call(
+        kernel,
+        name,
+        (pieces,),
+        in_specs,
+        [fixed(shape) for shape in shapes for _ in range(pieces)],
+        [jax.ShapeDtypeStruct(shape, bf16) for shape in shapes for _ in range(pieces)],
+        [pltpu.VMEM(shape, bf16) for shape in shapes],
+    )(*operands)
+    return [out[i * pieces : (i + 1) * pieces] for i in range(parts)]
+
+
+def weight_grads_plain(lefts, right, pieces, by_left, extras):
+    if not by_left:
+        wholes = [dot_rows(left, right).astype(bf16) for left in lefts]
+        return [jnp.split(whole, pieces, axis=1) for whole in wholes]
+    wholes = jnp.split(dot_rows(lefts[0], right).astype(bf16), len(extras) or 1, axis=1)
+    if extras:
+        wholes = [jnp.concatenate(pair, axis=1) for pair in zip(wholes, extras)]
+    return [jnp.split(whole, pieces, axis=0) for whole in wholes]
+
+
+def one_hot(rows, columns, hit):
+    row = lax.broadcasted_iota(jnp.int32, (rows, columns), 0)
+    column = lax.broadcasted_iota(jnp.int32, (rows, columns), 1)
+    return jnp.where(hit(row, column), 1.0, 0.0).astype(bf16)
+
+
+def table_movers(width, shard, piece, block_width):
+    table_rows = width // block_width * piece
+    return [
+        one_hot(
+            width,
+            shard,
+            lambda c, row, k=k: row == k * table_rows + c // block_width * piece + c % piece,
+        )
+        for k in range(3)
+    ]
+
+
+def unpack_tables(blocks, order, width, piece, block_width):
+    count = len(blocks)
+    shard = blocks[0].shape[0]
+    table_rows = width // block_width * piece
+
+    def kernel(order_ref, *refs):
+        flat = refs[:count]
+        gates, small, gains, kept = refs[count:]
+        owner = lax.broadcasted_iota(jnp.int32, (width, 256), 0) % block_width // piece
+        movers = table_movers(width, shard, piece, block_width)
+        picks = one_hot(8, shard, lambda row, column: column == 3 * table_rows + row)
+        for r in range(count):
+            table = flat[r][...]
+            mine = owner == order_ref[r]
+            for k in range(3):
+                value = dot(movers[k], table)
+                if r == 0:
+                    kept[k] = jnp.where(mine, value, 0.0)
+                else:
+                    kept[k] = jnp.where(mine, value, kept[k])
+            rows = dot(picks, table)
+            gains[:, r * shard : (r + 1) * shard] = rows[:, :shard]
+        spreader = one_hot(256, width, lambda row, column: row == column % block_width)
+        same = lax.broadcasted_iota(jnp.int32, (width, width), 0) // block_width == (
+            lax.broadcasted_iota(jnp.int32, (width, width), 1) // block_width
+        )
+        for k in range(2):
+            value = dot(kept[k].astype(bf16), spreader)
+            gates[:, k * width : (k + 1) * width] = jnp.where(same, value, 0.0).astype(bf16)
+        picker = one_hot(8, 256, lambda row, column: row == column)
+        small[...] = dot_back(picker, kept[2].astype(bf16))
+
+    return pl.pallas_call(
+        kernel,
+        grid_spec=pltpu.PrefetchScalarGridSpec(
+            num_scalar_prefetch=1,
+            grid=(1,),
+            in_specs=[fixed((shard, 256))] * count,
+            out_specs=[
+                fixed((width, 2 * width)),
+                fixed((8, width)),
+                fixed((8, count * shard)),
+            ],
+            scratch_shapes=[pltpu.VMEM((3, width, 256), f32)],
+        ),
+        out_shape=[
+            jax.ShapeDtypeStruct((width, 2 * width), bf16),
+            jax.ShapeDtypeStruct((8, width), f32),
+            jax.ShapeDtypeStruct((8, count * shard), f32),
+        ],
+        compiler_params=pltpu.CompilerParams(vmem_limit_bytes=vmem_bytes),
+        cost_estimate=light,
+        name="unpack_tables",
+    )(order, *blocks)
+
+
+def pack_tables(gate_grads, small_grads, order, count, shard, piece, block_width):
+    width = gate_grads.shape[0]
+
+    def kernel(order_ref, gate_ref, small_ref, left, right):
+        spreader = one_hot(256, width, lambda row, column: row == column % block_width)
+        same = lax.broadcasted_iota(jnp.int32, (width, width), 0) // block_width == (
+            lax.broadcasted_iota(jnp.int32, (width, width), 1) // block_width
+        )
+        folded = [
+            dot_back(
+                jnp.where(same, gate_ref[:, k * width : (k + 1) * width], 0.0).astype(bf16),
+                spreader,
+            )
+            for k in range(2)
+        ]
+        picker = one_hot(8, 256, lambda row, column: row == column)
+        folded.append(dot_rows(small_ref[...].astype(bf16), picker))
+        owner = lax.broadcasted_iota(jnp.int32, (width, 256), 0) % block_width // piece
+        movers = table_movers(width, shard, piece, block_width)
+        for r in range(count):
+            total = None
+            for k in range(3):
+                mine = jnp.where(owner == order_ref[r], folded[k], 0.0).astype(bf16)
+                term = dot_rows(movers[k], mine)
+                total = term if total is None else total + term
+            at = slice(r * shard, (r + 1) * shard)
+            left[at, :] = total[:, :128].astype(bf16)
+            right[at, :] = total[:, 128:].astype(bf16)
+
+    shape = (count * shard, 128)
+    return pl.pallas_call(
+        kernel,
+        grid_spec=pltpu.PrefetchScalarGridSpec(
+            num_scalar_prefetch=1,
+            grid=(1,),
+            in_specs=[fixed(gate_grads.shape), fixed(small_grads.shape)],
+            out_specs=[fixed(shape)] * 2,
+        ),
+        out_shape=[jax.ShapeDtypeStruct(shape, bf16)] * 2,
+        compiler_params=pltpu.CompilerParams(vmem_limit_bytes=vmem_bytes),
+        cost_estimate=light,
+        name="pack_tables",
+    )(order, gate_grads, small_grads)
+
+
+def prepare(whole, order, place, size, gain):
+    total, features = whole.shape
+    rows = total // 4
+    groups = features // size
+
+    def kernel(order_ref, place_ref, value_ref, gain_ref, out, own):
+        j = pl.program_id(0)
+
         def step(c, carry):
             at = pl.ds(pl.multiple_of(c * 16, 16), 16)
             value = value_ref[at, :].astype(f32)
             scale = lax.rsqrt(jnp.mean(value * value, axis=1, keepdims=True) + epsilon)
-            out_ref[at, :] = (value * scale * gain_ref[...]).astype(bf16)
+            for r in range(groups):
+                to = slice(r * size, (r + 1) * size)
+                start = pl.multiple_of(order_ref[r] * size, size)
+                part = value_ref[at, pl.ds(start, size)].astype(f32)
+                out[at, to] = (part * scale * gain_ref[:, to]).astype(bf16)
             return carry
 
-        lax.fori_loop(0, value_ref.shape[0] // 16, step, 0)
-
-    block = pl.BlockSpec((total // 4, features), lambda g: (g, 0))
-    return call(
+        lax.fori_loop(0, rows // 16, step, 0, unroll=2)
+
+        @pl.when(j == place_ref[0])
+        def _():
+            for r in range(groups):
+                start = pl.multiple_of(order_ref[r] * size, size)
+                own[:, r * size : (r + 1) * size] = value_ref[:, pl.ds(start, size)]
+
+    block = pl.BlockSpec((rows, features), lambda g, *_: (g, 0))
+    return pl.pallas_call(
         kernel,
-        "normalize",
-        (4,),
-        [block, fixed((1, features))],
-        block,
-        jax.ShapeDtypeStruct((total, features), bf16),
-    )(values, gain.reshape(1, features))
+        grid_spec=pltpu.PrefetchScalarGridSpec(
+            num_scalar_prefetch=2,
+            grid=(4,),
+            in_specs=[block, fixed((1, features))],
+            out_specs=[block, fixed((rows, features))],
+        ),
+        out_shape=[
+            jax.ShapeDtypeStruct((total, features), bf16),
+            jax.ShapeDtypeStruct((rows, features), bf16),
+        ],
+        compiler_params=pltpu.CompilerParams(vmem_limit_bytes=vmem_bytes),
+        cost_estimate=light,
+        name="prepare",
+    )(order, place, whole, gain.reshape(1, features))
 
 
 def move_columns(blocks, order, size):
@@ -591,14 +820,16 @@
         places = jnp.where(index % 2 == 0, index // 2, self.count - 1 - index // 2)
         return (places - self.place + self.count) % self.count
 
-    def direct(self, blocks):
-        total = blocks[0]
-        for r in range(1, self.count):
-            pairs = [
-                (self.order[i], self.order[(i + r) % self.count]) for i in range(self.count)
-            ]
-            total = total + lax.ppermute(blocks[r], "dp", pairs)
-        return total
+    def normal_in(self, rows, place, size, gain):
+        if size % 128 == 0:
+            return prepare(rows, self.block_of, place, size, gain)
+        whole = self.columns_in([rows], size)
+        value = whole.astype(f32)
+        scale = lax.rsqrt(jnp.mean(value * value, axis=1, keepdims=True) + epsilon)
+        own = whole.shape[0] // 4
+        return (value * scale * gain).astype(bf16), lax.dynamic_slice_in_dim(
+            whole, place[0] * own, own, axis=0
+        )
 
     def columns_in(self, blocks, size):
         if size % 128 == 0:
@@ -667,15 +898,15 @@
 
     def operand(self, way, hop, gate):
         distance = self.hops[way] - hop
-        value = self.part(distance if way == 1 else self.total - distance)
+        value = self.part[distance if way == 1 else self.total - distance]
         if hop:
             (got,) = gate(self.got[way])
-            value = value + got.astype(f32)
-        return value.astype(bf16)
+            value = (value.astype(f32) + got.astype(f32)).astype(bf16)
+        return value
 
     def result(self, gate):
         got = gate(*self.got)
-        return self.part(0) + got[0].astype(f32) + got[1].astype(f32)
+        return self.part[0].astype(f32) + got[0].astype(f32) + got[1].astype(f32)
 
 
 class Lanes:
@@ -706,7 +937,7 @@
     def start(self, way, chain, hop):
         (operand,) = self.gate(chain.operand(way, hop, self.gate))
         self.mark(operand)
-        self.now += chain.work + 1.5
+        self.now += chain.work + 2.0
         value = lax.ppermute(operand, "dp", self.ring.pairs[way])
         begin = max(self.now, self.link[way])
         self.link[way] = begin + operand.size / 22000.0
@@ -738,6 +969,10 @@
             time = max(time, self.now)
         self.now = max(self.now, time)
 
+    def serve(self, times):
+        for _ in range(2 * times):
+            self.step(float("inf"))
+
     def until(self, *chains):
         while any(chain.left for chain in chains):
             assert self.step(float("inf"))
@@ -753,17 +988,20 @@
 
 
 def tensor_gather(own):
-    across = lax.ppermute(own, "tensor", chip_pairs)
-    sibling = lax.ppermute(own, "tensor", core_pairs)
-    far = lax.ppermute(across, "tensor", core_pairs)
-    return [own, sibling, across, far]
+    return lax.all_gather(own, "tensor", axis=0, tiled=True)
+
+
+def tensor_reduce(whole):
+    return lax.psum_scatter(whole, "tensor", scatter_dimension=0, tiled=True)
 
 
 def tensor_scatter(blocks):
     own, sibling, across, far = blocks
     far = lax.ppermute(far, "tensor", core_pairs)
+    sibling, far = lax.optimization_barrier((sibling, far))
     sibling = lax.ppermute(sibling, "tensor", core_pairs)
     across = (across.astype(f32) + far.astype(f32)).astype(bf16)
+    across, sibling = lax.optimization_barrier((across, sibling))
     return own, sibling, across, lax.ppermute(across, "tensor", chip_pairs)
 
 
@@ -784,8 +1022,7 @@
 def norm_backward(values, scale, gain, grad):
     weighted = grad * gain
     inner = jnp.mean(weighted * values, axis=-1, keepdims=True)
-    row_grad = scale * weighted - values * (scale * scale * scale * inner)
-    return row_grad, jnp.sum(grad * values * scale, axis=0)
+    return scale * weighted - values * (scale * scale * scale * inner)
 
 
 def body(
@@ -821,20 +1058,26 @@
     units = gate_weight.shape[1]
     place = lax.axis_index("tensor").astype(jnp.int32).reshape(1)
 
+    table_rows = gate_blocks * piece
+    wide = 256
     columns = jnp.stack(
         [conv_weight[k] for k in range(taps)] + [conv_bias, rate_bias, entry_bias, decay_param],
         axis=-1,
     )
-    table = jnp.concatenate([rate_weight, entry_weight, columns], axis=-1)
-    table = table.reshape(gate_blocks * piece, table.shape[-1])
-    table_rows, table_columns = table.shape
-    wide = -(-table_columns // 128) * 128
-    high = -(-(table_rows + 2) // 16) * 16
-    gains = jnp.pad(jnp.stack([gain_mixer, gain_mlp]), ((0, 0), (0, wide - shard)))
+
+    def padded(rows):
+        return jnp.pad(rows, ((0, 0), (0, wide - rows.shape[1])))
+
     table = jnp.concatenate(
-        [jnp.pad(table, ((0, 0), (0, wide - table_columns))), gains], axis=0
-    )
-    table = jnp.pad(table, ((0, high - table_rows - 2), (0, 0)))
+        [
+            padded(rate_weight.reshape(table_rows, block_width)),
+            padded(entry_weight.reshape(table_rows, block_width)),
+            padded(columns.reshape(table_rows, taps + 4)),
+            padded(jnp.stack([gain_mixer, gain_mlp])),
+        ],
+        axis=0,
+    )
+    table = jnp.pad(table, ((0, shard - 3 * table_rows - 2), (0, 0)))
 
     masks = []
     for offset in range(1, taps):
@@ -847,8 +1090,8 @@
 
     half = units // 2
     halves = (slice(0, half), slice(half, units))
-    small_chain = Gather(ring, table, True, 0)
-    pair_chain = Gather(ring, jnp.concatenate([branch_weight, input_weight], axis=1), False, 0)
+    table_chain = Gather(ring, table, False, 0)
+    pair_chains = [Gather(ring, branch_weight, True, 0), Gather(ring, input_weight, False, 0)]
     output_chain = Gather(ring, output_weight, True, 1)
     gated_chains = [
         Gather(
@@ -860,71 +1103,60 @@
         for at in halves
     ]
     down_chains = [Gather(ring, down_weight[at], at.start == 0, 1) for at in halves]
-    input_blocks = tensor_gather(inputs)
-    lanes.add(pair_chain, small_chain, output_chain, *gated_chains, *down_chains)
-    lanes.catch_up(12.0)
-    cotangent_blocks = tensor_gather(cotangent)
-
-    lanes.until(small_chain)
-    tables = jnp.concatenate(small_chain.blocks, axis=0)
-    (tables,) = lanes.gate(tables)
-    by_block = tables.reshape(dp, high, wide)
-    gain_one = by_block[:, table_rows, :shard].reshape(features).astype(f32)
-    gain_two = by_block[:, table_rows + 1, :shard].reshape(features).astype(f32)
-    channel = jnp.arange(width)
-    owner = (channel % block_width) // piece
-    source = ring.steps_to(owner) * high + (channel // block_width) * piece + channel % piece
-    mover = (source[:, None] == jnp.arange(dp * high)[None, :]).astype(bf16)
-    whole_table = dot(mover, tables).astype(bf16)
-    gate_column = jnp.arange(2 * width)
-    picked = (gate_column // width) * block_width + gate_column % block_width
-    spreader = (jnp.arange(wide)[:, None] == picked[None, :]).astype(bf16)
-    same_block = (channel // block_width)[:, None] == (
-        (gate_column % width) // block_width
-    )[None, :]
-    gates = jnp.where(same_block, dot(whole_table, spreader), 0.0).astype(bf16)
-    picker = (jnp.arange(wide)[None, :] == (2 * block_width + jnp.arange(8))[:, None]).astype(bf16)
-    small = dot_back(picker, whole_table)
+    lanes.now = 10.0
+    input_rows = tensor_gather(inputs)
+    lanes.add(pair_chains[0], table_chain, pair_chains[1], output_chain, *gated_chains, *down_chains)
+    cotangent_rows = tensor_gather(cotangent)
+
+    lanes.until(table_chain)
+    gates, small, gains = unpack_tables(
+        lanes.gate(*table_chain.blocks),
+        ring.block_of,
+        width,
+        piece,
+        block_width,
+    )
+    gain_one, gain_two = gains[0], gains[1]
     decay_full = small[7:8]
     small = jnp.concatenate([small[:7], -lru_scale * jax.nn.softplus(-decay_full)], axis=0)
-
-    token_rows = ring.columns_in(input_blocks, shard)
-    mixer_rows = normalize(token_rows, gain_one)
+    mixer_rows, tokens_low = ring.normal_in(input_rows, place, shard, gain_one)
+    lanes.did(18.0, mixer_rows)
+    lanes.until(*pair_chains)
+    (mixer_rows,) = lanes.gate(mixer_rows)
+
     rows = inputs.shape[0]
-    lanes.did(25.0, mixer_rows, gates, small)
-    lanes.until(pair_chain)
-    (mixer_rows,) = lanes.gate(mixer_rows)
-    pre = collect(mixer_rows, [pair_chain.pieces()], False, "mixer_in")
-    lanes.did(11.0, pre)
+    start = jnp.zeros((1,), jnp.int32)
+    pair_weights = [chain.pieces() for chain in pair_chains]
+    pre = collect(mixer_rows, pair_weights, width, False, "mixer_in")
+    lanes.did(12.0, pre)
     (pre,) = lanes.gate(pre)
-    mixer_low, mixed, rate, entry, state = core_forward(place, pre, masks, gates, small, tensor)
+    mixer_low, mixed, rate, entry, state = core_forward(start, pre, masks, gates, small, tensor)
     lanes.did(21.0, mixer_low)
     lanes.until(output_chain)
     output_pieces = output_chain.pieces()
     (mixer_low,) = lanes.gate(mixer_low)
-    blocks = spread([(mixer_low, 0)], [output_pieces], 3, 4, False, "mixer_out")[::-1]
-    parts = tensor_scatter(blocks)
-    lanes.did(11.0, parts[2])
-    arrival = lanes.now + 26.0
-    (moved,) = lanes.gate(cotangent_blocks[0])
-    cotangent_rows = ring.columns_in([moved] + cotangent_blocks[1:], shard)
+    mixer_out = spread([(mixer_low, 0, width)], [output_pieces], place, (), False, "mixer_out")
+    lanes.did(9.0, mixer_out)
+    mixer_sum = tensor_reduce(mixer_out)
+    arrival = lanes.now + 46.0
+    (cotangent_rows,) = lanes.gate(cotangent_rows)
+    cotangent_rows = ring.columns_in([cotangent_rows], shard)
     lanes.did(5.0, cotangent_rows)
     lanes.catch_up(arrival)
-    parts = lanes.gate(*parts)
-    tokens = token_rows[:rows].astype(f32)
-    middle = tokens + summed(parts)
+    (mixer_sum,) = lanes.gate(mixer_sum)
+    tokens = tokens_low.astype(f32)
+    middle = tokens + mixer_sum.astype(f32)
     scale_two = row_scale(middle)
-    mlp_blocks = tensor_gather((middle * scale_two * gain_two).astype(bf16))
-    lanes.did(5.0, mlp_blocks[0])
-    lanes.catch_up(lanes.now + 28.0)
-    mlp_blocks = lanes.gate(*mlp_blocks)
-    mlp_rows = jnp.concatenate(mlp_blocks, axis=0)
-    lanes.did(5.0, mlp_rows)
+    mlp_own = (middle * scale_two * gain_two).astype(bf16)
+    lanes.did(5.0, mlp_own)
+    mlp_rows = tensor_gather(mlp_own)
+    lanes.catch_up(lanes.now + 34.0)
+    (mlp_rows,) = lanes.gate(mlp_rows)
 
     def columns_of(array, r):
         return lax.slice_in_dim(array, r * shard, (r + 1) * shard, axis=1)
 
-    hidden, acts, slopes, down_scatters = [], [], [], []
+    hidden, acts, slopes = [], [], []
     for h in range(2):
         lanes.until(gated_chains[h])
         (gated,) = lanes.gate(mlp_rows)
@@ -932,14 +1164,13 @@
         hidden.append(one)
         acts.append(two)
         slopes.append(three)
-        down_scatters.append(
-            Scatter(
-                ring,
-                lambda r, one=one: dot_rows(one, columns_of(cotangent_rows, r)),
-                h == 1,
-            )
-        )
-        lanes.did(12.0, one)
+        lanes.did(13.5, one)
+    lefts = lanes.gate(*hidden)
+    down_scatters = [
+        Scatter(ring, part, h == 1)
+        for h, part in enumerate(weight_grads(lefts, cotangent_rows, dp, False, "down_grads"))
+    ]
+    lanes.did(13.5, down_scatters[0].part[0])
     lanes.add(*down_scatters)
     gated_lows, gated_scatters = [], []
     for h in range(2):
@@ -947,112 +1178,131 @@
         (gated,) = lanes.gate(cotangent_rows)
         low = gated_backward(gated, down_chains[h].pieces(), acts[h], slopes[h])
         gated_lows.append(low)
-        gated_scatters.append(
-            Scatter(
-                ring,
-                lambda r, low=low: dot_rows(columns_of(mlp_rows, r), low),
-                h == 0,
-            )
-        )
         lanes.did(8.5, low)
-    lanes.add(*gated_scatters)
+    (gated,) = lanes.gate(gated_lows[0])
+    gated_scatters.append(
+        Scatter(ring, weight_grads([mlp_rows], gated, dp, True, "gated_grads")[0], True)
+    )
+    lanes.did(14.0, gated_scatters[0].part[0])
+    lanes.add(gated_scatters[0])
     weights = [chain.pieces() for chain in gated_chains]
 
-    def lefts():
-        return [(low, 0) for low in lanes.gate(*gated_lows)]
-
-    far, across = spread(lefts(), weights, 3, 2, True, "mlp_in_grad")
-    lanes.did(14.0, far)
-    sibling, own = spread(lefts(), weights, 1, 2, True, "mlp_in_grad")
-    parts = tensor_scatter([own, sibling, across, far])
-    lanes.did(14.0, own)
-    lanes.catch_up(lanes.now + 28.0)
-    parts = lanes.gate(*parts)
-    middle_norm_grad, gain_two_part = norm_backward(middle, scale_two, gain_two, summed(parts))
+    lefts = [(low, 0, 2 * half) for low in lanes.gate(*gated_lows)]
+    mlp_in_grad = spread(lefts, weights, place, (), True, "mlp_in_grad")
+    lanes.did(20.5, mlp_in_grad)
+    mlp_in_grad = tensor_reduce(mlp_in_grad)
+    arrival = lanes.now + 46.0
+    (gated,) = lanes.gate(gated_lows[1])
+    gated_scatters.append(
+        Scatter(ring, weight_grads([mlp_rows], gated, dp, True, "gated_grads")[0], False)
+    )
+    lanes.did(14.0, gated_scatters[1].part[0])
+    lanes.add(gated_scatters[1])
+    lanes.catch_up(arrival)
+    (mlp_in_grad,) = lanes.gate(mlp_in_grad)
+    middle_norm_grad = norm_backward(middle, scale_two, gain_two, mlp_in_grad.astype(f32))
     middle_grad = (
-        lax.slice_in_dim(cotangent_rows, 0, rows, axis=0).astype(f32) + middle_norm_grad
-    )
-    residual_blocks = tensor_gather(middle_grad.astype(bf16))
-    lanes.did(5.0, residual_blocks[0])
-    lanes.catch_up(lanes.now + 26.0)
-    residual_blocks = lanes.gate(*residual_blocks)
-    residual_rows = jnp.concatenate(residual_blocks, axis=0)
-    lanes.did(5.0, residual_rows)
-
+        lax.dynamic_slice_in_dim(cotangent_rows, place[0] * rows, rows, axis=0).astype(f32)
+        + middle_norm_grad
+    )
+    residual_own = middle_grad.astype(bf16)
+    lanes.did(6.0, residual_own)
+    residual_rows = tensor_gather(residual_own)
+    arrival = lanes.now + 34.0
+    late = [(low, 0, half) for low in lanes.gate(*hidden)]
+    mlp_out = spread(
+        late, [chain.pieces() for chain in down_chains], place, (), False, "mlp_out"
+    )
+    lanes.did(13.0, mlp_out)
+    lanes.catch_up(arrival)
+    mlp_out, residual_rows = lanes.gate(mlp_out, residual_rows)
+    mlp_sum = tensor_reduce(mlp_out)
+
+    mixer_grad = collect(residual_rows, [output_pieces], width, True, "mixer_grad")
+    lanes.did(8.0, mixer_grad)
     (residual_rows,) = lanes.gate(residual_rows)
-    mixer_grad = collect(residual_rows, [output_pieces], True, "mixer_grad")
-    lanes.did(8.0, mixer_grad)
+    output_scatter = Scatter(
+        ring, weight_grads([mixer_low], residual_rows, dp, False, "output_grads")[0], True
+    )
+    lanes.did(9.0, output_scatter.part[0])
+    lanes.add(output_scatter)
     (mixer_grad,) = lanes.gate(mixer_grad)
     pair_low, gate_grads, small_grads = core_backward(
-        place, mixer_grad, pre, mixed, rate, entry, state, masks, gates, small, tensor
+        start, mixer_grad, pre, mixed, rate, entry, state, masks, gates, small, tensor
     )
     lanes.did(28.0, pair_low)
-    output_scatter = Scatter(
-        ring, lambda r: dot_rows(mixer_low, columns_of(residual_rows, r)), True
-    )
-    whole_low = pair_low
-    pair_scatter = Scatter(ring, lambda r: dot_rows(columns_of(mixer_rows, r), whole_low), False)
-    lanes.add(output_scatter, pair_scatter)
+    decay_grad = lru_scale * small_grads[7:8] * jax.nn.sigmoid(-decay_full)
+    small_grads = jnp.concatenate([small_grads[:7], decay_grad], axis=0)
+    grad_tables = pack_tables(
+        gate_grads, small_grads, ring.block_of, dp, shard, piece, block_width
+    )
+    lanes.did(8.0, grad_tables[0])
+    (low,) = lanes.gate(pair_low)
+    pair_parts = weight_grads([mixer_rows], low, dp, True, "pair_grads", grad_tables)
+    pair_scatters = [Scatter(ring, part, h == 0) for h, part in enumerate(pair_parts)]
+    lanes.did(13.0, pair_parts[0][0])
+    lanes.add(*pair_scatters)
     (pair_low,) = lanes.gate(pair_low)
-    blocks = spread([(pair_low, 0)], [pair_chain.pieces()], 3, 4, True, "mixer_in_grad")[::-1]
-    parts = tensor_scatter(blocks)
-    lanes.did(14.0, parts[2])
-    arrival = lanes.now + 26.0
-
-    (gate_grads,) = lanes.gate(gate_grads)
-    decay_grad = lru_scale * small_grads[7:8] * jax.nn.sigmoid(-decay_full)
-    small_grads = jnp.concatenate([small_grads[:7], decay_grad], axis=0).astype(bf16)
-    grad_table = dot_back(
-        jnp.where(same_block, gate_grads, 0.0).astype(bf16), spreader
-    ) + dot_rows(small_grads, picker)
-    grad_tables = dot_rows(mover, grad_table.astype(bf16)).astype(bf16)
-    table_scatter = Scatter(
-        ring,
-        lambda r: lax.slice_in_dim(grad_tables, r * high, (r + 1) * high, axis=0).astype(f32),
+    mixer_in_grad = spread(
+        [(pair_low, 0, width), (pair_low, 1, width)],
+        pair_weights,
+        place,
+        (),
         True,
-    )
-    lanes.did(12.0, grad_tables)
-    lanes.add(table_scatter)
+        "mixer_in_grad",
+    )
+    lanes.did(12.0, mixer_in_grad)
+    mixer_in_grad = tensor_reduce(mixer_in_grad)
+    arrival = lanes.now + 48.0
+    (mlp_sum,) = lanes.gate(mlp_sum)
+    layer_out = ring.columns_out((middle + mlp_sum.astype(f32)).astype(bf16), shard)
+    lanes.did(6.0, layer_out)
     lanes.catch_up(arrival)
-    parts = lanes.gate(*parts)
-    tokens_norm_grad, gain_one_part = norm_backward(tokens, row_scale(tokens), gain_one, summed(parts))
+    (mixer_in_grad,) = lanes.gate(mixer_in_grad)
+    tokens_norm_grad = norm_backward(
+        tokens, row_scale(tokens), gain_one, mixer_in_grad.astype(f32)
+    )
     inputs_grad = ring.columns_out((middle_grad + tokens_norm_grad).astype(bf16), shard)
-    gain_parts = tensor_sum(jnp.stack([gain_one_part, gain_two_part]))
-    gain_sums = ring.direct([columns_of(gain_parts, r) for r in range(dp)])
-    lanes.did(8.0, inputs_grad)
-
-    late = lanes.gate(*hidden)
-    blocks = spread(
-        [(low, 0) for low in late],
-        [chain.pieces() for chain in down_chains],
-        3,
-        4,
-        False,
-        "mlp_out",
-    )[::-1]
-    parts = tensor_scatter(blocks)
-    lanes.did(14.0, parts[2])
-    lanes.catch_up(lanes.now + 26.0)
-    parts = lanes.gate(*parts)
-    layer_out = ring.columns_out((middle + summed(parts)).astype(bf16), shard)
-    lanes.did(5.0, layer_out)
-    lanes.until(
-        *down_scatters, *gated_scatters, output_scatter, pair_scatter, table_scatter
-    )
+    lanes.did(9.0, inputs_grad)
+    lanes.until(*down_scatters, *gated_scatters, output_scatter, *pair_scatters)
 
     free = lambda *values: values
-    table_grad = table_scatter.result(free)[:table_rows].reshape(gate_blocks, piece, wide)
-    rate_wgrad = table_grad[:, :, :block_width]
-    entry_wgrad = table_grad[:, :, block_width : 2 * block_width]
-    singles = [table_grad[:, :, 2 * block_width + k] for k in range(taps + 4)]
-    pair_wgrad = pair_scatter.result(free)
+    pair_wgrads = [scatter.result(free) for scatter in pair_scatters]
+    table_grad = jnp.concatenate([wgrad[:, width:] for wgrad in pair_wgrads], axis=1)
+    pair_wgrads = [wgrad[:, :width] for wgrad in pair_wgrads]
+    rate_wgrad, entry_wgrad, column_grads = [
+        table_grad[k * table_rows : (k + 1) * table_rows].reshape(gate_blocks, piece, wide)
+        for k in range(3)
+    ]
+    rate_wgrad = rate_wgrad[:, :, :block_width]
+    entry_wgrad = entry_wgrad[:, :, :block_width]
+    singles = [column_grads[:, :, k] for k in range(taps + 4)]
     gated_wgrads = [scatter.result(free) for scatter in gated_scatters]
+
+    def gain_grad(gain, own_weights, wgrads):
+        total = sum(
+            jnp.sum(weight[:, : wgrad.shape[1]].astype(f32) * wgrad, axis=1)
+            for weight, wgrad in zip(own_weights, wgrads)
+        )
+        return total / gain.astype(f32)
+
+    gain_grads = tensor_sum(
+        jnp.stack(
+            [
+                gain_grad(
+                    gain_mixer,
+                    [branch_weight, input_weight],
+                    pair_wgrads,
+                ),
+                gain_grad(gain_mlp, [chain.blocks[0] for chain in gated_chains], gated_wgrads),
+            ]
+        )
+    )
     return (
         layer_out,
         inputs_grad,
-        gain_sums[0],
-        pair_wgrad[:, :width],
-        pair_wgrad[:, width:],
+        gain_grads[0],
+        *pair_wgrads,
         jnp.stack(singles[:taps]),
         singles[taps],
         rate_wgrad,
@@ -1061,7 +1311,7 @@
         singles[taps + 2],
         singles[taps + 3],
         output_scatter.result(free),
-        gain_sums[1],
+        gain_grads[1],
         jnp.concatenate([wgrad[:, :half] for wgrad in gated_wgrads], axis=1),
         jnp.concatenate([wgrad[:, half:] for wgrad in gated_wgrads], axis=1),
         jnp.concatenate([scatter.result(free) for scatter in down_scatters], axis=0),

time: 787 us -> 702 us (0.89)
  matrix products: 105 us -> 0 us
  waiting for transfers between devices: 277 us -> 208 us
  Pallas kernels: 196 us -> 262 us
  other arithmetic: 38.9 us -> 73.2 us
  between operations: 2.53 us -> 15.9 us
  starting transfers between devices: 130 us -> 118 us
  local copies, waits for them, and re-layouts: 27.2 us -> 15.9 us
    dot_general x53 -> x0, matrix products: 105 us -> none  [the longest x49 99.9 us: dot_rows(): lax.dot_general(left, right, (((0,), (0,)), ((), ())), preferred_element_...]
    pallas_call x6 -> x12, Pallas kernels: 68.7 us -> 138 us  [the longest x5 65.1 us: weight_grads(): call(kernel, name, (pieces,), in_specs, [fixed(shape) for shape in shapes...]
    ppermute x31 -> x0, waiting for transfers between devices: 40.2 us -> none  [the longest x4 21.4 us: tensor_gather(): across = lax.ppermute(own, 'tensor', chip_pairs)]
    ppermute x98 -> x105, waiting for transfers between devices: 236 us -> 198 us  [start(): value = lax.ppermute(operand, 'dp', self.ring.pairs[way])]
    ppermute x31 -> x0, starting transfers between devices: 22.6 us -> none  [the longest x7 11.5 us: direct(): total = total + lax.ppermute(blocks[r], 'dp', pairs)]
    convert_element_type x18 -> x38, other arithmetic: 18.2 us -> 36.6 us  [the longest x35 29.4 us: operand(): value = (value.astype(f32) + got.astype(f32)).astype(bf16)]
    ppermute x98 -> x105, starting transfers between devices: 107 us -> 117 us  [start(): value = lax.ppermute(operand, 'dp', self.ring.pairs[way])]
    pallas_call x4 -> x3, Pallas kernels: 17.1 us -> 12.4 us  [move_columns(): pl.pallas_call(kernel, grid_spec=pltpu.PrefetchScalarGridSpec(num_scalar_...]
  transfers between devices with their start and end apart: 131 -> 115, of which waited for: 49 -> 50; matrix products, arithmetic and copies ran while one was open for 20% -> 10% of each run, Pallas kernels for 23% -> 34%
where the time goes in v3:
time: 702 us; the launch traced here: 693 us
  Pallas kernels  262 us (37%)
  waiting for transfers between devices  208 us (30%)
  starting transfers between devices  118 us (17%)
  other arithmetic  73.2 us (10%)
  local copies, waits for them, and re-layouts  15.9 us (2%)
  between operations  15.9 us (2%)
    ppermute x105, waiting for transfers between devices, start(): value = lax.ppermute(operand, 'dp', self.ring.pairs[way])  198 us
    ppermute x105, starting transfers between devices, start(): value = lax.ppermute(operand, 'dp', self.ring.pairs[way])  117 us
    pallas_call x5, Pallas kernels, weight_grads(): call(kernel, name, (pieces,), in_specs, [fixed(shape) for shape in shapes...  65.1 us
    pallas_call x4, Pallas kernels, spread(): pl.pallas_call(kernel, grid_spec=pltpu.PrefetchScalarGridSpec(num_scalar_...  50.2 us
    convert_element_type x35, other arithmetic, operand(): value = (value.astype(f32) + got.astype(f32)).astype(bf16)  29.4 us
    pallas_call x1, Pallas kernels, core_backward(): pl.pallas_call(core_backward_kernel, grid_spec=pltpu.PrefetchScalarGridSp...  28.6 us
    pallas_call x2, Pallas kernels, gated_forward(): call(kernel, 'gated_forward', (4,), [pl.BlockSpec((rows, features), lambd...  25.9 us
    pallas_call x1, Pallas kernels, core_forward(): pl.pallas_call(core_forward_kernel, grid_spec=pltpu.PrefetchScalarGridSpe...  20.8 us
  transfers between devices with their start and end apart: 115, of which 50 were waited for; matrix products, arithmetic and copies ran while one was open for 10% of the time, Pallas kernels for 34%

profile of v3, /device:TPU:0, one launch (start us, length us, event | category | flops | bytes accessed | tf_op | source)
XLA Modules:
  0.0 692.8 jit_solution(12143932916867239514)
XLA Ops:
  15.0 5.6 collective-permute-done.1.refs_2_.refs_3_
  27.6 6.8 collective-permute-done.4.refs_7_
  52.5 3.8 collective-permute-done.15.refs_5_.refs_6_
  65.4 6.6 unpack_tables.1
  73.6 8.3 %prepare.1 = (bf16[1024,2048]{1,0:T(8,128)(2,1)}, bf16[256,2048]{1,0:T(8,128)(2,1)}) custom-call(s32[8]{0:T(128)} %compare_select_fusion.5.order_ref, s32[1]{0:T(128)} %bitcast.place_ref, bf16[1024,2048]{1,0:T(8,128)(2,1)} %all-gather.5.cloned.1.call-done.value_ref, f32[1,2048]{1,0:T(1,128)} %get-tuple-element.602.gain_ref), custom_call_target="tpu_custom_call" | custom-call | flops 6000000000 | bytes 30000000 | tf_op jit(solution)/shard_map/prepare/pallas_call | solution.py:755
  86.5 6.4 collective-permute-done.19.refs_3_
  95.8 4.0 collective-permute-done.25.refs_12_.refs_13_
  102.0 3.6 collective-permute-done.23.refs_4_
  108.6 11.3 %mixer_in.1.branch.entry_pre.entry_tail = f32[1024,1280]{1,0:T(8,128)} custom-call(bf16[1024,2048]{1,0:T(8,128)(2,1)} %get-tuple-element.308.refs_0_, bf16[256,640]{1,0:T(8,128)(2,1)} %refs_2_.1, bf16[256,640]{1,0:T(8,128)(2,1)} %copy-done.106, bf16[256,640]{1,0:T(8,128)(2,1)} %copy-done.108, bf16[256,640]{1,0:T(8,128)(2,1)} %collective-permute-done.11.refs_4_.refs_5_, ...), custom_call_target="tpu_custom_call" | custom-call | flops 6000000000 | bytes 30000000 | tf_op jit(solution)/shard_map/mixer_in/pallas_call | solution.py:466
  124.4 20.8 %core_forward.1 = (bf16[1024,640]{1,0:T(8,128)(2,1)}, f32[1024,640]{1,0:T(8,128)}, f32[1024,640]{1,0:T(8,128)}, f32[1024,640]{1,0:T(8,128)}, f32[1024,640]{1,0:T(8,128)}) custom-call(s32[1]{0:T(128)} %constant.88.clone.1.place, f32[1024,1280]{1,0:T(8,128)} %mixer_in.1.branch.entry_pre.entry_tail, f32[1024,1280]{1,0:T(8,128)} %mixer_in.1.branch.entry_pre.entry_tail, ...), custom_call_target="tpu_custom_call" | custom-call | flops 6000000000 | bytes 30000000 | tf_op jit(solution)/shard_map/core_forward/pallas_call | solution.py:260
  146.0 7.1 %mixer_out.1 = bf16[1024,2048]{1,0:T(8,128)(2,1)} custom-call(s32[1]{0:T(128)} %bitcast.place_ref, bf16[1024,640]{1,0:T(8,128)(2,1)} %get-tuple-element.319.refs_0_, bf16[640,256]{1,0:T(8,128)(2,1)} %refs_1_.5, bf16[640,256]{1,0:T(8,128)(2,1)} %collective-permute-done.17.refs_2_, bf16[640,256]{1,0:T(8,128)(2,1)} %collective-permute-done.19.refs_3_, ...), custom_call_target="tpu_custom_call" | custom-call | flops 6000000000 | bytes 30000000 | tf_op jit(solution)/shard_map/mixer_out/pallas_call | solution.py:428
  157.2 6.3 move_columns.3.refs_2_.refs_0_
  163.5 8.4 %collective-permute-done.33.refs_2_.refs_11_ = bf16[256,1536]{1,0:T(8,128)(2,1)S(1)} collective-permute-done((bf16[256,1536]{1,0:T(8,128)(2,1)S(1)}, bf16[256,1536]{1,0:T(8,128)(2,1)S(1)}, u32[]{:S(2)}, u32[]{:S(2)}) %collective-permute-start.33) | collective-permute-done | bytes 786464 | tf_op jit(solution)/shard_map/ppermute | solution.py:941
  176.0 4.4 collective-permute-done.37.refs_4_.refs_5_
  182.0 6.7 collective-permute-done.35.refs_3_.refs_12_
  190.4 7.7 %reduce-scatter.5.cloned.1.call-done = bf16[256,2048]{1,0:T(8,128)(2,1)} async-done(((bf16[1024,2048]{1,0:T(8,128)(2,1)}), bf16[256,2048]{1,0:T(8,128)(2,1)}) %reduce-scatter.5.cloned.1.call-update) | async-done | bytes 1048592 | tf_op jit(solution)/shard_map/reduce_scatter | solution.py:995
  205.6 16.6 %collective-permute-done.41.refs_5_.refs_6_ = bf16[256,1536]{1,0:T(8,128)(2,1)S(1)} collective-permute-done((bf16[256,1536]{1,0:T(8,128)(2,1)}, bf16[256,1536]{1,0:T(8,128)(2,1)S(1)}, u32[]{:S(2)}, u32[]{:S(2)}) %collective-permute-start.41) | collective-permute-done | bytes 786464 | tf_op jit(solution)/shard_map/ppermute | solution.py:941
  225.8 6.4 collective-permute-done.39.refs_8_.refs_9_
  232.7 6.4 collective-permute-done.38.refs_4_.refs_13_
  240.6 13.0 %gated_forward.2 = (bf16[1024,768]{1,0:T(8,128)(2,1)}, bf16[1024,768]{1,0:T(8,128)(2,1)}, bf16[1024,768]{1,0:T(8,128)(2,1)}) custom-call(bf16[1024,2048]{1,0:T(8,128)(2,1)} %all-gather.9.cloned.1.call-done.refs_0_, bf16[256,1536]{1,0:T(8,128)(2,1)} %copy-done.10, bf16[256,1536]{1,0:T(8,128)(2,1)} %copy-done.14, ...), custom_call_target="tpu_custom_call" | custom-call | flops 6000000000 | bytes 30000000 | tf_op jit(solution)/shard_map/gated_forward/pallas_call | solution.py:504
  257.7 12.9 %gated_forward.3 = (bf16[1024,768]{1,0:T(8,128)(2,1)}, bf16[1024,768]{1,0:T(8,128)(2,1)}, bf16[1024,768]{1,0:T(8,128)(2,1)}) custom-call(bf16[1024,2048]{1,0:T(8,128)(2,1)} %all-gather.9.cloned.1.call-done.refs_0_, bf16[256,1536]{1,0:T(8,128)(2,1)} %copy-done.11, bf16[256,1536]{1,0:T(8,128)(2,1)} %copy-done.15, bf16[256,1536]{1,0:T(8,128)(2,1)} %copy-done.16, ...), custom_call_target="tpu_custom_call" | custom-call | flops 6000000000 | bytes 30000000 | tf_op jit(solution)/shard_map/gated_forward/pallas_call | solution.py:504
  274.2 14.1 %down_grads.1 = (bf16[768,256]{1,0:T(8,128)(2,1)}, bf16[768,256]{1,0:T(8,128)(2,1)}, bf16[768,256]{1,0:T(8,128)(2,1)}, bf16[768,256]{1,0:T(8,128)(2,1)}, bf16[76...) custom-call(bf16[1024,768]{1,0:T(8,128)(2,1)} %get-tuple-element.427, ...), custom_call_target="tpu_custom_call" | custom-call | flops 6000000000 | bytes 30000000 | tf_op jit(solution)/shard_map/down_grads/pallas_call | solution.py:586
  292.5 8.0 %collective-permute-done.51.refs_5_.refs_6_ = bf16[768,256]{1,0:T(8,128)(2,1)S(1)} collective-permute-done((bf16[768,256]{1,0:T(8,128)(2,1)S(1)}, bf16[768,256]{1,0:T(8,128)(2,1)S(1)}, u32[]{:S(2)}, u32[]{:S(2)}) %collective-permute-start.51) | collective-permute-done | bytes 393248 | tf_op jit(solution)/shard_map/ppermute | solution.py:941
  302.0 8.5 %gated_backward.2.refs_1_.refs_0_ = bf16[1024,1536]{1,0:T(8,128)(2,1)} custom-call(bf16[1024,2048]{1,0:T(8,128)(2,1)} %move_columns.3.refs_2_.refs_0_, bf16[768,256]{1,0:T(8,128)(2,1)} %get-tuple-element.328.refs_1_.refs_2_, bf16[768,256]{1,0:T(8,128)(2,1)} %collective-permute-done.45.refs_2_.refs_3_, bf16[768,256]{1,0:T(8,128)(2,1)} %copy-done.91, ...), custom_call_target="tpu_custom_call" | custom-call | flops 6000000000 | bytes 30000000 | tf_op jit(solution)/shard_map/gated_backward/pallas_call | solution.py:532
  313.7 3.6 collective-permute-done.58
  319.0 3.8 collective-permute-done.57.refs_5_.refs_14_
  327.4 8.5 %gated_backward.3.refs_1_ = bf16[1024,1536]{1,0:T(8,128)(2,1)} custom-call(bf16[1024,2048]{1,0:T(8,128)(2,1)} %move_columns.3.refs_2_.refs_0_, bf16[768,256]{1,0:T(8,128)(2,1)} %get-tuple-element.336.refs_1_.refs_10_, bf16[768,256]{1,0:T(8,128)(2,1)} %collective-permute-done.43.refs_2_.refs_11_, bf16[768,256]{1,0:T(8,128)(2,1)} %copy-done.93, ...), custom_call_target="tpu_custom_call" | custom-call | flops 6000000000 | bytes 30000000 | tf_op jit(solution)/shard_map/gated_backward/pallas_call | solution.py:532
  339.0 3.6 collective-permute-done.62
  344.3 13.6 %gated_grads.2 = (bf16[256,1536]{1,0:T(8,128)(2,1)}, bf16[256,1536]{1,0:T(8,128)(2,1)}, bf16[256,1536]{1,0:T(8,128)(2,1)}, bf16[256,1536]{1,0:T(8,128)(2,1)}, bf...) custom-call(bf16[1024,2048]{1,0:T(8,128)(2,1)} %all-gather.9.cloned., ...), custom_call_target="tpu_custom_call" | custom-call | flops 6000000000 | bytes 30000000 | tf_op jit(solution)/shard_map/gated_grads/pallas_call | solution.py:586
  359.6 20.1 %mlp_in_grad.1 = bf16[1024,2048]{1,0:T(8,128)(2,1)} custom-call(s32[1]{0:T(128)} %bitcast.place_ref, bf16[1024,1536]{1,0:T(8,128)(2,1)} %gated_backward.2.refs_1_.refs_0_, bf16[1024,1536]{1,0:T(8,128)(2,1)} %gated_backward.3.refs_1_, bf16[256,1536]{1,0:T(8,128)(2,1)} %copy-done.10, bf16[256,1536]{1,0:T(8,128)(2,1)} %copy-done.14, ...), custom_call_target="tpu_custom_call" | custom-call | flops 6000000000 | bytes 30000000 | tf_op jit(solution)/shard_map/mlp_in_grad/pallas_call | solution.py:428
  383.6 10.1 %collective-permute-done.70 = bf16[768,256]{1,0:T(8,128)(2,1)} collective-permute-done((bf16[768,256]{1,0:T(8,128)(2,1)}, bf16[768,256]{1,0:T(8,128)(2,1)}, u32[]{:S(2)}, u32[]{:S(2)}) %collective-permute-start.70) | collective-permute-done | bytes 393248 | tf_op jit(solution)/shard_map/ppermute | solution.py:941
  398.6 11.9 %collective-permute-done.68 = bf16[256,1536]{1,0:T(8,128)(2,1)} collective-permute-done((bf16[256,1536]{1,0:T(8,128)(2,1)}, bf16[256,1536]{1,0:T(8,128)(2,1)}, u32[]{:S(2)}, u32[]{:S(2)}) %collective-permute-start.68) | collective-permute-done | bytes 786464 | tf_op jit(solution)/shard_map/ppermute | solution.py:941
  412.4 13.7 %gated_grads.3 = (bf16[256,1536]{1,0:T(8,128)(2,1)}, bf16[256,1536]{1,0:T(8,128)(2,1)}, bf16[256,1536]{1,0:T(8,128)(2,1)}, bf16[256,1536]{1,0:T(8,128)(2,1)}, bf...) custom-call(bf16[1024,2048]{1,0:T(8,128)(2,1)} %all-gather.9.cloned., ...), custom_call_target="tpu_custom_call" | custom-call | flops 6000000000 | bytes 30000000 | tf_op jit(solution)/shard_map/gated_grads/pallas_call | solution.py:586
  429.4 6.3 collective-permute-done.74
  439.5 5.2 collective-permute-done.72
  456.3 12.0 %mlp_out.1 = bf16[1024,2048]{1,0:T(8,128)(2,1)} custom-call(s32[1]{0:T(128)} %bitcast.place_ref, bf16[1024,768]{1,0:T(8,128)(2,1)} %get-tuple-element.427.refs_0_, bf16[1024,768]{1,0:T(8,128)(2,1)} %get-tuple-element.428.refs_1_, bf16[768,256]{1,0:T(8,128)(2,1)} %get-tuple-element.328.refs_1_.refs_2_, ...), custom_call_target="tpu_custom_call" | custom-call | flops 6000000000 | bytes 30000000 | tf_op jit(solution)/shard_map/mlp_out/pallas_call | solution.py:428
  468.2 4.2 collective-permute-done.78
  476.7 6.1 collective-permute-done.77
  496.1 8.3 %mixer_grad.1.grad = f32[1024,640]{1,0:T(8,128)} custom-call(bf16[1024,2048]{1,0:T(8,128)(2,1)} %all-gather.11.cloned.1.call-done.refs_0_.refs_1_, bf16[640,256]{1,0:T(8,128)(2,1)} %refs_1_.5, bf16[640,256]{1,0:T(8,128)(2,1)} %collective-permute-done.17.refs_2_, bf16[640,256]{1,0:T(8,128)(2,1)} %collective-permute-done.19.refs_3_, ...), custom_call_target="tpu_custom_call" | custom-call | flops 6000000000 | bytes 30000000 | tf_op jit(solution)/shard_map/mixer_grad/pallas_call | solution.py:466
  504.4 9.6 %output_grads.1 = (bf16[640,256]{1,0:T(8,128)(2,1)}, bf16[640,256]{1,0:T(8,128)(2,1)}, bf16[640,256]{1,0:T(8,128)(2,1)}, bf16[640,256]{1,0:T(8,128)(2,1)}, bf16[...) custom-call(bf16[1024,640]{1,0:T(8,128)(2,1)} %get-tuple-element.319.refs_0, ...), custom_call_target="tpu_custom_call" | custom-call | flops 6000000000 | bytes 30000000 | tf_op jit(solution)/shard_map/output_grads/pallas_call | solution.py:586
  518.7 28.6 %core_backward.1 = (bf16[1024,1280]{1,0:T(8,128)(2,1)}, f32[640,1280]{1,0:T(8,128)}, f32[8,640]{1,0:T(8,128)}) custom-call(s32[1]{0:T(128)} %constant.88.clone.1.place, f32[1024,640]{1,0:T(8,128)} %mixer_grad.1.grad, f32[1024,1280]{1,0:T(8,128)} %mixer_in.1.branch.entry_pre.entry_tail, f32[1024,1280]{1,0:T(8,128)} %mixer_in.1.branch.entry_pre.entry_tail, ...), custom_call_target="tpu_custom_call" | custom-call | flops 6000000000 | bytes 30000000 | tf_op jit(solution)/shard_map/core_backward/pallas_call | solution.py:301
  554.3 7.3 %pack_tables.1 = (bf16[2048,128]{1,0:T(8,128)(2,1)}, bf16[2048,128]{1,0:T(8,128)(2,1)}) custom-call(s32[8]{0:T(128)} %compare_select_fusion.5.order_ref, f32[640,1280]{1,0:T(8,128)} %get-tuple-element.463.gate_ref, f32[8,640]{1,0:T(8,128)} %pad_maximum_fusion.9.small_ref), custom_call_target="tpu_custom_call" | custom-call | flops 6000000000 | bytes 30000000 | tf_op jit(solution)/shard_map/pack_tables/pallas_call | solution.py:712
  564.2 14.1 %pair_grads.1 = (bf16[256,768]{1,0:T(8,128)(2,1)}, bf16[256,768]{1,0:T(8,128)(2,1)}, bf16[256,768]{1,0:T(8,128)(2,1)}, bf16[256,768]{1,0:T(8,128)(2,1)}, bf16[25...) custom-call(bf16[1024,2048]{1,0:T(8,128)(2,1)} %get-tuple-element.30, ...), custom_call_target="tpu_custom_call" | custom-call | flops 6000000000 | bytes 30000000 | tf_op jit(solution)/shard_map/pair_grads/pallas_call | solution.py:586
  579.1 11.1 %mixer_in_grad.1 = bf16[1024,2048]{1,0:T(8,128)(2,1)} custom-call(s32[1]{0:T(128)} %bitcast.place_ref, bf16[1024,1280]{1,0:T(8,128)(2,1)} %get-tuple-element.485.refs_1_.refs_0_, bf16[1024,1280]{1,0:T(8,128)(2,1)} %get-tuple-element.485.refs_1_.refs_0_, bf16[256,640]{1,0:T(8,128)(2,1)} %refs_2_.1, bf16[256,640]{1,0:T(8,128)(2,1)} %copy-done.106, ...), custom_call_target="tpu_custom_call" | custom-call | flops 6000000000 | bytes 30000000 | tf_op jit(solution)/shard_map/mixer_in_grad/pallas_call | solution.py:428
  606.1 3.8 collective-permute-done.91
  613.6 4.8 collective-permute-done.95
  622.7 4.1 collective-permute-done.93
  646.0 6.1 collective-permute-done.99
  (590 shorter events, 252.7 us)
Async XLA Ops:
  7.3 66.3 %all-gather.5.cloned.1.call-start = ((), (), s32[]{:S(2)}) async-start(), calls=%async_computation.4 | async-start | bytes 5242880 | tf_op jit(solution)/shard_map/all_gather | solution.py:991
  8.1 149.2 %all-gather.7.cloned.1.call-start = ((), (), s32[]{:S(2)}) async-start(), calls=%async_computation.6 | async-start | bytes 5242880 | tf_op jit(solution)/shard_map/all_gather | solution.py:991
  8.8 189.3 %reduce-scatter.5.cloned.1.call-start = ((), (), s32[]{:S(2)}) async-start(), calls=%async_computation.5 | async-start | bytes 5242880 | tf_op jit(solution)/shard_map/reduce_scatter | solution.py:995
  56.4 25.5 %collective-permute-start.17 = (bf16[640,256]{1,0:T(8,128)(2,1)}, bf16[640,256]{1,0:T(8,128)(2,1)}, u32[]{:S(2)}, u32[]{:S(2)}) collective-permute-start(bf16[640,256]{1,0:T(8,128)(2,1)} %refs_1_.5), channel_id=1, source_target_pairs={{8,0},{16,8},{24,16},{28,24},{20,28},{12,20},{4,12},{0,4},{9,1},{1... | collective-permute-start | bytes 983048 | tf_op jit(solution)/shard_map/ppermute | solution.py:941
  59.9 23.2 %collective-permute-start.16 = (bf16[256,640]{1,0:T(8,128)(2,1)S(1)}, bf16[256,640]{1,0:T(8,128)(2,1)S(1)}, u32[]{:S(2)}, u32[]{:S(2)}) collective-permute-start(bf16[256,640]{1,0:T(8,128)(2,1)S(1)} %collective-permute-done.14.refs_16_.refs_17_), channel_id=1, source_target_pairs={{0,8},{8,16},{16,24},{24,28},{28,20},{20,12},{12,4},{4,0},{1,9},{9... | collective-permute-start | bytes 983048 | tf_op jit(solution)/shard_map/ppermute | solution.py:941
  63.4 20.9 %collective-permute-start.21 = (bf16[256,640]{1,0:T(8,128)(2,1)S(1)}, bf16[256,640]{1,0:T(8,128)(2,1)}, u32[]{:S(2)}, u32[]{:S(2)}) collective-permute-start(bf16[256,640]{1,0:T(8,128)(2,1)S(1)} %collective-permute-done.13.refs_10_.refs_11_), channel_id=1, source_target_pairs={{8,0},{16,8},{24,16},{28,24},{20,28},{12,20},{4,12},{0,4},{9,1},{1... | collective-permute-start | bytes 983048 | tf_op jit(solution)/shard_map/ppermute | solution.py:941
  64.6 21.0 %collective-permute-start.20 = (bf16[640,256]{1,0:T(8,128)(2,1)}, bf16[640,256]{1,0:T(8,128)(2,1)}, u32[]{:S(2)}, u32[]{:S(2)}) collective-permute-start(bf16[640,256]{1,0:T(8,128)(2,1)} %refs_1_.5), channel_id=1, source_target_pairs={{0,8},{8,16},{16,24},{24,28},{28,20},{20,12},{12,4},{4,0},{1,9},{9... | collective-permute-start | bytes 983048 | tf_op jit(solution)/shard_map/ppermute | solution.py:941
  99.8 21.8 %collective-permute-start.26 = (bf16[256,1536]{1,0:T(8,128)(2,1)S(1)}, bf16[256,1536]{1,0:T(8,128)(2,1)S(1)}, u32[]{:S(2)}, u32[]{:S(2)}) collective-permute-start(bf16[256,1536]{1,0:T(8,128)(2,1)S(1)} %pad_maximum_fusion.3.refs_1_.refs_2_), channel_id=1, source_target_pairs={{8,0},{16,8},{24,16},{28,24},{20,28},{12,20},{4,12},{0,4},{9,1},{1... | collective-permute-start | bytes 2359304 | tf_op jit(solution)/shard_map/ppermute | solution.py:941
  107.9 37.4 %collective-permute-start.30 = (bf16[256,1536]{1,0:T(8,128)(2,1)S(1)}, bf16[256,1536]{1,0:T(8,128)(2,1)}, u32[]{:S(2)}, u32[]{:S(2)}) collective-permute-start(bf16[256,1536]{1,0:T(8,128)(2,1)S(1)} %pad_maximum_fusion.3.refs_1_.refs_2_), channel_id=1, source_target_pairs={{0,8},{8,16},{16,24},{24,28},{28,20},{20,12},{12,4},{4,0},{1,9},{9... | collective-permute-start | bytes 2359304 | tf_op jit(solution)/shard_map/ppermute | solution.py:941
  120.0 25.3 %collective-permute-start.28 = (bf16[256,1536]{1,0:T(8,128)(2,1)S(1)}, bf16[256,1536]{1,0:T(8,128)(2,1)}, u32[]{:S(2)}, u32[]{:S(2)}) collective-permute-start(bf16[256,1536]{1,0:T(8,128)(2,1)S(1)} %pad_maximum_fusion.4.refs_1_.refs_10_), channel_id=1, source_target_pairs={{0,8},{8,16},{16,24},{24,28},{28,20},{20,12},{12,4},{4,0},{1,9},{9... | collective-permute-start | bytes 2359304 | tf_op jit(solution)/shard_map/ppermute | solution.py:941
  121.6 23.6 %collective-permute-start.29 = (bf16[256,1536]{1,0:T(8,128)(2,1)S(1)}, bf16[256,1536]{1,0:T(8,128)(2,1)}, u32[]{:S(2)}, u32[]{:S(2)}) collective-permute-start(bf16[256,1536]{1,0:T(8,128)(2,1)S(1)} %collective-permute-done.26.refs_2_.refs_3_), channel_id=1, source_target_pairs={{8,0},{16,8},{24,16},{28,24},{20,28},{12,20},{4,12},{0,4},{9,1},{1... | collective-permute-start | bytes 2359304 | tf_op jit(solution)/shard_map/ppermute | solution.py:941
  122.8 22.4 %collective-permute-start.31 = (bf16[640,256]{1,0:T(8,128)(2,1)S(1)}, bf16[640,256]{1,0:T(8,128)(2,1)S(1)}, u32[]{:S(2)}, u32[]{:S(2)}) collective-permute-start(bf16[640,256]{1,0:T(8,128)(2,1)S(1)} %collective-permute-done.23.refs_4_), channel_id=1, source_target_pairs={{8,0},{16,8},{24,16},{28,24},{20,28},{12,20},{4,12},{0,4},{9,1},{1... | collective-permute-start | bytes 983048 | tf_op jit(solution)/shard_map/ppermute | solution.py:941
  153.1 87.5 %all-gather.9.cloned.1.call-start = ((), (), s32[]{:S(2)}) async-start(), calls=%async_computation.7 | async-start | bytes 5242880 | tf_op jit(solution)/shard_map/all_gather | solution.py:991
  154.5 19.1 %collective-permute-start.32 = (bf16[256,1536]{1,0:T(8,128)(2,1)}, bf16[256,1536]{1,0:T(8,128)(2,1)}, u32[]{:S(2)}, u32[]{:S(2)}) collective-permute-start(bf16[256,1536]{1,0:T(8,128)(2,1)} %collective-permute-done.30.refs_8_.refs_9_), channel_id=1, source_target_pairs={{0,8},{8,16},{16,24},{24,28},{28,20},{20,12},{12,4},{4,0},{1,9},{9... | collective-permute-start | bytes 2359304 | tf_op jit(solution)/shard_map/ppermute | solution.py:941
  155.2 25.2 %collective-permute-start.37 = (bf16[256,1536]{1,0:T(8,128)(2,1)}, bf16[256,1536]{1,0:T(8,128)(2,1)}, u32[]{:S(2)}, u32[]{:S(2)}) collective-permute-start(bf16[256,1536]{1,0:T(8,128)(2,1)} %collective-permute-done.29.refs_3_.refs_4_), channel_id=1, source_target_pairs={{8,0},{16,8},{24,16},{28,24},{20,28},{12,20},{4,12},{0,4},{9,1},{1... | collective-permute-start | bytes 2359304 | tf_op jit(solution)/shard_map/ppermute | solution.py:941
  156.5 25.5 %collective-permute-start.36 = (bf16[256,1536]{1,0:T(8,128)(2,1)}, bf16[256,1536]{1,0:T(8,128)(2,1)}, u32[]{:S(2)}, u32[]{:S(2)}) collective-permute-start(bf16[256,1536]{1,0:T(8,128)(2,1)} %collective-permute-done.28.refs_8_.refs_17_), channel_id=1, source_target_pairs={{0,8},{8,16},{16,24},{24,28},{28,20},{20,12},{12,4},{4,0},{1,9},{9... | collective-permute-start | bytes 2359304 | tf_op jit(solution)/shard_map/ppermute | solution.py:941
  201.4 244.3 %reduce-scatter.7.cloned.1.call-start = ((), (), s32[]{:S(2)}) async-start(), calls=%async_computation.8 | async-start | bytes 5242880 | tf_op jit(solution)/shard_map/reduce_scatter | solution.py:995
  201.5 20.7 %collective-permute-start.41 = (bf16[256,1536]{1,0:T(8,128)(2,1)}, bf16[256,1536]{1,0:T(8,128)(2,1)S(1)}, u32[]{:S(2)}, u32[]{:S(2)}) collective-permute-start(bf16[256,1536]{1,0:T(8,128)(2,1)} %collective-permute-done.37.refs_4_.refs_5_), channel_id=1, source_target_pairs={{8,0},{16,8},{24,16},{28,24},{20,28},{12,20},{4,12},{0,4},{9,1},{1... | collective-permute-start | bytes 2359304 | tf_op jit(solution)/shard_map/ppermute | solution.py:941
  203.0 20.8 %collective-permute-start.40 = (bf16[256,1536]{1,0:T(8,128)(2,1)}, bf16[256,1536]{1,0:T(8,128)(2,1)}, u32[]{:S(2)}, u32[]{:S(2)}) collective-permute-start(bf16[256,1536]{1,0:T(8,128)(2,1)} %collective-permute-done.36.refs_7_.refs_16_), channel_id=1, source_target_pairs={{0,8},{8,16},{16,24},{24,28},{28,20},{20,12},{12,4},{4,0},{1,9},{9... | collective-permute-start | bytes 2359304 | tf_op jit(solution)/shard_map/ppermute | solution.py:941
  203.5 35.6 %collective-permute-start.38 = (bf16[256,1536]{1,0:T(8,128)(2,1)}, bf16[256,1536]{1,0:T(8,128)(2,1)}, u32[]{:S(2)}, u32[]{:S(2)}) collective-permute-start(bf16[256,1536]{1,0:T(8,128)(2,1)} %copy-done.16), channel_id=1, source_target_pairs={{8,0},{16,8},{24,16},{28,24},{20,28},{12,20},{4,12},{0,4},{9,1},{1... | collective-permute-start | bytes 2359304 | tf_op jit(solution)/shard_map/ppermute | solution.py:941
  205.0 27.2 %collective-permute-start.39 = (bf16[768,256]{1,0:T(8,128)(2,1)}, bf16[768,256]{1,0:T(8,128)(2,1)}, u32[]{:S(2)}, u32[]{:S(2)}) collective-permute-start(bf16[768,256]{1,0:T(8,128)(2,1)} %get-tuple-element.328.refs_1_.refs_2_), channel_id=1, source_target_pairs={{0,8},{8,16},{16,24},{24,28},{28,20},{20,12},{12,4},{4,0},{1,9},{9... | collective-permute-start | bytes 1179656 | tf_op jit(solution)/shard_map/ppermute | solution.py:941
  223.8 31.3 %collective-permute-start.44 = (bf16[256,1536]{1,0:T(8,128)(2,1)}, bf16[256,1536]{1,0:T(8,128)(2,1)}, u32[]{:S(2)}, u32[]{:S(2)}) collective-permute-start(bf16[256,1536]{1,0:T(8,128)(2,1)} %collective-permute-done.40.refs_6_.refs_15_), channel_id=1, source_target_pairs={{0,8},{8,16},{16,24},{24,28},{28,20},{20,12},{12,4},{4,0},{1,9},{9... | collective-permute-start | bytes 2359304 | tf_op jit(solution)/shard_map/ppermute | solution.py:941
  224.3 29.2 %collective-permute-start.45 = (bf16[768,256]{1,0:T(8,128)(2,1)}, bf16[768,256]{1,0:T(8,128)(2,1)}, u32[]{:S(2)}, u32[]{:S(2)}) collective-permute-start(bf16[768,256]{1,0:T(8,128)(2,1)} %get-tuple-element.328.refs_1_.refs_2_), channel_id=1, source_target_pairs={{8,0},{16,8},{24,16},{28,24},{20,28},{12,20},{4,12},{0,4},{9,1},{1... | collective-permute-start | bytes 1179656 | tf_op jit(solution)/shard_map/ppermute | solution.py:941
  232.2 24.9 %collective-permute-start.42 = (bf16[768,256]{1,0:T(8,128)(2,1)}, bf16[768,256]{1,0:T(8,128)(2,1)}, u32[]{:S(2)}, u32[]{:S(2)}) collective-permute-start(bf16[768,256]{1,0:T(8,128)(2,1)} %collective-permute-done.39.refs_8_.refs_9_), channel_id=1, source_target_pairs={{0,8},{8,16},{16,24},{24,28},{28,20},{20,12},{12,4},{4,0},{1,9},{9... | collective-permute-start | bytes 1179656 | tf_op jit(solution)/shard_map/ppermute | solution.py:941
  289.9 20.6 %collective-permute-start.55 = (bf16[768,256]{1,0:T(8,128)(2,1)S(1)}, bf16[768,256]{1,0:T(8,128)(2,1)S(1)}, u32[]{:S(2)}, u32[]{:S(2)}) collective-permute-start(bf16[768,256]{1,0:T(8,128)(2,1)S(1)} %collective-permute-done.53.refs_7_.refs_16_), channel_id=1, source_target_pairs={{0,8},{8,16},{16,24},{24,28},{28,20},{20,12},{12,4},{4,0},{1,9},{9... | collective-permute-start | bytes 1179656 | tf_op jit(solution)/shard_map/ppermute | solution.py:941
  290.5 20.9 %collective-permute-start.54 = (bf16[768,256]{1,0:T(8,128)(2,1)}, bf16[768,256]{1,0:T(8,128)(2,1)S(1)}, u32[]{:S(2)}, u32[]{:S(2)}) collective-permute-start(bf16[768,256]{1,0:T(8,128)(2,1)} %get-tuple-element.352), channel_id=1, source_target_pairs={{8,0},{16,8},{24,16},{28,24},{20,28},{12,20},{4,12},{0,4},{9,1},{1... | collective-permute-start | bytes 1179656 | tf_op jit(solution)/shard_map/ppermute | solution.py:941
  291.9 21.0 %collective-permute-start.59 = (bf16[768,256]{1,0:T(8,128)(2,1)}, bf16[768,256]{1,0:T(8,128)(2,1)S(1)}, u32[]{:S(2)}, u32[]{:S(2)}) collective-permute-start(bf16[768,256]{1,0:T(8,128)(2,1)} %get-tuple-element.353), channel_id=1, source_target_pairs={{0,8},{8,16},{16,24},{24,28},{28,20},{20,12},{12,4},{4,0},{1,9},{9... | collective-permute-start | bytes 1179656 | tf_op jit(solution)/shard_map/ppermute | solution.py:941
  313.1 22.8 %collective-permute-start.60 = (bf16[768,256]{1,0:T(8,128)(2,1)S(1)}, bf16[768,256]{1,0:T(8,128)(2,1)S(1)}, u32[]{:S(2)}, u32[]{:S(2)}) collective-permute-start(bf16[768,256]{1,0:T(8,128)(2,1)S(1)} %add_convert_fusion.29), channel_id=1, source_target_pairs={{0,8},{8,16},{16,24},{24,28},{28,20},{20,12},{12,4},{4,0},{1,9},{9... | collective-permute-start | bytes 1179656 | tf_op jit(solution)/shard_map/ppermute | solution.py:941
  317.4 19.2 %collective-permute-start.64 = (bf16[768,256]{1,0:T(8,128)(2,1)S(1)}, bf16[768,256]{1,0:T(8,128)(2,1)S(1)}, u32[]{:S(2)}, u32[]{:S(2)}) collective-permute-start(bf16[768,256]{1,0:T(8,128)(2,1)S(1)} %add_convert_fusion.28), channel_id=1, source_target_pairs={{8,0},{16,8},{24,16},{28,24},{20,28},{12,20},{4,12},{0,4},{9,1},{1... | collective-permute-start | bytes 1179656 | tf_op jit(solution)/shard_map/ppermute | solution.py:941
  336.8 21.1 %collective-permute-start.67 = (bf16[768,256]{1,0:T(8,128)(2,1)S(1)}, bf16[768,256]{1,0:T(8,128)(2,1)S(1)}, u32[]{:S(2)}, u32[]{:S(2)}) collective-permute-start(bf16[768,256]{1,0:T(8,128)(2,1)S(1)} %add_convert_fusion.25), channel_id=1, source_target_pairs={{8,0},{16,8},{24,16},{28,24},{20,28},{12,20},{4,12},{0,4},{9,1},{1... | collective-permute-start | bytes 1179656 | tf_op jit(solution)/shard_map/ppermute | solution.py:941
  338.4 19.5 %collective-permute-start.66 = (bf16[768,256]{1,0:T(8,128)(2,1)S(1)}, bf16[768,256]{1,0:T(8,128)(2,1)S(1)}, u32[]{:S(2)}, u32[]{:S(2)}) collective-permute-start(bf16[768,256]{1,0:T(8,128)(2,1)S(1)} %add_convert_fusion.24), channel_id=1, source_target_pairs={{0,8},{8,16},{16,24},{24,28},{28,20},{20,12},{12,4},{4,0},{1,9},{9... | collective-permute-start | bytes 1179656 | tf_op jit(solution)/shard_map/ppermute | solution.py:941
  379.7 107.6 %all-gather.11.cloned.1.call-start = ((), (), s32[]{:S(2)}) async-start(), calls=%async_computation.9 | async-start | bytes 5242880 | tf_op jit(solution)/shard_map/all_gather | solution.py:991
  381.8 28.7 %collective-permute-start.68 = (bf16[256,1536]{1,0:T(8,128)(2,1)}, bf16[256,1536]{1,0:T(8,128)(2,1)}, u32[]{:S(2)}, u32[]{:S(2)}) collective-permute-start(bf16[256,1536]{1,0:T(8,128)(2,1)} %get-tuple-element.396), channel_id=1, source_target_pairs={{0,8},{8,16},{16,24},{24,28},{28,20},{20,12},{12,4},{4,0},{1,9},{9... | collective-permute-start | bytes 2359304 | tf_op jit(solution)/shard_map/ppermute | solution.py:941
  394.9 31.3 %collective-permute-start.71 = (bf16[768,256]{1,0:T(8,128)(2,1)S(1)}, bf16[768,256]{1,0:T(8,128)(2,1)S(1)}, u32[]{:S(2)}, u32[]{:S(2)}) collective-permute-start(bf16[768,256]{1,0:T(8,128)(2,1)S(1)} %add_convert_fusion.21), channel_id=1, source_target_pairs={{0,8},{8,16},{16,24},{24,28},{28,20},{20,12},{12,4},{4,0},{1,9},{9... | collective-permute-start | bytes 1179656 | tf_op jit(solution)/shard_map/ppermute | solution.py:941
  397.2 31.1 %collective-permute-start.75 = (bf16[256,1536]{1,0:T(8,128)(2,1)S(1)}, bf16[256,1536]{1,0:T(8,128)(2,1)S(1)}, u32[]{:S(2)}, u32[]{:S(2)}) collective-permute-start(bf16[256,1536]{1,0:T(8,128)(2,1)S(1)} %add_convert_fusion.10), channel_id=1, source_target_pairs={{8,0},{16,8},{24,16},{28,24},{20,28},{12,20},{4,12},{0,4},{9,1},{1... | collective-permute-start | bytes 2359304 | tf_op jit(solution)/shard_map/ppermute | solution.py:941
  411.9 23.8 %collective-permute-start.74 = (bf16[256,1536]{1,0:T(8,128)(2,1)S(1)}, bf16[256,1536]{1,0:T(8,128)(2,1)S(1)}, u32[]{:S(2)}, u32[]{:S(2)}) collective-permute-start(bf16[256,1536]{1,0:T(8,128)(2,1)S(1)} %add_convert_fusion.9), channel_id=1, source_target_pairs={{0,8},{8,16},{16,24},{24,28},{28,20},{20,12},{12,4},{4,0},{1,9},{9... | collective-permute-start | bytes 2359304 | tf_op jit(solution)/shard_map/ppermute | solution.py:941
  451.9 179.2 %reduce-scatter.9.cloned.1.call-start = ((), (), s32[]{:S(2)}) async-start(), calls=%async_computation.10 | async-start | bytes 5242880 | tf_op jit(solution)/shard_map/reduce_scatter | solution.py:995
  452.0 20.5 %collective-permute-start.78 = (bf16[256,1536]{1,0:T(8,128)(2,1)}, bf16[256,1536]{1,0:T(8,128)(2,1)}, u32[]{:S(2)}, u32[]{:S(2)}) collective-permute-start(bf16[256,1536]{1,0:T(8,128)(2,1)} %add_convert_fusion.7), channel_id=1, source_target_pairs={{0,8},{8,16},{16,24},{24,28},{28,20},{20,12},{12,4},{4,0},{1,9},{9... | collective-permute-start | bytes 2359304 | tf_op jit(solution)/shard_map/ppermute | solution.py:941
  453.4 20.8 %collective-permute-start.79 = (bf16[256,1536]{1,0:T(8,128)(2,1)}, bf16[256,1536]{1,0:T(8,128)(2,1)}, u32[]{:S(2)}, u32[]{:S(2)}) collective-permute-start(bf16[256,1536]{1,0:T(8,128)(2,1)} %add_convert_fusion.8), channel_id=1, source_target_pairs={{8,0},{16,8},{24,16},{28,24},{20,28},{12,20},{4,12},{0,4},{9,1},{1... | collective-permute-start | bytes 2359304 | tf_op jit(solution)/shard_map/ppermute | solution.py:941
  454.1 28.8 %collective-permute-start.77 = (bf16[256,1536]{1,0:T(8,128)(2,1)}, bf16[256,1536]{1,0:T(8,128)(2,1)}, u32[]{:S(2)}, u32[]{:S(2)}) collective-permute-start(bf16[256,1536]{1,0:T(8,128)(2,1)} %add_convert_fusion.6), channel_id=1, source_target_pairs={{8,0},{16,8},{24,16},{28,24},{20,28},{12,20},{4,12},{0,4},{9,1},{1... | collective-permute-start | bytes 2359304 | tf_op jit(solution)/shard_map/ppermute | solution.py:941
  455.5 29.5 %collective-permute-start.76 = (bf16[256,1536]{1,0:T(8,128)(2,1)}, bf16[256,1536]{1,0:T(8,128)(2,1)}, u32[]{:S(2)}, u32[]{:S(2)}) collective-permute-start(bf16[256,1536]{1,0:T(8,128)(2,1)} %add_convert_fusion.5), channel_id=1, source_target_pairs={{0,8},{8,16},{16,24},{24,28},{28,20},{20,12},{12,4},{4,0},{1,9},{9... | collective-permute-start | bytes 2359304 | tf_op jit(solution)/shard_map/ppermute | solution.py:941
  487.3 189.9 %reduce-scatter.11.cloned.1.call-start = ((), (), s32[]{:S(2)}) async-start(), calls=%async_computation.11 | async-start | bytes 5242880 | tf_op jit(solution)/shard_map/reduce_scatter | solution.py:995
  492.6 21.4 %collective-permute-start.80 = (bf16[256,1536]{1,0:T(8,128)(2,1)S(1)}, bf16[256,1536]{1,0:T(8,128)(2,1)}, u32[]{:S(2)}, u32[]{:S(2)}) collective-permute-start(bf16[256,1536]{1,0:T(8,128)(2,1)S(1)} %copy-done.36), channel_id=1, source_target_pairs={{8,0},{16,8},{24,16},{28,24},{20,28},{12,20},{4,12},{0,4},{9,1},{1... | collective-permute-start | bytes 2359304 | tf_op jit(solution)/shard_map/ppermute | solution.py:941
  493.0 20.9 %collective-permute-start.81 = (bf16[256,1536]{1,0:T(8,128)(2,1)S(1)}, bf16[256,1536]{1,0:T(8,128)(2,1)S(1)}, u32[]{:S(2)}, u32[]{:S(2)}) collective-permute-start(bf16[256,1536]{1,0:T(8,128)(2,1)S(1)} %copy-done.35), channel_id=1, source_target_pairs={{0,8},{8,16},{16,24},{24,28},{28,20},{20,12},{12,4},{4,0},{1,9},{9... | collective-permute-start | bytes 2359304 | tf_op jit(solution)/shard_map/ppermute | solution.py:941
  494.6 54.8 %collective-permute-start.85 = (bf16[256,1536]{1,0:T(8,128)(2,1)S(1)}, bf16[256,1536]{1,0:T(8,128)(2,1)S(1)}, u32[]{:S(2)}, u32[]{:S(2)}) collective-permute-start(bf16[256,1536]{1,0:T(8,128)(2,1)S(1)} %copy-done.33), channel_id=1, source_target_pairs={{0,8},{8,16},{16,24},{24,28},{28,20},{20,12},{12,4},{4,0},{1,9},{9... | collective-permute-start | bytes 2359304 | tf_op jit(solution)/shard_map/ppermute | solution.py:941
  515.6 36.3 %collective-permute-start.83 = (bf16[256,1536]{1,0:T(8,128)(2,1)S(1)}, bf16[256,1536]{1,0:T(8,128)(2,1)S(1)}, u32[]{:S(2)}, u32[]{:S(2)}) collective-permute-start(bf16[256,1536]{1,0:T(8,128)(2,1)S(1)} %add_convert_fusion.1), channel_id=1, source_target_pairs={{8,0},{16,8},{24,16},{28,24},{20,28},{12,20},{4,12},{0,4},{9,1},{1... | collective-permute-start | bytes 2359304 | tf_op jit(solution)/shard_map/ppermute | solution.py:941
  516.6 32.8 %collective-permute-start.84 = (bf16[640,256]{1,0:T(8,128)(2,1)}, bf16[640,256]{1,0:T(8,128)(2,1)}, u32[]{:S(2)}, u32[]{:S(2)}) collective-permute-start(bf16[640,256]{1,0:T(8,128)(2,1)} %get-tuple-element.448), channel_id=1, source_target_pairs={{0,8},{8,16},{16,24},{24,28},{28,20},{20,12},{12,4},{4,0},{1,9},{9... | collective-permute-start | bytes 983048 | tf_op jit(solution)/shard_map/ppermute | solution.py:941
  517.7 34.2 %collective-permute-start.82 = (bf16[640,256]{1,0:T(8,128)(2,1)}, bf16[640,256]{1,0:T(8,128)(2,1)}, u32[]{:S(2)}, u32[]{:S(2)}) collective-permute-start(bf16[640,256]{1,0:T(8,128)(2,1)} %get-tuple-element.447), channel_id=1, source_target_pairs={{8,0},{16,8},{24,16},{28,24},{20,28},{12,20},{4,12},{0,4},{9,1},{1... | collective-permute-start | bytes 983048 | tf_op jit(solution)/shard_map/ppermute | solution.py:941
  (198 other events, 2613.0 us)
Sparse Core Ops, SparseCore 0:
  9.7 37.1 all-gather.4
  48.5 34.4 all-gather.6
  153.2 44.8 reduce-scatter.4
  201.5 34.4 all-gather.8
  379.8 44.4 reduce-scatter.6
  452.0 34.1 all-gather.10
  488.8 44.5 reduce-scatter.8
  590.4 43.4 reduce-scatter.10

commit v4 on v3

--- a/solution.py
+++ b/solution.py
@@ -98,7 +98,7 @@
         ).astype(bf16)
         return before
 
-    last_entry[...] = lax.fori_loop(0, length // 16, convolve, last_entry[...])
+    last_entry[...] = lax.fori_loop(0, length // 16, convolve, last_entry[...], unroll=4)
     pre[...] = jnp.dot(mixed_low[...], gates[...], preferred_element_type=f32)
     rate_bias = small[5:6, :]
     entry_bias = small[6:7, :]
@@ -128,11 +128,11 @@
         )
         return carry
 
-    last_state[...] = lax.fori_loop(0, length // 16, scan, last_state[...])
+    last_state[...] = lax.fori_loop(0, length // 16, scan, last_state[...], unroll=4)
 
 
 def core_backward_kernel(
-    place, grad, branch, entry_pre, mixed_in, rate_in, entry_in, state_in, state_tail, entry_tail,
+    place, grad, entry_pre, mixed_in, rate_in, entry_in, state_in, state_tail, entry_tail,
     masks, gates, small, low, gate_grads, small_grads,
     state_long, entry_long, gate_low, mixed_grad, sums, next_decay, next_carried, next_mixed,
 ):
@@ -156,7 +156,7 @@
     def reverse(step, carry):
         after_decay, carried_after = carry
         step = length // 16 - 1 - step
-        branch_parts, rate_parts, entry_parts = [], [], []
+        rate_parts, entry_parts = [], []
         for half in (1, 0):
             start = pl.multiple_of(step * 16 + half * 8, 8)
             at = pl.ds(start, 8)
@@ -165,11 +165,8 @@
             entry = entry_in[at, :]
             mixed = mixed_in[at, :]
             decay, square, factor = decay_terms(rate, slope, keep)
-            up = grad[at, :]
-            act, act_slope = gelu_both(branch[at, :])
             state = state_in[at, :]
-            branch_parts.append(up * state * act_slope)
-            value = up * act
+            value = grad[at, :]
             ahead = up_by(decay, after_decay, 1, rows)
             after_decay = decay
             for shift in (1, 2, 4):
@@ -191,13 +188,12 @@
             rate_parts.append(rate_pre_grad)
             entry_parts.append(entry_pre_grad)
         both = pl.ds(pl.multiple_of(step * 16, 16), 16)
-        low[both, :width] = jnp.concatenate(branch_parts[::-1], axis=0).astype(bf16)
         gate_low[both, :width] = jnp.concatenate(rate_parts[::-1], axis=0).astype(bf16)
         gate_low[both, width:] = jnp.concatenate(entry_parts[::-1], axis=0).astype(bf16)
         return after_decay, carried_after
 
     after_decay, carried_after = lax.fori_loop(
-        0, length // 16, reverse, (next_decay[...], next_carried[...])
+        0, length // 16, reverse, (next_decay[...], next_carried[...]), unroll=4
     )
     next_decay[...] = after_decay
     next_carried[...] = carried_after
@@ -231,7 +227,7 @@
                 total += up_by(masked[k - 1], after[k - 1], k, rows) * taps[k]
             after = masked
             parts.append(total)
-        low[pl.ds(pl.multiple_of(step * 16, 16), 16), width:] = jnp.concatenate(
+        low[pl.ds(pl.multiple_of(step * 16, 16), 16), :] = jnp.concatenate(
             parts[::-1], axis=0
         ).astype(bf16)
         return after
@@ -241,6 +237,7 @@
         length // 16,
         convolve,
         [next_mixed[8 * k : 8 * k + 8, :] for k in range(3)],
+        unroll=4,
     )
     for k in range(3):
         next_mixed[8 * k : 8 * k + 8, :] = after[k]
@@ -305,7 +302,6 @@
             grid=(blocks,),
             in_specs=[
                 wide(0),
-                wide(0),
                 wide(1),
                 wide(0),
                 wide(0),
@@ -318,7 +314,7 @@
                 whole(small.shape),
             ],
             out_specs=[
-                pl.BlockSpec((length, 2 * width), lambda g, t: (back(g) ^ t[0], 0)),
+                wide(0),
                 whole(gates.shape),
                 whole((8, width)),
             ],
@@ -334,14 +330,14 @@
             ],
         ),
         out_shape=[
-            jax.ShapeDtypeStruct((total, 2 * width), bf16),
+            jax.ShapeDtypeStruct((total, width), bf16),
             jax.ShapeDtypeStruct(gates.shape, f32),
             jax.ShapeDtypeStruct((8, width), f32),
         ],
         compiler_params=pltpu.CompilerParams(vmem_limit_bytes=vmem_bytes),
         cost_estimate=light,
         name="core_backward",
-    )(place, grad, pre, pre, mixed, rate, entry, state, state, pre, masks, gates, small)
+    )(place, grad, pre, mixed, rate, entry, state, state, pre, masks, gates, small)
 
 
 def dot(left, right):
@@ -375,7 +371,7 @@
     )
 
 
-def spread(lefts, weights, place, blocks, transposed, name):
+def spread(lefts, weights, place, blocks, transposed, name, base=None):
     total = lefts[0][0].shape[0]
     rows = total // 4
     pieces = len(weights[0])
@@ -389,7 +385,7 @@
     def kernel(place_ref, *refs):
         left = [ref[...] for ref in refs[:terms]]
         flat = refs[terms : terms + terms * pieces]
-        outs = refs[terms + terms * pieces :]
+        outs = refs[terms + terms * pieces + (base is not None) :]
         result = outs[-1]
         at = 0
         for r in range(pieces):
@@ -402,6 +398,8 @@
                     weight = weight[...]
                 term = product(left[i], weight)
                 value = term if value is None else value + term
+            if base is not None:
+                value += refs[terms + terms * pieces][:, at : at + sizes[r]].astype(f32)
             result[:, at : at + sizes[r]] = value.astype(bf16)
             at += sizes[r]
         if blocks:
@@ -431,7 +429,8 @@
             num_scalar_prefetch=1,
             grid=(count,),
             in_specs=[left_spec(column, width) for _, column, width in lefts]
-            + [fixed(w.shape) for group in weights for w in group],
+            + [fixed(w.shape) for group in weights for w in group]
+            + [pl.BlockSpec((rows, features), lambda g, t: (g, 0))] * (base is not None),
             out_specs=out_specs,
             scratch_shapes=scratch,
         ),
@@ -439,7 +438,7 @@
         compiler_params=pltpu.CompilerParams(vmem_limit_bytes=vmem_bytes),
         cost_estimate=light,
         name=name,
-    )(place, *[left for left, _, _ in lefts], *[w for group in weights for w in group])
+    )(place, *[left for left, _, _ in lefts], *[w for group in weights for w in group], *([] if base is None else [base]))
 
 
 def collect(left, weights, width, transposed, name):
@@ -472,6 +471,41 @@
         pl.BlockSpec((rows, count * width), lambda g: (g, 0)),
         jax.ShapeDtypeStruct((total, count * width), f32),
     )(left, *[w for group in weights for w in group])
+
+
+def mixer_back(left, weights, pre, state):
+    total, features = left.shape
+    rows = total // 4
+    pieces = len(weights)
+    sizes = [w.shape[1] for w in weights]
+    width = state.shape[1]
+
+    def kernel(*refs):
+        branch_ref, state_ref, state_grad, branch_low = refs[1 + pieces :]
+        at = 0
+        value = None
+        for r in range(pieces):
+            term = dot_back(refs[0][:, at : at + sizes[r]], refs[1 + r][...])
+            value = term if value is None else value + term
+            at += sizes[r]
+        act, slope = gelu_both(branch_ref[...])
+        state_grad[...] = value * act
+        branch_low[...] = (value * state_ref[...] * slope).astype(bf16)
+
+    block = pl.BlockSpec((rows, width), lambda g: (g, 0))
+    return call(
+        kernel,
+        "mixer_back",
+        (4,),
+        [pl.BlockSpec((rows, features), lambda g: (g, 0))]
+        + [fixed(w.shape) for w in weights]
+        + [block] * 2,
+        [block] * 2,
+        [
+            jax.ShapeDtypeStruct((total, width), f32),
+            jax.ShapeDtypeStruct((total, width), bf16),
+        ],
+    )(left, *weights, pre, state)
 
 
 def gated_forward(left, weights):
@@ -682,7 +716,7 @@
 def pack_tables(gate_grads, small_grads, order, count, shard, piece, block_width):
     width = gate_grads.shape[0]
 
-    def kernel(order_ref, gate_ref, small_ref, left, right):
+    def kernel(order_ref, gate_ref, small_ref, out):
         spreader = one_hot(256, width, lambda row, column: row == column % block_width)
         same = lax.broadcasted_iota(jnp.int32, (width, width), 0) // block_width == (
             lax.broadcasted_iota(jnp.int32, (width, width), 1) // block_width
@@ -705,19 +739,18 @@
                 term = dot_rows(movers[k], mine)
                 total = term if total is None else total + term
             at = slice(r * shard, (r + 1) * shard)
-            left[at, :] = total[:, :128].astype(bf16)
-            right[at, :] = total[:, 128:].astype(bf16)
-
-    shape = (count * shard, 128)
+            out[at, :] = total.astype(bf16)
+
+    shape = (count * shard, 256)
     return pl.pallas_call(
         kernel,
         grid_spec=pltpu.PrefetchScalarGridSpec(
             num_scalar_prefetch=1,
             grid=(1,),
             in_specs=[fixed(gate_grads.shape), fixed(small_grads.shape)],
-            out_specs=[fixed(shape)] * 2,
+            out_specs=fixed(shape),
         ),
-        out_shape=[jax.ShapeDtypeStruct(shape, bf16)] * 2,
+        out_shape=jax.ShapeDtypeStruct(shape, bf16),
         compiler_params=pltpu.CompilerParams(vmem_limit_bytes=vmem_bytes),
         cost_estimate=light,
         name="pack_tables",
@@ -1173,31 +1206,39 @@
     lanes.did(13.5, down_scatters[0].part[0])
     lanes.add(*down_scatters)
     gated_lows, gated_scatters = [], []
-    for h in range(2):
+
+    def gated_back(h):
         lanes.until(down_chains[h])
         (gated,) = lanes.gate(cotangent_rows)
-        low = gated_backward(gated, down_chains[h].pieces(), acts[h], slopes[h])
-        gated_lows.append(low)
-        lanes.did(8.5, low)
-    (gated,) = lanes.gate(gated_lows[0])
-    gated_scatters.append(
-        Scatter(ring, weight_grads([mlp_rows], gated, dp, True, "gated_grads")[0], True)
-    )
-    lanes.did(14.0, gated_scatters[0].part[0])
-    lanes.add(gated_scatters[0])
-    weights = [chain.pieces() for chain in gated_chains]
-
-    lefts = [(low, 0, 2 * half) for low in lanes.gate(*gated_lows)]
-    mlp_in_grad = spread(lefts, weights, place, (), True, "mlp_in_grad")
-    lanes.did(20.5, mlp_in_grad)
+        gated_lows.append(gated_backward(gated, down_chains[h].pieces(), acts[h], slopes[h]))
+        lanes.did(8.5, gated_lows[h])
+
+    def gated_grads(h):
+        (gated,) = lanes.gate(gated_lows[h])
+        (part,) = weight_grads([mlp_rows], gated, dp, True, "gated_grads")
+        gated_scatters.append(Scatter(ring, part, h == 0))
+        lanes.did(14.0, part[0])
+        lanes.add(gated_scatters[h])
+
+    gated_back(0)
+    gated_back(1)
+    mlp_in_grad = None
+    for h in range(2):
+        (gated,) = lanes.gate(gated_lows[h])
+        mlp_in_grad = spread(
+            [(gated, 0, 2 * half)],
+            [gated_chains[h].pieces()],
+            place,
+            (),
+            True,
+            "mlp_in_grad",
+            mlp_in_grad,
+        )
+        lanes.did(11.0, mlp_in_grad)
     mlp_in_grad = tensor_reduce(mlp_in_grad)
     arrival = lanes.now + 46.0
-    (gated,) = lanes.gate(gated_lows[1])
-    gated_scatters.append(
-        Scatter(ring, weight_grads([mlp_rows], gated, dp, True, "gated_grads")[0], False)
-    )
-    lanes.did(14.0, gated_scatters[1].part[0])
-    lanes.add(gated_scatters[1])
+    gated_grads(0)
+    gated_grads(1)
     lanes.catch_up(arrival)
     (mlp_in_grad,) = lanes.gate(mlp_in_grad)
     middle_norm_grad = norm_backward(middle, scale_two, gain_two, mlp_in_grad.astype(f32))
@@ -1218,42 +1259,48 @@
     mlp_out, residual_rows = lanes.gate(mlp_out, residual_rows)
     mlp_sum = tensor_reduce(mlp_out)
 
-    mixer_grad = collect(residual_rows, [output_pieces], width, True, "mixer_grad")
-    lanes.did(8.0, mixer_grad)
+    state_grad, branch_low = mixer_back(residual_rows, output_pieces, pre, state)
+    lanes.did(10.5, state_grad)
+    (state_grad,) = lanes.gate(state_grad)
+    entry_low, gate_grads, small_grads = core_backward(
+        start, state_grad, pre, mixed, rate, entry, state, masks, gates, small, tensor
+    )
+    lanes.did(23.0, entry_low)
     (residual_rows,) = lanes.gate(residual_rows)
-    output_scatter = Scatter(
-        ring, weight_grads([mixer_low], residual_rows, dp, False, "output_grads")[0], True
-    )
-    lanes.did(9.0, output_scatter.part[0])
+    (part,) = weight_grads([mixer_low], residual_rows, dp, False, "output_grads")
+    output_scatter = Scatter(ring, part, True)
+    lanes.did(9.5, part[0])
     lanes.add(output_scatter)
-    (mixer_grad,) = lanes.gate(mixer_grad)
-    pair_low, gate_grads, small_grads = core_backward(
-        start, mixer_grad, pre, mixed, rate, entry, state, masks, gates, small, tensor
-    )
-    lanes.did(28.0, pair_low)
+    (low,) = lanes.gate(branch_low)
+    (part,) = weight_grads([mixer_rows], low, dp, True, "branch_grads")
+    pair_scatters = [Scatter(ring, part, False)]
+    lanes.did(8.0, part[0])
+    lanes.add(pair_scatters[0])
     decay_grad = lru_scale * small_grads[7:8] * jax.nn.sigmoid(-decay_full)
     small_grads = jnp.concatenate([small_grads[:7], decay_grad], axis=0)
+    (gate_grads,) = lanes.gate(gate_grads)
     grad_tables = pack_tables(
         gate_grads, small_grads, ring.block_of, dp, shard, piece, block_width
     )
-    lanes.did(8.0, grad_tables[0])
-    (low,) = lanes.gate(pair_low)
-    pair_parts = weight_grads([mixer_rows], low, dp, True, "pair_grads", grad_tables)
-    pair_scatters = [Scatter(ring, part, h == 0) for h, part in enumerate(pair_parts)]
-    lanes.did(13.0, pair_parts[0][0])
-    lanes.add(*pair_scatters)
-    (pair_low,) = lanes.gate(pair_low)
+    lanes.did(7.5, grad_tables)
+    (low,) = lanes.gate(entry_low)
+    (part,) = weight_grads([mixer_rows], low, dp, True, "input_grads", (grad_tables,))
+    pair_scatters.append(Scatter(ring, part, True))
+    lanes.did(9.0, part[0])
+    lanes.add(pair_scatters[1])
+    branch_late, entry_late = lanes.gate(branch_low, entry_low)
     mixer_in_grad = spread(
-        [(pair_low, 0, width), (pair_low, 1, width)],
+        [(branch_late, 0, width), (entry_late, 0, width)],
         pair_weights,
         place,
         (),
         True,
         "mixer_in_grad",
     )
-    lanes.did(12.0, mixer_in_grad)
+    lanes.did(11.5, mixer_in_grad)
     mixer_in_grad = tensor_reduce(mixer_in_grad)
-    arrival = lanes.now + 48.0
+    arrival = lanes.now + 30.0
+
     (mlp_sum,) = lanes.gate(mlp_sum)
     layer_out = ring.columns_out((middle + mlp_sum.astype(f32)).astype(bf16), shard)
     lanes.did(6.0, layer_out)
@@ -1268,7 +1315,7 @@
 
     free = lambda *values: values
     pair_wgrads = [scatter.result(free) for scatter in pair_scatters]
-    table_grad = jnp.concatenate([wgrad[:, width:] for wgrad in pair_wgrads], axis=1)
+    table_grad = pair_wgrads[1][:, width:]
     pair_wgrads = [wgrad[:, :width] for wgrad in pair_wgrads]
     rate_wgrad, entry_wgrad, column_grads = [
         table_grad[k * table_rows : (k + 1) * table_rows].reshape(gate_blocks, piece, wide)

time: 702 us -> 674 us (0.960)
  waiting for transfers between devices: 208 us -> 191 us
  other arithmetic: 73.2 us -> 63 us
    ppermute x105, waiting for transfers between devices: 198 us -> 180 us  [start(): value = lax.ppermute(operand, 'dp', self.ring.pairs[way])]
    pallas_call x0 -> x1, Pallas kernels: none -> 10.2 us  [mixer_back(): call(kernel, 'mixer_back', (4,), [pl.BlockSpec((rows, features), lambda g...]
    pallas_call x2 -> x1, Pallas kernels: 19.6 us -> 11.3 us  [collect(): call(kernel, name, (4,), [pl.BlockSpec((rows, features), lambda g: (g, 0)...]
    pallas_call x5 -> x6, Pallas kernels: 65.1 us -> 71.1 us  [weight_grads(): call(kernel, name, (pieces,), in_specs, [fixed(shape) for shape in shapes...]
    pallas_call x4 -> x5, Pallas kernels: 50.2 us -> 53.3 us  [spread(): pl.pallas_call(kernel, grid_spec=pltpu.PrefetchScalarGridSpec(num_scalar_...]
  transfers between devices with their start and end apart: 115 -> 115, of which waited for: 50 -> 45; matrix products, arithmetic and copies ran while one was open for 10% -> 9% of each run, Pallas kernels for 34% -> 38%
where the time goes in v4:
time: 674 us; the launch traced here: 664 us
  Pallas kernels  263 us (39%)
  waiting for transfers between devices  191 us (28%)
  starting transfers between devices  117 us (17%)
  other arithmetic  63 us (9%)
  between operations  15.9 us (2%)
  local copies, waits for them, and re-layouts  14.9 us (2%)
    ppermute x105, waiting for transfers between devices, start(): value = lax.ppermute(operand, 'dp', self.ring.pairs[way])  180 us
    ppermute x105, starting transfers between devices, start(): value = lax.ppermute(operand, 'dp', self.ring.pairs[way])  116 us
    pallas_call x6, Pallas kernels, weight_grads(): call(kernel, name, (pieces,), in_specs, [fixed(shape) for shape in shapes...  71.1 us
    pallas_call x5, Pallas kernels, spread(): pl.pallas_call(kernel, grid_spec=pltpu.PrefetchScalarGridSpec(num_scalar_...  53.3 us
    convert_element_type x35, other arithmetic, operand(): value = (value.astype(f32) + got.astype(f32)).astype(bf16)  27.4 us
    pallas_call x2, Pallas kernels, gated_forward(): call(kernel, 'gated_forward', (4,), [pl.BlockSpec((rows, features), lambd...  25.9 us
    pallas_call x1, Pallas kernels, core_backward(): pl.pallas_call(core_backward_kernel, grid_spec=pltpu.PrefetchScalarGridSp...  23.5 us
    pallas_call x2, Pallas kernels, gated_backward(): call(kernel, 'gated_backward', (4,), [pl.BlockSpec((rows, features), lamb...  17.1 us
  transfers between devices with their start and end apart: 115, of which 45 were waited for; matrix products, arithmetic and copies ran while one was open for 9% of the time, Pallas kernels for 38%

profile of v4, /device:TPU:0, one launch (start us, length us, event | category | flops | bytes accessed | tf_op | source)
XLA Modules:
  0.0 664.0 jit_solution(18186786017793308132)
XLA Ops:
  15.1 5.6 collective-permute-done.1.refs_2_.refs_3_
  27.6 6.8 %collective-permute-done.4.refs_7_ = bf16[256,256]{1,0:T(8,128)(2,1)S(1)} collective-permute-done((bf16[256,256]{1,0:T(8,128)(2,1)S(1)}, bf16[256,256]{1,0:T(8,128)(2,1)S(1)}, u32[]{:S(2)}, u32[]{:S(2)}) %collective-permute-start.4) | collective-permute-done | bytes 131104 | tf_op jit(solution)/shard_map/ppermute | solution.py:974
  52.5 3.8 collective-permute-done.15.refs_5_.refs_6_
  65.4 6.6 unpack_tables.1
  73.6 8.3 %prepare.1 = (bf16[1024,2048]{1,0:T(8,128)(2,1)}, bf16[256,2048]{1,0:T(8,128)(2,1)}) custom-call(s32[8]{0:T(128)} %compare_select_fusion.5.order_ref, s32[1]{0:T(128)} %bitcast.place_ref, bf16[1024,2048]{1,0:T(8,128)(2,1)} %all-gather.5.cloned.1.call-done.value_ref, f32[1,2048]{1,0:T(1,128)} %get-tuple-element.608.gain_ref), custom_call_target="tpu_custom_call" | custom-call | flops 6000000000 | bytes 30000000 | tf_op jit(solution)/shard_map/prepare/pallas_call | solution.py:788
  86.5 6.4 collective-permute-done.19.refs_3_
  95.8 4.0 collective-permute-done.25.refs_12_.refs_13_
  102.0 3.6 collective-permute-done.23.refs_4_
  108.7 11.3 %mixer_in.1.branch.entry_pre.refs_9_.entry_tail = f32[1024,1280]{1,0:T(8,128)} custom-call(bf16[1024,2048]{1,0:T(8,128)(2,1)} %get-tuple-element.311.refs_0_, bf16[256,640]{1,0:T(8,128)(2,1)} %refs_2_.1, bf16[256,640]{1,0:T(8,128)(2,1)} %copy-done.111, bf16[256,640]{1,0:T(8,128)(2,1)} %copy-done.113, ...), custom_call_target="tpu_custom_call" | custom-call | flops 6000000000 | bytes 30000000 | tf_op jit(solution)/shard_map/mixer_in/pallas_call | solution.py:465
  124.2 16.4 %core_forward.1 = (bf16[1024,640]{1,0:T(8,128)(2,1)}, f32[1024,640]{1,0:T(8,128)}, f32[1024,640]{1,0:T(8,128)}, f32[1024,640]{1,0:T(8,128)}, f32[1024,640]{1,0:T(8,128)}) custom-call(s32[1]{0:T(128)} %constant.88.clone.1.place, f32[1024,1280]{1,0:T(8,128)} %mixer_in.1.branch.entry_pre.refs_9_.entry_tail, ...), custom_call_target="tpu_custom_call" | custom-call | flops 6000000000 | bytes 30000000 | tf_op jit(solution)/shard_map/core_forward/pallas_call | solution.py:257
  141.4 7.1 %mixer_out.1 = bf16[1024,2048]{1,0:T(8,128)(2,1)} custom-call(s32[1]{0:T(128)} %bitcast.place_ref, bf16[1024,640]{1,0:T(8,128)(2,1)} %get-tuple-element.322.refs_0_, bf16[640,256]{1,0:T(8,128)(2,1)} %refs_1_.5, bf16[640,256]{1,0:T(8,128)(2,1)} %collective-permute-done.17.refs_2_, bf16[640,256]{1,0:T(8,128)(2,1)} %collective-permute-done.19.refs_3_, ...), custom_call_target="tpu_custom_call" | custom-call | flops 6000000000 | bytes 30000000 | tf_op jit(solution)/shard_map/mixer_out/pallas_call | solution.py:426
  153.6 5.7 move_columns.3.refs_2_.refs_0_
  159.3 10.9 %collective-permute-done.33.refs_2_ = bf16[256,1536]{1,0:T(8,128)(2,1)} collective-permute-done((bf16[256,1536]{1,0:T(8,128)(2,1)S(1)}, bf16[256,1536]{1,0:T(8,128)(2,1)}, u32[]{:S(2)}, u32[]{:S(2)}) %collective-permute-start.33) | collective-permute-done | bytes 786464 | tf_op jit(solution)/shard_map/ppermute | solution.py:974
  173.2 7.9 %collective-permute-done.37.refs_4_ = bf16[256,1536]{1,0:T(8,128)(2,1)} collective-permute-done((bf16[256,1536]{1,0:T(8,128)(2,1)}, bf16[256,1536]{1,0:T(8,128)(2,1)}, u32[]{:S(2)}, u32[]{:S(2)}) %collective-permute-start.37) | collective-permute-done | bytes 786464 | tf_op jit(solution)/shard_map/ppermute | solution.py:974
  182.5 6.9 %collective-permute-done.35.refs_3_ = bf16[256,1536]{1,0:T(8,128)(2,1)S(1)} collective-permute-done((bf16[256,1536]{1,0:T(8,128)(2,1)}, bf16[256,1536]{1,0:T(8,128)(2,1)S(1)}, u32[]{:S(2)}, u32[]{:S(2)}) %collective-permute-start.35) | collective-permute-done | bytes 786464 | tf_op jit(solution)/shard_map/ppermute | solution.py:974
  201.0 16.6 %collective-permute-done.41.refs_5_ = bf16[256,1536]{1,0:T(8,128)(2,1)S(1)} collective-permute-done((bf16[256,1536]{1,0:T(8,128)(2,1)}, bf16[256,1536]{1,0:T(8,128)(2,1)S(1)}, u32[]{:S(2)}, u32[]{:S(2)}) %collective-permute-start.41) | collective-permute-done | bytes 786464 | tf_op jit(solution)/shard_map/ppermute | solution.py:974
  221.2 6.3 collective-permute-done.39.refs_8_.refs_9_
  228.0 6.4 collective-permute-done.38.refs_4_
  236.8 12.9 %gated_forward.2 = (bf16[1024,768]{1,0:T(8,128)(2,1)}, bf16[1024,768]{1,0:T(8,128)(2,1)}, bf16[1024,768]{1,0:T(8,128)(2,1)}) custom-call(bf16[1024,2048]{1,0:T(8,128)(2,1)} %all-gather.9.cloned.1.call-done.refs_0_, bf16[256,1536]{1,0:T(8,128)(2,1)} %copy-done.21, bf16[256,1536]{1,0:T(8,128)(2,1)} %copy-done.94, ...), custom_call_target="tpu_custom_call" | custom-call | flops 6000000000 | bytes 30000000 | tf_op jit(solution)/shard_map/gated_forward/pallas_call | solution.py:538
  253.8 13.0 %gated_forward.3 = (bf16[1024,768]{1,0:T(8,128)(2,1)}, bf16[1024,768]{1,0:T(8,128)(2,1)}, bf16[1024,768]{1,0:T(8,128)(2,1)}) custom-call(bf16[1024,2048]{1,0:T(8,128)(2,1)} %all-gather.9.cloned.1.call-done.refs_0_, bf16[256,1536]{1,0:T(8,128)(2,1)} %copy-done.22, bf16[256,1536]{1,0:T(8,128)(2,1)} %collective-permute-done.33.refs_2_, ...), custom_call_target="tpu_custom_call" | custom-call | flops 6000000000 | bytes 30000000 | tf_op jit(solution)/shard_map/gated_forward/pallas_call | solution.py:538
  270.4 14.1 %down_grads.1 = (bf16[768,256]{1,0:T(8,128)(2,1)}, bf16[768,256]{1,0:T(8,128)(2,1)}, bf16[768,256]{1,0:T(8,128)(2,1)}, bf16[768,256]{1,0:T(8,128)(2,1)}, bf16[76...) custom-call(bf16[1024,768]{1,0:T(8,128)(2,1)} %get-tuple-element.418, ...), custom_call_target="tpu_custom_call" | custom-call | flops 6000000000 | bytes 30000000 | tf_op jit(solution)/shard_map/down_grads/pallas_call | solution.py:620
  288.7 8.0 %collective-permute-done.55.refs_5_.refs_6_ = bf16[768,256]{1,0:T(8,128)(2,1)S(1)} collective-permute-done((bf16[768,256]{1,0:T(8,128)(2,1)S(1)}, bf16[768,256]{1,0:T(8,128)(2,1)S(1)}, u32[]{:S(2)}, u32[]{:S(2)}) %collective-permute-start.55) | collective-permute-done | bytes 393248 | tf_op jit(solution)/shard_map/ppermute | solution.py:974
  298.3 8.6 %gated_backward.2.refs_0_.refs_1_ = bf16[1024,1536]{1,0:T(8,128)(2,1)} custom-call(bf16[1024,2048]{1,0:T(8,128)(2,1)} %move_columns.3.refs_2_.refs_0_, bf16[768,256]{1,0:T(8,128)(2,1)} %get-tuple-element.331.refs_1_.refs_2_, bf16[768,256]{1,0:T(8,128)(2,1)} %collective-permute-done.45.refs_2_.refs_3_, bf16[768,256]{1,0:T(8,128)(2,1)} %copy-done.100, ...), custom_call_target="tpu_custom_call" | custom-call | flops 6000000000 | bytes 30000000 | tf_op jit(solution)/shard_map/gated_backward/pallas_call | solution.py:566
  309.9 3.6 collective-permute-done.58
  323.6 8.6 %gated_backward.3.refs_0_.refs_1_ = bf16[1024,1536]{1,0:T(8,128)(2,1)} custom-call(bf16[1024,2048]{1,0:T(8,128)(2,1)} %move_columns.3.refs_2_.refs_0_, bf16[768,256]{1,0:T(8,128)(2,1)} %copy-done.41, bf16[768,256]{1,0:T(8,128)(2,1)} %collective-permute-done.43.refs_2_.refs_11_, bf16[768,256]{1,0:T(8,128)(2,1)} %copy-done.102, bf16[768,256]{1,0:T(8,128)(2,1)} %copy-done.106, ...), custom_call_target="tpu_custom_call" | custom-call | flops 6000000000 | bytes 30000000 | tf_op jit(solution)/shard_map/gated_backward/pallas_call | solution.py:566
  335.2 3.5 collective-permute-done.60
  340.4 11.4 %mlp_in_grad.2.refs_9_ = bf16[1024,2048]{1,0:T(8,128)(2,1)} custom-call(s32[1]{0:T(128)} %bitcast.place_ref, bf16[1024,1536]{1,0:T(8,128)(2,1)} %gated_backward.2.refs_0_.refs_1_, bf16[256,1536]{1,0:T(8,128)(2,1)} %copy-done.21, bf16[256,1536]{1,0:T(8,128)(2,1)} %copy-done.94, bf16[256,1536]{1,0:T(8,128)(2,1)} %collective-permute-done.29.refs_3_, ...), custom_call_target="tpu_custom_call" | custom-call | flops 6000000000 | bytes 30000000 | tf_op jit(solution)/shard_map/mlp_in_grad/pallas_call | solution.py:426
  353.4 11.8 %mlp_in_grad.3 = bf16[1024,2048]{1,0:T(8,128)(2,1)} custom-call(s32[1]{0:T(128)} %bitcast.place_ref, bf16[1024,1536]{1,0:T(8,128)(2,1)} %gated_backward.3.refs_0_.refs_1_, bf16[256,1536]{1,0:T(8,128)(2,1)} %copy-done.22, bf16[256,1536]{1,0:T(8,128)(2,1)} %collective-permute-done.33.refs_2_, bf16[256,1536]{1,0:T(8,128)(2,1)} %copy-done.95, ...), custom_call_target="tpu_custom_call" | custom-call | flops 6000000000 | bytes 30000000 | tf_op jit(solution)/shard_map/mlp_in_grad/pallas_call | solution.py:426
  365.9 13.7 %gated_grads.2 = (bf16[256,1536]{1,0:T(8,128)(2,1)}, bf16[256,1536]{1,0:T(8,128)(2,1)}, bf16[256,1536]{1,0:T(8,128)(2,1)}, bf16[256,1536]{1,0:T(8,128)(2,1)}, bf...) custom-call(bf16[1024,2048]{1,0:T(8,128)(2,1)} %all-gather.9.cloned., ...), custom_call_target="tpu_custom_call" | custom-call | flops 6000000000 | bytes 30000000 | tf_op jit(solution)/shard_map/gated_grads/pallas_call | solution.py:620
  383.5 13.7 %gated_grads.3 = (bf16[256,1536]{1,0:T(8,128)(2,1)}, bf16[256,1536]{1,0:T(8,128)(2,1)}, bf16[256,1536]{1,0:T(8,128)(2,1)}, bf16[256,1536]{1,0:T(8,128)(2,1)}, bf...) custom-call(bf16[1024,2048]{1,0:T(8,128)(2,1)} %all-gather.9.cloned., ...), custom_call_target="tpu_custom_call" | custom-call | flops 6000000000 | bytes 30000000 | tf_op jit(solution)/shard_map/gated_grads/pallas_call | solution.py:620
  398.2 5.5 collective-permute-done.69
  404.8 4.3 reduce-scatter.7.cloned.1.call-done
  419.2 11.9 %mlp_out.1 = bf16[1024,2048]{1,0:T(8,128)(2,1)} custom-call(s32[1]{0:T(128)} %bitcast.place_ref, bf16[1024,768]{1,0:T(8,128)(2,1)} %get-tuple-element.418.refs_0_, bf16[1024,768]{1,0:T(8,128)(2,1)} %get-tuple-element.419.refs_1_, bf16[768,256]{1,0:T(8,128)(2,1)} %get-tuple-element.331.refs_1_.refs_2_, ...), custom_call_target="tpu_custom_call" | custom-call | flops 6000000000 | bytes 30000000 | tf_op jit(solution)/shard_map/mlp_out/pallas_call | solution.py:426
  431.2 4.4 collective-permute-done.75
  442.4 10.0 %collective-permute-done.73 = bf16[256,1536]{1,0:T(8,128)(2,1)} collective-permute-done((bf16[256,1536]{1,0:T(8,128)(2,1)}, bf16[256,1536]{1,0:T(8,128)(2,1)}, u32[]{:S(2)}, u32[]{:S(2)}) %collective-permute-start.73) | collective-permute-done | bytes 786464 | tf_op jit(solution)/shard_map/ppermute | solution.py:974
  458.9 10.2 %mixer_back.1 = (f32[1024,640]{1,0:T(8,128)}, bf16[1024,640]{1,0:T(8,128)(2,1)}) custom-call(bf16[1024,2048]{1,0:T(8,128)(2,1)} %all-gather.11.cloned.1.call-done.refs_0_.refs_1_, bf16[640,256]{1,0:T(8,128)(2,1)} %refs_1_.5, bf16[640,256]{1,0:T(8,128)(2,1)} %collective-permute-done.17.refs_2_, bf16[640,256]{1,0:T(8,128)(2,1)} %collective-permute-done.19.refs_3_, ...), custom_call_target="tpu_custom_call" | custom-call | flops 6000000000 | bytes 30000000 | tf_op jit(solution)/shard_map/mixer_back/pallas_call | solution.py:496
  475.0 23.5 %core_backward.1 = (bf16[1024,640]{1,0:T(8,128)(2,1)}, f32[640,1280]{1,0:T(8,128)}, f32[8,640]{1,0:T(8,128)}) custom-call(s32[1]{0:T(128)} %constant.88.clone.1.place, f32[1024,640]{1,0:T(8,128)} %get-tuple-element.442.grad, f32[1024,1280]{1,0:T(8,128)} %mixer_in.1.branch.entry_pre.refs_9_.entry_tail, f32[1024,640]{1,0:T(8,128)} %get-tuple-element.443.mixed_in, ...), custom_call_target="tpu_custom_call" | custom-call | flops 6000000000 | bytes 30000000 | tf_op jit(solution)/shard_map/core_backward/pallas_call | solution.py:298
  504.5 9.7 %output_grads.1 = (bf16[640,256]{1,0:T(8,128)(2,1)}, bf16[640,256]{1,0:T(8,128)(2,1)}, bf16[640,256]{1,0:T(8,128)(2,1)}, bf16[640,256]{1,0:T(8,128)(2,1)}, bf16[...) custom-call(bf16[1024,640]{1,0:T(8,128)(2,1)} %get-tuple-element.322.refs_0, ...), custom_call_target="tpu_custom_call" | custom-call | flops 6000000000 | bytes 30000000 | tf_op jit(solution)/shard_map/output_grads/pallas_call | solution.py:620
  516.2 9.7 %branch_grads.1 = (bf16[256,640]{1,0:T(8,128)(2,1)}, bf16[256,640]{1,0:T(8,128)(2,1)}, bf16[256,640]{1,0:T(8,128)(2,1)}, bf16[256,640]{1,0:T(8,128)(2,1)}, bf16[...) custom-call(bf16[1024,2048]{1,0:T(8,128)(2,1)} %get-tuple-element.311.refs_, ...), custom_call_target="tpu_custom_call" | custom-call | flops 6000000000 | bytes 30000000 | tf_op jit(solution)/shard_map/branch_grads/pallas_call | solution.py:620
  528.2 7.3 %pack_tables.1.refs_2_ = bf16[2048,256]{1,0:T(8,128)(2,1)} custom-call(s32[8]{0:T(128)} %compare_select_fusion.5.order_ref, f32[640,1280]{1,0:T(8,128)} %get-tuple-element.470.gate_ref, f32[8,640]{1,0:T(8,128)} %pad_maximum_fusion.6.small_ref), custom_call_target="tpu_custom_call" | custom-call | flops 6000000000 | bytes 30000000 | tf_op jit(solution)/shard_map/pack_tables/pallas_call | solution.py:745
  540.1 6.2 collective-permute-done.87
  548.6 10.2 %input_grads.1 = (bf16[256,896]{1,0:T(8,128)(2,1)}, bf16[256,896]{1,0:T(8,128)(2,1)}, bf16[256,896]{1,0:T(8,128)(2,1)}, bf16[256,896]{1,0:T(8,128)(2,1)}, bf16[2...) custom-call(bf16[1024,2048]{1,0:T(8,128)(2,1)} %get-tuple-element.311.refs_0, ...), custom_call_target="tpu_custom_call" | custom-call | flops 6000000000 | bytes 30000000 | tf_op jit(solution)/shard_map/input_grads/pallas_call | solution.py:620
  561.3 11.1 %mixer_in_grad.1 = bf16[1024,2048]{1,0:T(8,128)(2,1)} custom-call(s32[1]{0:T(128)} %bitcast.place_ref, bf16[1024,640]{1,0:T(8,128)(2,1)} %get-tuple-element.503.refs_1_.refs_0_, bf16[1024,640]{1,0:T(8,128)(2,1)} %get-tuple-element.504.refs_1_, bf16[256,640]{1,0:T(8,128)(2,1)} %refs_2_.1, bf16[256,640]{1,0:T(8,128)(2,1)} %copy-done.111, ...), custom_call_target="tpu_custom_call" | custom-call | flops 6000000000 | bytes 30000000 | tf_op jit(solution)/shard_map/mixer_in_grad/pallas_call | solution.py:426
  589.0 3.9 collective-permute-done.97
  594.7 5.4 collective-permute-done.96
  619.1 7.7 %collective-permute-done.102 = bf16[256,896]{1,0:T(8,128)(2,1)S(1)} collective-permute-done((bf16[256,896]{1,0:T(8,128)(2,1)S(1)}, bf16[256,896]{1,0:T(8,128)(2,1)S(1)}, u32[]{:S(2)}, u32[]{:S(2)}) %collective-permute-start.102) | collective-permute-done | bytes 458784 | tf_op jit(solution)/shard_map/ppermute | solution.py:974
  630.0 3.5 fusion.4.refs_0_
  645.4 3.9 collective-permute-done.104
  (601 shorter events, 236.2 us)
Async XLA Ops:
  7.3 66.3 %all-gather.5.cloned.1.call-start = ((), (), s32[]{:S(2)}) async-start(), calls=%async_computation.4 | async-start | bytes 5242880 | tf_op jit(solution)/shard_map/all_gather | solution.py:1024
  8.1 145.6 %all-gather.7.cloned.1.call-start = ((), (), s32[]{:S(2)}) async-start(), calls=%async_computation.6 | async-start | bytes 5242880 | tf_op jit(solution)/shard_map/all_gather | solution.py:1024
  8.8 184.7 %reduce-scatter.5.cloned.1.call-start = ((), (), s32[]{:S(2)}) async-start(), calls=%async_computation.5 | async-start | bytes 5242880 | tf_op jit(solution)/shard_map/reduce_scatter | solution.py:1028
  56.4 25.5 %collective-permute-start.17 = (bf16[640,256]{1,0:T(8,128)(2,1)}, bf16[640,256]{1,0:T(8,128)(2,1)}, u32[]{:S(2)}, u32[]{:S(2)}) collective-permute-start(bf16[640,256]{1,0:T(8,128)(2,1)} %refs_1_.5), channel_id=1, source_target_pairs={{8,0},{16,8},{24,16},{28,24},{20,28},{12,20},{4,12},{0,4},{9,1},{1... | collective-permute-start | bytes 983048 | tf_op jit(solution)/shard_map/ppermute | solution.py:974
  59.9 23.2 %collective-permute-start.16 = (bf16[256,640]{1,0:T(8,128)(2,1)S(1)}, bf16[256,640]{1,0:T(8,128)(2,1)S(1)}, u32[]{:S(2)}, u32[]{:S(2)}) collective-permute-start(bf16[256,640]{1,0:T(8,128)(2,1)S(1)} %collective-permute-done.14.refs_16_.refs_17_), channel_id=1, source_target_pairs={{0,8},{8,16},{16,24},{24,28},{28,20},{20,12},{12,4},{4,0},{1,9},{9... | collective-permute-start | bytes 983048 | tf_op jit(solution)/shard_map/ppermute | solution.py:974
  63.4 20.9 %collective-permute-start.21 = (bf16[256,640]{1,0:T(8,128)(2,1)S(1)}, bf16[256,640]{1,0:T(8,128)(2,1)}, u32[]{:S(2)}, u32[]{:S(2)}) collective-permute-start(bf16[256,640]{1,0:T(8,128)(2,1)S(1)} %collective-permute-done.13.refs_10_.refs_11_), channel_id=1, source_target_pairs={{8,0},{16,8},{24,16},{28,24},{20,28},{12,20},{4,12},{0,4},{9,1},{1... | collective-permute-start | bytes 983048 | tf_op jit(solution)/shard_map/ppermute | solution.py:974
  64.6 21.0 %collective-permute-start.20 = (bf16[640,256]{1,0:T(8,128)(2,1)}, bf16[640,256]{1,0:T(8,128)(2,1)}, u32[]{:S(2)}, u32[]{:S(2)}) collective-permute-start(bf16[640,256]{1,0:T(8,128)(2,1)} %refs_1_.5), channel_id=1, source_target_pairs={{0,8},{8,16},{16,24},{24,28},{28,20},{20,12},{12,4},{4,0},{1,9},{9... | collective-permute-start | bytes 983048 | tf_op jit(solution)/shard_map/ppermute | solution.py:974
  99.8 21.9 %collective-permute-start.26 = (bf16[256,1536]{1,0:T(8,128)(2,1)S(1)}, bf16[256,1536]{1,0:T(8,128)(2,1)S(1)}, u32[]{:S(2)}, u32[]{:S(2)}) collective-permute-start(bf16[256,1536]{1,0:T(8,128)(2,1)S(1)} %pad_maximum_fusion.3.refs_1_), channel_id=1, source_target_pairs={{8,0},{16,8},{24,16},{28,24},{20,28},{12,20},{4,12},{0,4},{9,1},{1... | collective-permute-start | bytes 2359304 | tf_op jit(solution)/shard_map/ppermute | solution.py:974
  107.9 32.8 %collective-permute-start.30 = (bf16[256,1536]{1,0:T(8,128)(2,1)S(1)}, bf16[256,1536]{1,0:T(8,128)(2,1)}, u32[]{:S(2)}, u32[]{:S(2)}) collective-permute-start(bf16[256,1536]{1,0:T(8,128)(2,1)S(1)} %pad_maximum_fusion.3.refs_1_), channel_id=1, source_target_pairs={{0,8},{8,16},{16,24},{24,28},{28,20},{20,12},{12,4},{4,0},{1,9},{9... | collective-permute-start | bytes 2359304 | tf_op jit(solution)/shard_map/ppermute | solution.py:974
  120.0 20.6 %collective-permute-start.28 = (bf16[256,1536]{1,0:T(8,128)(2,1)S(1)}, bf16[256,1536]{1,0:T(8,128)(2,1)}, u32[]{:S(2)}, u32[]{:S(2)}) collective-permute-start(bf16[256,1536]{1,0:T(8,128)(2,1)S(1)} %pad_maximum_fusion.4.refs_1_), channel_id=1, source_target_pairs={{0,8},{8,16},{16,24},{24,28},{28,20},{20,12},{12,4},{4,0},{1,9},{9... | collective-permute-start | bytes 2359304 | tf_op jit(solution)/shard_map/ppermute | solution.py:974
  148.5 88.3 %all-gather.9.cloned.1.call-start = ((), (), s32[]{:S(2)}) async-start(), calls=%async_computation.7 | async-start | bytes 5242880 | tf_op jit(solution)/shard_map/all_gather | solution.py:1024
  149.6 20.6 %collective-permute-start.33 = (bf16[256,1536]{1,0:T(8,128)(2,1)S(1)}, bf16[256,1536]{1,0:T(8,128)(2,1)}, u32[]{:S(2)}, u32[]{:S(2)}) collective-permute-start(bf16[256,1536]{1,0:T(8,128)(2,1)S(1)} %copy-done.23), channel_id=1, source_target_pairs={{8,0},{16,8},{24,16},{28,24},{20,28},{12,20},{4,12},{0,4},{9,1},{1... | collective-permute-start | bytes 2359304 | tf_op jit(solution)/shard_map/ppermute | solution.py:974
  150.9 20.8 %collective-permute-start.32 = (bf16[256,1536]{1,0:T(8,128)(2,1)}, bf16[256,1536]{1,0:T(8,128)(2,1)}, u32[]{:S(2)}, u32[]{:S(2)}) collective-permute-start(bf16[256,1536]{1,0:T(8,128)(2,1)} %collective-permute-done.30.refs_8_), channel_id=1, source_target_pairs={{0,8},{8,16},{16,24},{24,28},{28,20},{20,12},{12,4},{4,0},{1,9},{9... | collective-permute-start | bytes 2359304 | tf_op jit(solution)/shard_map/ppermute | solution.py:974
  151.6 29.5 %collective-permute-start.37 = (bf16[256,1536]{1,0:T(8,128)(2,1)}, bf16[256,1536]{1,0:T(8,128)(2,1)}, u32[]{:S(2)}, u32[]{:S(2)}) collective-permute-start(bf16[256,1536]{1,0:T(8,128)(2,1)} %collective-permute-done.29.refs_3_), channel_id=1, source_target_pairs={{8,0},{16,8},{24,16},{28,24},{20,28},{12,20},{4,12},{0,4},{9,1},{1... | collective-permute-start | bytes 2359304 | tf_op jit(solution)/shard_map/ppermute | solution.py:974
  152.9 29.6 %collective-permute-start.36 = (bf16[256,1536]{1,0:T(8,128)(2,1)}, bf16[256,1536]{1,0:T(8,128)(2,1)}, u32[]{:S(2)}, u32[]{:S(2)}) collective-permute-start(bf16[256,1536]{1,0:T(8,128)(2,1)} %collective-permute-done.28.refs_8_), channel_id=1, source_target_pairs={{0,8},{8,16},{16,24},{24,28},{28,20},{20,12},{12,4},{4,0},{1,9},{9... | collective-permute-start | bytes 2359304 | tf_op jit(solution)/shard_map/ppermute | solution.py:974
  171.7 19.3 %collective-permute-start.34 = (bf16[256,1536]{1,0:T(8,128)(2,1)}, bf16[256,1536]{1,0:T(8,128)(2,1)}, u32[]{:S(2)}, u32[]{:S(2)}) collective-permute-start(bf16[256,1536]{1,0:T(8,128)(2,1)} %collective-permute-done.32.refs_7_), channel_id=1, source_target_pairs={{0,8},{8,16},{16,24},{24,28},{28,20},{20,12},{12,4},{4,0},{1,9},{9... | collective-permute-start | bytes 2359304 | tf_op jit(solution)/shard_map/ppermute | solution.py:974
  196.8 212.3 %reduce-scatter.7.cloned.1.call-start = ((), (), s32[]{:S(2)}) async-start(), calls=%async_computation.8 | async-start | bytes 5242880 | tf_op jit(solution)/shard_map/reduce_scatter | solution.py:1028
  196.9 20.7 %collective-permute-start.41 = (bf16[256,1536]{1,0:T(8,128)(2,1)}, bf16[256,1536]{1,0:T(8,128)(2,1)S(1)}, u32[]{:S(2)}, u32[]{:S(2)}) collective-permute-start(bf16[256,1536]{1,0:T(8,128)(2,1)} %collective-permute-done.37.refs_4_), channel_id=1, source_target_pairs={{8,0},{16,8},{24,16},{28,24},{20,28},{12,20},{4,12},{0,4},{9,1},{1... | collective-permute-start | bytes 2359304 | tf_op jit(solution)/shard_map/ppermute | solution.py:974
  198.4 20.8 %collective-permute-start.40 = (bf16[256,1536]{1,0:T(8,128)(2,1)}, bf16[256,1536]{1,0:T(8,128)(2,1)}, u32[]{:S(2)}, u32[]{:S(2)}) collective-permute-start(bf16[256,1536]{1,0:T(8,128)(2,1)} %collective-permute-done.36.refs_7_), channel_id=1, source_target_pairs={{0,8},{8,16},{16,24},{24,28},{28,20},{20,12},{12,4},{4,0},{1,9},{9... | collective-permute-start | bytes 2359304 | tf_op jit(solution)/shard_map/ppermute | solution.py:974
  198.9 35.5 %collective-permute-start.38 = (bf16[256,1536]{1,0:T(8,128)(2,1)}, bf16[256,1536]{1,0:T(8,128)(2,1)S(1)}, u32[]{:S(2)}, u32[]{:S(2)}) collective-permute-start(bf16[256,1536]{1,0:T(8,128)(2,1)} %copy-done.95), channel_id=1, source_target_pairs={{8,0},{16,8},{24,16},{28,24},{20,28},{12,20},{4,12},{0,4},{9,1},{1... | collective-permute-start | bytes 2359304 | tf_op jit(solution)/shard_map/ppermute | solution.py:974
  200.4 27.1 %collective-permute-start.39 = (bf16[768,256]{1,0:T(8,128)(2,1)S(1)}, bf16[768,256]{1,0:T(8,128)(2,1)S(1)}, u32[]{:S(2)}, u32[]{:S(2)}) collective-permute-start(bf16[768,256]{1,0:T(8,128)(2,1)S(1)} %copy-done.42), channel_id=1, source_target_pairs={{0,8},{8,16},{16,24},{24,28},{28,20},{20,12},{12,4},{4,0},{1,9},{9... | collective-permute-start | bytes 1179656 | tf_op jit(solution)/shard_map/ppermute | solution.py:974
  219.2 32.1 %collective-permute-start.44 = (bf16[256,1536]{1,0:T(8,128)(2,1)}, bf16[256,1536]{1,0:T(8,128)(2,1)}, u32[]{:S(2)}, u32[]{:S(2)}) collective-permute-start(bf16[256,1536]{1,0:T(8,128)(2,1)} %collective-permute-done.40.refs_6_), channel_id=1, source_target_pairs={{0,8},{8,16},{16,24},{24,28},{28,20},{20,12},{12,4},{4,0},{1,9},{9... | collective-permute-start | bytes 2359304 | tf_op jit(solution)/shard_map/ppermute | solution.py:974
  219.7 30.0 %collective-permute-start.45 = (bf16[768,256]{1,0:T(8,128)(2,1)S(1)}, bf16[768,256]{1,0:T(8,128)(2,1)}, u32[]{:S(2)}, u32[]{:S(2)}) collective-permute-start(bf16[768,256]{1,0:T(8,128)(2,1)S(1)} %copy-done.42), channel_id=1, source_target_pairs={{8,0},{16,8},{24,16},{28,24},{20,28},{12,20},{4,12},{0,4},{9,1},{1... | collective-permute-start | bytes 1179656 | tf_op jit(solution)/shard_map/ppermute | solution.py:974
  227.5 25.8 %collective-permute-start.42 = (bf16[768,256]{1,0:T(8,128)(2,1)S(1)}, bf16[768,256]{1,0:T(8,128)(2,1)}, u32[]{:S(2)}, u32[]{:S(2)}) collective-permute-start(bf16[768,256]{1,0:T(8,128)(2,1)S(1)} %collective-permute-done.39.refs_8_.refs_9_), channel_id=1, source_target_pairs={{0,8},{8,16},{16,24},{24,28},{28,20},{20,12},{12,4},{4,0},{1,9},{9... | collective-permute-start | bytes 1179656 | tf_op jit(solution)/shard_map/ppermute | solution.py:974
  286.1 20.8 %collective-permute-start.54 = (bf16[768,256]{1,0:T(8,128)(2,1)S(1)}, bf16[768,256]{1,0:T(8,128)(2,1)S(1)}, u32[]{:S(2)}, u32[]{:S(2)}) collective-permute-start(bf16[768,256]{1,0:T(8,128)(2,1)S(1)} %collective-permute-done.51.refs_7_.refs_16_), channel_id=1, source_target_pairs={{0,8},{8,16},{16,24},{24,28},{28,20},{20,12},{12,4},{4,0},{1,9},{9... | collective-permute-start | bytes 1179656 | tf_op jit(solution)/shard_map/ppermute | solution.py:974
  286.6 20.9 %collective-permute-start.53 = (bf16[768,256]{1,0:T(8,128)(2,1)}, bf16[768,256]{1,0:T(8,128)(2,1)S(1)}, u32[]{:S(2)}, u32[]{:S(2)}) collective-permute-start(bf16[768,256]{1,0:T(8,128)(2,1)} %get-tuple-element.355), channel_id=1, source_target_pairs={{8,0},{16,8},{24,16},{28,24},{20,28},{12,20},{4,12},{0,4},{9,1},{1... | collective-permute-start | bytes 1179656 | tf_op jit(solution)/shard_map/ppermute | solution.py:974
  288.1 21.1 %collective-permute-start.59 = (bf16[768,256]{1,0:T(8,128)(2,1)}, bf16[768,256]{1,0:T(8,128)(2,1)S(1)}, u32[]{:S(2)}, u32[]{:S(2)}) collective-permute-start(bf16[768,256]{1,0:T(8,128)(2,1)} %get-tuple-element.358), channel_id=1, source_target_pairs={{0,8},{8,16},{16,24},{24,28},{28,20},{20,12},{12,4},{4,0},{1,9},{9... | collective-permute-start | bytes 1179656 | tf_op jit(solution)/shard_map/ppermute | solution.py:974
  309.3 22.9 %collective-permute-start.63 = (bf16[768,256]{1,0:T(8,128)(2,1)S(1)}, bf16[768,256]{1,0:T(8,128)(2,1)S(1)}, u32[]{:S(2)}, u32[]{:S(2)}) collective-permute-start(bf16[768,256]{1,0:T(8,128)(2,1)S(1)} %add_convert_fusion.24), channel_id=1, source_target_pairs={{0,8},{8,16},{16,24},{24,28},{28,20},{20,12},{12,4},{4,0},{1,9},{9... | collective-permute-start | bytes 1179656 | tf_op jit(solution)/shard_map/ppermute | solution.py:974
  365.2 93.6 %all-gather.11.cloned.1.call-start = ((), (), s32[]{:S(2)}) async-start(), calls=%async_computation.9 | async-start | bytes 5242880 | tf_op jit(solution)/shard_map/all_gather | solution.py:1024
  381.8 21.9 %collective-permute-start.69 = (bf16[256,1536]{1,0:T(8,128)(2,1)}, bf16[256,1536]{1,0:T(8,128)(2,1)S(1)}, u32[]{:S(2)}, u32[]{:S(2)}) collective-permute-start(bf16[256,1536]{1,0:T(8,128)(2,1)} %get-tuple-element.405), channel_id=1, source_target_pairs={{0,8},{8,16},{16,24},{24,28},{28,20},{20,12},{12,4},{4,0},{1,9},{9... | collective-permute-start | bytes 2359304 | tf_op jit(solution)/shard_map/ppermute | solution.py:974
  414.7 189.9 %reduce-scatter.9.cloned.1.call-start = ((), (), s32[]{:S(2)}) async-start(), calls=%async_computation.10 | async-start | bytes 5242880 | tf_op jit(solution)/shard_map/reduce_scatter | solution.py:1028
  414.7 20.8 %collective-permute-start.75 = (bf16[256,1536]{1,0:T(8,128)(2,1)}, bf16[256,1536]{1,0:T(8,128)(2,1)}, u32[]{:S(2)}, u32[]{:S(2)}) collective-permute-start(bf16[256,1536]{1,0:T(8,128)(2,1)} %get-tuple-element.411), channel_id=1, source_target_pairs={{8,0},{16,8},{24,16},{28,24},{20,28},{12,20},{4,12},{0,4},{9,1},{1... | collective-permute-start | bytes 2359304 | tf_op jit(solution)/shard_map/ppermute | solution.py:974
  416.2 23.3 %collective-permute-start.74 = (bf16[256,1536]{1,0:T(8,128)(2,1)}, bf16[256,1536]{1,0:T(8,128)(2,1)}, u32[]{:S(2)}, u32[]{:S(2)}) collective-permute-start(bf16[256,1536]{1,0:T(8,128)(2,1)} %get-tuple-element.412), channel_id=1, source_target_pairs={{0,8},{8,16},{16,24},{24,28},{28,20},{20,12},{12,4},{4,0},{1,9},{9... | collective-permute-start | bytes 2359304 | tf_op jit(solution)/shard_map/ppermute | solution.py:974
  416.8 35.6 %collective-permute-start.73 = (bf16[256,1536]{1,0:T(8,128)(2,1)}, bf16[256,1536]{1,0:T(8,128)(2,1)}, u32[]{:S(2)}, u32[]{:S(2)}) collective-permute-start(bf16[256,1536]{1,0:T(8,128)(2,1)} %add_convert_fusion.10), channel_id=1, source_target_pairs={{8,0},{16,8},{24,16},{28,24},{20,28},{12,20},{4,12},{0,4},{9,1},{1... | collective-permute-start | bytes 2359304 | tf_op jit(solution)/shard_map/ppermute | solution.py:974
  418.3 37.8 %collective-permute-start.72 = (bf16[256,1536]{1,0:T(8,128)(2,1)}, bf16[256,1536]{1,0:T(8,128)(2,1)}, u32[]{:S(2)}, u32[]{:S(2)}) collective-permute-start(bf16[256,1536]{1,0:T(8,128)(2,1)} %add_convert_fusion.9), channel_id=1, source_target_pairs={{0,8},{8,16},{16,24},{24,28},{28,20},{20,12},{12,4},{4,0},{1,9},{9... | collective-permute-start | bytes 2359304 | tf_op jit(solution)/shard_map/ppermute | solution.py:974
  438.1 31.2 %collective-permute-start.77 = (bf16[256,1536]{1,0:T(8,128)(2,1)}, bf16[256,1536]{1,0:T(8,128)(2,1)}, u32[]{:S(2)}, u32[]{:S(2)}) collective-permute-start(bf16[256,1536]{1,0:T(8,128)(2,1)} %add_convert_fusion.8), channel_id=1, source_target_pairs={{8,0},{16,8},{24,16},{28,24},{20,28},{12,20},{4,12},{0,4},{9,1},{1... | collective-permute-start | bytes 2359304 | tf_op jit(solution)/shard_map/ppermute | solution.py:974
  441.8 31.1 %collective-permute-start.76 = (bf16[256,1536]{1,0:T(8,128)(2,1)}, bf16[256,1536]{1,0:T(8,128)(2,1)}, u32[]{:S(2)}, u32[]{:S(2)}) collective-permute-start(bf16[256,1536]{1,0:T(8,128)(2,1)} %add_convert_fusion.7), channel_id=1, source_target_pairs={{0,8},{8,16},{16,24},{24,28},{28,20},{20,12},{12,4},{4,0},{1,9},{9... | collective-permute-start | bytes 2359304 | tf_op jit(solution)/shard_map/ppermute | solution.py:974
  454.6 43.9 %collective-permute-start.81 = (bf16[256,1536]{1,0:T(8,128)(2,1)}, bf16[256,1536]{1,0:T(8,128)(2,1)}, u32[]{:S(2)}, u32[]{:S(2)}) collective-permute-start(bf16[256,1536]{1,0:T(8,128)(2,1)} %add_convert_fusion.6), channel_id=1, source_target_pairs={{8,0},{16,8},{24,16},{28,24},{20,28},{12,20},{4,12},{0,4},{9,1},{1... | collective-permute-start | bytes 2359304 | tf_op jit(solution)/shard_map/ppermute | solution.py:974
  458.3 40.3 %collective-permute-start.80 = (bf16[256,1536]{1,0:T(8,128)(2,1)}, bf16[256,1536]{1,0:T(8,128)(2,1)}, u32[]{:S(2)}, u32[]{:S(2)}) collective-permute-start(bf16[256,1536]{1,0:T(8,128)(2,1)} %add_convert_fusion.5), channel_id=1, source_target_pairs={{0,8},{8,16},{16,24},{24,28},{28,20},{20,12},{12,4},{4,0},{1,9},{9... | collective-permute-start | bytes 2359304 | tf_op jit(solution)/shard_map/ppermute | solution.py:974
  458.9 169.3 %reduce-scatter.11.cloned.1.call-start = ((), (), s32[]{:S(2)}) async-start(), calls=%async_computation.11 | async-start | bytes 5242880 | tf_op jit(solution)/shard_map/reduce_scatter | solution.py:1028
  471.6 30.8 %collective-permute-start.79 = (bf16[256,1536]{1,0:T(8,128)(2,1)}, bf16[256,1536]{1,0:T(8,128)(2,1)S(1)}, u32[]{:S(2)}, u32[]{:S(2)}) collective-permute-start(bf16[256,1536]{1,0:T(8,128)(2,1)} %add_convert_fusion.4), channel_id=1, source_target_pairs={{8,0},{16,8},{24,16},{28,24},{20,28},{12,20},{4,12},{0,4},{9,1},{1... | collective-permute-start | bytes 2359304 | tf_op jit(solution)/shard_map/ppermute | solution.py:974
  474.3 30.2 %collective-permute-start.78 = (bf16[256,1536]{1,0:T(8,128)(2,1)S(1)}, bf16[256,1536]{1,0:T(8,128)(2,1)S(1)}, u32[]{:S(2)}, u32[]{:S(2)}) collective-permute-start(bf16[256,1536]{1,0:T(8,128)(2,1)S(1)} %add_convert_fusion.3), channel_id=1, source_target_pairs={{0,8},{8,16},{16,24},{24,28},{28,20},{20,12},{12,4},{4,0},{1,9},{9... | collective-permute-start | bytes 2359304 | tf_op jit(solution)/shard_map/ppermute | solution.py:974
  500.0 25.9 %collective-permute-start.85 = (bf16[256,1536]{1,0:T(8,128)(2,1)S(1)}, bf16[256,1536]{1,0:T(8,128)(2,1)S(1)}, u32[]{:S(2)}, u32[]{:S(2)}) collective-permute-start(bf16[256,1536]{1,0:T(8,128)(2,1)S(1)} %add_convert_fusion.2), channel_id=1, source_target_pairs={{0,8},{8,16},{16,24},{24,28},{28,20},{20,12},{12,4},{4,0},{1,9},{9... | collective-permute-start | bytes 2359304 | tf_op jit(solution)/shard_map/ppermute | solution.py:974
  503.4 22.5 %collective-permute-start.84 = (bf16[256,1536]{1,0:T(8,128)(2,1)}, bf16[256,1536]{1,0:T(8,128)(2,1)S(1)}, u32[]{:S(2)}, u32[]{:S(2)}) collective-permute-start(bf16[256,1536]{1,0:T(8,128)(2,1)} %add_convert_fusion.1), channel_id=1, source_target_pairs={{8,0},{16,8},{24,16},{28,24},{20,28},{12,20},{4,12},{0,4},{9,1},{1... | collective-permute-start | bytes 2359304 | tf_op jit(solution)/shard_map/ppermute | solution.py:974
  514.2 22.4 %collective-permute-start.82 = (bf16[640,256]{1,0:T(8,128)(2,1)}, bf16[640,256]{1,0:T(8,128)(2,1)S(1)}, u32[]{:S(2)}, u32[]{:S(2)}) collective-permute-start(bf16[640,256]{1,0:T(8,128)(2,1)} %get-tuple-element.458), channel_id=1, source_target_pairs={{8,0},{16,8},{24,16},{28,24},{20,28},{12,20},{4,12},{0,4},{9,1},{1... | collective-permute-start | bytes 983048 | tf_op jit(solution)/shard_map/ppermute | solution.py:974
  515.5 20.0 %collective-permute-start.83 = (bf16[640,256]{1,0:T(8,128)(2,1)}, bf16[640,256]{1,0:T(8,128)(2,1)S(1)}, u32[]{:S(2)}, u32[]{:S(2)}) collective-permute-start(bf16[640,256]{1,0:T(8,128)(2,1)} %get-tuple-element.461), channel_id=1, source_target_pairs={{0,8},{8,16},{16,24},{24,28},{28,20},{20,12},{12,4},{4,0},{1,9},{9... | collective-permute-start | bytes 983048 | tf_op jit(solution)/shard_map/ppermute | solution.py:974
  537.9 20.9 %collective-permute-start.93 = (bf16[256,640]{1,0:T(8,128)(2,1)S(1)}, bf16[256,640]{1,0:T(8,128)(2,1)S(1)}, u32[]{:S(2)}, u32[]{:S(2)}) collective-permute-start(bf16[256,640]{1,0:T(8,128)(2,1)S(1)} %add_convert_fusion.33), channel_id=1, source_target_pairs={{8,0},{16,8},{24,16},{28,24},{20,28},{12,20},{4,12},{0,4},{9,1},{1... | collective-permute-start | bytes 983048 | tf_op jit(solution)/shard_map/ppermute | solution.py:974
  539.4 20.3 %collective-permute-start.92 = (bf16[256,640]{1,0:T(8,128)(2,1)S(1)}, bf16[256,640]{1,0:T(8,128)(2,1)S(1)}, u32[]{:S(2)}, u32[]{:S(2)}) collective-permute-start(bf16[256,640]{1,0:T(8,128)(2,1)S(1)} %add_convert_fusion.32), channel_id=1, source_target_pairs={{0,8},{8,16},{16,24},{24,28},{28,20},{20,12},{12,4},{4,0},{1,9},{9... | collective-permute-start | bytes 983048 | tf_op jit(solution)/shard_map/ppermute | solution.py:974
  (204 other events, 2542.5 us)
Sparse Core Ops, SparseCore 0:
  9.7 37.1 all-gather.4
  48.5 34.4 all-gather.6
  148.6 44.8 reduce-scatter.4
  196.9 34.4 all-gather.8
  365.3 43.7 reduce-scatter.6
  414.8 34.4 all-gather.10
  459.0 44.4 reduce-scatter.8
  572.6 44.0 reduce-scatter.10

commit v5 on v4

--- a/solution.py
+++ b/solution.py
@@ -98,7 +98,7 @@
         ).astype(bf16)
         return before
 
-    last_entry[...] = lax.fori_loop(0, length // 16, convolve, last_entry[...], unroll=4)
+    last_entry[...] = lax.fori_loop(0, length // 16, convolve, last_entry[...], unroll=8)
     pre[...] = jnp.dot(mixed_low[...], gates[...], preferred_element_type=f32)
     rate_bias = small[5:6, :]
     entry_bias = small[6:7, :]
@@ -128,7 +128,7 @@
         )
         return carry
 
-    last_state[...] = lax.fori_loop(0, length // 16, scan, last_state[...], unroll=4)
+    last_state[...] = lax.fori_loop(0, length // 16, scan, last_state[...], unroll=8)
 
 
 def core_backward_kernel(
@@ -193,7 +193,7 @@
         return after_decay, carried_after
 
     after_decay, carried_after = lax.fori_loop(
-        0, length // 16, reverse, (next_decay[...], next_carried[...]), unroll=4
+        0, length // 16, reverse, (next_decay[...], next_carried[...]), unroll=8
     )
     next_decay[...] = after_decay
     next_carried[...] = carried_after
@@ -237,7 +237,7 @@
         length // 16,
         convolve,
         [next_mixed[8 * k : 8 * k + 8, :] for k in range(3)],
-        unroll=4,
+        unroll=8,
     )
     for k in range(3):
         next_mixed[8 * k : 8 * k + 8, :] = after[k]
@@ -776,7 +776,7 @@
                 out[at, to] = (part * scale * gain_ref[:, to]).astype(bf16)
             return carry
 
-        lax.fori_loop(0, rows // 16, step, 0, unroll=2)
+        lax.fori_loop(0, rows // 16, step, 0, unroll=4)
 
         @pl.when(j == place_ref[0])
         def _():
@@ -1276,6 +1276,11 @@
     pair_scatters = [Scatter(ring, part, False)]
     lanes.did(8.0, part[0])
     lanes.add(pair_scatters[0])
+    (late,) = lanes.gate(branch_low)
+    mixer_in_grad = spread(
+        [(late, 0, width)], pair_weights[:1], place, (), True, "mixer_in_grad"
+    )
+    lanes.did(6.5, mixer_in_grad)
     decay_grad = lru_scale * small_grads[7:8] * jax.nn.sigmoid(-decay_full)
     small_grads = jnp.concatenate([small_grads[:7], decay_grad], axis=0)
     (gate_grads,) = lanes.gate(gate_grads)
@@ -1288,22 +1293,19 @@
     pair_scatters.append(Scatter(ring, part, True))
     lanes.did(9.0, part[0])
     lanes.add(pair_scatters[1])
-    branch_late, entry_late = lanes.gate(branch_low, entry_low)
+    (late,) = lanes.gate(entry_low)
     mixer_in_grad = spread(
-        [(branch_late, 0, width), (entry_late, 0, width)],
-        pair_weights,
-        place,
-        (),
-        True,
-        "mixer_in_grad",
-    )
-    lanes.did(11.5, mixer_in_grad)
+        [(late, 0, width)], pair_weights[1:], place, (), True, "mixer_in_grad", mixer_in_grad
+    )
+    lanes.did(7.5, mixer_in_grad)
     mixer_in_grad = tensor_reduce(mixer_in_grad)
     arrival = lanes.now + 30.0
 
     (mlp_sum,) = lanes.gate(mlp_sum)
     layer_out = ring.columns_out((middle + mlp_sum.astype(f32)).astype(bf16), shard)
     lanes.did(6.0, layer_out)
+    lanes.until(*gated_scatters)
+    gated_wgrads = [scatter.result(lanes.gate) for scatter in gated_scatters]
     lanes.catch_up(arrival)
     (mixer_in_grad,) = lanes.gate(mixer_in_grad)
     tokens_norm_grad = norm_backward(
@@ -1324,7 +1326,6 @@
     rate_wgrad = rate_wgrad[:, :, :block_width]
     entry_wgrad = entry_wgrad[:, :, :block_width]
     singles = [column_grads[:, :, k] for k in range(taps + 4)]
-    gated_wgrads = [scatter.result(free) for scatter in gated_scatters]
 
     def gain_grad(gain, own_weights, wgrads):
         total = sum(

time: 674 us -> 669 us (level)
    ppermute x105, waiting for transfers between devices: 180 us -> 170 us  [start(): value = lax.ppermute(operand, 'dp', self.ring.pairs[way])]
    reduce_scatter x4, waiting for transfers between devices: 6.87 us -> 14.4 us  [tensor_reduce(): return lax.psum_scatter(whole, 'tensor', scatter_dimension=0, tiled=True)]
    pallas_call x5 -> x6, Pallas kernels: 53.3 us -> 57.5 us  [spread(): pl.pallas_call(kernel, grid_spec=pltpu.PrefetchScalarGridSpec(num_scalar_...]
  transfers between devices with their start and end apart: 115 -> 115, of which waited for: 45 -> 41; matrix products, arithmetic and copies ran while one was open for 9% -> 8% of each run, Pallas kernels for 38% -> 39%
where the time goes in v5:
time: 669 us; the launch traced here: 660 us
  Pallas kernels  266 us (40%)
  waiting for transfers between devices  187 us (28%)
  starting transfers between devices  118 us (18%)
  other arithmetic  60.6 us (9%)
  between operations  15.9 us (2%)
  local copies, waits for them, and re-layouts  12.7 us (2%)
    ppermute x105, waiting for transfers between devices, start(): value = lax.ppermute(operand, 'dp', self.ring.pairs[way])  170 us
    ppermute x105, starting transfers between devices, start(): value = lax.ppermute(operand, 'dp', self.ring.pairs[way])  117 us
    pallas_call x6, Pallas kernels, weight_grads(): call(kernel, name, (pieces,), in_specs, [fixed(shape) for shape in shapes...  71.5 us
    pallas_call x6, Pallas kernels, spread(): pl.pallas_call(kernel, grid_spec=pltpu.PrefetchScalarGridSpec(num_scalar_...  57.5 us
    convert_element_type x35, other arithmetic, operand(): value = (value.astype(f32) + got.astype(f32)).astype(bf16)  26.7 us
    pallas_call x2, Pallas kernels, gated_forward(): call(kernel, 'gated_forward', (4,), [pl.BlockSpec((rows, features), lambd...  25.9 us
    pallas_call x1, Pallas kernels, core_backward(): pl.pallas_call(core_backward_kernel, grid_spec=pltpu.PrefetchScalarGridSp...  23.7 us
    pallas_call x2, Pallas kernels, gated_backward(): call(kernel, 'gated_backward', (4,), [pl.BlockSpec((rows, features), lamb...  17.1 us
  transfers between devices with their start and end apart: 115, of which 41 were waited for; matrix products, arithmetic and copies ran while one was open for 8% of the time, Pallas kernels for 39%

profile of v5, /device:TPU:0, one launch (start us, length us, event | category | flops | bytes accessed | tf_op | source)
XLA Modules:
  0.0 659.7 jit_solution(17607616766796621340)
XLA Ops:
  15.1 5.6 collective-permute-done.1.refs_2_
  27.6 6.8 %collective-permute-done.4.refs_7_ = bf16[256,256]{1,0:T(8,128)(2,1)S(1)} collective-permute-done((bf16[256,256]{1,0:T(8,128)(2,1)S(1)}, bf16[256,256]{1,0:T(8,128)(2,1)S(1)}, u32[]{:S(2)}, u32[]{:S(2)}) %collective-permute-start.4) | collective-permute-done | bytes 131104 | tf_op jit(solution)/shard_map/ppermute | solution.py:974
  52.5 3.8 collective-permute-done.15.refs_5_
  60.0 3.4 collective-permute-done.13.refs_10_.refs_2_
  65.4 6.6 %unpack_tables.1 = (bf16[640,1280]{1,0:T(8,128)(2,1)}, f32[8,640]{1,0:T(8,128)}, f32[8,2048]{1,0:T(8,128)}) custom-call(s32[8]{0:T(128)} %compare_select_fusion.5.order_ref, bf16[256,256]{1,0:T(8,128)(2,1)} %copy-done.78, bf16[256,256]{1,0:T(8,128)(2,1)} %copy-done.128, bf16[256,256]{1,0:T(8,128)(2,1)} %copy-done.130, bf16[256,256]{1,0:T(8,128)(2,1)} %copy-done.132, ...), custom_call_target="tpu_custom_call" | custom-call | flops 6000000000 | bytes 30000000 | tf_op jit(solution)/shard_map/unpack_tables/pallas_call | solution.py:692
  73.6 7.1 %prepare.1 = (bf16[1024,2048]{1,0:T(8,128)(2,1)}, bf16[256,2048]{1,0:T(8,128)(2,1)}) custom-call(s32[8]{0:T(128)} %compare_select_fusion.5.order_ref, s32[1]{0:T(128)} %bitcast.place_ref, bf16[1024,2048]{1,0:T(8,128)(2,1)} %all-gather.5.cloned.1.call-done.value_ref, f32[1,2048]{1,0:T(1,128)} %get-tuple-element.616.gain_ref), custom_call_target="tpu_custom_call" | custom-call | flops 6000000000 | bytes 30000000 | tf_op jit(solution)/shard_map/prepare/pallas_call | solution.py:788
  85.3 6.3 collective-permute-done.19.refs_3_
  94.5 4.1 collective-permute-done.25.refs_12_.refs_4_
  107.5 11.3 %mixer_in.1.branch.entry_pre.refs_9_.entry_tail = f32[1024,1280]{1,0:T(8,128)} custom-call(bf16[1024,2048]{1,0:T(8,128)(2,1)} %get-tuple-element.315.refs_0_, bf16[256,640]{1,0:T(8,128)(2,1)} %refs_1_.8, bf16[256,640]{1,0:T(8,128)(2,1)} %copy-done.110, bf16[256,640]{1,0:T(8,128)(2,1)} %copy-done.114, bf16[256,640]{1,0:T(8,128)(2,1)} %collective-permute-done.11.refs_4_, ...), custom_call_target="tpu_custom_call" | custom-call | flops 6000000000 | bytes 30000000 | tf_op jit(solution)/shard_map/mixer_in/pallas_call | solution.py:465
  123.2 16.2 %core_forward.1 = (bf16[1024,640]{1,0:T(8,128)(2,1)}, f32[1024,640]{1,0:T(8,128)}, f32[1024,640]{1,0:T(8,128)}, f32[1024,640]{1,0:T(8,128)}, f32[1024,640]{1,0:T(8,128)}) custom-call(s32[1]{0:T(128)} %constant.88.clone.1.place, f32[1024,1280]{1,0:T(8,128)} %mixer_in.1.branch.entry_pre.refs_9_.entry_tail, ...), custom_call_target="tpu_custom_call" | custom-call | flops 6000000000 | bytes 30000000 | tf_op jit(solution)/shard_map/core_forward/pallas_call | solution.py:257
  140.2 7.1 %mixer_out.1 = bf16[1024,2048]{1,0:T(8,128)(2,1)} custom-call(s32[1]{0:T(128)} %bitcast.place_ref, bf16[1024,640]{1,0:T(8,128)(2,1)} %get-tuple-element.326.refs_0_, bf16[640,256]{1,0:T(8,128)(2,1)} %refs_1_.7, bf16[640,256]{1,0:T(8,128)(2,1)} %collective-permute-done.17.refs_2_, bf16[640,256]{1,0:T(8,128)(2,1)} %copy-done.123, ...), custom_call_target="tpu_custom_call" | custom-call | flops 6000000000 | bytes 30000000 | tf_op jit(solution)/shard_map/mixer_out/pallas_call | solution.py:426
  152.5 5.6 move_columns.3.refs_2_.refs_0_
  158.1 10.9 %collective-permute-done.33.refs_2_ = bf16[256,1536]{1,0:T(8,128)(2,1)} collective-permute-done((bf16[256,1536]{1,0:T(8,128)(2,1)S(1)}, bf16[256,1536]{1,0:T(8,128)(2,1)}, u32[]{:S(2)}, u32[]{:S(2)}) %collective-permute-start.33) | collective-permute-done | bytes 786464 | tf_op jit(solution)/shard_map/ppermute | solution.py:974
  171.1 8.8 %collective-permute-done.37.refs_4_ = bf16[256,1536]{1,0:T(8,128)(2,1)} collective-permute-done((bf16[256,1536]{1,0:T(8,128)(2,1)}, bf16[256,1536]{1,0:T(8,128)(2,1)}, u32[]{:S(2)}, u32[]{:S(2)}) %collective-permute-start.37) | collective-permute-done | bytes 786464 | tf_op jit(solution)/shard_map/ppermute | solution.py:974
  180.4 7.9 %collective-permute-done.35.refs_3_ = bf16[256,1536]{1,0:T(8,128)(2,1)S(1)} collective-permute-done((bf16[256,1536]{1,0:T(8,128)(2,1)}, bf16[256,1536]{1,0:T(8,128)(2,1)S(1)}, u32[]{:S(2)}, u32[]{:S(2)}) %collective-permute-start.35) | collective-permute-done | bytes 786464 | tf_op jit(solution)/shard_map/ppermute | solution.py:974
  199.8 16.6 %collective-permute-done.41.refs_5_ = bf16[256,1536]{1,0:T(8,128)(2,1)S(1)} collective-permute-done((bf16[256,1536]{1,0:T(8,128)(2,1)}, bf16[256,1536]{1,0:T(8,128)(2,1)S(1)}, u32[]{:S(2)}, u32[]{:S(2)}) %collective-permute-start.41) | collective-permute-done | bytes 786464 | tf_op jit(solution)/shard_map/ppermute | solution.py:974
  220.0 6.3 collective-permute-done.39.refs_8_.refs_9_
  226.8 6.4 collective-permute-done.38.refs_4_
  235.6 12.9 %gated_forward.2 = (bf16[1024,768]{1,0:T(8,128)(2,1)}, bf16[1024,768]{1,0:T(8,128)(2,1)}, bf16[1024,768]{1,0:T(8,128)(2,1)}) custom-call(bf16[1024,2048]{1,0:T(8,128)(2,1)} %all-gather.9.cloned.1.call-done.refs_0_, bf16[256,1536]{1,0:T(8,128)(2,1)} %copy-done.25, bf16[256,1536]{1,0:T(8,128)(2,1)} %copy-done.93, ...), custom_call_target="tpu_custom_call" | custom-call | flops 6000000000 | bytes 30000000 | tf_op jit(solution)/shard_map/gated_forward/pallas_call | solution.py:538
  252.6 13.0 %gated_forward.3 = (bf16[1024,768]{1,0:T(8,128)(2,1)}, bf16[1024,768]{1,0:T(8,128)(2,1)}, bf16[1024,768]{1,0:T(8,128)(2,1)}) custom-call(bf16[1024,2048]{1,0:T(8,128)(2,1)} %all-gather.9.cloned.1.call-done.refs_0_, bf16[256,1536]{1,0:T(8,128)(2,1)} %copy-done.26, bf16[256,1536]{1,0:T(8,128)(2,1)} %collective-permute-done.33.refs_2_, ...), custom_call_target="tpu_custom_call" | custom-call | flops 6000000000 | bytes 30000000 | tf_op jit(solution)/shard_map/gated_forward/pallas_call | solution.py:538
  269.2 14.1 %down_grads.1 = (bf16[768,256]{1,0:T(8,128)(2,1)}, bf16[768,256]{1,0:T(8,128)(2,1)}, bf16[768,256]{1,0:T(8,128)(2,1)}, bf16[768,256]{1,0:T(8,128)(2,1)}, bf16[76...) custom-call(bf16[1024,768]{1,0:T(8,128)(2,1)} %get-tuple-element.422, ...), custom_call_target="tpu_custom_call" | custom-call | flops 6000000000 | bytes 30000000 | tf_op jit(solution)/shard_map/down_grads/pallas_call | solution.py:620
  287.7 7.8 %collective-permute-done.55.refs_5_.refs_6_ = bf16[768,256]{1,0:T(8,128)(2,1)S(1)} collective-permute-done((bf16[768,256]{1,0:T(8,128)(2,1)S(1)}, bf16[768,256]{1,0:T(8,128)(2,1)S(1)}, u32[]{:S(2)}, u32[]{:S(2)}) %collective-permute-start.55) | collective-permute-done | bytes 393248 | tf_op jit(solution)/shard_map/ppermute | solution.py:974
  297.0 8.6 %gated_backward.2.refs_0_.refs_1_ = bf16[1024,1536]{1,0:T(8,128)(2,1)} custom-call(bf16[1024,2048]{1,0:T(8,128)(2,1)} %move_columns.3.refs_2_.refs_0_, bf16[768,256]{1,0:T(8,128)(2,1)} %copy-done.41, bf16[768,256]{1,0:T(8,128)(2,1)} %collective-permute-done.45.refs_2_.refs_3_, bf16[768,256]{1,0:T(8,128)(2,1)} %copy-done.99, bf16[768,256]{1,0:T(8,128)(2,1)} %copy-done.103, ...), custom_call_target="tpu_custom_call" | custom-call | flops 6000000000 | bytes 30000000 | tf_op jit(solution)/shard_map/gated_backward/pallas_call | solution.py:566
  308.6 3.8 collective-permute-done.58
  322.4 8.5 %gated_backward.3.refs_0_.refs_1_ = bf16[1024,1536]{1,0:T(8,128)(2,1)} custom-call(bf16[1024,2048]{1,0:T(8,128)(2,1)} %move_columns.3.refs_2_.refs_0_, bf16[768,256]{1,0:T(8,128)(2,1)} %copy-done.40, bf16[768,256]{1,0:T(8,128)(2,1)} %collective-permute-done.43.refs_2_.refs_11_, bf16[768,256]{1,0:T(8,128)(2,1)} %copy-done.101, bf16[768,256]{1,0:T(8,128)(2,1)} %copy-done.105, ...), custom_call_target="tpu_custom_call" | custom-call | flops 6000000000 | bytes 30000000 | tf_op jit(solution)/shard_map/gated_backward/pallas_call | solution.py:566
  334.1 3.6 collective-permute-done.60
  339.3 11.6 %mlp_in_grad.2.refs_9_ = bf16[1024,2048]{1,0:T(8,128)(2,1)} custom-call(s32[1]{0:T(128)} %bitcast.place_ref, bf16[1024,1536]{1,0:T(8,128)(2,1)} %gated_backward.2.refs_0_.refs_1_, bf16[256,1536]{1,0:T(8,128)(2,1)} %copy-done.25, bf16[256,1536]{1,0:T(8,128)(2,1)} %copy-done.93, bf16[256,1536]{1,0:T(8,128)(2,1)} %collective-permute-done.29.refs_3_, ...), custom_call_target="tpu_custom_call" | custom-call | flops 6000000000 | bytes 30000000 | tf_op jit(solution)/shard_map/mlp_in_grad/pallas_call | solution.py:426
  352.4 11.8 %mlp_in_grad.3 = bf16[1024,2048]{1,0:T(8,128)(2,1)} custom-call(s32[1]{0:T(128)} %bitcast.place_ref, bf16[1024,1536]{1,0:T(8,128)(2,1)} %gated_backward.3.refs_0_.refs_1_, bf16[256,1536]{1,0:T(8,128)(2,1)} %copy-done.26, bf16[256,1536]{1,0:T(8,128)(2,1)} %collective-permute-done.33.refs_2_, bf16[256,1536]{1,0:T(8,128)(2,1)} %copy-done.95, ...), custom_call_target="tpu_custom_call" | custom-call | flops 6000000000 | bytes 30000000 | tf_op jit(solution)/shard_map/mlp_in_grad/pallas_call | solution.py:426
  364.9 13.8 %gated_grads.2 = (bf16[256,1536]{1,0:T(8,128)(2,1)}, bf16[256,1536]{1,0:T(8,128)(2,1)}, bf16[256,1536]{1,0:T(8,128)(2,1)}, bf16[256,1536]{1,0:T(8,128)(2,1)}, bf...) custom-call(bf16[1024,2048]{1,0:T(8,128)(2,1)} %all-gather.9.cloned., ...), custom_call_target="tpu_custom_call" | custom-call | flops 6000000000 | bytes 30000000 | tf_op jit(solution)/shard_map/gated_grads/pallas_call | solution.py:620
  382.3 13.8 %gated_grads.3 = (bf16[256,1536]{1,0:T(8,128)(2,1)}, bf16[256,1536]{1,0:T(8,128)(2,1)}, bf16[256,1536]{1,0:T(8,128)(2,1)}, bf16[256,1536]{1,0:T(8,128)(2,1)}, bf...) custom-call(bf16[1024,2048]{1,0:T(8,128)(2,1)} %all-gather.9.cloned., ...), custom_call_target="tpu_custom_call" | custom-call | flops 6000000000 | bytes 30000000 | tf_op jit(solution)/shard_map/gated_grads/pallas_call | solution.py:620
  397.2 5.3 collective-permute-done.69
  403.5 4.4 reduce-scatter.7.cloned.1.call-done
  418.1 11.9 %mlp_out.1 = bf16[1024,2048]{1,0:T(8,128)(2,1)} custom-call(s32[1]{0:T(128)} %bitcast.place_ref, bf16[1024,768]{1,0:T(8,128)(2,1)} %get-tuple-element.422.refs_0_, bf16[1024,768]{1,0:T(8,128)(2,1)} %get-tuple-element.423.refs_1_, bf16[768,256]{1,0:T(8,128)(2,1)} %copy-done.41, bf16[768,256]{1,0:T(8,128)(2,1)} %collective-permute-done.45.refs_2_.refs_3_, ...), custom_call_target="tpu_custom_call" | custom-call | flops 6000000000 | bytes 30000000 | tf_op jit(solution)/shard_map/mlp_out/pallas_call | solution.py:426
  430.0 4.4 collective-permute-done.75
  441.2 10.0 %collective-permute-done.73 = bf16[256,1536]{1,0:T(8,128)(2,1)} collective-permute-done((bf16[256,1536]{1,0:T(8,128)(2,1)}, bf16[256,1536]{1,0:T(8,128)(2,1)}, u32[]{:S(2)}, u32[]{:S(2)}) %collective-permute-start.73) | collective-permute-done | bytes 786464 | tf_op jit(solution)/shard_map/ppermute | solution.py:974
  457.7 9.5 %mixer_back.1 = (f32[1024,640]{1,0:T(8,128)}, bf16[1024,640]{1,0:T(8,128)(2,1)}) custom-call(bf16[1024,2048]{1,0:T(8,128)(2,1)} %all-gather.11.cloned.1.call-done.refs_0_.refs_1_, bf16[640,256]{1,0:T(8,128)(2,1)} %refs_1_.7, bf16[640,256]{1,0:T(8,128)(2,1)} %collective-permute-done.17.refs_2_, bf16[640,256]{1,0:T(8,128)(2,1)} %copy-done.123, ...), custom_call_target="tpu_custom_call" | custom-call | flops 6000000000 | bytes 30000000 | tf_op jit(solution)/shard_map/mixer_back/pallas_call | solution.py:496
  474.1 23.7 %core_backward.1 = (bf16[1024,640]{1,0:T(8,128)(2,1)}, f32[640,1280]{1,0:T(8,128)}, f32[8,640]{1,0:T(8,128)}) custom-call(s32[1]{0:T(128)} %constant.88.clone.1.place, f32[1024,640]{1,0:T(8,128)} %get-tuple-element.449.grad, f32[1024,1280]{1,0:T(8,128)} %mixer_in.1.branch.entry_pre.refs_9_.entry_tail, f32[1024,640]{1,0:T(8,128)} %get-tuple-element.450.mixed_in, ...), custom_call_target="tpu_custom_call" | custom-call | flops 6000000000 | bytes 30000000 | tf_op jit(solution)/shard_map/core_backward/pallas_call | solution.py:298
  503.8 9.7 %output_grads.1 = (bf16[640,256]{1,0:T(8,128)(2,1)}, bf16[640,256]{1,0:T(8,128)(2,1)}, bf16[640,256]{1,0:T(8,128)(2,1)}, bf16[640,256]{1,0:T(8,128)(2,1)}, bf16[...) custom-call(bf16[1024,640]{1,0:T(8,128)(2,1)} %get-tuple-element.326.refs_0, ...), custom_call_target="tpu_custom_call" | custom-call | flops 6000000000 | bytes 30000000 | tf_op jit(solution)/shard_map/output_grads/pallas_call | solution.py:620
  515.5 9.7 %branch_grads.1 = (bf16[256,640]{1,0:T(8,128)(2,1)}, bf16[256,640]{1,0:T(8,128)(2,1)}, bf16[256,640]{1,0:T(8,128)(2,1)}, bf16[256,640]{1,0:T(8,128)(2,1)}, bf16[...) custom-call(bf16[1024,2048]{1,0:T(8,128)(2,1)} %get-tuple-element.315.refs_, ...), custom_call_target="tpu_custom_call" | custom-call | flops 6000000000 | bytes 30000000 | tf_op jit(solution)/shard_map/branch_grads/pallas_call | solution.py:620
  527.4 7.1 %mixer_in_grad.2.refs_9_ = bf16[1024,2048]{1,0:T(8,128)(2,1)} custom-call(s32[1]{0:T(128)} %bitcast.place_ref, bf16[1024,640]{1,0:T(8,128)(2,1)} %get-tuple-element.475.refs_1_.refs_0_, bf16[256,640]{1,0:T(8,128)(2,1)} %refs_1_.8, bf16[256,640]{1,0:T(8,128)(2,1)} %copy-done.110, bf16[256,640]{1,0:T(8,128)(2,1)} %copy-done.114, ...), custom_call_target="tpu_custom_call" | custom-call | flops 6000000000 | bytes 30000000 | tf_op jit(solution)/shard_map/mixer_in_grad/pallas_call | solution.py:426
  539.2 6.2 collective-permute-done.89
  547.8 7.3 %pack_tables.1.refs_2_ = bf16[2048,256]{1,0:T(8,128)(2,1)} custom-call(s32[8]{0:T(128)} %compare_select_fusion.5.order_ref, f32[640,1280]{1,0:T(8,128)} %get-tuple-element.492.gate_ref, f32[8,640]{1,0:T(8,128)} %pad_maximum_fusion.6.small_ref), custom_call_target="tpu_custom_call" | custom-call | flops 6000000000 | bytes 30000000 | tf_op jit(solution)/shard_map/pack_tables/pallas_call | solution.py:745
  559.6 10.4 %input_grads.1 = (bf16[256,896]{1,0:T(8,128)(2,1)}, bf16[256,896]{1,0:T(8,128)(2,1)}, bf16[256,896]{1,0:T(8,128)(2,1)}, bf16[256,896]{1,0:T(8,128)(2,1)}, bf16[2...) custom-call(bf16[1024,2048]{1,0:T(8,128)(2,1)} %get-tuple-element.315.refs_0, ...), custom_call_target="tpu_custom_call" | custom-call | flops 6000000000 | bytes 30000000 | tf_op jit(solution)/shard_map/input_grads/pallas_call | solution.py:620
  570.8 8.0 %mixer_in_grad.3 = bf16[1024,2048]{1,0:T(8,128)(2,1)} custom-call(s32[1]{0:T(128)} %bitcast.place_ref, bf16[1024,640]{1,0:T(8,128)(2,1)} %get-tuple-element.510.refs_1_.refs_0_, bf16[256,640]{1,0:T(8,128)(2,1)} %refs_1_.9, bf16[256,640]{1,0:T(8,128)(2,1)} %copy-done.111, bf16[256,640]{1,0:T(8,128)(2,1)} %copy-done.117, bf16[256,640]{1,0:T(8,128)(2,1)} %copy-done.121, ...), custom_call_target="tpu_custom_call" | custom-call | flops 6000000000 | bytes 30000000 | tf_op jit(solution)/shard_map/mixer_in_grad/pallas_call | solution.py:426
  608.0 4.5 collective-permute-done.101
  616.3 6.7 %reduce-scatter.11.cloned.1.call-done = bf16[256,2048]{1,0:T(8,128)(2,1)} async-done(((bf16[1024,2048]{1,0:T(8,128)(2,1)}), bf16[256,2048]{1,0:T(8,128)(2,1)}) %reduce-scatter.11.cloned.1.call-update) | async-done | bytes 1048592 | tf_op jit(solution)/shard_map/reduce_scatter | solution.py:1028
  624.8 3.5 fusion.4.refs_0_
  635.6 9.4 %collective-permute-done.104 = bf16[256,896]{1,0:T(8,128)(2,1)S(1)} collective-permute-done((bf16[256,896]{1,0:T(8,128)(2,1)S(1)}, bf16[256,896]{1,0:T(8,128)(2,1)S(1)}, u32[]{:S(2)}, u32[]{:S(2)}) %collective-permute-start.104) | collective-permute-done | bytes 458784 | tf_op jit(solution)/shard_map/ppermute | solution.py:974
  (602 shorter events, 228.0 us)
Async XLA Ops:
  7.3 66.3 %all-gather.5.cloned.1.call-start = ((), (), s32[]{:S(2)}) async-start(), calls=%async_computation.4 | async-start | bytes 5242880 | tf_op jit(solution)/shard_map/all_gather | solution.py:1024
  8.1 144.4 %all-gather.7.cloned.1.call-start = ((), (), s32[]{:S(2)}) async-start(), calls=%async_computation.6 | async-start | bytes 5242880 | tf_op jit(solution)/shard_map/all_gather | solution.py:1024
  8.8 183.5 %reduce-scatter.5.cloned.1.call-start = ((), (), s32[]{:S(2)}) async-start(), calls=%async_computation.5 | async-start | bytes 5242880 | tf_op jit(solution)/shard_map/reduce_scatter | solution.py:1028
  56.4 24.3 %collective-permute-start.17 = (bf16[640,256]{1,0:T(8,128)(2,1)}, bf16[640,256]{1,0:T(8,128)(2,1)}, u32[]{:S(2)}, u32[]{:S(2)}) collective-permute-start(bf16[640,256]{1,0:T(8,128)(2,1)} %refs_1_.7), channel_id=1, source_target_pairs={{8,0},{16,8},{24,16},{28,24},{20,28},{12,20},{4,12},{0,4},{9,1},{1... | collective-permute-start | bytes 983048 | tf_op jit(solution)/shard_map/ppermute | solution.py:974
  59.5 22.5 %collective-permute-start.16 = (bf16[256,640]{1,0:T(8,128)(2,1)S(1)}, bf16[256,640]{1,0:T(8,128)(2,1)S(1)}, u32[]{:S(2)}, u32[]{:S(2)}) collective-permute-start(bf16[256,640]{1,0:T(8,128)(2,1)S(1)} %collective-permute-done.14.refs_16_.refs_8_), channel_id=1, source_target_pairs={{0,8},{8,16},{16,24},{24,28},{28,20},{20,12},{12,4},{4,0},{1,9},{9... | collective-permute-start | bytes 983048 | tf_op jit(solution)/shard_map/ppermute | solution.py:974
  63.4 19.7 %collective-permute-start.21 = (bf16[256,640]{1,0:T(8,128)(2,1)S(1)}, bf16[256,640]{1,0:T(8,128)(2,1)S(1)}, u32[]{:S(2)}, u32[]{:S(2)}) collective-permute-start(bf16[256,640]{1,0:T(8,128)(2,1)S(1)} %collective-permute-done.13.refs_10_.refs_2_), channel_id=1, source_target_pairs={{8,0},{16,8},{24,16},{28,24},{20,28},{12,20},{4,12},{0,4},{9,1},{1... | collective-permute-start | bytes 983048 | tf_op jit(solution)/shard_map/ppermute | solution.py:974
  64.6 19.8 %collective-permute-start.20 = (bf16[640,256]{1,0:T(8,128)(2,1)}, bf16[640,256]{1,0:T(8,128)(2,1)}, u32[]{:S(2)}, u32[]{:S(2)}) collective-permute-start(bf16[640,256]{1,0:T(8,128)(2,1)} %refs_1_.7), channel_id=1, source_target_pairs={{0,8},{8,16},{16,24},{24,28},{28,20},{20,12},{12,4},{4,0},{1,9},{9... | collective-permute-start | bytes 983048 | tf_op jit(solution)/shard_map/ppermute | solution.py:974
  98.6 21.9 %collective-permute-start.26 = (bf16[256,1536]{1,0:T(8,128)(2,1)S(1)}, bf16[256,1536]{1,0:T(8,128)(2,1)S(1)}, u32[]{:S(2)}, u32[]{:S(2)}) collective-permute-start(bf16[256,1536]{1,0:T(8,128)(2,1)S(1)} %pad_maximum_fusion.3.refs_1_), channel_id=1, source_target_pairs={{8,0},{16,8},{24,16},{28,24},{20,28},{12,20},{4,12},{0,4},{9,1},{1... | collective-permute-start | bytes 2359304 | tf_op jit(solution)/shard_map/ppermute | solution.py:974
  106.7 32.8 %collective-permute-start.30 = (bf16[256,1536]{1,0:T(8,128)(2,1)S(1)}, bf16[256,1536]{1,0:T(8,128)(2,1)S(1)}, u32[]{:S(2)}, u32[]{:S(2)}) collective-permute-start(bf16[256,1536]{1,0:T(8,128)(2,1)S(1)} %pad_maximum_fusion.3.refs_1_), channel_id=1, source_target_pairs={{0,8},{8,16},{16,24},{24,28},{28,20},{20,12},{12,4},{4,0},{1,9},{9... | collective-permute-start | bytes 2359304 | tf_op jit(solution)/shard_map/ppermute | solution.py:974
  118.8 20.7 %collective-permute-start.28 = (bf16[256,1536]{1,0:T(8,128)(2,1)S(1)}, bf16[256,1536]{1,0:T(8,128)(2,1)}, u32[]{:S(2)}, u32[]{:S(2)}) collective-permute-start(bf16[256,1536]{1,0:T(8,128)(2,1)S(1)} %pad_maximum_fusion.4.refs_1_), channel_id=1, source_target_pairs={{0,8},{8,16},{16,24},{24,28},{28,20},{20,12},{12,4},{4,0},{1,9},{9... | collective-permute-start | bytes 2359304 | tf_op jit(solution)/shard_map/ppermute | solution.py:974
  120.5 19.0 %collective-permute-start.29 = (bf16[256,1536]{1,0:T(8,128)(2,1)S(1)}, bf16[256,1536]{1,0:T(8,128)(2,1)}, u32[]{:S(2)}, u32[]{:S(2)}) collective-permute-start(bf16[256,1536]{1,0:T(8,128)(2,1)S(1)} %collective-permute-done.26.refs_2_), channel_id=1, source_target_pairs={{8,0},{16,8},{24,16},{28,24},{20,28},{12,20},{4,12},{0,4},{9,1},{1... | collective-permute-start | bytes 2359304 | tf_op jit(solution)/shard_map/ppermute | solution.py:974
  147.3 88.3 %all-gather.9.cloned.1.call-start = ((), (), s32[]{:S(2)}) async-start(), calls=%async_computation.7 | async-start | bytes 5242880 | tf_op jit(solution)/shard_map/all_gather | solution.py:1024
  148.4 20.6 %collective-permute-start.33 = (bf16[256,1536]{1,0:T(8,128)(2,1)S(1)}, bf16[256,1536]{1,0:T(8,128)(2,1)}, u32[]{:S(2)}, u32[]{:S(2)}) collective-permute-start(bf16[256,1536]{1,0:T(8,128)(2,1)S(1)} %copy-done.27), channel_id=1, source_target_pairs={{8,0},{16,8},{24,16},{28,24},{20,28},{12,20},{4,12},{0,4},{9,1},{1... | collective-permute-start | bytes 2359304 | tf_op jit(solution)/shard_map/ppermute | solution.py:974
  149.5 20.6 %collective-permute-start.32 = (bf16[256,1536]{1,0:T(8,128)(2,1)S(1)}, bf16[256,1536]{1,0:T(8,128)(2,1)}, u32[]{:S(2)}, u32[]{:S(2)}) collective-permute-start(bf16[256,1536]{1,0:T(8,128)(2,1)S(1)} %collective-permute-done.30.refs_8_), channel_id=1, source_target_pairs={{0,8},{8,16},{16,24},{24,28},{28,20},{20,12},{12,4},{4,0},{1,9},{9... | collective-permute-start | bytes 2359304 | tf_op jit(solution)/shard_map/ppermute | solution.py:974
  150.4 29.5 %collective-permute-start.37 = (bf16[256,1536]{1,0:T(8,128)(2,1)}, bf16[256,1536]{1,0:T(8,128)(2,1)}, u32[]{:S(2)}, u32[]{:S(2)}) collective-permute-start(bf16[256,1536]{1,0:T(8,128)(2,1)} %collective-permute-done.29.refs_3_), channel_id=1, source_target_pairs={{8,0},{16,8},{24,16},{28,24},{20,28},{12,20},{4,12},{0,4},{9,1},{1... | collective-permute-start | bytes 2359304 | tf_op jit(solution)/shard_map/ppermute | solution.py:974
  151.6 28.8 %collective-permute-start.36 = (bf16[256,1536]{1,0:T(8,128)(2,1)}, bf16[256,1536]{1,0:T(8,128)(2,1)}, u32[]{:S(2)}, u32[]{:S(2)}) collective-permute-start(bf16[256,1536]{1,0:T(8,128)(2,1)} %collective-permute-done.28.refs_8_), channel_id=1, source_target_pairs={{0,8},{8,16},{16,24},{24,28},{28,20},{20,12},{12,4},{4,0},{1,9},{9... | collective-permute-start | bytes 2359304 | tf_op jit(solution)/shard_map/ppermute | solution.py:974
  169.0 19.2 %collective-permute-start.35 = (bf16[256,1536]{1,0:T(8,128)(2,1)}, bf16[256,1536]{1,0:T(8,128)(2,1)S(1)}, u32[]{:S(2)}, u32[]{:S(2)}) collective-permute-start(bf16[256,1536]{1,0:T(8,128)(2,1)} %collective-permute-done.33.refs_2_), channel_id=1, source_target_pairs={{8,0},{16,8},{24,16},{28,24},{20,28},{12,20},{4,12},{0,4},{9,1},{1... | collective-permute-start | bytes 2359304 | tf_op jit(solution)/shard_map/ppermute | solution.py:974
  195.6 212.3 %reduce-scatter.7.cloned.1.call-start = ((), (), s32[]{:S(2)}) async-start(), calls=%async_computation.8 | async-start | bytes 5242880 | tf_op jit(solution)/shard_map/reduce_scatter | solution.py:1028
  195.7 20.7 %collective-permute-start.41 = (bf16[256,1536]{1,0:T(8,128)(2,1)}, bf16[256,1536]{1,0:T(8,128)(2,1)S(1)}, u32[]{:S(2)}, u32[]{:S(2)}) collective-permute-start(bf16[256,1536]{1,0:T(8,128)(2,1)} %collective-permute-done.37.refs_4_), channel_id=1, source_target_pairs={{8,0},{16,8},{24,16},{28,24},{20,28},{12,20},{4,12},{0,4},{9,1},{1... | collective-permute-start | bytes 2359304 | tf_op jit(solution)/shard_map/ppermute | solution.py:974
  197.2 20.8 %collective-permute-start.40 = (bf16[256,1536]{1,0:T(8,128)(2,1)}, bf16[256,1536]{1,0:T(8,128)(2,1)}, u32[]{:S(2)}, u32[]{:S(2)}) collective-permute-start(bf16[256,1536]{1,0:T(8,128)(2,1)} %collective-permute-done.36.refs_7_), channel_id=1, source_target_pairs={{0,8},{8,16},{16,24},{24,28},{28,20},{20,12},{12,4},{4,0},{1,9},{9... | collective-permute-start | bytes 2359304 | tf_op jit(solution)/shard_map/ppermute | solution.py:974
  197.7 35.5 %collective-permute-start.38 = (bf16[256,1536]{1,0:T(8,128)(2,1)}, bf16[256,1536]{1,0:T(8,128)(2,1)S(1)}, u32[]{:S(2)}, u32[]{:S(2)}) collective-permute-start(bf16[256,1536]{1,0:T(8,128)(2,1)} %copy-done.95), channel_id=1, source_target_pairs={{8,0},{16,8},{24,16},{28,24},{20,28},{12,20},{4,12},{0,4},{9,1},{1... | collective-permute-start | bytes 2359304 | tf_op jit(solution)/shard_map/ppermute | solution.py:974
  199.2 27.1 %collective-permute-start.39 = (bf16[768,256]{1,0:T(8,128)(2,1)S(1)}, bf16[768,256]{1,0:T(8,128)(2,1)S(1)}, u32[]{:S(2)}, u32[]{:S(2)}) collective-permute-start(bf16[768,256]{1,0:T(8,128)(2,1)S(1)} %get-tuple-element.335.refs_1_.refs_2_), channel_id=1, source_target_pairs={{0,8},{8,16},{16,24},{24,28},{28,20},{20,12},{12,4},{4,0},{1,9},{9... | collective-permute-start | bytes 1179656 | tf_op jit(solution)/shard_map/ppermute | solution.py:974
  218.0 32.1 %collective-permute-start.44 = (bf16[256,1536]{1,0:T(8,128)(2,1)}, bf16[256,1536]{1,0:T(8,128)(2,1)}, u32[]{:S(2)}, u32[]{:S(2)}) collective-permute-start(bf16[256,1536]{1,0:T(8,128)(2,1)} %collective-permute-done.40.refs_6_), channel_id=1, source_target_pairs={{0,8},{8,16},{16,24},{24,28},{28,20},{20,12},{12,4},{4,0},{1,9},{9... | collective-permute-start | bytes 2359304 | tf_op jit(solution)/shard_map/ppermute | solution.py:974
  218.5 30.0 %collective-permute-start.45 = (bf16[768,256]{1,0:T(8,128)(2,1)S(1)}, bf16[768,256]{1,0:T(8,128)(2,1)}, u32[]{:S(2)}, u32[]{:S(2)}) collective-permute-start(bf16[768,256]{1,0:T(8,128)(2,1)S(1)} %get-tuple-element.335.refs_1_.refs_2_), channel_id=1, source_target_pairs={{8,0},{16,8},{24,16},{28,24},{20,28},{12,20},{4,12},{0,4},{9,1},{1... | collective-permute-start | bytes 1179656 | tf_op jit(solution)/shard_map/ppermute | solution.py:974
  226.3 25.8 %collective-permute-start.42 = (bf16[768,256]{1,0:T(8,128)(2,1)S(1)}, bf16[768,256]{1,0:T(8,128)(2,1)}, u32[]{:S(2)}, u32[]{:S(2)}) collective-permute-start(bf16[768,256]{1,0:T(8,128)(2,1)S(1)} %collective-permute-done.39.refs_8_.refs_9_), channel_id=1, source_target_pairs={{0,8},{8,16},{16,24},{24,28},{28,20},{20,12},{12,4},{4,0},{1,9},{9... | collective-permute-start | bytes 1179656 | tf_op jit(solution)/shard_map/ppermute | solution.py:974
  284.9 20.7 %collective-permute-start.54 = (bf16[768,256]{1,0:T(8,128)(2,1)S(1)}, bf16[768,256]{1,0:T(8,128)(2,1)S(1)}, u32[]{:S(2)}, u32[]{:S(2)}) collective-permute-start(bf16[768,256]{1,0:T(8,128)(2,1)S(1)} %collective-permute-done.51.refs_7_.refs_16_), channel_id=1, source_target_pairs={{0,8},{8,16},{16,24},{24,28},{28,20},{20,12},{12,4},{4,0},{1,9},{9... | collective-permute-start | bytes 1179656 | tf_op jit(solution)/shard_map/ppermute | solution.py:974
  285.5 20.7 %collective-permute-start.53 = (bf16[768,256]{1,0:T(8,128)(2,1)}, bf16[768,256]{1,0:T(8,128)(2,1)S(1)}, u32[]{:S(2)}, u32[]{:S(2)}) collective-permute-start(bf16[768,256]{1,0:T(8,128)(2,1)} %get-tuple-element.359), channel_id=1, source_target_pairs={{8,0},{16,8},{24,16},{28,24},{20,28},{12,20},{4,12},{0,4},{9,1},{1... | collective-permute-start | bytes 1179656 | tf_op jit(solution)/shard_map/ppermute | solution.py:974
  286.9 20.9 %collective-permute-start.59 = (bf16[768,256]{1,0:T(8,128)(2,1)}, bf16[768,256]{1,0:T(8,128)(2,1)S(1)}, u32[]{:S(2)}, u32[]{:S(2)}) collective-permute-start(bf16[768,256]{1,0:T(8,128)(2,1)} %get-tuple-element.362), channel_id=1, source_target_pairs={{0,8},{8,16},{16,24},{24,28},{28,20},{20,12},{12,4},{4,0},{1,9},{9... | collective-permute-start | bytes 1179656 | tf_op jit(solution)/shard_map/ppermute | solution.py:974
  307.9 23.0 %collective-permute-start.63 = (bf16[768,256]{1,0:T(8,128)(2,1)S(1)}, bf16[768,256]{1,0:T(8,128)(2,1)S(1)}, u32[]{:S(2)}, u32[]{:S(2)}) collective-permute-start(bf16[768,256]{1,0:T(8,128)(2,1)S(1)} %add_convert_fusion.24), channel_id=1, source_target_pairs={{0,8},{8,16},{16,24},{24,28},{28,20},{20,12},{12,4},{4,0},{1,9},{9... | collective-permute-start | bytes 1179656 | tf_op jit(solution)/shard_map/ppermute | solution.py:974
  312.5 19.2 %collective-permute-start.62 = (bf16[768,256]{1,0:T(8,128)(2,1)S(1)}, bf16[768,256]{1,0:T(8,128)(2,1)S(1)}, u32[]{:S(2)}, u32[]{:S(2)}) collective-permute-start(bf16[768,256]{1,0:T(8,128)(2,1)S(1)} %add_convert_fusion.23), channel_id=1, source_target_pairs={{8,0},{16,8},{24,16},{28,24},{20,28},{12,20},{4,12},{0,4},{9,1},{1... | collective-permute-start | bytes 1179656 | tf_op jit(solution)/shard_map/ppermute | solution.py:974
  364.2 93.5 %all-gather.11.cloned.1.call-start = ((), (), s32[]{:S(2)}) async-start(), calls=%async_computation.9 | async-start | bytes 5242880 | tf_op jit(solution)/shard_map/all_gather | solution.py:1024
  380.9 21.5 %collective-permute-start.69 = (bf16[256,1536]{1,0:T(8,128)(2,1)}, bf16[256,1536]{1,0:T(8,128)(2,1)S(1)}, u32[]{:S(2)}, u32[]{:S(2)}) collective-permute-start(bf16[256,1536]{1,0:T(8,128)(2,1)} %get-tuple-element.409), channel_id=1, source_target_pairs={{0,8},{8,16},{16,24},{24,28},{28,20},{20,12},{12,4},{4,0},{1,9},{9... | collective-permute-start | bytes 2359304 | tf_op jit(solution)/shard_map/ppermute | solution.py:974
  413.5 178.1 %reduce-scatter.9.cloned.1.call-start = ((), (), s32[]{:S(2)}) async-start(), calls=%async_computation.10 | async-start | bytes 5242880 | tf_op jit(solution)/shard_map/reduce_scatter | solution.py:1028
  413.6 20.8 %collective-permute-start.75 = (bf16[256,1536]{1,0:T(8,128)(2,1)}, bf16[256,1536]{1,0:T(8,128)(2,1)}, u32[]{:S(2)}, u32[]{:S(2)}) collective-permute-start(bf16[256,1536]{1,0:T(8,128)(2,1)} %get-tuple-element.415), channel_id=1, source_target_pairs={{8,0},{16,8},{24,16},{28,24},{20,28},{12,20},{4,12},{0,4},{9,1},{1... | collective-permute-start | bytes 2359304 | tf_op jit(solution)/shard_map/ppermute | solution.py:974
  415.1 23.3 %collective-permute-start.74 = (bf16[256,1536]{1,0:T(8,128)(2,1)}, bf16[256,1536]{1,0:T(8,128)(2,1)}, u32[]{:S(2)}, u32[]{:S(2)}) collective-permute-start(bf16[256,1536]{1,0:T(8,128)(2,1)} %get-tuple-element.416), channel_id=1, source_target_pairs={{0,8},{8,16},{16,24},{24,28},{28,20},{20,12},{12,4},{4,0},{1,9},{9... | collective-permute-start | bytes 2359304 | tf_op jit(solution)/shard_map/ppermute | solution.py:974
  415.7 35.6 %collective-permute-start.73 = (bf16[256,1536]{1,0:T(8,128)(2,1)}, bf16[256,1536]{1,0:T(8,128)(2,1)}, u32[]{:S(2)}, u32[]{:S(2)}) collective-permute-start(bf16[256,1536]{1,0:T(8,128)(2,1)} %add_convert_fusion.10), channel_id=1, source_target_pairs={{8,0},{16,8},{24,16},{28,24},{20,28},{12,20},{4,12},{0,4},{9,1},{1... | collective-permute-start | bytes 2359304 | tf_op jit(solution)/shard_map/ppermute | solution.py:974
  417.1 37.8 %collective-permute-start.72 = (bf16[256,1536]{1,0:T(8,128)(2,1)}, bf16[256,1536]{1,0:T(8,128)(2,1)}, u32[]{:S(2)}, u32[]{:S(2)}) collective-permute-start(bf16[256,1536]{1,0:T(8,128)(2,1)} %add_convert_fusion.9), channel_id=1, source_target_pairs={{0,8},{8,16},{16,24},{24,28},{28,20},{20,12},{12,4},{4,0},{1,9},{9... | collective-permute-start | bytes 2359304 | tf_op jit(solution)/shard_map/ppermute | solution.py:974
  436.9 31.2 %collective-permute-start.77 = (bf16[256,1536]{1,0:T(8,128)(2,1)}, bf16[256,1536]{1,0:T(8,128)(2,1)}, u32[]{:S(2)}, u32[]{:S(2)}) collective-permute-start(bf16[256,1536]{1,0:T(8,128)(2,1)} %add_convert_fusion.8), channel_id=1, source_target_pairs={{8,0},{16,8},{24,16},{28,24},{20,28},{12,20},{4,12},{0,4},{9,1},{1... | collective-permute-start | bytes 2359304 | tf_op jit(solution)/shard_map/ppermute | solution.py:974
  440.7 31.5 %collective-permute-start.76 = (bf16[256,1536]{1,0:T(8,128)(2,1)}, bf16[256,1536]{1,0:T(8,128)(2,1)}, u32[]{:S(2)}, u32[]{:S(2)}) collective-permute-start(bf16[256,1536]{1,0:T(8,128)(2,1)} %add_convert_fusion.7), channel_id=1, source_target_pairs={{0,8},{8,16},{16,24},{24,28},{28,20},{20,12},{12,4},{4,0},{1,9},{9... | collective-permute-start | bytes 2359304 | tf_op jit(solution)/shard_map/ppermute | solution.py:974
  453.5 44.4 %collective-permute-start.81 = (bf16[256,1536]{1,0:T(8,128)(2,1)}, bf16[256,1536]{1,0:T(8,128)(2,1)}, u32[]{:S(2)}, u32[]{:S(2)}) collective-permute-start(bf16[256,1536]{1,0:T(8,128)(2,1)} %add_convert_fusion.6), channel_id=1, source_target_pairs={{8,0},{16,8},{24,16},{28,24},{20,28},{12,20},{4,12},{0,4},{9,1},{1... | collective-permute-start | bytes 2359304 | tf_op jit(solution)/shard_map/ppermute | solution.py:974
  457.2 40.7 %collective-permute-start.80 = (bf16[256,1536]{1,0:T(8,128)(2,1)}, bf16[256,1536]{1,0:T(8,128)(2,1)}, u32[]{:S(2)}, u32[]{:S(2)}) collective-permute-start(bf16[256,1536]{1,0:T(8,128)(2,1)} %add_convert_fusion.5), channel_id=1, source_target_pairs={{0,8},{8,16},{16,24},{24,28},{28,20},{20,12},{12,4},{4,0},{1,9},{9... | collective-permute-start | bytes 2359304 | tf_op jit(solution)/shard_map/ppermute | solution.py:974
  468.1 154.9 %reduce-scatter.11.cloned.1.call-start = ((), (), s32[]{:S(2)}) async-start(), calls=%async_computation.11 | async-start | bytes 5242880 | tf_op jit(solution)/shard_map/reduce_scatter | solution.py:1028
  470.7 31.5 %collective-permute-start.79 = (bf16[256,1536]{1,0:T(8,128)(2,1)}, bf16[256,1536]{1,0:T(8,128)(2,1)S(1)}, u32[]{:S(2)}, u32[]{:S(2)}) collective-permute-start(bf16[256,1536]{1,0:T(8,128)(2,1)} %add_convert_fusion.4), channel_id=1, source_target_pairs={{8,0},{16,8},{24,16},{28,24},{20,28},{12,20},{4,12},{0,4},{9,1},{1... | collective-permute-start | bytes 2359304 | tf_op jit(solution)/shard_map/ppermute | solution.py:974
  473.5 30.3 %collective-permute-start.78 = (bf16[256,1536]{1,0:T(8,128)(2,1)S(1)}, bf16[256,1536]{1,0:T(8,128)(2,1)S(1)}, u32[]{:S(2)}, u32[]{:S(2)}) collective-permute-start(bf16[256,1536]{1,0:T(8,128)(2,1)S(1)} %add_convert_fusion.3), channel_id=1, source_target_pairs={{0,8},{8,16},{16,24},{24,28},{28,20},{20,12},{12,4},{4,0},{1,9},{9... | collective-permute-start | bytes 2359304 | tf_op jit(solution)/shard_map/ppermute | solution.py:974
  499.3 26.0 %collective-permute-start.83 = (bf16[256,1536]{1,0:T(8,128)(2,1)S(1)}, bf16[256,1536]{1,0:T(8,128)(2,1)S(1)}, u32[]{:S(2)}, u32[]{:S(2)}) collective-permute-start(bf16[256,1536]{1,0:T(8,128)(2,1)S(1)} %add_convert_fusion.2), channel_id=1, source_target_pairs={{0,8},{8,16},{16,24},{24,28},{28,20},{20,12},{12,4},{4,0},{1,9},{9... | collective-permute-start | bytes 2359304 | tf_op jit(solution)/shard_map/ppermute | solution.py:974
  503.2 22.1 %collective-permute-start.82 = (bf16[256,1536]{1,0:T(8,128)(2,1)}, bf16[256,1536]{1,0:T(8,128)(2,1)S(1)}, u32[]{:S(2)}, u32[]{:S(2)}) collective-permute-start(bf16[256,1536]{1,0:T(8,128)(2,1)} %add_convert_fusion.1), channel_id=1, source_target_pairs={{8,0},{16,8},{24,16},{28,24},{20,28},{12,20},{4,12},{0,4},{9,1},{1... | collective-permute-start | bytes 2359304 | tf_op jit(solution)/shard_map/ppermute | solution.py:974
  513.5 22.6 %collective-permute-start.85 = (bf16[640,256]{1,0:T(8,128)(2,1)}, bf16[640,256]{1,0:T(8,128)(2,1)S(1)}, u32[]{:S(2)}, u32[]{:S(2)}) collective-permute-start(bf16[640,256]{1,0:T(8,128)(2,1)} %get-tuple-element.462), channel_id=1, source_target_pairs={{8,0},{16,8},{24,16},{28,24},{20,28},{12,20},{4,12},{0,4},{9,1},{1... | collective-permute-start | bytes 983048 | tf_op jit(solution)/shard_map/ppermute | solution.py:974
  514.9 19.6 %collective-permute-start.86 = (bf16[640,256]{1,0:T(8,128)(2,1)}, bf16[640,256]{1,0:T(8,128)(2,1)S(1)}, u32[]{:S(2)}, u32[]{:S(2)}) collective-permute-start(bf16[640,256]{1,0:T(8,128)(2,1)} %get-tuple-element.463), channel_id=1, source_target_pairs={{0,8},{8,16},{16,24},{24,28},{28,20},{20,12},{12,4},{4,0},{1,9},{9... | collective-permute-start | bytes 983048 | tf_op jit(solution)/shard_map/ppermute | solution.py:974
  (204 other events, 2685.5 us)
Sparse Core Ops, SparseCore 0:
  9.7 37.1 all-gather.4
  48.5 34.4 all-gather.6
  147.4 44.8 reduce-scatter.4
  195.7 34.4 all-gather.8
  364.3 43.5 reduce-scatter.6
  413.7 34.4 all-gather.10
  468.2 44.4 reduce-scatter.8
  579.0 44.0 reduce-scatter.10

commit v6 on v5

--- a/solution.py
+++ b/solution.py
@@ -1299,7 +1299,7 @@
     )
     lanes.did(7.5, mixer_in_grad)
     mixer_in_grad = tensor_reduce(mixer_in_grad)
-    arrival = lanes.now + 30.0
+    arrival = lanes.now + 50.0
 
     (mlp_sum,) = lanes.gate(mlp_sum)
     layer_out = ring.columns_out((middle + mlp_sum.astype(f32)).astype(bf16), shard)

time: 669 us -> 668 us (level)
    ppermute x105, waiting for transfers between devices: 170 us -> 179 us  [start(): value = lax.ppermute(operand, 'dp', self.ring.pairs[way])]
  transfers between devices with their start and end apart: 115 -> 115, of which waited for: 41 -> 43; matrix products, arithmetic and copies ran while one was open for 8% -> 8% of each run, Pallas kernels for 39% -> 38%
where the time goes in v6:
time: 668 us; the launch traced here: 658 us
  Pallas kernels  266 us (40%)
  waiting for transfers between devices  190 us (28%)
  starting transfers between devices  117 us (18%)
  other arithmetic  57.9 us (9%)
  between operations  15.9 us (2%)
  local copies, waits for them, and re-layouts  11.5 us (2%)
    ppermute x105, waiting for transfers between devices, start(): value = lax.ppermute(operand, 'dp', self.ring.pairs[way])  179 us
    ppermute x105, starting transfers between devices, start(): value = lax.ppermute(operand, 'dp', self.ring.pairs[way])  116 us
    pallas_call x6, Pallas kernels, weight_grads(): call(kernel, name, (pieces,), in_specs, [fixed(shape) for shape in shapes...  71.3 us
    pallas_call x6, Pallas kernels, spread(): pl.pallas_call(kernel, grid_spec=pltpu.PrefetchScalarGridSpec(num_scalar_...  57.5 us
    pallas_call x2, Pallas kernels, gated_forward(): call(kernel, 'gated_forward', (4,), [pl.BlockSpec((rows, features), lambd...  25.9 us
    convert_element_type x35, other arithmetic, operand(): value = (value.astype(f32) + got.astype(f32)).astype(bf16)  23.8 us
    pallas_call x1, Pallas kernels, core_backward(): pl.pallas_call(core_backward_kernel, grid_spec=pltpu.PrefetchScalarGridSp...  23.7 us
    pallas_call x2, Pallas kernels, gated_backward(): call(kernel, 'gated_backward', (4,), [pl.BlockSpec((rows, features), lamb...  17.1 us
  transfers between devices with their start and end apart: 115, of which 43 were waited for; matrix products, arithmetic and copies ran while one was open for 8% of the time, Pallas kernels for 38%

profile of v6, /device:TPU:0, one launch (start us, length us, event | category | flops | bytes accessed | tf_op | source)
XLA Modules:
  0.0 658.0 jit_solution(16977643985353102216)
XLA Ops:
  15.1 5.6 collective-permute-done.1.refs_2_
  27.6 6.8 %collective-permute-done.4.refs_7_ = bf16[256,256]{1,0:T(8,128)(2,1)S(1)} collective-permute-done((bf16[256,256]{1,0:T(8,128)(2,1)S(1)}, bf16[256,256]{1,0:T(8,128)(2,1)S(1)}, u32[]{:S(2)}, u32[]{:S(2)}) %collective-permute-start.4) | collective-permute-done | bytes 131104 | tf_op jit(solution)/shard_map/ppermute | solution.py:974
  52.6 3.8 collective-permute-done.15.refs_5_
  65.4 6.6 %unpack_tables.1 = (bf16[640,1280]{1,0:T(8,128)(2,1)}, f32[8,640]{1,0:T(8,128)}, f32[8,2048]{1,0:T(8,128)}) custom-call(s32[8]{0:T(128)} %compare_select_fusion.5.order_ref, bf16[256,256]{1,0:T(8,128)(2,1)} %copy-done.78, bf16[256,256]{1,0:T(8,128)(2,1)} %copy-done.124, bf16[256,256]{1,0:T(8,128)(2,1)} %copy-done.126, bf16[256,256]{1,0:T(8,128)(2,1)} %copy-done.128, ...), custom_call_target="tpu_custom_call" | custom-call | flops 6000000000 | bytes 30000000 | tf_op jit(solution)/shard_map/unpack_tables/pallas_call | solution.py:692
  73.6 7.1 %prepare.1 = (bf16[1024,2048]{1,0:T(8,128)(2,1)}, bf16[256,2048]{1,0:T(8,128)(2,1)}) custom-call(s32[8]{0:T(128)} %compare_select_fusion.5.order_ref, s32[1]{0:T(128)} %bitcast.place_ref, bf16[1024,2048]{1,0:T(8,128)(2,1)} %all-gather.5.cloned.1.call-done.value_ref, f32[1,2048]{1,0:T(1,128)} %get-tuple-element.616.gain_ref), custom_call_target="tpu_custom_call" | custom-call | flops 6000000000 | bytes 30000000 | tf_op jit(solution)/shard_map/prepare/pallas_call | solution.py:788
  85.3 6.4 collective-permute-done.19.refs_3_
  94.6 4.0 collective-permute-done.25.refs_12_.refs_4_
  107.5 11.3 %mixer_in.1.branch.entry_pre.refs_9_.entry_tail = f32[1024,1280]{1,0:T(8,128)} custom-call(bf16[1024,2048]{1,0:T(8,128)(2,1)} %get-tuple-element.315.refs_0_, bf16[256,640]{1,0:T(8,128)(2,1)} %refs_1_.8, bf16[256,640]{1,0:T(8,128)(2,1)} %copy-done.108, bf16[256,640]{1,0:T(8,128)(2,1)} %copy-done.112, bf16[256,640]{1,0:T(8,128)(2,1)} %collective-permute-done.11.refs_4_, ...), custom_call_target="tpu_custom_call" | custom-call | flops 6000000000 | bytes 30000000 | tf_op jit(solution)/shard_map/mixer_in/pallas_call | solution.py:465
  123.3 16.2 %core_forward.1 = (bf16[1024,640]{1,0:T(8,128)(2,1)}, f32[1024,640]{1,0:T(8,128)}, f32[1024,640]{1,0:T(8,128)}, f32[1024,640]{1,0:T(8,128)}, f32[1024,640]{1,0:T(8,128)}) custom-call(s32[1]{0:T(128)} %constant.88.clone.1.place, f32[1024,1280]{1,0:T(8,128)} %mixer_in.1.branch.entry_pre.refs_9_.entry_tail, ...), custom_call_target="tpu_custom_call" | custom-call | flops 6000000000 | bytes 30000000 | tf_op jit(solution)/shard_map/core_forward/pallas_call | solution.py:257
  140.3 7.1 %mixer_out.1 = bf16[1024,2048]{1,0:T(8,128)(2,1)} custom-call(s32[1]{0:T(128)} %bitcast.place_ref, bf16[1024,640]{1,0:T(8,128)(2,1)} %get-tuple-element.326.refs_0_, bf16[640,256]{1,0:T(8,128)(2,1)} %refs_1_.7, bf16[640,256]{1,0:T(8,128)(2,1)} %collective-permute-done.17.refs_2_, bf16[640,256]{1,0:T(8,128)(2,1)} %collective-permute-done.19.refs_3_, ...), custom_call_target="tpu_custom_call" | custom-call | flops 6000000000 | bytes 30000000 | tf_op jit(solution)/shard_map/mixer_out/pallas_call | solution.py:426
  152.6 5.6 move_columns.3.refs_2_.refs_0_
  158.2 10.9 %collective-permute-done.33.refs_2_ = bf16[256,1536]{1,0:T(8,128)(2,1)} collective-permute-done((bf16[256,1536]{1,0:T(8,128)(2,1)S(1)}, bf16[256,1536]{1,0:T(8,128)(2,1)}, u32[]{:S(2)}, u32[]{:S(2)}) %collective-permute-start.33) | collective-permute-done | bytes 786464 | tf_op jit(solution)/shard_map/ppermute | solution.py:974
  171.4 8.5 %collective-permute-done.37.refs_4_ = bf16[256,1536]{1,0:T(8,128)(2,1)} collective-permute-done((bf16[256,1536]{1,0:T(8,128)(2,1)}, bf16[256,1536]{1,0:T(8,128)(2,1)}, u32[]{:S(2)}, u32[]{:S(2)}) %collective-permute-start.37) | collective-permute-done | bytes 786464 | tf_op jit(solution)/shard_map/ppermute | solution.py:974
  180.6 7.8 %collective-permute-done.35.refs_3_ = bf16[256,1536]{1,0:T(8,128)(2,1)} collective-permute-done((bf16[256,1536]{1,0:T(8,128)(2,1)}, bf16[256,1536]{1,0:T(8,128)(2,1)}, u32[]{:S(2)}, u32[]{:S(2)}) %collective-permute-start.35) | collective-permute-done | bytes 786464 | tf_op jit(solution)/shard_map/ppermute | solution.py:974
  199.9 16.6 %collective-permute-done.41.refs_5_ = bf16[256,1536]{1,0:T(8,128)(2,1)S(1)} collective-permute-done((bf16[256,1536]{1,0:T(8,128)(2,1)}, bf16[256,1536]{1,0:T(8,128)(2,1)S(1)}, u32[]{:S(2)}, u32[]{:S(2)}) %collective-permute-start.41) | collective-permute-done | bytes 786464 | tf_op jit(solution)/shard_map/ppermute | solution.py:974
  220.1 6.3 collective-permute-done.39.refs_8_.refs_9_
  227.0 6.4 collective-permute-done.38.refs_4_
  235.7 12.9 %gated_forward.2 = (bf16[1024,768]{1,0:T(8,128)(2,1)}, bf16[1024,768]{1,0:T(8,128)(2,1)}, bf16[1024,768]{1,0:T(8,128)(2,1)}) custom-call(bf16[1024,2048]{1,0:T(8,128)(2,1)} %all-gather.9.cloned.1.call-done.refs_0_, bf16[256,1536]{1,0:T(8,128)(2,1)} %copy-done.24, bf16[256,1536]{1,0:T(8,128)(2,1)} %copy-done.93, ...), custom_call_target="tpu_custom_call" | custom-call | flops 6000000000 | bytes 30000000 | tf_op jit(solution)/shard_map/gated_forward/pallas_call | solution.py:538
  252.7 13.0 %gated_forward.3 = (bf16[1024,768]{1,0:T(8,128)(2,1)}, bf16[1024,768]{1,0:T(8,128)(2,1)}, bf16[1024,768]{1,0:T(8,128)(2,1)}) custom-call(bf16[1024,2048]{1,0:T(8,128)(2,1)} %all-gather.9.cloned.1.call-done.refs_0_, bf16[256,1536]{1,0:T(8,128)(2,1)} %copy-done.25, bf16[256,1536]{1,0:T(8,128)(2,1)} %collective-permute-done.33.refs_2_, ...), custom_call_target="tpu_custom_call" | custom-call | flops 6000000000 | bytes 30000000 | tf_op jit(solution)/shard_map/gated_forward/pallas_call | solution.py:538
  269.3 14.1 %down_grads.1 = (bf16[768,256]{1,0:T(8,128)(2,1)}, bf16[768,256]{1,0:T(8,128)(2,1)}, bf16[768,256]{1,0:T(8,128)(2,1)}, bf16[768,256]{1,0:T(8,128)(2,1)}, bf16[76...) custom-call(bf16[1024,768]{1,0:T(8,128)(2,1)} %get-tuple-element.422, ...), custom_call_target="tpu_custom_call" | custom-call | flops 6000000000 | bytes 30000000 | tf_op jit(solution)/shard_map/down_grads/pallas_call | solution.py:620
  287.8 7.8 %collective-permute-done.55.refs_5_.refs_6_ = bf16[768,256]{1,0:T(8,128)(2,1)S(1)} collective-permute-done((bf16[768,256]{1,0:T(8,128)(2,1)S(1)}, bf16[768,256]{1,0:T(8,128)(2,1)S(1)}, u32[]{:S(2)}, u32[]{:S(2)}) %collective-permute-start.55) | collective-permute-done | bytes 393248 | tf_op jit(solution)/shard_map/ppermute | solution.py:974
  297.1 8.5 %gated_backward.2.refs_0_.refs_1_ = bf16[1024,1536]{1,0:T(8,128)(2,1)} custom-call(bf16[1024,2048]{1,0:T(8,128)(2,1)} %move_columns.3.refs_2_.refs_0_, bf16[768,256]{1,0:T(8,128)(2,1)} %copy-done.42, bf16[768,256]{1,0:T(8,128)(2,1)} %collective-permute-done.45.refs_2_.refs_3_, bf16[768,256]{1,0:T(8,128)(2,1)} %copy-done.97, bf16[768,256]{1,0:T(8,128)(2,1)} %copy-done.101, ...), custom_call_target="tpu_custom_call" | custom-call | flops 6000000000 | bytes 30000000 | tf_op jit(solution)/shard_map/gated_backward/pallas_call | solution.py:566
  308.6 3.8 collective-permute-done.58
  322.6 8.5 %gated_backward.3.refs_0_.refs_1_ = bf16[1024,1536]{1,0:T(8,128)(2,1)} custom-call(bf16[1024,2048]{1,0:T(8,128)(2,1)} %move_columns.3.refs_2_.refs_0_, bf16[768,256]{1,0:T(8,128)(2,1)} %copy-done.41, bf16[768,256]{1,0:T(8,128)(2,1)} %collective-permute-done.43.refs_2_.refs_11_, bf16[768,256]{1,0:T(8,128)(2,1)} %copy-done.99, bf16[768,256]{1,0:T(8,128)(2,1)} %copy-done.103, ...), custom_call_target="tpu_custom_call" | custom-call | flops 6000000000 | bytes 30000000 | tf_op jit(solution)/shard_map/gated_backward/pallas_call | solution.py:566
  334.2 3.6 collective-permute-done.60
  339.4 11.6 %mlp_in_grad.2.refs_9_ = bf16[1024,2048]{1,0:T(8,128)(2,1)} custom-call(s32[1]{0:T(128)} %bitcast.place_ref, bf16[1024,1536]{1,0:T(8,128)(2,1)} %gated_backward.2.refs_0_.refs_1_, bf16[256,1536]{1,0:T(8,128)(2,1)} %copy-done.24, bf16[256,1536]{1,0:T(8,128)(2,1)} %copy-done.93, bf16[256,1536]{1,0:T(8,128)(2,1)} %collective-permute-done.29.refs_3_, ...), custom_call_target="tpu_custom_call" | custom-call | flops 6000000000 | bytes 30000000 | tf_op jit(solution)/shard_map/mlp_in_grad/pallas_call | solution.py:426
  352.5 11.8 %mlp_in_grad.3 = bf16[1024,2048]{1,0:T(8,128)(2,1)} custom-call(s32[1]{0:T(128)} %bitcast.place_ref, bf16[1024,1536]{1,0:T(8,128)(2,1)} %gated_backward.3.refs_0_.refs_1_, bf16[256,1536]{1,0:T(8,128)(2,1)} %copy-done.25, bf16[256,1536]{1,0:T(8,128)(2,1)} %collective-permute-done.33.refs_2_, bf16[256,1536]{1,0:T(8,128)(2,1)} %collective-permute-done.35.refs_3_, ...), custom_call_target="tpu_custom_call" | custom-call | flops 6000000000 | bytes 30000000 | tf_op jit(solution)/shard_map/mlp_in_grad/pallas_call | solution.py:426
  365.0 13.7 %gated_grads.2 = (bf16[256,1536]{1,0:T(8,128)(2,1)}, bf16[256,1536]{1,0:T(8,128)(2,1)}, bf16[256,1536]{1,0:T(8,128)(2,1)}, bf16[256,1536]{1,0:T(8,128)(2,1)}, bf...) custom-call(bf16[1024,2048]{1,0:T(8,128)(2,1)} %all-gather.9.cloned., ...), custom_call_target="tpu_custom_call" | custom-call | flops 6000000000 | bytes 30000000 | tf_op jit(solution)/shard_map/gated_grads/pallas_call | solution.py:620
  382.5 13.8 %gated_grads.3 = (bf16[256,1536]{1,0:T(8,128)(2,1)}, bf16[256,1536]{1,0:T(8,128)(2,1)}, bf16[256,1536]{1,0:T(8,128)(2,1)}, bf16[256,1536]{1,0:T(8,128)(2,1)}, bf...) custom-call(bf16[1024,2048]{1,0:T(8,128)(2,1)} %all-gather.9.cloned., ...), custom_call_target="tpu_custom_call" | custom-call | flops 6000000000 | bytes 30000000 | tf_op jit(solution)/shard_map/gated_grads/pallas_call | solution.py:620
  397.4 5.3 collective-permute-done.69
  403.8 4.4 reduce-scatter.7.cloned.1.call-done
  418.1 11.9 %mlp_out.1 = bf16[1024,2048]{1,0:T(8,128)(2,1)} custom-call(s32[1]{0:T(128)} %bitcast.place_ref, bf16[1024,768]{1,0:T(8,128)(2,1)} %get-tuple-element.422.refs_0_, bf16[1024,768]{1,0:T(8,128)(2,1)} %get-tuple-element.423.refs_1_, bf16[768,256]{1,0:T(8,128)(2,1)} %copy-done.42, bf16[768,256]{1,0:T(8,128)(2,1)} %collective-permute-done.45.refs_2_.refs_3_, ...), custom_call_target="tpu_custom_call" | custom-call | flops 6000000000 | bytes 30000000 | tf_op jit(solution)/shard_map/mlp_out/pallas_call | solution.py:426
  429.9 4.6 collective-permute-done.75
  441.4 10.0 %collective-permute-done.73 = bf16[256,1536]{1,0:T(8,128)(2,1)} collective-permute-done((bf16[256,1536]{1,0:T(8,128)(2,1)}, bf16[256,1536]{1,0:T(8,128)(2,1)}, u32[]{:S(2)}, u32[]{:S(2)}) %collective-permute-start.73) | collective-permute-done | bytes 786464 | tf_op jit(solution)/shard_map/ppermute | solution.py:974
  457.9 9.5 %mixer_back.1 = (f32[1024,640]{1,0:T(8,128)}, bf16[1024,640]{1,0:T(8,128)(2,1)}) custom-call(bf16[1024,2048]{1,0:T(8,128)(2,1)} %all-gather.11.cloned.1.call-done.refs_0_.refs_1_, bf16[640,256]{1,0:T(8,128)(2,1)} %refs_1_.7, bf16[640,256]{1,0:T(8,128)(2,1)} %collective-permute-done.17.refs_2_, bf16[640,256]{1,0:T(8,128)(2,1)} %collective-permute-done.19.refs_3_, ...), custom_call_target="tpu_custom_call" | custom-call | flops 6000000000 | bytes 30000000 | tf_op jit(solution)/shard_map/mixer_back/pallas_call | solution.py:496
  474.3 23.7 %core_backward.1 = (bf16[1024,640]{1,0:T(8,128)(2,1)}, f32[640,1280]{1,0:T(8,128)}, f32[8,640]{1,0:T(8,128)}) custom-call(s32[1]{0:T(128)} %constant.88.clone.1.place, f32[1024,640]{1,0:T(8,128)} %get-tuple-element.449.grad, f32[1024,1280]{1,0:T(8,128)} %mixer_in.1.branch.entry_pre.refs_9_.entry_tail, f32[1024,640]{1,0:T(8,128)} %get-tuple-element.450.mixed_in, ...), custom_call_target="tpu_custom_call" | custom-call | flops 6000000000 | bytes 30000000 | tf_op jit(solution)/shard_map/core_backward/pallas_call | solution.py:298
  504.0 9.7 %output_grads.1 = (bf16[640,256]{1,0:T(8,128)(2,1)}, bf16[640,256]{1,0:T(8,128)(2,1)}, bf16[640,256]{1,0:T(8,128)(2,1)}, bf16[640,256]{1,0:T(8,128)(2,1)}, bf16[...) custom-call(bf16[1024,640]{1,0:T(8,128)(2,1)} %get-tuple-element.326.refs_0, ...), custom_call_target="tpu_custom_call" | custom-call | flops 6000000000 | bytes 30000000 | tf_op jit(solution)/shard_map/output_grads/pallas_call | solution.py:620
  515.7 9.7 %branch_grads.1 = (bf16[256,640]{1,0:T(8,128)(2,1)}, bf16[256,640]{1,0:T(8,128)(2,1)}, bf16[256,640]{1,0:T(8,128)(2,1)}, bf16[256,640]{1,0:T(8,128)(2,1)}, bf16[...) custom-call(bf16[1024,2048]{1,0:T(8,128)(2,1)} %get-tuple-element.315.refs_, ...), custom_call_target="tpu_custom_call" | custom-call | flops 6000000000 | bytes 30000000 | tf_op jit(solution)/shard_map/branch_grads/pallas_call | solution.py:620
  527.5 7.1 %mixer_in_grad.2.refs_9_ = bf16[1024,2048]{1,0:T(8,128)(2,1)} custom-call(s32[1]{0:T(128)} %bitcast.place_ref, bf16[1024,640]{1,0:T(8,128)(2,1)} %get-tuple-element.475.refs_1_.refs_0_, bf16[256,640]{1,0:T(8,128)(2,1)} %refs_1_.8, bf16[256,640]{1,0:T(8,128)(2,1)} %copy-done.108, bf16[256,640]{1,0:T(8,128)(2,1)} %copy-done.112, ...), custom_call_target="tpu_custom_call" | custom-call | flops 6000000000 | bytes 30000000 | tf_op jit(solution)/shard_map/mixer_in_grad/pallas_call | solution.py:426
  539.3 6.2 collective-permute-done.89
  548.2 7.3 %pack_tables.1.refs_2_ = bf16[2048,256]{1,0:T(8,128)(2,1)} custom-call(s32[8]{0:T(128)} %compare_select_fusion.5.order_ref, f32[640,1280]{1,0:T(8,128)} %get-tuple-element.492.gate_ref, f32[8,640]{1,0:T(8,128)} %pad_maximum_fusion.6.small_ref), custom_call_target="tpu_custom_call" | custom-call | flops 6000000000 | bytes 30000000 | tf_op jit(solution)/shard_map/pack_tables/pallas_call | solution.py:745
  559.8 10.4 %input_grads.1 = (bf16[256,896]{1,0:T(8,128)(2,1)}, bf16[256,896]{1,0:T(8,128)(2,1)}, bf16[256,896]{1,0:T(8,128)(2,1)}, bf16[256,896]{1,0:T(8,128)(2,1)}, bf16[2...) custom-call(bf16[1024,2048]{1,0:T(8,128)(2,1)} %get-tuple-element.315.refs_0, ...), custom_call_target="tpu_custom_call" | custom-call | flops 6000000000 | bytes 30000000 | tf_op jit(solution)/shard_map/input_grads/pallas_call | solution.py:620
  570.9 8.0 %mixer_in_grad.3 = bf16[1024,2048]{1,0:T(8,128)(2,1)} custom-call(s32[1]{0:T(128)} %bitcast.place_ref, bf16[1024,640]{1,0:T(8,128)(2,1)} %get-tuple-element.510.refs_1_.refs_0_, bf16[256,640]{1,0:T(8,128)(2,1)} %refs_1_.9, bf16[256,640]{1,0:T(8,128)(2,1)} %copy-done.109, bf16[256,640]{1,0:T(8,128)(2,1)} %copy-done.115, bf16[256,640]{1,0:T(8,128)(2,1)} %copy-done.118, ...), custom_call_target="tpu_custom_call" | custom-call | flops 6000000000 | bytes 30000000 | tf_op jit(solution)/shard_map/mixer_in_grad/pallas_call | solution.py:426
  594.7 3.5 move_columns.4
  605.1 6.6 %collective-permute-done.101 = bf16[256,896]{1,0:T(8,128)(2,1)S(1)} collective-permute-done((bf16[256,896]{1,0:T(8,128)(2,1)S(1)}, bf16[256,896]{1,0:T(8,128)(2,1)S(1)}, u32[]{:S(2)}, u32[]{:S(2)}) %collective-permute-start.101) | collective-permute-done | bytes 458784 | tf_op jit(solution)/shard_map/ppermute | solution.py:974
  616.2 8.8 %collective-permute-done.102 = bf16[256,896]{1,0:T(8,128)(2,1)S(1)} collective-permute-done((bf16[256,896]{1,0:T(8,128)(2,1)S(1)}, bf16[256,896]{1,0:T(8,128)(2,1)S(1)}, u32[]{:S(2)}, u32[]{:S(2)}) %collective-permute-start.102) | collective-permute-done | bytes 458784 | tf_op jit(solution)/shard_map/ppermute | solution.py:974
  627.6 6.3 collective-permute-done.104
  644.4 3.6 fusion.4.refs_0_
  (594 shorter events, 225.3 us)
Async XLA Ops:
  7.3 66.3 %all-gather.5.cloned.1.call-start = ((), (), s32[]{:S(2)}) async-start(), calls=%async_computation.4 | async-start | bytes 5242880 | tf_op jit(solution)/shard_map/all_gather | solution.py:1024
  8.1 144.5 %all-gather.7.cloned.1.call-start = ((), (), s32[]{:S(2)}) async-start(), calls=%async_computation.6 | async-start | bytes 5242880 | tf_op jit(solution)/shard_map/all_gather | solution.py:1024
  8.8 183.7 %reduce-scatter.5.cloned.1.call-start = ((), (), s32[]{:S(2)}) async-start(), calls=%async_computation.5 | async-start | bytes 5242880 | tf_op jit(solution)/shard_map/reduce_scatter | solution.py:1028
  56.4 24.3 %collective-permute-start.17 = (bf16[640,256]{1,0:T(8,128)(2,1)}, bf16[640,256]{1,0:T(8,128)(2,1)}, u32[]{:S(2)}, u32[]{:S(2)}) collective-permute-start(bf16[640,256]{1,0:T(8,128)(2,1)} %refs_1_.7), channel_id=1, source_target_pairs={{8,0},{16,8},{24,16},{28,24},{20,28},{12,20},{4,12},{0,4},{9,1},{1... | collective-permute-start | bytes 983048 | tf_op jit(solution)/shard_map/ppermute | solution.py:974
  59.5 22.5 %collective-permute-start.16 = (bf16[256,640]{1,0:T(8,128)(2,1)S(1)}, bf16[256,640]{1,0:T(8,128)(2,1)S(1)}, u32[]{:S(2)}, u32[]{:S(2)}) collective-permute-start(bf16[256,640]{1,0:T(8,128)(2,1)S(1)} %collective-permute-done.14.refs_16_.refs_8_), channel_id=1, source_target_pairs={{0,8},{8,16},{16,24},{24,28},{28,20},{20,12},{12,4},{4,0},{1,9},{9... | collective-permute-start | bytes 983048 | tf_op jit(solution)/shard_map/ppermute | solution.py:974
  63.4 19.7 %collective-permute-start.21 = (bf16[256,640]{1,0:T(8,128)(2,1)S(1)}, bf16[256,640]{1,0:T(8,128)(2,1)S(1)}, u32[]{:S(2)}, u32[]{:S(2)}) collective-permute-start(bf16[256,640]{1,0:T(8,128)(2,1)S(1)} %collective-permute-done.13.refs_10_.refs_2_), channel_id=1, source_target_pairs={{8,0},{16,8},{24,16},{28,24},{20,28},{12,20},{4,12},{0,4},{9,1},{1... | collective-permute-start | bytes 983048 | tf_op jit(solution)/shard_map/ppermute | solution.py:974
  64.6 19.8 %collective-permute-start.20 = (bf16[640,256]{1,0:T(8,128)(2,1)}, bf16[640,256]{1,0:T(8,128)(2,1)}, u32[]{:S(2)}, u32[]{:S(2)}) collective-permute-start(bf16[640,256]{1,0:T(8,128)(2,1)} %refs_1_.7), channel_id=1, source_target_pairs={{0,8},{8,16},{16,24},{24,28},{28,20},{20,12},{12,4},{4,0},{1,9},{9... | collective-permute-start | bytes 983048 | tf_op jit(solution)/shard_map/ppermute | solution.py:974
  98.6 21.9 %collective-permute-start.26 = (bf16[256,1536]{1,0:T(8,128)(2,1)S(1)}, bf16[256,1536]{1,0:T(8,128)(2,1)S(1)}, u32[]{:S(2)}, u32[]{:S(2)}) collective-permute-start(bf16[256,1536]{1,0:T(8,128)(2,1)S(1)} %pad_maximum_fusion.3.refs_1_), channel_id=1, source_target_pairs={{8,0},{16,8},{24,16},{28,24},{20,28},{12,20},{4,12},{0,4},{9,1},{1... | collective-permute-start | bytes 2359304 | tf_op jit(solution)/shard_map/ppermute | solution.py:974
  106.7 32.9 %collective-permute-start.30 = (bf16[256,1536]{1,0:T(8,128)(2,1)S(1)}, bf16[256,1536]{1,0:T(8,128)(2,1)}, u32[]{:S(2)}, u32[]{:S(2)}) collective-permute-start(bf16[256,1536]{1,0:T(8,128)(2,1)S(1)} %pad_maximum_fusion.3.refs_1_), channel_id=1, source_target_pairs={{0,8},{8,16},{16,24},{24,28},{28,20},{20,12},{12,4},{4,0},{1,9},{9... | collective-permute-start | bytes 2359304 | tf_op jit(solution)/shard_map/ppermute | solution.py:974
  118.9 20.7 %collective-permute-start.28 = (bf16[256,1536]{1,0:T(8,128)(2,1)S(1)}, bf16[256,1536]{1,0:T(8,128)(2,1)}, u32[]{:S(2)}, u32[]{:S(2)}) collective-permute-start(bf16[256,1536]{1,0:T(8,128)(2,1)S(1)} %pad_maximum_fusion.4.refs_1_), channel_id=1, source_target_pairs={{0,8},{8,16},{16,24},{24,28},{28,20},{20,12},{12,4},{4,0},{1,9},{9... | collective-permute-start | bytes 2359304 | tf_op jit(solution)/shard_map/ppermute | solution.py:974
  120.5 19.1 %collective-permute-start.29 = (bf16[256,1536]{1,0:T(8,128)(2,1)S(1)}, bf16[256,1536]{1,0:T(8,128)(2,1)}, u32[]{:S(2)}, u32[]{:S(2)}) collective-permute-start(bf16[256,1536]{1,0:T(8,128)(2,1)S(1)} %collective-permute-done.26.refs_2_), channel_id=1, source_target_pairs={{8,0},{16,8},{24,16},{28,24},{20,28},{12,20},{4,12},{0,4},{9,1},{1... | collective-permute-start | bytes 2359304 | tf_op jit(solution)/shard_map/ppermute | solution.py:974
  147.5 88.2 %all-gather.9.cloned.1.call-start = ((), (), s32[]{:S(2)}) async-start(), calls=%async_computation.7 | async-start | bytes 5242880 | tf_op jit(solution)/shard_map/all_gather | solution.py:1024
  148.5 20.6 %collective-permute-start.33 = (bf16[256,1536]{1,0:T(8,128)(2,1)S(1)}, bf16[256,1536]{1,0:T(8,128)(2,1)}, u32[]{:S(2)}, u32[]{:S(2)}) collective-permute-start(bf16[256,1536]{1,0:T(8,128)(2,1)S(1)} %copy-done.26), channel_id=1, source_target_pairs={{8,0},{16,8},{24,16},{28,24},{20,28},{12,20},{4,12},{0,4},{9,1},{1... | collective-permute-start | bytes 2359304 | tf_op jit(solution)/shard_map/ppermute | solution.py:974
  149.6 20.8 %collective-permute-start.32 = (bf16[256,1536]{1,0:T(8,128)(2,1)}, bf16[256,1536]{1,0:T(8,128)(2,1)}, u32[]{:S(2)}, u32[]{:S(2)}) collective-permute-start(bf16[256,1536]{1,0:T(8,128)(2,1)} %collective-permute-done.30.refs_8_), channel_id=1, source_target_pairs={{0,8},{8,16},{16,24},{24,28},{28,20},{20,12},{12,4},{4,0},{1,9},{9... | collective-permute-start | bytes 2359304 | tf_op jit(solution)/shard_map/ppermute | solution.py:974
  150.6 29.4 %collective-permute-start.37 = (bf16[256,1536]{1,0:T(8,128)(2,1)}, bf16[256,1536]{1,0:T(8,128)(2,1)}, u32[]{:S(2)}, u32[]{:S(2)}) collective-permute-start(bf16[256,1536]{1,0:T(8,128)(2,1)} %collective-permute-done.29.refs_3_), channel_id=1, source_target_pairs={{8,0},{16,8},{24,16},{28,24},{20,28},{12,20},{4,12},{0,4},{9,1},{1... | collective-permute-start | bytes 2359304 | tf_op jit(solution)/shard_map/ppermute | solution.py:974
  151.7 29.0 %collective-permute-start.36 = (bf16[256,1536]{1,0:T(8,128)(2,1)}, bf16[256,1536]{1,0:T(8,128)(2,1)}, u32[]{:S(2)}, u32[]{:S(2)}) collective-permute-start(bf16[256,1536]{1,0:T(8,128)(2,1)} %collective-permute-done.28.refs_8_), channel_id=1, source_target_pairs={{0,8},{8,16},{16,24},{24,28},{28,20},{20,12},{12,4},{4,0},{1,9},{9... | collective-permute-start | bytes 2359304 | tf_op jit(solution)/shard_map/ppermute | solution.py:974
  169.1 19.3 %collective-permute-start.35 = (bf16[256,1536]{1,0:T(8,128)(2,1)}, bf16[256,1536]{1,0:T(8,128)(2,1)}, u32[]{:S(2)}, u32[]{:S(2)}) collective-permute-start(bf16[256,1536]{1,0:T(8,128)(2,1)} %collective-permute-done.33.refs_2_), channel_id=1, source_target_pairs={{8,0},{16,8},{24,16},{28,24},{20,28},{12,20},{4,12},{0,4},{9,1},{1... | collective-permute-start | bytes 2359304 | tf_op jit(solution)/shard_map/ppermute | solution.py:974
  195.7 212.4 %reduce-scatter.7.cloned.1.call-start = ((), (), s32[]{:S(2)}) async-start(), calls=%async_computation.8 | async-start | bytes 5242880 | tf_op jit(solution)/shard_map/reduce_scatter | solution.py:1028
  195.8 20.7 %collective-permute-start.41 = (bf16[256,1536]{1,0:T(8,128)(2,1)}, bf16[256,1536]{1,0:T(8,128)(2,1)S(1)}, u32[]{:S(2)}, u32[]{:S(2)}) collective-permute-start(bf16[256,1536]{1,0:T(8,128)(2,1)} %collective-permute-done.37.refs_4_), channel_id=1, source_target_pairs={{8,0},{16,8},{24,16},{28,24},{20,28},{12,20},{4,12},{0,4},{9,1},{1... | collective-permute-start | bytes 2359304 | tf_op jit(solution)/shard_map/ppermute | solution.py:974
  197.3 20.8 %collective-permute-start.40 = (bf16[256,1536]{1,0:T(8,128)(2,1)}, bf16[256,1536]{1,0:T(8,128)(2,1)}, u32[]{:S(2)}, u32[]{:S(2)}) collective-permute-start(bf16[256,1536]{1,0:T(8,128)(2,1)} %collective-permute-done.36.refs_7_), channel_id=1, source_target_pairs={{0,8},{8,16},{16,24},{24,28},{28,20},{20,12},{12,4},{4,0},{1,9},{9... | collective-permute-start | bytes 2359304 | tf_op jit(solution)/shard_map/ppermute | solution.py:974
  197.9 35.5 %collective-permute-start.38 = (bf16[256,1536]{1,0:T(8,128)(2,1)}, bf16[256,1536]{1,0:T(8,128)(2,1)S(1)}, u32[]{:S(2)}, u32[]{:S(2)}) collective-permute-start(bf16[256,1536]{1,0:T(8,128)(2,1)} %collective-permute-done.35.refs_3_), channel_id=1, source_target_pairs={{8,0},{16,8},{24,16},{28,24},{20,28},{12,20},{4,12},{0,4},{9,1},{1... | collective-permute-start | bytes 2359304 | tf_op jit(solution)/shard_map/ppermute | solution.py:974
  199.3 27.1 %collective-permute-start.39 = (bf16[768,256]{1,0:T(8,128)(2,1)S(1)}, bf16[768,256]{1,0:T(8,128)(2,1)S(1)}, u32[]{:S(2)}, u32[]{:S(2)}) collective-permute-start(bf16[768,256]{1,0:T(8,128)(2,1)S(1)} %get-tuple-element.335.refs_1_.refs_2_), channel_id=1, source_target_pairs={{0,8},{8,16},{16,24},{24,28},{28,20},{20,12},{12,4},{4,0},{1,9},{9... | collective-permute-start | bytes 1179656 | tf_op jit(solution)/shard_map/ppermute | solution.py:974
  218.1 32.1 %collective-permute-start.44 = (bf16[256,1536]{1,0:T(8,128)(2,1)}, bf16[256,1536]{1,0:T(8,128)(2,1)}, u32[]{:S(2)}, u32[]{:S(2)}) collective-permute-start(bf16[256,1536]{1,0:T(8,128)(2,1)} %collective-permute-done.40.refs_6_), channel_id=1, source_target_pairs={{0,8},{8,16},{16,24},{24,28},{28,20},{20,12},{12,4},{4,0},{1,9},{9... | collective-permute-start | bytes 2359304 | tf_op jit(solution)/shard_map/ppermute | solution.py:974
  218.7 30.0 %collective-permute-start.45 = (bf16[768,256]{1,0:T(8,128)(2,1)S(1)}, bf16[768,256]{1,0:T(8,128)(2,1)}, u32[]{:S(2)}, u32[]{:S(2)}) collective-permute-start(bf16[768,256]{1,0:T(8,128)(2,1)S(1)} %get-tuple-element.335.refs_1_.refs_2_), channel_id=1, source_target_pairs={{8,0},{16,8},{24,16},{28,24},{20,28},{12,20},{4,12},{0,4},{9,1},{1... | collective-permute-start | bytes 1179656 | tf_op jit(solution)/shard_map/ppermute | solution.py:974
  226.4 25.8 %collective-permute-start.42 = (bf16[768,256]{1,0:T(8,128)(2,1)S(1)}, bf16[768,256]{1,0:T(8,128)(2,1)}, u32[]{:S(2)}, u32[]{:S(2)}) collective-permute-start(bf16[768,256]{1,0:T(8,128)(2,1)S(1)} %collective-permute-done.39.refs_8_.refs_9_), channel_id=1, source_target_pairs={{0,8},{8,16},{16,24},{24,28},{28,20},{20,12},{12,4},{4,0},{1,9},{9... | collective-permute-start | bytes 1179656 | tf_op jit(solution)/shard_map/ppermute | solution.py:974
  285.0 20.6 %collective-permute-start.54 = (bf16[768,256]{1,0:T(8,128)(2,1)S(1)}, bf16[768,256]{1,0:T(8,128)(2,1)S(1)}, u32[]{:S(2)}, u32[]{:S(2)}) collective-permute-start(bf16[768,256]{1,0:T(8,128)(2,1)S(1)} %collective-permute-done.51.refs_7_.refs_16_), channel_id=1, source_target_pairs={{0,8},{8,16},{16,24},{24,28},{28,20},{20,12},{12,4},{4,0},{1,9},{9... | collective-permute-start | bytes 1179656 | tf_op jit(solution)/shard_map/ppermute | solution.py:974
  285.6 20.7 %collective-permute-start.53 = (bf16[768,256]{1,0:T(8,128)(2,1)}, bf16[768,256]{1,0:T(8,128)(2,1)S(1)}, u32[]{:S(2)}, u32[]{:S(2)}) collective-permute-start(bf16[768,256]{1,0:T(8,128)(2,1)} %get-tuple-element.359), channel_id=1, source_target_pairs={{8,0},{16,8},{24,16},{28,24},{20,28},{12,20},{4,12},{0,4},{9,1},{1... | collective-permute-start | bytes 1179656 | tf_op jit(solution)/shard_map/ppermute | solution.py:974
  287.1 20.9 %collective-permute-start.59 = (bf16[768,256]{1,0:T(8,128)(2,1)}, bf16[768,256]{1,0:T(8,128)(2,1)S(1)}, u32[]{:S(2)}, u32[]{:S(2)}) collective-permute-start(bf16[768,256]{1,0:T(8,128)(2,1)} %get-tuple-element.362), channel_id=1, source_target_pairs={{0,8},{8,16},{16,24},{24,28},{28,20},{20,12},{12,4},{4,0},{1,9},{9... | collective-permute-start | bytes 1179656 | tf_op jit(solution)/shard_map/ppermute | solution.py:974
  308.0 23.1 %collective-permute-start.63 = (bf16[768,256]{1,0:T(8,128)(2,1)S(1)}, bf16[768,256]{1,0:T(8,128)(2,1)S(1)}, u32[]{:S(2)}, u32[]{:S(2)}) collective-permute-start(bf16[768,256]{1,0:T(8,128)(2,1)S(1)} %add_convert_fusion.24), channel_id=1, source_target_pairs={{0,8},{8,16},{16,24},{24,28},{28,20},{20,12},{12,4},{4,0},{1,9},{9... | collective-permute-start | bytes 1179656 | tf_op jit(solution)/shard_map/ppermute | solution.py:974
  312.6 19.2 %collective-permute-start.62 = (bf16[768,256]{1,0:T(8,128)(2,1)S(1)}, bf16[768,256]{1,0:T(8,128)(2,1)S(1)}, u32[]{:S(2)}, u32[]{:S(2)}) collective-permute-start(bf16[768,256]{1,0:T(8,128)(2,1)S(1)} %add_convert_fusion.23), channel_id=1, source_target_pairs={{8,0},{16,8},{24,16},{28,24},{20,28},{12,20},{4,12},{0,4},{9,1},{1... | collective-permute-start | bytes 1179656 | tf_op jit(solution)/shard_map/ppermute | solution.py:974
  364.4 93.5 %all-gather.11.cloned.1.call-start = ((), (), s32[]{:S(2)}) async-start(), calls=%async_computation.9 | async-start | bytes 5242880 | tf_op jit(solution)/shard_map/all_gather | solution.py:1024
  381.0 21.7 %collective-permute-start.69 = (bf16[256,1536]{1,0:T(8,128)(2,1)}, bf16[256,1536]{1,0:T(8,128)(2,1)S(1)}, u32[]{:S(2)}, u32[]{:S(2)}) collective-permute-start(bf16[256,1536]{1,0:T(8,128)(2,1)} %get-tuple-element.409), channel_id=1, source_target_pairs={{0,8},{8,16},{16,24},{24,28},{28,20},{20,12},{12,4},{4,0},{1,9},{9... | collective-permute-start | bytes 2359304 | tf_op jit(solution)/shard_map/ppermute | solution.py:974
  413.7 178.2 %reduce-scatter.9.cloned.1.call-start = ((), (), s32[]{:S(2)}) async-start(), calls=%async_computation.10 | async-start | bytes 5242880 | tf_op jit(solution)/shard_map/reduce_scatter | solution.py:1028
  413.8 20.8 %collective-permute-start.75 = (bf16[256,1536]{1,0:T(8,128)(2,1)}, bf16[256,1536]{1,0:T(8,128)(2,1)}, u32[]{:S(2)}, u32[]{:S(2)}) collective-permute-start(bf16[256,1536]{1,0:T(8,128)(2,1)} %get-tuple-element.415), channel_id=1, source_target_pairs={{8,0},{16,8},{24,16},{28,24},{20,28},{12,20},{4,12},{0,4},{9,1},{1... | collective-permute-start | bytes 2359304 | tf_op jit(solution)/shard_map/ppermute | solution.py:974
  415.3 23.3 %collective-permute-start.74 = (bf16[256,1536]{1,0:T(8,128)(2,1)}, bf16[256,1536]{1,0:T(8,128)(2,1)}, u32[]{:S(2)}, u32[]{:S(2)}) collective-permute-start(bf16[256,1536]{1,0:T(8,128)(2,1)} %get-tuple-element.416), channel_id=1, source_target_pairs={{0,8},{8,16},{16,24},{24,28},{28,20},{20,12},{12,4},{4,0},{1,9},{9... | collective-permute-start | bytes 2359304 | tf_op jit(solution)/shard_map/ppermute | solution.py:974
  415.9 35.6 %collective-permute-start.73 = (bf16[256,1536]{1,0:T(8,128)(2,1)}, bf16[256,1536]{1,0:T(8,128)(2,1)}, u32[]{:S(2)}, u32[]{:S(2)}) collective-permute-start(bf16[256,1536]{1,0:T(8,128)(2,1)} %add_convert_fusion.10), channel_id=1, source_target_pairs={{8,0},{16,8},{24,16},{28,24},{20,28},{12,20},{4,12},{0,4},{9,1},{1... | collective-permute-start | bytes 2359304 | tf_op jit(solution)/shard_map/ppermute | solution.py:974
  417.3 37.8 %collective-permute-start.72 = (bf16[256,1536]{1,0:T(8,128)(2,1)}, bf16[256,1536]{1,0:T(8,128)(2,1)}, u32[]{:S(2)}, u32[]{:S(2)}) collective-permute-start(bf16[256,1536]{1,0:T(8,128)(2,1)} %add_convert_fusion.9), channel_id=1, source_target_pairs={{0,8},{8,16},{16,24},{24,28},{28,20},{20,12},{12,4},{4,0},{1,9},{9... | collective-permute-start | bytes 2359304 | tf_op jit(solution)/shard_map/ppermute | solution.py:974
  437.1 31.2 %collective-permute-start.77 = (bf16[256,1536]{1,0:T(8,128)(2,1)}, bf16[256,1536]{1,0:T(8,128)(2,1)}, u32[]{:S(2)}, u32[]{:S(2)}) collective-permute-start(bf16[256,1536]{1,0:T(8,128)(2,1)} %add_convert_fusion.8), channel_id=1, source_target_pairs={{8,0},{16,8},{24,16},{28,24},{20,28},{12,20},{4,12},{0,4},{9,1},{1... | collective-permute-start | bytes 2359304 | tf_op jit(solution)/shard_map/ppermute | solution.py:974
  440.9 31.5 %collective-permute-start.76 = (bf16[256,1536]{1,0:T(8,128)(2,1)}, bf16[256,1536]{1,0:T(8,128)(2,1)}, u32[]{:S(2)}, u32[]{:S(2)}) collective-permute-start(bf16[256,1536]{1,0:T(8,128)(2,1)} %add_convert_fusion.7), channel_id=1, source_target_pairs={{0,8},{8,16},{16,24},{24,28},{28,20},{20,12},{12,4},{4,0},{1,9},{9... | collective-permute-start | bytes 2359304 | tf_op jit(solution)/shard_map/ppermute | solution.py:974
  453.7 44.4 %collective-permute-start.81 = (bf16[256,1536]{1,0:T(8,128)(2,1)}, bf16[256,1536]{1,0:T(8,128)(2,1)}, u32[]{:S(2)}, u32[]{:S(2)}) collective-permute-start(bf16[256,1536]{1,0:T(8,128)(2,1)} %add_convert_fusion.6), channel_id=1, source_target_pairs={{8,0},{16,8},{24,16},{28,24},{20,28},{12,20},{4,12},{0,4},{9,1},{1... | collective-permute-start | bytes 2359304 | tf_op jit(solution)/shard_map/ppermute | solution.py:974
  457.4 40.7 %collective-permute-start.80 = (bf16[256,1536]{1,0:T(8,128)(2,1)}, bf16[256,1536]{1,0:T(8,128)(2,1)}, u32[]{:S(2)}, u32[]{:S(2)}) collective-permute-start(bf16[256,1536]{1,0:T(8,128)(2,1)} %add_convert_fusion.5), channel_id=1, source_target_pairs={{0,8},{8,16},{16,24},{24,28},{28,20},{20,12},{12,4},{4,0},{1,9},{9... | collective-permute-start | bytes 2359304 | tf_op jit(solution)/shard_map/ppermute | solution.py:974
  468.3 174.3 %reduce-scatter.11.cloned.1.call-start = ((), (), s32[]{:S(2)}) async-start(), calls=%async_computation.11 | async-start | bytes 5242880 | tf_op jit(solution)/shard_map/reduce_scatter | solution.py:1028
  470.9 31.5 %collective-permute-start.79 = (bf16[256,1536]{1,0:T(8,128)(2,1)}, bf16[256,1536]{1,0:T(8,128)(2,1)S(1)}, u32[]{:S(2)}, u32[]{:S(2)}) collective-permute-start(bf16[256,1536]{1,0:T(8,128)(2,1)} %add_convert_fusion.4), channel_id=1, source_target_pairs={{8,0},{16,8},{24,16},{28,24},{20,28},{12,20},{4,12},{0,4},{9,1},{1... | collective-permute-start | bytes 2359304 | tf_op jit(solution)/shard_map/ppermute | solution.py:974
  473.7 30.3 %collective-permute-start.78 = (bf16[256,1536]{1,0:T(8,128)(2,1)S(1)}, bf16[256,1536]{1,0:T(8,128)(2,1)S(1)}, u32[]{:S(2)}, u32[]{:S(2)}) collective-permute-start(bf16[256,1536]{1,0:T(8,128)(2,1)S(1)} %add_convert_fusion.3), channel_id=1, source_target_pairs={{0,8},{8,16},{16,24},{24,28},{28,20},{20,12},{12,4},{4,0},{1,9},{9... | collective-permute-start | bytes 2359304 | tf_op jit(solution)/shard_map/ppermute | solution.py:974
  499.5 25.9 %collective-permute-start.83 = (bf16[256,1536]{1,0:T(8,128)(2,1)S(1)}, bf16[256,1536]{1,0:T(8,128)(2,1)S(1)}, u32[]{:S(2)}, u32[]{:S(2)}) collective-permute-start(bf16[256,1536]{1,0:T(8,128)(2,1)S(1)} %add_convert_fusion.2), channel_id=1, source_target_pairs={{0,8},{8,16},{16,24},{24,28},{28,20},{20,12},{12,4},{4,0},{1,9},{9... | collective-permute-start | bytes 2359304 | tf_op jit(solution)/shard_map/ppermute | solution.py:974
  503.4 22.0 %collective-permute-start.82 = (bf16[256,1536]{1,0:T(8,128)(2,1)}, bf16[256,1536]{1,0:T(8,128)(2,1)S(1)}, u32[]{:S(2)}, u32[]{:S(2)}) collective-permute-start(bf16[256,1536]{1,0:T(8,128)(2,1)} %add_convert_fusion.1), channel_id=1, source_target_pairs={{8,0},{16,8},{24,16},{28,24},{20,28},{12,20},{4,12},{0,4},{9,1},{1... | collective-permute-start | bytes 2359304 | tf_op jit(solution)/shard_map/ppermute | solution.py:974
  513.7 22.6 %collective-permute-start.85 = (bf16[640,256]{1,0:T(8,128)(2,1)}, bf16[640,256]{1,0:T(8,128)(2,1)S(1)}, u32[]{:S(2)}, u32[]{:S(2)}) collective-permute-start(bf16[640,256]{1,0:T(8,128)(2,1)} %get-tuple-element.462), channel_id=1, source_target_pairs={{8,0},{16,8},{24,16},{28,24},{20,28},{12,20},{4,12},{0,4},{9,1},{1... | collective-permute-start | bytes 983048 | tf_op jit(solution)/shard_map/ppermute | solution.py:974
  515.1 19.5 %collective-permute-start.86 = (bf16[640,256]{1,0:T(8,128)(2,1)}, bf16[640,256]{1,0:T(8,128)(2,1)S(1)}, u32[]{:S(2)}, u32[]{:S(2)}) collective-permute-start(bf16[640,256]{1,0:T(8,128)(2,1)} %get-tuple-element.463), channel_id=1, source_target_pairs={{0,8},{8,16},{16,24},{24,28},{28,20},{20,12},{12,4},{4,0},{1,9},{9... | collective-permute-start | bytes 983048 | tf_op jit(solution)/shard_map/ppermute | solution.py:974
  (200 other events, 2615.6 us)
Sparse Core Ops, SparseCore 0:
  9.7 37.1 all-gather.4
  48.5 34.4 all-gather.6
  147.6 44.8 reduce-scatter.4
  195.9 34.4 all-gather.8
  364.5 43.6 reduce-scatter.6
  413.8 34.4 all-gather.10
  468.4 44.5 reduce-scatter.8
  579.1 44.0 reduce-scatter.10
